TPU v7x, 512 devices: a whole 4x8x8 slice. The times are simulated.
512 devices in a mesh: seq: 32 (over x, z), head: 16 (over y, core).
Axes of the slice: x: 4, y: 8, z: 8, core: 2. Of those that a mesh axis runs over, the one named last changes fastest.
Arguments:
- queries: bfloat16 [32768, 16, 128], P('seq', 'head'), may hold values from -6 to 6
- keys: bfloat16 [32768, 16, 128], P('seq', 'head'), may hold values from -0.26516504 to 0.26516504
- values: bfloat16 [32768, 16, 128], P('seq', 'head'), may hold values from -6 to 6
- key_gain: float32 [16, 128], P('head'), may hold values from 0.25 to 2.5
- reg: float32 [16], P('head'), may hold values from 0.5 to 4
- norm_gain: float32 [16, 128], P('head'), may hold values from 0.5 to 1.5
- out_weight: bfloat16 [2048, 2048], P('head'), may hold values from -0.1875 to 0.1875
Outputs:
- mixed: bfloat16 [32768, 2048], P('seq', 'head')
All inputs are finite; a program needn't handle non-finite values.
Results may differ from a plain program's by a relative error of at most 0.0058.
Values sent between devices are 32-bit elements; how exact they have to be, the bound alone decides.
No kernel may reach another device: no remote copies, remote signals or barrier semaphores. Data moves between devices by JAX's collectives and lax.ppermute only.
A program may use at most 64 MiB of HBM per device.

v0:
```python
import jax
import jax.numpy as jnp
from jax import lax
from jax.experimental import pallas as pl
from jax.experimental.pallas import tpu as pltpu
from jax.sharding import PartitionSpec as P

ITERS = 15
BLOCK = 128
F32 = jnp.float32
BF16 = jnp.bfloat16


def mm(a, b):
    return jnp.dot(a, b, preferred_element_type=F32)


def halves(value):
    high = value.astype(BF16)
    return high, (value - high.astype(F32)).astype(BF16)


def state_kernel(k_ref, v_ref, gain_ref, out_ref):
    gained = (k_ref[...].astype(F32) * gain_ref[...]).astype(BF16)
    width = gained.shape[1]
    over_tokens = (((0,), (0,)), ((), ()))
    out_ref[0:width, :] = lax.dot_general(
        gained, gained, over_tokens, preferred_element_type=F32
    )
    out_ref[width:, :] = lax.dot_general(
        v_ref[...], gained, over_tokens, preferred_element_type=F32
    )


def local_state(keys, values, gain):
    width = keys.shape[1]
    return pl.pallas_call(
        state_kernel,
        out_shape=jax.ShapeDtypeStruct((2 * width, width), F32),
        name="local_state",
    )(keys, values, gain)


def prefix_kernel(x_ref, o_ref):
    pieces, rows = o_ref.shape[0], o_ref.shape[1]
    total = jnp.zeros(o_ref.shape[1:], F32)
    for piece in range(pieces):
        o_ref[piece] = total
        total = total + x_ref[piece]


def exclusive(pieces):
    return pl.pallas_call(
        prefix_kernel,
        out_shape=jax.ShapeDtypeStruct(pieces.shape, F32),
        name="prefix",
    )(pieces)


def solve_kernel(
    reg_ref, q_ref, k_ref, v_ref, before_ref, gain_ref, norm_ref, out_ref,
    first, second, last, x_ref, r_ref, p_ref,
):
    width = q_ref.shape[1]
    blocks = q_ref.shape[0] // BLOCK
    lam = reg_ref[0]
    row = lax.broadcasted_iota(jnp.int32, (BLOCK, BLOCK), 0)
    col = lax.broadcasted_iota(jnp.int32, (BLOCK, BLOCK), 1)
    causal = row <= col
    h_state = before_ref[0:width, :]
    g_state = before_ref[width:, :]
    gain = gain_ref[...]
    starts = []
    for b in range(blocks):
        rows = pl.ds(b * BLOCK, BLOCK)
        key = (k_ref[rows, :].astype(F32) * gain).astype(BF16)
        key_t = key.astype(F32).T.astype(BF16)
        val_t = v_ref[rows, :].astype(F32).T.astype(BF16)
        high, low = halves(h_state)
        first[b, 0:width, 0:width] = high
        first[b, 0:width, width:] = high
        first[b, width:, 0:width] = key
        first[b, width:, width:] = key
        second[b, :, 0:BLOCK] = key_t
        second[b, :, BLOCK : 2 * BLOCK] = key_t
        second[b, :, 2 * BLOCK :] = low
        high, low = halves(g_state)
        last[b, :, 0:BLOCK] = val_t
        last[b, :, BLOCK : 2 * BLOCK] = val_t
        last[b, :, 2 * BLOCK : 3 * BLOCK] = low
        last[b, :, 3 * BLOCK : 4 * BLOCK] = high
        if b + 1 < blocks:
            h_state = h_state + mm(key_t, key)
            g_state = g_state + mm(val_t, key)
        query = q_ref[rows, :].astype(F32).T
        x_ref[b] = jnp.zeros_like(query)
        r_ref[b] = query
        p_ref[b] = query
        starts.append(jnp.sum(query * query, axis=0, keepdims=True))

    def step(_, rrs):
        news = []
        for b in range(blocks):
            p = p_ref[b]
            p_high, p_low = halves(p)
            one = mm(first[b], jnp.concatenate([p_high, p_low], axis=0))
            s_high, s_low = halves(jnp.where(causal, one[width:], 0.0))
            two = mm(second[b], jnp.concatenate([s_high, s_low, p_high], axis=0))
            w = one[:width] + two + lam * p
            rr = rrs[b]
            active = rr > 1e-30
            curve = jnp.sum(p * w, axis=0, keepdims=True)
            alpha = jnp.where(active, rr / jnp.where(active, curve, 1.0), 0.0)
            x_ref[b] = x_ref[b] + alpha * p
            r = r_ref[b] - alpha * w
            r_ref[b] = r
            new = jnp.sum(r * r, axis=0, keepdims=True)
            ratio = jnp.where(active, new / jnp.where(active, rr, 1.0), 0.0)
            p_ref[b] = r + ratio * p
            news.append(new)
        return tuple(news)

    lax.fori_loop(0, ITERS, step, tuple(starts))

    norm_col = jnp.broadcast_to(norm_ref[...], (BLOCK, width)).T
    for b in range(blocks):
        x_high, x_low = halves(x_ref[b])
        key = first[b, width:, :]
        scores = mm(key, jnp.concatenate([x_high, x_low], axis=0))
        s_high, s_low = halves(jnp.where(causal, scores, 0.0))
        read = mm(
            last[b],
            jnp.concatenate([s_high, s_low, x_high, x_high], axis=0),
        ) + mm(last[b, :, 3 * BLOCK :], x_low)
        square = jnp.mean(read * read, axis=0, keepdims=True)
        normed = read * norm_col * lax.rsqrt(square + 1e-06)
        out_ref[:, b * BLOCK : (b + 1) * BLOCK] = normed.astype(BF16)


def solve(reg, queries, keys, values, before, gain, norm_gain):
    tokens, width = queries.shape
    blocks = tokens // BLOCK
    vmem = pl.BlockSpec(memory_space=pltpu.VMEM)
    return pl.pallas_call(
        solve_kernel,
        out_shape=jax.ShapeDtypeStruct((width, tokens), BF16),
        in_specs=[pl.BlockSpec(memory_space=pltpu.SMEM)] + [vmem] * 6,
        out_specs=vmem,
        scratch_shapes=[
            pltpu.VMEM((blocks, 2 * BLOCK, 2 * width), BF16),
            pltpu.VMEM((blocks, width, 3 * BLOCK), BF16),
            pltpu.VMEM((blocks, width, 4 * BLOCK), BF16),
            pltpu.VMEM((blocks, width, BLOCK), F32),
            pltpu.VMEM((blocks, width, BLOCK), F32),
            pltpu.VMEM((blocks, width, BLOCK), F32),
        ],
        compiler_params=pltpu.CompilerParams(vmem_limit_bytes=40 * 2**20),
        name="solve",
    )(reg, queries, keys, values, before, gain, norm_gain)


def body(queries, keys, values, key_gain, reg, norm_gain, out_weight):
    width = keys.shape[2]
    devices = lax.axis_size("seq")
    key_rows, value_rows, query_rows = keys[:, 0, :], values[:, 0, :], queries[:, 0, :]
    state = local_state(key_rows, value_rows, key_gain)
    rows = 2 * width // devices
    parts = lax.all_to_all(
        state.reshape(devices, rows, width), "seq", 0, 0
    )
    earlier = exclusive(parts)
    before = lax.all_to_all(earlier, "seq", 0, 0)
    before = before.reshape(2 * width, width)
    normed = solve(reg, query_rows, key_rows, value_rows, before, key_gain, norm_gain)
    summed = lax.psum_scatter(
        lax.dot_general(
            out_weight, normed, (((0,), (0,)), ((), ())), preferred_element_type=F32
        ),
        "head",
        scatter_dimension=0,
        tiled=True,
    )
    return summed.T.astype(BF16)


def solution(mesh):
    return jax.shard_map(
        body,
        mesh=mesh,
        in_specs=(
            P("seq", "head", None),
            P("seq", "head", None),
            P("seq", "head", None),
            P("head", None),
            P("head"),
            P("head", None),
            P("head", None),
        ),
        out_specs=P("seq", "head"),
        check_vma=False,
    )
```

profile of v0, /device:TPU:1, one launch (start us, length us, event | category | flops | bytes accessed | tf_op | source)
XLA Modules:
  0.0 165.9 jit_solution(15897089840798990590)
XLA Ops:
  6.5 0.0 copy-start
  6.5 2.1 %local_state.1 = f32[256,128]{1,0:T(8,128)} custom-call(bf16[1024,128]{1,0:T(8,128)(2,1)} %bitcast.11, bf16[1024,128]{1,0:T(8,128)(2,1)} %bitcast.13, f32[1,128]{1,0:T(1,128)} %gain_ref.3), custom_call_target="tpu_custom_call" | custom-call | tf_op jit(solution)/shard_map/local_state/pallas_call | solution.py:37
  8.6 23.0 %all_to_all.10.x_ref = f32[32,8,128]{2,1,0:T(8,128)} all-to-all(f32[32,8,128]{2,1,0:T(8,128)} %bitcast.17), channel_id=1, replica_groups=mesh['seq'=32,'head'=16] {'seq'}, dimensions={0} | all-to-all | bytes 262144 | tf_op jit(solution)/shard_map/all_to_all | solution.py:168
  31.6 1.6 prefix.1
  33.2 3.9 %all-to-all-start.1 = ((f32[32,8,128]{2,1,0:T(8,128)}), f32[32,8,128]{2,1,0:T(8,128)S(1)}, u32[]{:S(2)}, u32[]{:S(2)}) async-start(f32[32,8,128]{2,1,0:T(8,128)} %prefix.1), calls=%async_computation.1 | async-start | bytes 262144 | tf_op jit(solution)/shard_map/all_to_all | solution.py:172
  37.1 0.0 reduce-scatter.2.cloned.1.call-start
  37.8 8.4 %all-to-all-done.1 = f32[32,8,128]{2,1,0:T(8,128)S(1)} async-done(((f32[32,8,128]{2,1,0:T(8,128)}), f32[32,8,128]{2,1,0:T(8,128)S(1)}, u32[]{:S(2)}, u32[]{:S(2)}) %all-to-all-start.1) | async-done | bytes 131104 | tf_op jit(solution)/shard_map/all_to_all | solution.py:172
  46.2 0.0 copy-start.1
  46.2 0.9 copy-done.1
  47.2 0.0 copy-start.2
  47.2 0.9 copy-done.2
  48.1 0.0 copy-start.3
  48.1 0.9 copy-done.3
  49.1 0.0 copy-start.4
  49.1 0.7 copy-done.4
  49.7 0.0 copy-start.5
  49.7 0.7 copy-done.5
  50.4 33.9 %solve.1 = bf16[128,1024]{1,0:T(8,128)(2,1)S(1)} custom-call(f32[1]{0:T(128)S(6)} %copy.8.reg_ref, bf16[1024,128]{1,0:T(8,128)(2,1)S(1)} %bitcast.16, bf16[1024,128]{1,0:T(8,128)(2,1)S(1)} %bitcast.12, bf16[1024,128]{1,0:T(8,128)(2,1)S(1)} %bitcast.14, f32[256,128]{1,0:T(8,128)S(1)} %bitcast.15, f32[1,128]{1,0:T(1,128)S(1)} %copy-done.4, f32[1,128]{1,0:T(1,128)S(1)} %copy-done.5), custom_call_target="tpu_custom_call" | custom-call | tf_op jit(solution)/shard_map/solve/pallas_call | solution.py:144
  84.3 0.0 copy-done
  84.3 4.5 %convolution_bitcast_fusion = f32[2048,1024]{0,1:T(8,128)} fusion(bf16[128,1024]{1,0:T(8,128)(2,1)S(1)} %solve.1, bf16[128,2048]{1,0:T(8,128)(2,1)S(1)} %copy-done), kind=kOutput, calls=%fused_computation | convolution fusion | flops 536870912 | bytes 9175040 | tf_op jit(solution)/shard_map/dot_general | solution.py:176
  88.8 0.0 reduce-scatter.2.cloned.1.call-update
  88.8 68.4 %reduce-scatter.2.cloned.1.call-done = f32[128,1024]{0,1:T(8,128)} async-done(((f32[2048,1024]{0,1:T(8,128)}), f32[128,1024]{0,1:T(8,128)}) %reduce-scatter.2.cloned.1.call-update) | async-done | bytes 524304 | tf_op jit(solution)/shard_map/reduce_scatter | solution.py:175
  157.3 1.8 %convert_bitcast_fusion = bf16[1024,128]{1,0:T(8,128)(2,1)} fusion(f32[128,1024]{0,1:T(8,128)} %reduce-scatter.2.cloned.1.call-done), kind=kLoop, calls=%fused_computation.1 | loop fusion | flops 131072 | bytes 786432 | tf_op jit(solution)/shard_map/convert_element_type | solution.py:183
Async XLA Ops:
  6.5 77.7 %copy-start = (bf16[128,2048]{1,0:T(8,128)(2,1)S(1)}, bf16[128,2048]{1,0:T(8,128)(2,1)}, u32[]{:S(2)}) copy-start(bf16[128,2048]{1,0:T(8,128)(2,1)} %param.13) | copy-start | bytes 1572868
  33.2 13.0 %all-to-all-start.1 = ((f32[32,8,128]{2,1,0:T(8,128)}), f32[32,8,128]{2,1,0:T(8,128)S(1)}, u32[]{:S(2)}, u32[]{:S(2)}) async-start(f32[32,8,128]{2,1,0:T(8,128)} %prefix.1), calls=%async_computation.1 | async-start | bytes 262144 | tf_op jit(solution)/shard_map/all_to_all | solution.py:172
  37.1 120.2 %reduce-scatter.2.cloned.1.call-start = ((), (), s32[]{:S(2)}) async-start(), calls=%async_computation.3 | async-start | bytes 8912896 | tf_op jit(solution)/shard_map/reduce_scatter | solution.py:175
  46.2 1.0 copy-start.1
  47.2 0.9 copy-start.2
  48.1 0.9 copy-start.3
  49.1 0.7 copy-start.4
  49.7 0.7 copy-start.5
Sparse Core Ops, SparseCore 0:
  88.9 68.2 reduce-scatter.1
where the time goes:
time: 168 us; the launch traced here: 166 us
  waiting for transfers between devices  76.9 us (46%)
  Pallas kernels  37.6 us (22%)
  blocking collectives  23 us (14%)
  between operations  14.1 us (8%)
  matrix products  4.51 us (3%)
  local copies, waits for them, and re-layouts  4.16 us (2%)
  starting transfers between devices  3.9 us (2%)
  other arithmetic  1.77 us (1%)
    reduce_scatter x1, waiting for transfers between devices, body(): lax.psum_scatter(lax.dot_general(out_weight, normed, (((0,), (0,)), ((),...  68.4 us
    pallas_call x1, Pallas kernels, solve(): pl.pallas_call(solve_kernel, out_shape=jax.ShapeDtypeStruct((width, token...  33.9 us
    all_to_all x1, blocking collectives, body(): parts = lax.all_to_all(state.reshape(devices, rows, width), 'seq', 0, 0)  23 us
    all_to_all x1, waiting for transfers between devices, body(): before = lax.all_to_all(earlier, 'seq', 0, 0)  8.44 us
    dot_general x1, matrix products, body(): lax.dot_general(out_weight, normed, (((0,), (0,)), ((), ())), preferred_e...  4.51 us
    unnamed x12, local copies, waits for them, and re-layouts  4.16 us
    all_to_all x1, starting transfers between devices, body(): before = lax.all_to_all(earlier, 'seq', 0, 0)  3.86 us
  transfers between devices with their start and end apart: 2, of which 2 were waited for; matrix products, arithmetic and copies ran while one was open for 0% of the time, Pallas kernels for 0%

commit v1 on v0

--- a/solution.py
+++ b/solution.py
@@ -1,3 +1,5 @@
+import functools
+
 import jax
 import jax.numpy as jnp
 from jax import lax
@@ -59,8 +61,18 @@
 
 def solve_kernel(
     reg_ref, q_ref, k_ref, v_ref, before_ref, gain_ref, norm_ref, out_ref,
-    first, second, last, x_ref, r_ref, p_ref,
+    q_buf, k_buf, v_buf, first, second, last, x_ref, r_ref, p_ref, sems,
 ):
+    copies = [
+        pltpu.make_async_copy(source, target, sems.at[i])
+        for i, (source, target) in enumerate(
+            ((k_ref, k_buf), (v_ref, v_buf), (q_ref, q_buf))
+        )
+    ]
+    for copy in copies:
+        copy.start()
+    for copy in copies:
+        copy.wait()
     width = q_ref.shape[1]
     blocks = q_ref.shape[0] // BLOCK
     lam = reg_ref[0]
@@ -73,9 +85,9 @@
     starts = []
     for b in range(blocks):
         rows = pl.ds(b * BLOCK, BLOCK)
-        key = (k_ref[rows, :].astype(F32) * gain).astype(BF16)
+        key = (k_buf[rows, :].astype(F32) * gain).astype(BF16)
         key_t = key.astype(F32).T.astype(BF16)
-        val_t = v_ref[rows, :].astype(F32).T.astype(BF16)
+        val_t = v_buf[rows, :].astype(F32).T.astype(BF16)
         high, low = halves(h_state)
         first[b, 0:width, 0:width] = high
         first[b, 0:width, width:] = high
@@ -92,7 +104,7 @@
         if b + 1 < blocks:
             h_state = h_state + mm(key_t, key)
             g_state = g_state + mm(val_t, key)
-        query = q_ref[rows, :].astype(F32).T
+        query = q_buf[rows, :].astype(F32).T
         x_ref[b] = jnp.zeros_like(query)
         r_ref[b] = query
         p_ref[b] = query
@@ -134,7 +146,7 @@
         ) + mm(last[b, :, 3 * BLOCK :], x_low)
         square = jnp.mean(read * read, axis=0, keepdims=True)
         normed = read * norm_col * lax.rsqrt(square + 1e-06)
-        out_ref[:, b * BLOCK : (b + 1) * BLOCK] = normed.astype(BF16)
+        out_ref[b * BLOCK : (b + 1) * BLOCK, :] = normed.T.astype(BF16).astype(F32)
 
 
 def solve(reg, queries, keys, values, before, gain, norm_gain):
@@ -143,20 +155,113 @@
     vmem = pl.BlockSpec(memory_space=pltpu.VMEM)
     return pl.pallas_call(
         solve_kernel,
-        out_shape=jax.ShapeDtypeStruct((width, tokens), BF16),
-        in_specs=[pl.BlockSpec(memory_space=pltpu.SMEM)] + [vmem] * 6,
+        out_shape=jax.ShapeDtypeStruct((tokens, width), F32),
+        in_specs=[pl.BlockSpec(memory_space=pltpu.SMEM)]
+        + [pl.BlockSpec(memory_space=pl.ANY)] * 3
+        + [vmem] * 3,
         out_specs=vmem,
         scratch_shapes=[
+            pltpu.VMEM((tokens, width), BF16),
+            pltpu.VMEM((tokens, width), BF16),
+            pltpu.VMEM((tokens, width), BF16),
             pltpu.VMEM((blocks, 2 * BLOCK, 2 * width), BF16),
             pltpu.VMEM((blocks, width, 3 * BLOCK), BF16),
             pltpu.VMEM((blocks, width, 4 * BLOCK), BF16),
             pltpu.VMEM((blocks, width, BLOCK), F32),
             pltpu.VMEM((blocks, width, BLOCK), F32),
             pltpu.VMEM((blocks, width, BLOCK), F32),
+            pltpu.SemaphoreType.DMA((3,)),
         ],
+        cost_estimate=pl.CostEstimate(
+            flops=60 * 10**9, bytes_accessed=2**21, transcendentals=0
+        ),
         compiler_params=pltpu.CompilerParams(vmem_limit_bytes=40 * 2**20),
         name="solve",
     )(reg, queries, keys, values, before, gain, norm_gain)
+
+
+def join_kernel(axis, a_ref, b_ref, out_ref):
+    out_ref[...] = jnp.concatenate([a_ref[...], b_ref[...]], axis=axis).astype(BF16)
+
+
+def joined(first, second, axis):
+    shape = list(first.shape)
+    shape[axis] *= 2
+    return pl.pallas_call(
+        functools.partial(join_kernel, axis),
+        out_shape=jax.ShapeDtypeStruct(tuple(shape), BF16),
+        compiler_params=pltpu.CompilerParams(vmem_limit_bytes=24 * 2**20),
+        name="joined",
+    )(first, second)
+
+
+def sort_kernel(core_ref, w_ref, mine_ref, theirs_ref):
+    chips, _, width = mine_ref.shape
+    first_core = core_ref[0] == 0
+    for chip in range(chips):
+        zero = w_ref[:, 2 * chip * width : (2 * chip + 1) * width].astype(F32)
+        one = w_ref[:, (2 * chip + 1) * width : (2 * chip + 2) * width].astype(F32)
+        mine_ref[chip] = jnp.where(first_core, zero, one)
+        theirs_ref[chip] = jnp.where(first_core, one, zero)
+
+
+def sorted_weight(out_weight):
+    width = out_weight.shape[0]
+    chips = out_weight.shape[1] // (2 * width)
+    core = lax.rem(lax.axis_index("head").astype(jnp.uint32), jnp.uint32(2))
+    core = core.astype(jnp.int32).reshape(1)
+    shape = jax.ShapeDtypeStruct((chips, width, width), F32)
+    return pl.pallas_call(
+        sort_kernel,
+        out_shape=(shape, shape),
+        in_specs=[
+            pl.BlockSpec(memory_space=pltpu.SMEM),
+            pl.BlockSpec(memory_space=pltpu.VMEM),
+        ],
+        name="sorted_weight",
+    )(core, out_weight)
+
+
+def swapped(value):
+    heads = lax.axis_size("head")
+    return lax.ppermute(value, "head", [(i, i ^ 1) for i in range(heads)])
+
+
+def project(normed, weight_pair):
+    tokens, width = normed.shape
+    heads = lax.axis_size("head")
+    place = lax.axis_index("head")
+    chips = heads // 2
+    chip = lax.div(place.astype(jnp.uint32), jnp.uint32(2))
+    right = [(i, (i + 2) % heads) for i in range(heads)]
+    left = [(i, (i - 2) % heads) for i in range(heads)]
+    weights = joined(*weight_pair, 1)
+    both = joined(normed, swapped(normed), 1)
+    half = tokens // 2
+    early, late = both[:half], both[half:]
+
+    def part(rows, ahead):
+        index = lax.rem(chip + jnp.uint32((ahead + chips) % chips), jnp.uint32(chips))
+        columns = lax.dynamic_index_in_dim(weights, index, axis=0, keepdims=False)
+        return jnp.dot(rows, columns, preferred_element_type=F32)
+
+    far = chips // 2
+    flows = {}
+    for away in range(far, 0, -1):
+        for sign, perm in ((1, right), (-1, left)):
+            for name, rows in (("early", early), ("late", late)):
+                key = (sign, name)
+                if away == far and key not in ((1, "early"), (-1, "late")):
+                    continue
+                term = part(rows, sign * away)
+                if key in flows:
+                    term = flows[key] + term
+                flows[key] = lax.ppermute(term, "head", perm)
+    done = [
+        part(rows, 0) + flows[(1, name)] + flows[(-1, name)]
+        for name, rows in (("early", early), ("late", late))
+    ]
+    return jnp.concatenate(done, axis=0).astype(BF16)
 
 
 def body(queries, keys, values, key_gain, reg, norm_gain, out_weight):
@@ -169,18 +274,13 @@
         state.reshape(devices, rows, width), "seq", 0, 0
     )
     earlier = exclusive(parts)
+    earlier, out_weight = lax.optimization_barrier((earlier, out_weight))
     before = lax.all_to_all(earlier, "seq", 0, 0)
+    mine, theirs = sorted_weight(out_weight)
+    before, *weight_pair = lax.optimization_barrier((before, mine, swapped(theirs)))
     before = before.reshape(2 * width, width)
     normed = solve(reg, query_rows, key_rows, value_rows, before, key_gain, norm_gain)
-    summed = lax.psum_scatter(
-        lax.dot_general(
-            out_weight, normed, (((0,), (0,)), ((), ())), preferred_element_type=F32
-        ),
-        "head",
-        scatter_dimension=0,
-        tiled=True,
-    )
-    return summed.T.astype(BF16)
+    return project(normed, weight_pair)
 
 
 def solution(mesh):

time: 168 us -> 146 us (0.87)
  starting transfers between devices: 3.9 us -> 67.6 us
  waiting for transfers between devices: 76.9 us -> 28.3 us
  blocking collectives: 23 us -> 0 us
  between operations: 14.1 us -> 1.13 us
  local copies, waits for them, and re-layouts: 4.16 us -> 1.31 us
  Pallas kernels: 37.6 us -> 40 us
    reduce_scatter x1 -> x0, waiting for transfers between devices: 68.4 us -> none  [body(): lax.psum_scatter(lax.dot_general(out_weight, normed, (((0,), (0,)), ((),...]
    ppermute x0 -> x16, starting transfers between devices: none -> 50.1 us  [the longest x14 42.2 us: project(): flows[key] = lax.ppermute(term, 'head', perm)]
    all_to_all x1 -> x0, blocking collectives: 23 us -> none  [body(): parts = lax.all_to_all(state.reshape(devices, rows, width), 'seq', 0, 0)]
    all_to_all x0 -> x1, starting transfers between devices: none -> 13.7 us  [body(): parts = lax.all_to_all(state.reshape(devices, rows, width), 'seq', 0, 0)]
    ppermute x0 -> x16, waiting for transfers between devices: none -> 10.5 us  [the longest x14 9.08 us: project(): flows[key] = lax.ppermute(term, 'head', perm)]
    all_to_all x0 -> x1, waiting for transfers between devices: none -> 9.15 us  [body(): parts = lax.all_to_all(state.reshape(devices, rows, width), 'seq', 0, 0)]
    unnamed x12 -> x14, local copies, waits for them, and re-layouts: 4.16 us -> 1.31 us
    pallas_call x1 -> x4, Pallas kernels: 33.9 us -> 36.3 us  [the longest x1 34 us: solve(): pl.pallas_call(solve_kernel, out_shape=jax.ShapeDtypeStruct((tokens, widt...]
  transfers between devices with their start and end apart: 2 -> 18, of which waited for: 2 -> 7; matrix products, arithmetic and copies ran while one was open for 0% -> 2% of each run, Pallas kernels for 0% -> 0%
where the time goes in v1:
time: 146 us; the launch traced here: 143 us
  starting transfers between devices  67.6 us (46%)
  Pallas kernels  40 us (27%)
  waiting for transfers between devices  28.3 us (19%)
  matrix products  3.61 us (2%)
    ppermute x14, starting transfers between devices, project(): flows[key] = lax.ppermute(term, 'head', perm)  42.2 us
    pallas_call x1, Pallas kernels, solve(): pl.pallas_call(solve_kernel, out_shape=jax.ShapeDtypeStruct((tokens, widt...  34 us
    all_to_all x1, starting transfers between devices, body(): parts = lax.all_to_all(state.reshape(devices, rows, width), 'seq', 0, 0)  13.7 us
    all_to_all x1, waiting for transfers between devices, body(): parts = lax.all_to_all(state.reshape(devices, rows, width), 'seq', 0, 0)  9.15 us
    ppermute x14, waiting for transfers between devices, project(): flows[key] = lax.ppermute(term, 'head', perm)  9.08 us
    all_to_all x1, waiting for transfers between devices, body(): before = lax.all_to_all(earlier, 'seq', 0, 0)  8.64 us
    ppermute x2, starting transfers between devices, swapped(): return lax.ppermute(value, 'head', [(i, i ^ 1) for i in range(heads)])  7.91 us
    all_to_all x1, starting transfers between devices, body(): before = lax.all_to_all(earlier, 'seq', 0, 0)  3.86 us
  transfers between devices with their start and end apart: 18, of which 7 were waited for; matrix products, arithmetic and copies ran while one was open for 2% of the time, Pallas kernels for 0%

profile of v1, /device:TPU:1, one launch (start us, length us, event | category | flops | bytes accessed | tf_op | source)
XLA Modules:
  0.0 143.0 jit_solution(9345821875245884239)
XLA Ops:
  0.0 2.0 %local_state.1 = f32[256,128]{1,0:T(8,128)} custom-call(bf16[1024,128]{1,0:T(8,128)(2,1)} %bitcast.46, bf16[1024,128]{1,0:T(8,128)(2,1)} %bitcast.48, f32[1,128]{1,0:T(1,128)} %gain_ref.3), custom_call_target="tpu_custom_call" | custom-call | tf_op jit(solution)/shard_map/local_state/pallas_call | solution.py:39
  2.0 13.7 %all-to-all-start = ((f32[32,8,128]{2,1,0:T(8,128)}), f32[32,8,128]{2,1,0:T(8,128)S(1)}, u32[]{:S(2)}, u32[]{:S(2)}) async-start(f32[32,8,128]{2,1,0:T(8,128)} %bitcast.52), calls=%async_computation | async-start | bytes 262144 | tf_op jit(solution)/shard_map/all_to_all | solution.py:273
  15.8 9.1 %all-to-all-done.x_ref = f32[32,8,128]{2,1,0:T(8,128)S(1)} async-done(((f32[32,8,128]{2,1,0:T(8,128)}), f32[32,8,128]{2,1,0:T(8,128)S(1)}, u32[]{:S(2)}, u32[]{:S(2)}) %all-to-all-start) | async-done | bytes 131104 | tf_op jit(solution)/shard_map/all_to_all | solution.py:273
  27.2 2.2 %sorted_weight.1 = (f32[8,128,128]{2,1,0:T(8,128)}, f32[8,128,128]{2,1,0:T(8,128)}) custom-call(s32[1]{0:T(128)} %bitcast.4.core_ref, bf16[128,2048]{1,0:T(8,128)(2,1)} %w_ref), custom_call_target="tpu_custom_call" | custom-call | tf_op jit(solution)/shard_map/sorted_weight/pallas_call | solution.py:214
  29.3 4.1 %collective-permute-start = (f32[8,128,128]{2,1,0:T(8,128)}, f32[8,128,128]{2,1,0:T(8,128)S(1)}, u32[]{:S(2)}, u32[]{:S(2)}) collective-permute-start(f32[8,128,128]{2,1,0:T(8,128)} %get-tuple-element.15), channel_id=1, source_target_pairs={{0,1},{1,0},{2,3},{3,2},{4,5},{5,4},{6,7},{7,6},{8,9},{9,8},{10,11... | collective-permute-start | bytes 1572872 | tf_op jit(solution)/shard_map/ppermute | solution.py:227
  33.5 3.9 %all-to-all-start.1 = ((f32[32,8,128]{2,1,0:T(8,128)}), f32[32,8,128]{2,1,0:T(8,128)S(1)}, u32[]{:S(2)}, u32[]{:S(2)}) async-start(f32[32,8,128]{2,1,0:T(8,128)} %prefix.1), calls=%async_computation.1 | async-start | bytes 262144 | tf_op jit(solution)/shard_map/all_to_all | solution.py:278
  38.0 8.6 %all-to-all-done.1 = f32[32,8,128]{2,1,0:T(8,128)S(1)} async-done(((f32[32,8,128]{2,1,0:T(8,128)}), f32[32,8,128]{2,1,0:T(8,128)S(1)}, u32[]{:S(2)}, u32[]{:S(2)}) %all-to-all-start.1) | async-done | bytes 131104 | tf_op jit(solution)/shard_map/all_to_all | solution.py:278
  47.3 34.0 %solve.1.a_ref = f32[1024,128]{1,0:T(8,128)S(1)} custom-call(f32[1]{0:T(128)S(6)} %copy.8.reg_ref, bf16[1024,128]{1,0:T(8,128)(2,1)S(1)} %bitcast.51, bf16[1024,128]{1,0:T(8,128)(2,1)S(1)} %bitcast.47, bf16[1024,128]{1,0:T(8,128)(2,1)S(1)} %bitcast.49, f32[256,128]{1,0:T(8,128)S(1)} %bitcast.50, f32[1,128]{1,0:T(1,128)S(1)} %copy-done.3, f32[1,128]{1,0:T(1,128)S(1)} %copy-done.5), custom_call_target="tpu_custom_call" | custom-call | flops 60000002048 | bytes 2097152 | tf_op jit(solution)/shard_map/solve/pallas_call | solution.py:156
  81.3 3.8 %collective-permute-start.1 = (f32[1024,128]{1,0:T(8,128)S(1)}, f32[1024,128]{1,0:T(8,128)S(1)}, u32[]{:S(2)}, u32[]{:S(2)}) collective-permute-start(f32[1024,128]{1,0:T(8,128)S(1)} %solve.1.a_ref), channel_id=1, source_target_pairs={{0,1},{1,0},{2,3},{3,2},{4,5},{5,4},{6,7},{7,6},{8,9},{9,8},{10,11... | collective-permute-start | bytes 1572872 | tf_op jit(solution)/shard_map/ppermute | solution.py:227
  88.1 5.1 %collective-permute-start.12 = (f32[512,128]{1,0:T(8,128)S(1)}, f32[512,128]{1,0:T(8,128)S(1)}, u32[]{:S(2)}, u32[]{:S(2)}) collective-permute-start(f32[512,128]{1,0:T(8,128)S(1)} %fusion.28), channel_id=1, source_target_pairs={{0,14},{1,15},{2,0},{3,1},{4,2},{5,3},{6,4},{7,5},{8,6},{9,7},{10,... | collective-permute-start | bytes 786440 | tf_op jit(solution)/shard_map/ppermute | solution.py:259
  93.5 1.9 %collective-permute-start.9 = (f32[512,128]{1,0:T(8,128)S(1)}, f32[512,128]{1,0:T(8,128)S(1)}, u32[]{:S(2)}, u32[]{:S(2)}) collective-permute-start(f32[512,128]{1,0:T(8,128)S(1)} %fusion.24), channel_id=1, source_target_pairs={{0,2},{1,3},{2,4},{3,5},{4,6},{5,7},{6,8},{7,9},{8,10},{9,11},{10,... | collective-permute-start | bytes 786440 | tf_op jit(solution)/shard_map/ppermute | solution.py:259
  95.4 1.9 %collective-permute-start.2 = (f32[512,128]{1,0:T(8,128)S(1)}, f32[512,128]{1,0:T(8,128)S(1)}, u32[]{:S(2)}, u32[]{:S(2)}) collective-permute-start(f32[512,128]{1,0:T(8,128)S(1)} %fusion.30), channel_id=1, source_target_pairs={{0,2},{1,3},{2,4},{3,5},{4,6},{5,7},{6,8},{7,9},{8,10},{9,11},{10,... | collective-permute-start | bytes 786440 | tf_op jit(solution)/shard_map/ppermute | solution.py:259
  98.6 5.3 %collective-permute-start.13 = (f32[512,128]{1,0:T(8,128)S(1)}, f32[512,128]{1,0:T(8,128)S(1)}, u32[]{:S(2)}, u32[]{:S(2)}) collective-permute-start(f32[512,128]{1,0:T(8,128)S(1)} %add.87), channel_id=1, source_target_pairs={{0,14},{1,15},{2,0},{3,1},{4,2},{5,3},{6,4},{7,5},{8,6},{9,7},{10,... | collective-permute-start | bytes 786440 | tf_op jit(solution)/shard_map/ppermute | solution.py:259
  104.1 1.9 %collective-permute-start.6 = (f32[512,128]{1,0:T(8,128)S(1)}, f32[512,128]{1,0:T(8,128)S(1)}, u32[]{:S(2)}, u32[]{:S(2)}) collective-permute-start(f32[512,128]{1,0:T(8,128)S(1)} %fusion.14), channel_id=1, source_target_pairs={{0,14},{1,15},{2,0},{3,1},{4,2},{5,3},{6,4},{7,5},{8,6},{9,7},{10,... | collective-permute-start | bytes 786440 | tf_op jit(solution)/shard_map/ppermute | solution.py:259
  106.4 3.4 %collective-permute-start.10 = (f32[512,128]{1,0:T(8,128)S(1)}, f32[512,128]{1,0:T(8,128)S(1)}, u32[]{:S(2)}, u32[]{:S(2)}) collective-permute-start(f32[512,128]{1,0:T(8,128)S(1)} %add.84), channel_id=1, source_target_pairs={{0,2},{1,3},{2,4},{3,5},{4,6},{5,7},{6,8},{7,9},{8,10},{9,11},{10,... | collective-permute-start | bytes 786440 | tf_op jit(solution)/shard_map/ppermute | solution.py:259
  109.8 1.9 %collective-permute-start.3 = (f32[512,128]{1,0:T(8,128)S(1)}, f32[512,128]{1,0:T(8,128)S(1)}, u32[]{:S(2)}, u32[]{:S(2)}) collective-permute-start(f32[512,128]{1,0:T(8,128)S(1)} %add.72), channel_id=1, source_target_pairs={{0,2},{1,3},{2,4},{3,5},{4,6},{5,7},{6,8},{7,9},{8,10},{9,11},{10,... | collective-permute-start | bytes 786440 | tf_op jit(solution)/shard_map/ppermute | solution.py:259
  111.7 4.6 %collective-permute-start.14 = (f32[512,128]{1,0:T(8,128)S(1)}, f32[512,128]{1,0:T(8,128)S(1)}, u32[]{:S(2)}, u32[]{:S(2)}) collective-permute-start(f32[512,128]{1,0:T(8,128)S(1)} %add.88), channel_id=1, source_target_pairs={{0,14},{1,15},{2,0},{3,1},{4,2},{5,3},{6,4},{7,5},{8,6},{9,7},{10,... | collective-permute-start | bytes 786440 | tf_op jit(solution)/shard_map/ppermute | solution.py:259
  116.8 2.4 %collective-permute-start.7 = (f32[512,128]{1,0:T(8,128)S(1)}, f32[512,128]{1,0:T(8,128)S(1)}, u32[]{:S(2)}, u32[]{:S(2)}) collective-permute-start(f32[512,128]{1,0:T(8,128)S(1)} %add.80), channel_id=1, source_target_pairs={{0,14},{1,15},{2,0},{3,1},{4,2},{5,3},{6,4},{7,5},{8,6},{9,7},{10,... | collective-permute-start | bytes 786440 | tf_op jit(solution)/shard_map/ppermute | solution.py:259
  119.3 2.8 %collective-permute-start.11 = (f32[512,128]{1,0:T(8,128)S(1)}, f32[512,128]{1,0:T(8,128)S(1)}, u32[]{:S(2)}, u32[]{:S(2)}) collective-permute-start(f32[512,128]{1,0:T(8,128)S(1)} %add.85), channel_id=1, source_target_pairs={{0,2},{1,3},{2,4},{3,5},{4,6},{5,7},{6,8},{7,9},{8,10},{9,11},{10,... | collective-permute-start | bytes 786440 | tf_op jit(solution)/shard_map/ppermute | solution.py:259
  122.2 1.9 %collective-permute-start.4 = (f32[512,128]{1,0:T(8,128)S(1)}, f32[512,128]{1,0:T(8,128)S(1)}, u32[]{:S(2)}, u32[]{:S(2)}) collective-permute-start(f32[512,128]{1,0:T(8,128)S(1)} %add.74), channel_id=1, source_target_pairs={{0,2},{1,3},{2,4},{3,5},{4,6},{5,7},{6,8},{7,9},{8,10},{9,11},{10,... | collective-permute-start | bytes 786440 | tf_op jit(solution)/shard_map/ppermute | solution.py:259
  124.2 4.6 %collective-permute-start.15 = (f32[512,128]{1,0:T(8,128)S(1)}, f32[512,128]{1,0:T(8,128)S(1)}, u32[]{:S(2)}, u32[]{:S(2)}) collective-permute-start(f32[512,128]{1,0:T(8,128)S(1)} %add.89), channel_id=1, source_target_pairs={{0,14},{1,15},{2,0},{3,1},{4,2},{5,3},{6,4},{7,5},{8,6},{9,7},{10,... | collective-permute-start | bytes 786440 | tf_op jit(solution)/shard_map/ppermute | solution.py:259
  129.3 2.4 %collective-permute-start.8 = (f32[512,128]{1,0:T(8,128)S(1)}, f32[512,128]{1,0:T(8,128)S(1)}, u32[]{:S(2)}, u32[]{:S(2)}) collective-permute-start(f32[512,128]{1,0:T(8,128)S(1)} %add.82), channel_id=1, source_target_pairs={{0,14},{1,15},{2,0},{3,1},{4,2},{5,3},{6,4},{7,5},{8,6},{9,7},{10,... | collective-permute-start | bytes 786440 | tf_op jit(solution)/shard_map/ppermute | solution.py:259
  133.7 1.9 %collective-permute-start.5 = (f32[512,128]{1,0:T(8,128)S(1)}, f32[512,128]{1,0:T(8,128)S(1)}, u32[]{:S(2)}, u32[]{:S(2)}) collective-permute-start(f32[512,128]{1,0:T(8,128)S(1)} %add.76), channel_id=1, source_target_pairs={{0,2},{1,3},{2,4},{3,5},{4,6},{5,7},{6,8},{7,9},{8,10},{9,11},{10,... | collective-permute-start | bytes 786440 | tf_op jit(solution)/shard_map/ppermute | solution.py:259
  137.7 4.3 %collective-permute-done.5 = f32[512,128]{1,0:T(8,128)S(1)} collective-permute-done((f32[512,128]{1,0:T(8,128)S(1)}, f32[512,128]{1,0:T(8,128)S(1)}, u32[]{:S(2)}, u32[]{:S(2)}) %collective-permute-start.5) | collective-permute-done | bytes 262176 | tf_op jit(solution)/shard_map/ppermute | solution.py:259
  (59 shorter events, 13.9 us)
Async XLA Ops:
  2.0 22.9 %all-to-all-start = ((f32[32,8,128]{2,1,0:T(8,128)}), f32[32,8,128]{2,1,0:T(8,128)S(1)}, u32[]{:S(2)}, u32[]{:S(2)}) async-start(f32[32,8,128]{2,1,0:T(8,128)} %bitcast.52), calls=%async_computation | async-start | bytes 262144 | tf_op jit(solution)/shard_map/all_to_all | solution.py:273
  27.2 19.5 %copy-start.2 = (bf16[1024,1,128]{2,0,1:T(8,128)(2,1)S(1)}, bf16[1024,1,128]{2,0,1:T(8,128)(2,1)}, u32[]{:S(2)}) copy-start(bf16[1024,1,128]{2,0,1:T(8,128)(2,1)} %param.9) | copy-start | bytes 786436
  27.2 19.5 %copy-start.4 = (bf16[1024,1,128]{2,0,1:T(8,128)(2,1)S(1)}, bf16[1024,1,128]{2,0,1:T(8,128)(2,1)}, u32[]{:S(2)}) copy-start(bf16[1024,1,128]{2,0,1:T(8,128)(2,1)} %param.7) | copy-start | bytes 786436
  29.3 17.3 %copy-start.1 = (bf16[1024,1,128]{2,0,1:T(8,128)(2,1)S(1)}, bf16[1024,1,128]{2,0,1:T(8,128)(2,1)}, u32[]{:S(2)}) copy-start(bf16[1024,1,128]{2,0,1:T(8,128)(2,1)} %param.8) | copy-start | bytes 786436
  29.3 17.3 %collective-permute-start = (f32[8,128,128]{2,1,0:T(8,128)}, f32[8,128,128]{2,1,0:T(8,128)S(1)}, u32[]{:S(2)}, u32[]{:S(2)}) collective-permute-start(f32[8,128,128]{2,1,0:T(8,128)} %get-tuple-element.15), channel_id=1, source_target_pairs={{0,1},{1,0},{2,3},{3,2},{4,5},{5,4},{6,7},{7,6},{8,9},{9,8},{10,11... | collective-permute-start | bytes 1572872 | tf_op jit(solution)/shard_map/ppermute | solution.py:227
  33.5 13.2 %all-to-all-start.1 = ((f32[32,8,128]{2,1,0:T(8,128)}), f32[32,8,128]{2,1,0:T(8,128)S(1)}, u32[]{:S(2)}, u32[]{:S(2)}) async-start(f32[32,8,128]{2,1,0:T(8,128)} %prefix.1), calls=%async_computation.1 | async-start | bytes 262144 | tf_op jit(solution)/shard_map/all_to_all | solution.py:278
  46.6 0.7 copy-start.3
  46.6 0.7 copy-start.5
  47.3 37.9 %copy-start = (f32[8,128,128]{2,1,0:T(8,128)S(1)}, f32[8,128,128]{2,1,0:T(8,128)}, u32[]{:S(2)}) copy-start(f32[8,128,128]{2,1,0:T(8,128)} %get-tuple-element.17.a_ref) | copy-start | bytes 1572868
  81.3 5.3 %collective-permute-start.1 = (f32[1024,128]{1,0:T(8,128)S(1)}, f32[1024,128]{1,0:T(8,128)S(1)}, u32[]{:S(2)}, u32[]{:S(2)}) collective-permute-start(f32[1024,128]{1,0:T(8,128)S(1)} %solve.1.a_ref), channel_id=1, source_target_pairs={{0,1},{1,0},{2,3},{3,2},{4,5},{5,4},{6,7},{7,6},{8,9},{9,8},{10,11... | collective-permute-start | bytes 1572872 | tf_op jit(solution)/shard_map/ppermute | solution.py:227
  88.1 10.4 %collective-permute-start.12 = (f32[512,128]{1,0:T(8,128)S(1)}, f32[512,128]{1,0:T(8,128)S(1)}, u32[]{:S(2)}, u32[]{:S(2)}) collective-permute-start(f32[512,128]{1,0:T(8,128)S(1)} %fusion.28), channel_id=1, source_target_pairs={{0,14},{1,15},{2,0},{3,1},{4,2},{5,3},{6,4},{7,5},{8,6},{9,7},{10,... | collective-permute-start | bytes 786440 | tf_op jit(solution)/shard_map/ppermute | solution.py:259
  93.5 12.8 %collective-permute-start.9 = (f32[512,128]{1,0:T(8,128)S(1)}, f32[512,128]{1,0:T(8,128)S(1)}, u32[]{:S(2)}, u32[]{:S(2)}) collective-permute-start(f32[512,128]{1,0:T(8,128)S(1)} %fusion.24), channel_id=1, source_target_pairs={{0,2},{1,3},{2,4},{3,5},{4,6},{5,7},{6,8},{7,9},{8,10},{9,11},{10,... | collective-permute-start | bytes 786440 | tf_op jit(solution)/shard_map/ppermute | solution.py:259
  95.4 14.3 %collective-permute-start.2 = (f32[512,128]{1,0:T(8,128)S(1)}, f32[512,128]{1,0:T(8,128)S(1)}, u32[]{:S(2)}, u32[]{:S(2)}) collective-permute-start(f32[512,128]{1,0:T(8,128)S(1)} %fusion.30), channel_id=1, source_target_pairs={{0,2},{1,3},{2,4},{3,5},{4,6},{5,7},{6,8},{7,9},{8,10},{9,11},{10,... | collective-permute-start | bytes 786440 | tf_op jit(solution)/shard_map/ppermute | solution.py:259
  98.6 13.1 %collective-permute-start.13 = (f32[512,128]{1,0:T(8,128)S(1)}, f32[512,128]{1,0:T(8,128)S(1)}, u32[]{:S(2)}, u32[]{:S(2)}) collective-permute-start(f32[512,128]{1,0:T(8,128)S(1)} %add.87), channel_id=1, source_target_pairs={{0,14},{1,15},{2,0},{3,1},{4,2},{5,3},{6,4},{7,5},{8,6},{9,7},{10,... | collective-permute-start | bytes 786440 | tf_op jit(solution)/shard_map/ppermute | solution.py:259
  104.1 12.6 %collective-permute-start.6 = (f32[512,128]{1,0:T(8,128)S(1)}, f32[512,128]{1,0:T(8,128)S(1)}, u32[]{:S(2)}, u32[]{:S(2)}) collective-permute-start(f32[512,128]{1,0:T(8,128)S(1)} %fusion.14), channel_id=1, source_target_pairs={{0,14},{1,15},{2,0},{3,1},{4,2},{5,3},{6,4},{7,5},{8,6},{9,7},{10,... | collective-permute-start | bytes 786440 | tf_op jit(solution)/shard_map/ppermute | solution.py:259
  106.4 12.9 %collective-permute-start.10 = (f32[512,128]{1,0:T(8,128)S(1)}, f32[512,128]{1,0:T(8,128)S(1)}, u32[]{:S(2)}, u32[]{:S(2)}) collective-permute-start(f32[512,128]{1,0:T(8,128)S(1)} %add.84), channel_id=1, source_target_pairs={{0,2},{1,3},{2,4},{3,5},{4,6},{5,7},{6,8},{7,9},{8,10},{9,11},{10,... | collective-permute-start | bytes 786440 | tf_op jit(solution)/shard_map/ppermute | solution.py:259
  109.8 12.4 %collective-permute-start.3 = (f32[512,128]{1,0:T(8,128)S(1)}, f32[512,128]{1,0:T(8,128)S(1)}, u32[]{:S(2)}, u32[]{:S(2)}) collective-permute-start(f32[512,128]{1,0:T(8,128)S(1)} %add.72), channel_id=1, source_target_pairs={{0,2},{1,3},{2,4},{3,5},{4,6},{5,7},{6,8},{7,9},{8,10},{9,11},{10,... | collective-permute-start | bytes 786440 | tf_op jit(solution)/shard_map/ppermute | solution.py:259
  111.7 12.4 %collective-permute-start.14 = (f32[512,128]{1,0:T(8,128)S(1)}, f32[512,128]{1,0:T(8,128)S(1)}, u32[]{:S(2)}, u32[]{:S(2)}) collective-permute-start(f32[512,128]{1,0:T(8,128)S(1)} %add.88), channel_id=1, source_target_pairs={{0,14},{1,15},{2,0},{3,1},{4,2},{5,3},{6,4},{7,5},{8,6},{9,7},{10,... | collective-permute-start | bytes 786440 | tf_op jit(solution)/shard_map/ppermute | solution.py:259
  116.8 12.4 %collective-permute-start.7 = (f32[512,128]{1,0:T(8,128)S(1)}, f32[512,128]{1,0:T(8,128)S(1)}, u32[]{:S(2)}, u32[]{:S(2)}) collective-permute-start(f32[512,128]{1,0:T(8,128)S(1)} %add.80), channel_id=1, source_target_pairs={{0,14},{1,15},{2,0},{3,1},{4,2},{5,3},{6,4},{7,5},{8,6},{9,7},{10,... | collective-permute-start | bytes 786440 | tf_op jit(solution)/shard_map/ppermute | solution.py:259
  119.3 16.3 %collective-permute-start.11 = (f32[512,128]{1,0:T(8,128)S(1)}, f32[512,128]{1,0:T(8,128)S(1)}, u32[]{:S(2)}, u32[]{:S(2)}) collective-permute-start(f32[512,128]{1,0:T(8,128)S(1)} %add.85), channel_id=1, source_target_pairs={{0,2},{1,3},{2,4},{3,5},{4,6},{5,7},{6,8},{7,9},{8,10},{9,11},{10,... | collective-permute-start | bytes 786440 | tf_op jit(solution)/shard_map/ppermute | solution.py:259
  122.2 11.4 %collective-permute-start.4 = (f32[512,128]{1,0:T(8,128)S(1)}, f32[512,128]{1,0:T(8,128)S(1)}, u32[]{:S(2)}, u32[]{:S(2)}) collective-permute-start(f32[512,128]{1,0:T(8,128)S(1)} %add.74), channel_id=1, source_target_pairs={{0,2},{1,3},{2,4},{3,5},{4,6},{5,7},{6,8},{7,9},{8,10},{9,11},{10,... | collective-permute-start | bytes 786440 | tf_op jit(solution)/shard_map/ppermute | solution.py:259
  124.2 11.4 %collective-permute-start.15 = (f32[512,128]{1,0:T(8,128)S(1)}, f32[512,128]{1,0:T(8,128)S(1)}, u32[]{:S(2)}, u32[]{:S(2)}) collective-permute-start(f32[512,128]{1,0:T(8,128)S(1)} %add.89), channel_id=1, source_target_pairs={{0,14},{1,15},{2,0},{3,1},{4,2},{5,3},{6,4},{7,5},{8,6},{9,7},{10,... | collective-permute-start | bytes 786440 | tf_op jit(solution)/shard_map/ppermute | solution.py:259
  129.3 8.4 %collective-permute-start.8 = (f32[512,128]{1,0:T(8,128)S(1)}, f32[512,128]{1,0:T(8,128)S(1)}, u32[]{:S(2)}, u32[]{:S(2)}) collective-permute-start(f32[512,128]{1,0:T(8,128)S(1)} %add.82), channel_id=1, source_target_pairs={{0,14},{1,15},{2,0},{3,1},{4,2},{5,3},{6,4},{7,5},{8,6},{9,7},{10,... | collective-permute-start | bytes 786440 | tf_op jit(solution)/shard_map/ppermute | solution.py:259
  133.7 8.3 %collective-permute-start.5 = (f32[512,128]{1,0:T(8,128)S(1)}, f32[512,128]{1,0:T(8,128)S(1)}, u32[]{:S(2)}, u32[]{:S(2)}) collective-permute-start(f32[512,128]{1,0:T(8,128)S(1)} %add.76), channel_id=1, source_target_pairs={{0,2},{1,3},{2,4},{3,5},{4,6},{5,7},{6,8},{7,9},{8,10},{9,11},{10,... | collective-permute-start | bytes 786440 | tf_op jit(solution)/shard_map/ppermute | solution.py:259
  (1 other events, 0.7 us)

commit v2 on v0

--- a/solution.py
+++ b/solution.py
@@ -1,3 +1,5 @@
+import functools
+
 import jax
 import jax.numpy as jnp
 from jax import lax
@@ -59,8 +61,18 @@
 
 def solve_kernel(
     reg_ref, q_ref, k_ref, v_ref, before_ref, gain_ref, norm_ref, out_ref,
-    first, second, last, x_ref, r_ref, p_ref,
+    q_buf, k_buf, v_buf, first, second, last, x_ref, r_ref, p_ref, sems,
 ):
+    copies = [
+        pltpu.make_async_copy(source, target, sems.at[i])
+        for i, (source, target) in enumerate(
+            ((k_ref, k_buf), (v_ref, v_buf), (q_ref, q_buf))
+        )
+    ]
+    for copy in copies:
+        copy.start()
+    for copy in copies:
+        copy.wait()
     width = q_ref.shape[1]
     blocks = q_ref.shape[0] // BLOCK
     lam = reg_ref[0]
@@ -73,9 +85,9 @@
     starts = []
     for b in range(blocks):
         rows = pl.ds(b * BLOCK, BLOCK)
-        key = (k_ref[rows, :].astype(F32) * gain).astype(BF16)
+        key = (k_buf[rows, :].astype(F32) * gain).astype(BF16)
         key_t = key.astype(F32).T.astype(BF16)
-        val_t = v_ref[rows, :].astype(F32).T.astype(BF16)
+        val_t = v_buf[rows, :].astype(F32).T.astype(BF16)
         high, low = halves(h_state)
         first[b, 0:width, 0:width] = high
         first[b, 0:width, width:] = high
@@ -92,7 +104,7 @@
         if b + 1 < blocks:
             h_state = h_state + mm(key_t, key)
             g_state = g_state + mm(val_t, key)
-        query = q_ref[rows, :].astype(F32).T
+        query = q_buf[rows, :].astype(F32).T
         x_ref[b] = jnp.zeros_like(query)
         r_ref[b] = query
         p_ref[b] = query
@@ -100,24 +112,31 @@
 
     def step(_, rrs):
         news = []
-        for b in range(blocks):
-            p = p_ref[b]
-            p_high, p_low = halves(p)
-            one = mm(first[b], jnp.concatenate([p_high, p_low], axis=0))
-            s_high, s_low = halves(jnp.where(causal, one[width:], 0.0))
-            two = mm(second[b], jnp.concatenate([s_high, s_low, p_high], axis=0))
-            w = one[:width] + two + lam * p
-            rr = rrs[b]
-            active = rr > 1e-30
-            curve = jnp.sum(p * w, axis=0, keepdims=True)
-            alpha = jnp.where(active, rr / jnp.where(active, curve, 1.0), 0.0)
-            x_ref[b] = x_ref[b] + alpha * p
-            r = r_ref[b] - alpha * w
-            r_ref[b] = r
-            new = jnp.sum(r * r, axis=0, keepdims=True)
-            ratio = jnp.where(active, new / jnp.where(active, rr, 1.0), 0.0)
-            p_ref[b] = r + ratio * p
-            news.append(new)
+        for group in (range(blocks),):
+            ps = {b: p_ref[b] for b in group}
+            hs = {b: halves(ps[b]) for b in group}
+            one = {
+                b: mm(first[b], jnp.concatenate(hs[b], axis=0)) for b in group
+            }
+            ss = {b: halves(jnp.where(causal, one[b][width:], 0.0)) for b in group}
+            two = {
+                b: mm(second[b], jnp.concatenate([*ss[b], hs[b][0]], axis=0))
+                for b in group
+            }
+            for b in group:
+                p = p_ref[b]
+                w = one[b][:width] + two[b] + lam * p
+                rr = rrs[b]
+                active = rr > 1e-30
+                curve = jnp.sum(p * w, axis=0, keepdims=True)
+                alpha = jnp.where(active, rr / jnp.where(active, curve, 1.0), 0.0)
+                x_ref[b] = x_ref[b] + alpha * p
+                r = r_ref[b] - alpha * w
+                r_ref[b] = r
+                new = jnp.sum(r * r, axis=0, keepdims=True)
+                ratio = jnp.where(active, new / jnp.where(active, rr, 1.0), 0.0)
+                p_ref[b] = r + ratio * p
+                news.append(new)
         return tuple(news)
 
     lax.fori_loop(0, ITERS, step, tuple(starts))
@@ -134,7 +153,7 @@
         ) + mm(last[b, :, 3 * BLOCK :], x_low)
         square = jnp.mean(read * read, axis=0, keepdims=True)
         normed = read * norm_col * lax.rsqrt(square + 1e-06)
-        out_ref[:, b * BLOCK : (b + 1) * BLOCK] = normed.astype(BF16)
+        out_ref[b * BLOCK : (b + 1) * BLOCK, :] = normed.T.astype(BF16).astype(F32)
 
 
 def solve(reg, queries, keys, values, before, gain, norm_gain):
@@ -143,20 +162,116 @@
     vmem = pl.BlockSpec(memory_space=pltpu.VMEM)
     return pl.pallas_call(
         solve_kernel,
-        out_shape=jax.ShapeDtypeStruct((width, tokens), BF16),
-        in_specs=[pl.BlockSpec(memory_space=pltpu.SMEM)] + [vmem] * 6,
+        out_shape=jax.ShapeDtypeStruct((tokens, width), F32),
+        in_specs=[pl.BlockSpec(memory_space=pltpu.SMEM)]
+        + [pl.BlockSpec(memory_space=pl.ANY)] * 3
+        + [vmem] * 3,
         out_specs=vmem,
         scratch_shapes=[
+            pltpu.VMEM((tokens, width), BF16),
+            pltpu.VMEM((tokens, width), BF16),
+            pltpu.VMEM((tokens, width), BF16),
             pltpu.VMEM((blocks, 2 * BLOCK, 2 * width), BF16),
             pltpu.VMEM((blocks, width, 3 * BLOCK), BF16),
             pltpu.VMEM((blocks, width, 4 * BLOCK), BF16),
             pltpu.VMEM((blocks, width, BLOCK), F32),
             pltpu.VMEM((blocks, width, BLOCK), F32),
             pltpu.VMEM((blocks, width, BLOCK), F32),
+            pltpu.SemaphoreType.DMA((3,)),
         ],
+        cost_estimate=pl.CostEstimate(
+            flops=60 * 10**9, bytes_accessed=2**21, transcendentals=0
+        ),
         compiler_params=pltpu.CompilerParams(vmem_limit_bytes=40 * 2**20),
         name="solve",
     )(reg, queries, keys, values, before, gain, norm_gain)
+
+
+def swapped(value):
+    heads = lax.axis_size("head")
+    return lax.ppermute(value, "head", [(i, i ^ 1) for i in range(heads)])
+
+
+def join_weight_kernel(own_ref, other_ref, out_ref):
+    chips, double, columns = out_ref.shape
+    half = double // 2
+    for chip in range(chips):
+        here = slice(chip * columns, (chip + 1) * columns)
+        out_ref[chip, 0:half, :] = own_ref[:, here]
+        out_ref[chip, half:, :] = other_ref[:, here].astype(BF16)
+
+
+def join_weight(own, other):
+    width, columns = own.shape
+    return pl.pallas_call(
+        join_weight_kernel,
+        out_shape=jax.ShapeDtypeStruct((columns // (2 * width), 2 * width, 2 * width), BF16),
+        name="join_weight",
+    )(own, other)
+
+
+def join_rows_kernel(own_ref, other_ref, out_ref):
+    width = own_ref.shape[1]
+    out_ref[:, 0:width] = own_ref[...].astype(BF16)
+    out_ref[:, width:] = other_ref[...].astype(BF16)
+
+
+def join_rows(own, other):
+    tokens, width = own.shape
+    return pl.pallas_call(
+        join_rows_kernel,
+        out_shape=jax.ShapeDtypeStruct((tokens, 2 * width), BF16),
+        name="join_rows",
+    )(own, other)
+
+
+def project(normed, weights):
+    tokens, width = normed.shape
+    heads = lax.axis_size("head")
+    place = lax.axis_index("head").astype(jnp.uint32)
+    chips = heads // 2
+    chip, core = lax.div(place, jnp.uint32(2)), lax.rem(place, jnp.uint32(2))
+    left_going = core == 1
+    ring = [(i, (i + (2 if i % 2 == 0 else heads - 2)) % heads) for i in range(heads)]
+    both = join_rows(normed, swapped(normed))
+    half = tokens // 2
+    early, late = both[:half], both[half:]
+    rows = (
+        jnp.where(left_going, late, early),
+        jnp.where(left_going, early, late),
+    )
+
+    def part(piece, away):
+        ahead = jnp.where(left_going, jnp.uint32(chips - away), jnp.uint32(away % chips))
+        index = lax.rem(chip + ahead, jnp.uint32(chips))
+        columns = lax.dynamic_index_in_dim(weights, index, axis=0, keepdims=False)
+        return jnp.dot(rows[piece], columns, preferred_element_type=F32)
+
+    flows = [None, None]
+    for away in range(chips // 2, 0, -1):
+        for piece in (0, 1):
+            if away == chips // 2 and piece == 1:
+                continue
+            term = part(piece, away)
+            if flows[piece] is not None:
+                term = flows[piece] + term
+            flows[piece] = lax.ppermute(term, "head", ring)
+
+    def columns_of(value, other):
+        zero, one = value[:, :width], value[:, width:]
+        return jnp.where(left_going != other, one, zero)
+
+    given = [swapped(columns_of(flow, True)) for flow in flows]
+    done = [
+        columns_of(part(piece, 0) + flows[piece], False) + given[1 - piece]
+        for piece in (0, 1)
+    ]
+    first, second = (value.astype(BF16) for value in done)
+    return jnp.where(
+        left_going,
+        jnp.concatenate([second, first], axis=0),
+        jnp.concatenate([first, second], axis=0),
+    )
 
 
 def body(queries, keys, values, key_gain, reg, norm_gain, out_weight):
@@ -165,22 +280,14 @@
     key_rows, value_rows, query_rows = keys[:, 0, :], values[:, 0, :], queries[:, 0, :]
     state = local_state(key_rows, value_rows, key_gain)
     rows = 2 * width // devices
-    parts = lax.all_to_all(
-        state.reshape(devices, rows, width), "seq", 0, 0
-    )
-    earlier = exclusive(parts)
-    before = lax.all_to_all(earlier, "seq", 0, 0)
+    state, out_weight = lax.optimization_barrier((state, out_weight))
+    parts = lax.all_to_all(state.reshape(devices, rows, width), "seq", 0, 0)
+    weights = join_weight(out_weight, swapped(out_weight.astype(F32)))
+    parts, weights = lax.optimization_barrier((parts, weights))
+    before = lax.all_to_all(exclusive(parts), "seq", 0, 0)
     before = before.reshape(2 * width, width)
     normed = solve(reg, query_rows, key_rows, value_rows, before, key_gain, norm_gain)
-    summed = lax.psum_scatter(
-        lax.dot_general(
-            out_weight, normed, (((0,), (0,)), ((), ())), preferred_element_type=F32
-        ),
-        "head",
-        scatter_dimension=0,
-        tiled=True,
-    )
-    return summed.T.astype(BF16)
+    return project(normed, weights)
 
 
 def solution(mesh):

time: 168 us -> 126 us (0.75)
  starting transfers between devices: 3.9 us -> 70.1 us
  waiting for transfers between devices: 76.9 us -> 21 us
  blocking collectives: 23 us -> 0 us
  Pallas kernels: 37.6 us -> 23.1 us
  between operations: 14.1 us -> 0.99 us
  other arithmetic: 1.77 us -> 4.29 us
    reduce_scatter x1 -> x0, waiting for transfers between devices: 68.4 us -> none  [body(): lax.psum_scatter(lax.dot_general(out_weight, normed, (((0,), (0,)), ((),...]
    ppermute x0 -> x11, starting transfers between devices: none -> 58 us  [the longest x7 32.3 us: project(): flows[piece] = lax.ppermute(term, 'head', ring)]
    all_to_all x1 -> x0, blocking collectives: 23 us -> none  [body(): parts = lax.all_to_all(state.reshape(devices, rows, width), 'seq', 0, 0)]
    pallas_call x1 -> x3, Pallas kernels: 33.9 us -> 19.4 us  [the longest x1 14.8 us: solve(): pl.pallas_call(solve_kernel, out_shape=jax.ShapeDtypeStruct((tokens, widt...]
    all_to_all x1 -> x2, starting transfers between devices: 3.86 us -> 12.1 us  [the longest x1 7.52 us: body(): parts = lax.all_to_all(state.reshape(devices, rows, width), 'seq', 0, 0)]
    ppermute x0 -> x11, waiting for transfers between devices: none -> 6.8 us  [the longest x7 4.45 us: project(): flows[piece] = lax.ppermute(term, 'head', ring)]
    all_to_all x1 -> x2, waiting for transfers between devices: 8.44 us -> 14.2 us  [the longest x1 8.55 us: body(): before = lax.all_to_all(exclusive(parts), 'seq', 0, 0)]
    add x0 -> x5, other arithmetic: none -> 2.19 us  [project(): term = flows[piece] + term]
  transfers between devices with their start and end apart: 2 -> 13, of which waited for: 2 -> 9; matrix products, arithmetic and copies ran while one was open for 0% -> 4% of each run, Pallas kernels for 0% -> 2%
where the time goes in v2:
time: 126 us; the launch traced here: 125 us
  starting transfers between devices  70.1 us (56%)
  Pallas kernels  23.1 us (18%)
  waiting for transfers between devices  21 us (17%)
  other arithmetic  4.29 us (3%)
  local copies, waits for them, and re-layouts  3.08 us (2%)
  matrix products  2.87 us (2%)
    ppermute x7, starting transfers between devices, project(): flows[piece] = lax.ppermute(term, 'head', ring)  32.3 us
    ppermute x4, starting transfers between devices, swapped(): return lax.ppermute(value, 'head', [(i, i ^ 1) for i in range(heads)])  25.7 us
    pallas_call x1, Pallas kernels, solve(): pl.pallas_call(solve_kernel, out_shape=jax.ShapeDtypeStruct((tokens, widt...  14.8 us
    all_to_all x1, waiting for transfers between devices, body(): before = lax.all_to_all(exclusive(parts), 'seq', 0, 0)  8.55 us
    all_to_all x1, starting transfers between devices, body(): parts = lax.all_to_all(state.reshape(devices, rows, width), 'seq', 0, 0)  7.52 us
    all_to_all x1, waiting for transfers between devices, body(): parts = lax.all_to_all(state.reshape(devices, rows, width), 'seq', 0, 0)  5.63 us
    all_to_all x1, starting transfers between devices, body(): before = lax.all_to_all(exclusive(parts), 'seq', 0, 0)  4.54 us
    ppermute x7, waiting for transfers between devices, project(): flows[piece] = lax.ppermute(term, 'head', ring)  4.45 us
  transfers between devices with their start and end apart: 13, of which 9 were waited for; matrix products, arithmetic and copies ran while one was open for 4% of the time, Pallas kernels for 2%

profile of v2, /device:TPU:1, one launch (start us, length us, event | category | flops | bytes accessed | tf_op | source)
XLA Modules:
  0.0 125.4 jit_solution(4416952889172122704)
XLA Ops:
  0.0 2.1 %local_state.1 = f32[256,128]{1,0:T(8,128)} custom-call(bf16[1024,128]{1,0:T(8,128)(2,1)} %bitcast.37, bf16[1024,128]{1,0:T(8,128)(2,1)} %bitcast.39, f32[1,128]{1,0:T(1,128)} %gain_ref.3), custom_call_target="tpu_custom_call" | custom-call | tf_op jit(solution)/shard_map/local_state/pallas_call | solution.py:39
  2.2 8.8 %collective-permute-start = (f32[128,2048]{1,0:T(8,128)S(1)}, f32[128,2048]{1,0:T(8,128)S(1)}, u32[]{:S(2)}, u32[]{:S(2)}) collective-permute-start(f32[128,2048]{1,0:T(8,128)S(1)} %convert_element_type.13), channel_id=1, source_target_pairs={{0,1},{1,0},{2,3},{3,2},{4,5},{5,4},{6,7},{7,6},{8,9},{9,8},{10,11... | collective-permute-start | bytes 3145736 | tf_op jit(solution)/shard_map/ppermute | solution.py:192
  11.0 7.5 %all-to-all-start = ((f32[32,8,128]{2,1,0:T(8,128)}), f32[32,8,128]{2,1,0:T(8,128)S(1)}, u32[]{:S(2)}, u32[]{:S(2)}) async-start(f32[32,8,128]{2,1,0:T(8,128)} %bitcast.3), calls=%async_computation | async-start | bytes 262144 | tf_op jit(solution)/shard_map/all_to_all | solution.py:284
  19.5 2.5 %join_weight.1 = bf16[8,256,256]{2,1,0:T(8,128)(2,1)} custom-call(bf16[128,2048]{1,0:T(8,128)(2,1)} %own_ref, f32[128,2048]{1,0:T(8,128)} %copy-done.8), custom_call_target="tpu_custom_call" | custom-call | tf_op jit(solution)/shard_map/join_weight/pallas_call | solution.py:206
  22.1 5.6 %all-to-all-done.x_ref = f32[32,8,128]{2,1,0:T(8,128)S(1)} async-done(((f32[32,8,128]{2,1,0:T(8,128)}), f32[32,8,128]{2,1,0:T(8,128)S(1)}, u32[]{:S(2)}, u32[]{:S(2)}) %all-to-all-start) | async-done | bytes 131104 | tf_op jit(solution)/shard_map/all_to_all | solution.py:284
  28.3 1.6 %prefix.1 = f32[32,8,128]{2,1,0:T(8,128)} custom-call(f32[32,8,128]{2,1,0:T(8,128)} %copy-done.10), custom_call_target="tpu_custom_call" | custom-call | tf_op jit(solution)/shard_map/prefix/pallas_call | solution.py:55
  29.9 4.5 %all-to-all-start.1 = ((f32[32,8,128]{2,1,0:T(8,128)}), f32[32,8,128]{2,1,0:T(8,128)S(1)}, u32[]{:S(2)}, u32[]{:S(2)}) async-start(f32[32,8,128]{2,1,0:T(8,128)} %prefix.1), calls=%async_computation.1 | async-start | bytes 262144 | tf_op jit(solution)/shard_map/all_to_all | solution.py:287
  35.1 8.5 %all-to-all-done.1 = f32[32,8,128]{2,1,0:T(8,128)S(1)} async-done(((f32[32,8,128]{2,1,0:T(8,128)}), f32[32,8,128]{2,1,0:T(8,128)S(1)}, u32[]{:S(2)}, u32[]{:S(2)}) %all-to-all-start.1) | async-done | bytes 131104 | tf_op jit(solution)/shard_map/all_to_all | solution.py:287
  44.3 14.8 %solve.1.own_ref = f32[1024,128]{1,0:T(8,128)S(1)} custom-call(f32[1]{0:T(128)S(6)} %copy.8.reg_ref, bf16[1024,128]{1,0:T(8,128)(2,1)S(1)} %bitcast.42, bf16[1024,128]{1,0:T(8,128)(2,1)S(1)} %bitcast.38, bf16[1024,128]{1,0:T(8,128)(2,1)S(1)} %bitcast.40, f32[256,128]{1,0:T(8,128)S(1)} %bitcast.41, f32[1,128]{1,0:T(1,128)S(1)} %copy-done.3, ...), custom_call_target="tpu_custom_call" | custom-call | flops 60000002048 | bytes 2097152 | tf_op jit(solution)/shard_map/solve/pallas_call | solution.py:163
  59.2 4.5 %collective-permute-start.1 = (f32[1024,128]{1,0:T(8,128)S(1)}, f32[1024,128]{1,0:T(8,128)S(1)}, u32[]{:S(2)}, u32[]{:S(2)}) collective-permute-start(f32[1024,128]{1,0:T(8,128)S(1)} %solve.1.own_ref), channel_id=1, source_target_pairs={{0,1},{1,0},{2,3},{3,2},{4,5},{5,4},{6,7},{7,6},{8,9},{9,8},{10,11... | collective-permute-start | bytes 1572872 | tf_op jit(solution)/shard_map/ppermute | solution.py:192
  63.7 1.5 %collective-permute-done.1.other_ref = f32[1024,128]{1,0:T(8,128)S(1)} collective-permute-done((f32[1024,128]{1,0:T(8,128)S(1)}, f32[1024,128]{1,0:T(8,128)S(1)}, u32[]{:S(2)}, u32[]{:S(2)}) %collective-permute-start.1) | collective-permute-done | bytes 524320 | tf_op jit(solution)/shard_map/ppermute | solution.py:192
  65.9 2.1 %join_rows.1 = bf16[1024,256]{1,0:T(8,128)(2,1)} custom-call(f32[1024,128]{1,0:T(8,128)} %copy-done, f32[1024,128]{1,0:T(8,128)} %copy-done.9), custom_call_target="tpu_custom_call" | custom-call | tf_op jit(solution)/shard_map/join_rows/pallas_call | solution.py:221
  69.3 5.1 %collective-permute-start.5 = (f32[512,256]{1,0:T(8,128)S(1)}, f32[512,256]{1,0:T(8,128)S(1)}, u32[]{:S(2)}, u32[]{:S(2)}) collective-permute-start(f32[512,256]{1,0:T(8,128)S(1)} %fusion.4), channel_id=1, source_target_pairs={{0,2},{1,15},{2,4},{3,1},{4,6},{5,3},{6,8},{7,5},{8,10},{9,7},{10,... | collective-permute-start | bytes 1572872 | tf_op jit(solution)/shard_map/ppermute | solution.py:258
  75.5 3.0 %collective-permute-start.2 = (f32[512,256]{1,0:T(8,128)}, f32[512,256]{1,0:T(8,128)S(1)}, u32[]{:S(2)}, u32[]{:S(2)}) collective-permute-start(f32[512,256]{1,0:T(8,128)} %fusion.16), channel_id=1, source_target_pairs={{0,2},{1,15},{2,4},{3,1},{4,6},{5,3},{6,8},{7,5},{8,10},{9,7},{10,... | collective-permute-start | bytes 1572872 | tf_op jit(solution)/shard_map/ppermute | solution.py:258
  78.7 1.9 %collective-permute-done.5 = f32[512,256]{1,0:T(8,128)S(1)} collective-permute-done((f32[512,256]{1,0:T(8,128)S(1)}, f32[512,256]{1,0:T(8,128)S(1)}, u32[]{:S(2)}, u32[]{:S(2)}) %collective-permute-start.5) | collective-permute-done | bytes 524320 | tf_op jit(solution)/shard_map/ppermute | solution.py:258
  80.6 5.0 %collective-permute-start.6 = (f32[512,256]{1,0:T(8,128)S(1)}, f32[512,256]{1,0:T(8,128)}, u32[]{:S(2)}, u32[]{:S(2)}) collective-permute-start(f32[512,256]{1,0:T(8,128)S(1)} %add.54), channel_id=1, source_target_pairs={{0,2},{1,15},{2,4},{3,1},{4,6},{5,3},{6,8},{7,5},{8,10},{9,7},{10,... | collective-permute-start | bytes 1572872 | tf_op jit(solution)/shard_map/ppermute | solution.py:258
  86.4 4.9 %collective-permute-start.3 = (f32[512,256]{1,0:T(8,128)S(1)}, f32[512,256]{1,0:T(8,128)S(1)}, u32[]{:S(2)}, u32[]{:S(2)}) collective-permute-start(f32[512,256]{1,0:T(8,128)S(1)} %add.49), channel_id=1, source_target_pairs={{0,2},{1,15},{2,4},{3,1},{4,6},{5,3},{6,8},{7,5},{8,10},{9,7},{10,... | collective-permute-start | bytes 1572872 | tf_op jit(solution)/shard_map/ppermute | solution.py:258
  91.8 1.1 add.55
  92.9 5.1 %collective-permute-start.7 = (f32[512,256]{1,0:T(8,128)S(1)}, f32[512,256]{1,0:T(8,128)S(1)}, u32[]{:S(2)}, u32[]{:S(2)}) collective-permute-start(f32[512,256]{1,0:T(8,128)S(1)} %add.55), channel_id=1, source_target_pairs={{0,2},{1,15},{2,4},{3,1},{4,6},{5,3},{6,8},{7,5},{8,10},{9,7},{10,... | collective-permute-start | bytes 1572872 | tf_op jit(solution)/shard_map/ppermute | solution.py:258
  98.4 4.1 %collective-permute-start.4 = (f32[512,256]{1,0:T(8,128)S(1)}, f32[512,256]{1,0:T(8,128)S(1)}, u32[]{:S(2)}, u32[]{:S(2)}) collective-permute-start(f32[512,256]{1,0:T(8,128)S(1)} %add.51), channel_id=1, source_target_pairs={{0,2},{1,15},{2,4},{3,1},{4,6},{5,3},{6,8},{7,5},{8,10},{9,7},{10,... | collective-permute-start | bytes 1572872 | tf_op jit(solution)/shard_map/ppermute | solution.py:258
  102.8 1.4 %collective-permute-done.7 = f32[512,256]{1,0:T(8,128)S(1)} collective-permute-done((f32[512,256]{1,0:T(8,128)S(1)}, f32[512,256]{1,0:T(8,128)S(1)}, u32[]{:S(2)}, u32[]{:S(2)}) %collective-permute-start.7) | collective-permute-done | bytes 524320 | tf_op jit(solution)/shard_map/ppermute | solution.py:258
  105.0 5.0 %collective-permute-start.8 = (f32[512,256]{1,0:T(8,128)}, f32[512,256]{1,0:T(8,128)S(1)}, u32[]{:S(2)}, u32[]{:S(2)}) collective-permute-start(f32[512,256]{1,0:T(8,128)} %add.56), channel_id=1, source_target_pairs={{0,2},{1,15},{2,4},{3,1},{4,6},{5,3},{6,8},{7,5},{8,10},{9,7},{10,... | collective-permute-start | bytes 1572872 | tf_op jit(solution)/shard_map/ppermute | solution.py:258
  110.1 5.6 %collective-permute-start.10 = (f32[512,128]{1,0:T(8,128)S(1)}, f32[512,128]{1,0:T(8,128)S(1)}, u32[]{:S(2)}, u32[]{:S(2)}) collective-permute-start(f32[512,128]{1,0:T(8,128)S(1)} %slice_select_fusion), channel_id=1, source_target_pairs={{0,1},{1,0},{2,3},{3,2},{4,5},{5,4},{6,7},{7,6},{8,9},{9,8},{10,11... | collective-permute-start | bytes 786440 | tf_op jit(solution)/shard_map/ppermute | solution.py:192
  116.5 6.9 %collective-permute-start.9 = (f32[512,128]{1,0:T(8,128)S(1)}, f32[512,128]{1,0:T(8,128)S(1)}, u32[]{:S(2)}, u32[]{:S(2)}) collective-permute-start(f32[512,128]{1,0:T(8,128)S(1)} %slice_select_fusion.2), channel_id=1, source_target_pairs={{0,1},{1,0},{2,3},{3,2},{4,5},{5,4},{6,7},{7,6},{8,9},{9,8},{10,11... | collective-permute-start | bytes 786440 | tf_op jit(solution)/shard_map/ppermute | solution.py:192
  (50 shorter events, 11.2 us)
Async XLA Ops:
  0.0 2.1 %copy-start.7 = (bf16[128,2048]{1,0:T(8,128)(2,1)S(1)}, bf16[128,2048]{1,0:T(8,128)(2,1)}, u32[]{:S(2)}) copy-start(bf16[128,2048]{1,0:T(8,128)(2,1)} %own_ref) | copy-start | bytes 1572868
  2.2 16.3 %collective-permute-start = (f32[128,2048]{1,0:T(8,128)S(1)}, f32[128,2048]{1,0:T(8,128)S(1)}, u32[]{:S(2)}, u32[]{:S(2)}) collective-permute-start(f32[128,2048]{1,0:T(8,128)S(1)} %convert_element_type.13), channel_id=1, source_target_pairs={{0,1},{1,0},{2,3},{3,2},{4,5},{5,4},{6,7},{7,6},{8,9},{9,8},{10,11... | collective-permute-start | bytes 3145736 | tf_op jit(solution)/shard_map/ppermute | solution.py:192
  11.0 16.7 %all-to-all-start = ((f32[32,8,128]{2,1,0:T(8,128)}), f32[32,8,128]{2,1,0:T(8,128)S(1)}, u32[]{:S(2)}, u32[]{:S(2)}) async-start(f32[32,8,128]{2,1,0:T(8,128)} %bitcast.3), calls=%async_computation | async-start | bytes 262144 | tf_op jit(solution)/shard_map/all_to_all | solution.py:284
  18.5 1.0 copy-start.8
  19.5 24.1 %copy-start.4 = (bf16[1024,1,128]{2,0,1:T(8,128)(2,1)S(1)}, bf16[1024,1,128]{2,0,1:T(8,128)(2,1)}, u32[]{:S(2)}) copy-start(bf16[1024,1,128]{2,0,1:T(8,128)(2,1)} %param.7) | copy-start | bytes 786436
  22.1 21.6 %copy-start.1 = (bf16[1024,1,128]{2,0,1:T(8,128)(2,1)S(1)}, bf16[1024,1,128]{2,0,1:T(8,128)(2,1)}, u32[]{:S(2)}) copy-start(bf16[1024,1,128]{2,0,1:T(8,128)(2,1)} %param.8) | copy-start | bytes 786436
  22.1 21.6 %copy-start.2 = (bf16[1024,1,128]{2,0,1:T(8,128)(2,1)S(1)}, bf16[1024,1,128]{2,0,1:T(8,128)(2,1)}, u32[]{:S(2)}) copy-start(bf16[1024,1,128]{2,0,1:T(8,128)(2,1)} %param.9) | copy-start | bytes 786436
  27.7 0.7 copy-start.10
  29.9 13.7 %all-to-all-start.1 = ((f32[32,8,128]{2,1,0:T(8,128)}), f32[32,8,128]{2,1,0:T(8,128)S(1)}, u32[]{:S(2)}, u32[]{:S(2)}) async-start(f32[32,8,128]{2,1,0:T(8,128)} %prefix.1), calls=%async_computation.1 | async-start | bytes 262144 | tf_op jit(solution)/shard_map/all_to_all | solution.py:287
  43.7 0.7 copy-start.3
  43.7 0.7 copy-start.5
  59.2 6.0 %copy-start = (f32[1024,128]{1,0:T(8,128)}, f32[1024,128]{1,0:T(8,128)S(1)}, u32[]{:S(2)}) copy-start(f32[1024,128]{1,0:T(8,128)S(1)} %solve.1.own_ref) | copy-start | bytes 1572868
  59.2 6.0 %collective-permute-start.1 = (f32[1024,128]{1,0:T(8,128)S(1)}, f32[1024,128]{1,0:T(8,128)S(1)}, u32[]{:S(2)}, u32[]{:S(2)}) collective-permute-start(f32[1024,128]{1,0:T(8,128)S(1)} %solve.1.own_ref), channel_id=1, source_target_pairs={{0,1},{1,0},{2,3},{3,2},{4,5},{5,4},{6,7},{7,6},{8,9},{9,8},{10,11... | collective-permute-start | bytes 1572872 | tf_op jit(solution)/shard_map/ppermute | solution.py:192
  63.6 5.4 %copy-start.6 = (bf16[8,256,256]{2,1,0:T(8,128)(2,1)S(1)}, bf16[8,256,256]{2,1,0:T(8,128)(2,1)}, u32[]{:S(2)}) copy-start(bf16[8,256,256]{2,1,0:T(8,128)(2,1)} %join_weight.1) | copy-start | bytes 3145732
  65.1 0.8 copy-start.9
  69.3 11.2 %collective-permute-start.5 = (f32[512,256]{1,0:T(8,128)S(1)}, f32[512,256]{1,0:T(8,128)S(1)}, u32[]{:S(2)}, u32[]{:S(2)}) collective-permute-start(f32[512,256]{1,0:T(8,128)S(1)} %fusion.4), channel_id=1, source_target_pairs={{0,2},{1,15},{2,4},{3,1},{4,6},{5,3},{6,8},{7,5},{8,10},{9,7},{10,... | collective-permute-start | bytes 1572872 | tf_op jit(solution)/shard_map/ppermute | solution.py:258
  75.5 10.8 %collective-permute-start.2 = (f32[512,256]{1,0:T(8,128)}, f32[512,256]{1,0:T(8,128)S(1)}, u32[]{:S(2)}, u32[]{:S(2)}) collective-permute-start(f32[512,256]{1,0:T(8,128)} %fusion.16), channel_id=1, source_target_pairs={{0,2},{1,15},{2,4},{3,1},{4,6},{5,3},{6,8},{7,5},{8,10},{9,7},{10,... | collective-permute-start | bytes 1572872 | tf_op jit(solution)/shard_map/ppermute | solution.py:258
  80.6 11.2 %collective-permute-start.6 = (f32[512,256]{1,0:T(8,128)S(1)}, f32[512,256]{1,0:T(8,128)}, u32[]{:S(2)}, u32[]{:S(2)}) collective-permute-start(f32[512,256]{1,0:T(8,128)S(1)} %add.54), channel_id=1, source_target_pairs={{0,2},{1,15},{2,4},{3,1},{4,6},{5,3},{6,8},{7,5},{8,10},{9,7},{10,... | collective-permute-start | bytes 1572872 | tf_op jit(solution)/shard_map/ppermute | solution.py:258
  86.4 11.9 %collective-permute-start.3 = (f32[512,256]{1,0:T(8,128)S(1)}, f32[512,256]{1,0:T(8,128)S(1)}, u32[]{:S(2)}, u32[]{:S(2)}) collective-permute-start(f32[512,256]{1,0:T(8,128)S(1)} %add.49), channel_id=1, source_target_pairs={{0,2},{1,15},{2,4},{3,1},{4,6},{5,3},{6,8},{7,5},{8,10},{9,7},{10,... | collective-permute-start | bytes 1572872 | tf_op jit(solution)/shard_map/ppermute | solution.py:258
  92.9 11.2 %collective-permute-start.7 = (f32[512,256]{1,0:T(8,128)S(1)}, f32[512,256]{1,0:T(8,128)S(1)}, u32[]{:S(2)}, u32[]{:S(2)}) collective-permute-start(f32[512,256]{1,0:T(8,128)S(1)} %add.55), channel_id=1, source_target_pairs={{0,2},{1,15},{2,4},{3,1},{4,6},{5,3},{6,8},{7,5},{8,10},{9,7},{10,... | collective-permute-start | bytes 1572872 | tf_op jit(solution)/shard_map/ppermute | solution.py:258
  98.4 11.7 %collective-permute-start.4 = (f32[512,256]{1,0:T(8,128)S(1)}, f32[512,256]{1,0:T(8,128)S(1)}, u32[]{:S(2)}, u32[]{:S(2)}) collective-permute-start(f32[512,256]{1,0:T(8,128)S(1)} %add.51), channel_id=1, source_target_pairs={{0,2},{1,15},{2,4},{3,1},{4,6},{5,3},{6,8},{7,5},{8,10},{9,7},{10,... | collective-permute-start | bytes 1572872 | tf_op jit(solution)/shard_map/ppermute | solution.py:258
  105.0 11.4 %collective-permute-start.8 = (f32[512,256]{1,0:T(8,128)}, f32[512,256]{1,0:T(8,128)S(1)}, u32[]{:S(2)}, u32[]{:S(2)}) collective-permute-start(f32[512,256]{1,0:T(8,128)} %add.56), channel_id=1, source_target_pairs={{0,2},{1,15},{2,4},{3,1},{4,6},{5,3},{6,8},{7,5},{8,10},{9,7},{10,... | collective-permute-start | bytes 1572872 | tf_op jit(solution)/shard_map/ppermute | solution.py:258
  110.1 13.6 %collective-permute-start.10 = (f32[512,128]{1,0:T(8,128)S(1)}, f32[512,128]{1,0:T(8,128)S(1)}, u32[]{:S(2)}, u32[]{:S(2)}) collective-permute-start(f32[512,128]{1,0:T(8,128)S(1)} %slice_select_fusion), channel_id=1, source_target_pairs={{0,1},{1,0},{2,3},{3,2},{4,5},{5,4},{6,7},{7,6},{8,9},{9,8},{10,11... | collective-permute-start | bytes 786440 | tf_op jit(solution)/shard_map/ppermute | solution.py:192
  116.5 8.1 %collective-permute-start.9 = (f32[512,128]{1,0:T(8,128)S(1)}, f32[512,128]{1,0:T(8,128)S(1)}, u32[]{:S(2)}, u32[]{:S(2)}) collective-permute-start(f32[512,128]{1,0:T(8,128)S(1)} %slice_select_fusion.2), channel_id=1, source_target_pairs={{0,1},{1,0},{2,3},{3,2},{4,5},{5,4},{6,7},{7,6},{8,9},{9,8},{10,11... | collective-permute-start | bytes 786440 | tf_op jit(solution)/shard_map/ppermute | solution.py:192

commit v3 on v2

--- a/solution.py
+++ b/solution.py
@@ -60,7 +60,7 @@
 
 
 def solve_kernel(
-    reg_ref, q_ref, k_ref, v_ref, before_ref, gain_ref, norm_ref, out_ref,
+    reg_ref, q_ref, k_ref, v_ref, before_ref, gain_ref, norm_ref, early_ref, late_ref,
     q_buf, k_buf, v_buf, first, second, last, x_ref, r_ref, p_ref, sems,
 ):
     copies = [
@@ -153,7 +153,9 @@
         ) + mm(last[b, :, 3 * BLOCK :], x_low)
         square = jnp.mean(read * read, axis=0, keepdims=True)
         normed = read * norm_col * lax.rsqrt(square + 1e-06)
-        out_ref[b * BLOCK : (b + 1) * BLOCK, :] = normed.T.astype(BF16).astype(F32)
+        out_ref = early_ref if 2 * b < blocks else late_ref
+        place = (b % (blocks // 2)) * BLOCK
+        out_ref[place : place + BLOCK, :] = normed.T.astype(BF16).astype(F32)
 
 
 def solve(reg, queries, keys, values, before, gain, norm_gain):
@@ -162,11 +164,11 @@
     vmem = pl.BlockSpec(memory_space=pltpu.VMEM)
     return pl.pallas_call(
         solve_kernel,
-        out_shape=jax.ShapeDtypeStruct((tokens, width), F32),
+        out_shape=(jax.ShapeDtypeStruct((tokens // 2, width), F32),) * 2,
         in_specs=[pl.BlockSpec(memory_space=pltpu.SMEM)]
         + [pl.BlockSpec(memory_space=pl.ANY)] * 3
         + [vmem] * 3,
-        out_specs=vmem,
+        out_specs=(vmem, vmem),
         scratch_shapes=[
             pltpu.VMEM((tokens, width), BF16),
             pltpu.VMEM((tokens, width), BF16),
@@ -210,68 +212,82 @@
     )(own, other)
 
 
-def join_rows_kernel(own_ref, other_ref, out_ref):
+def open_kernel(where_ref, own_ref, other_ref, weights_ref, rows_ref, far_ref):
     width = own_ref.shape[1]
-    out_ref[:, 0:width] = own_ref[...].astype(BF16)
-    out_ref[:, width:] = other_ref[...].astype(BF16)
-
-
-def join_rows(own, other):
+    rows = jnp.concatenate([own_ref[...], other_ref[...]], axis=1).astype(BF16)
+    rows_ref[...] = rows
+    columns = weights_ref[where_ref[0]]
+    columns = jnp.where(where_ref[1] == 0, columns[:, :width], columns[:, width:])
+    far_ref[...] = mm(rows, columns)
+
+
+def opening(where, own, other, weights):
     tokens, width = own.shape
-    return pl.pallas_call(
-        join_rows_kernel,
-        out_shape=jax.ShapeDtypeStruct((tokens, 2 * width), BF16),
-        name="join_rows",
-    )(own, other)
+    vmem = pl.BlockSpec(memory_space=pltpu.VMEM)
+    return pl.pallas_call(
+        open_kernel,
+        out_shape=(
+            jax.ShapeDtypeStruct((tokens, 2 * width), BF16),
+            jax.ShapeDtypeStruct((tokens, width), F32),
+        ),
+        in_specs=[pl.BlockSpec(memory_space=pltpu.SMEM), vmem, vmem, vmem],
+        out_specs=(vmem, vmem),
+        name="opening",
+    )(where, own, other, weights)
 
 
 def project(normed, weights):
-    tokens, width = normed.shape
+    width = normed[0].shape[1]
     heads = lax.axis_size("head")
     place = lax.axis_index("head").astype(jnp.uint32)
     chips = heads // 2
     chip, core = lax.div(place, jnp.uint32(2)), lax.rem(place, jnp.uint32(2))
     left_going = core == 1
-    ring = [(i, (i + (2 if i % 2 == 0 else heads - 2)) % heads) for i in range(heads)]
-    both = join_rows(normed, swapped(normed))
-    half = tokens // 2
-    early, late = both[:half], both[half:]
-    rows = (
-        jnp.where(left_going, late, early),
-        jnp.where(left_going, early, late),
-    )
-
-    def part(piece, away):
+    step = lambda i: 2 if i % 2 == 0 else heads - 2
+    ring = [(i, (i + step(i)) % heads) for i in range(heads)]
+    cross = [(i, ((i + step(i)) % heads) ^ 1) for i in range(heads)]
+
+    def index_of(away):
         ahead = jnp.where(left_going, jnp.uint32(chips - away), jnp.uint32(away % chips))
-        index = lax.rem(chip + ahead, jnp.uint32(chips))
-        columns = lax.dynamic_index_in_dim(weights, index, axis=0, keepdims=False)
-        return jnp.dot(rows[piece], columns, preferred_element_type=F32)
-
-    flows = [None, None]
-    for away in range(chips // 2, 0, -1):
-        for piece in (0, 1):
-            if away == chips // 2 and piece == 1:
-                continue
-            term = part(piece, away)
-            if flows[piece] is not None:
-                term = flows[piece] + term
-            flows[piece] = lax.ppermute(term, "head", ring)
-
-    def columns_of(value, other):
-        zero, one = value[:, :width], value[:, width:]
-        return jnp.where(left_going != other, one, zero)
-
-    given = [swapped(columns_of(flow, True)) for flow in flows]
-    done = [
-        columns_of(part(piece, 0) + flows[piece], False) + given[1 - piece]
-        for piece in (0, 1)
-    ]
-    first, second = (value.astype(BF16) for value in done)
-    return jnp.where(
-        left_going,
-        jnp.concatenate([second, first], axis=0),
-        jnp.concatenate([first, second], axis=0),
-    )
+        return lax.rem(chip + ahead, jnp.uint32(chips))
+
+    def part(rows, away):
+        columns = lax.dynamic_index_in_dim(weights, index_of(away), axis=0, keepdims=False)
+        return jnp.dot(rows, columns, preferred_element_type=F32)
+
+    def own_columns(value):
+        return jnp.where(left_going, value[:, width:], value[:, :width])
+
+    def other_columns(value):
+        return jnp.where(left_going, value[:, :width], value[:, width:])
+
+    where = jnp.stack([index_of(chips // 2), core]).astype(jnp.int32)
+    others = [swapped(half) for half in normed]
+    halves_of, flows = [], []
+    for own, other in zip(normed, others):
+        rows, far = opening(where, own, other, weights)
+        halves_of.append(rows)
+        flows.append(lax.ppermute(far, "head", ring))
+    for away in range(chips // 2 - 1, 1, -1):
+        for piece, rows in enumerate(halves_of):
+            flow = flows[piece]
+            if flow.shape[1] == width:
+                blank = jnp.zeros_like(flow)
+                flow = jnp.concatenate(
+                    [
+                        jnp.where(left_going, blank, flow),
+                        jnp.where(left_going, flow, blank),
+                    ],
+                    axis=1,
+                )
+            flows[piece] = lax.ppermute(flow + part(rows, away), "head", ring)
+    done = []
+    for piece, rows in enumerate(halves_of):
+        last = flows[piece] + part(rows, 1)
+        same = lax.ppermute(own_columns(last), "head", ring)
+        crossed = lax.ppermute(other_columns(last), "head", cross)
+        done.append((own_columns(part(rows, 0)) + same + crossed).astype(BF16))
+    return jnp.concatenate(done, axis=0)
 
 
 def body(queries, keys, values, key_gain, reg, norm_gain, out_weight):

time: 126 us -> 124 us (0.984)
  starting transfers between devices: 70.1 us -> 65.3 us
  waiting for transfers between devices: 21 us -> 24 us
  Pallas kernels: 23.1 us -> 25.7 us
  other arithmetic: 4.29 us -> 1.94 us
    ppermute x4 -> x3, starting transfers between devices: 25.7 us -> 15.2 us  [swapped(): return lax.ppermute(value, 'head', [(i, i ^ 1) for i in range(heads)])]
    ppermute x7 -> x10, starting transfers between devices: 32.3 us -> 38.1 us  [the longest x4 14.8 us: project(): flows[piece] = lax.ppermute(flow + part(rows, away), 'head', ring)]
    ppermute x7 -> x10, waiting for transfers between devices: 4.45 us -> 9.81 us  [the longest x4 4 us: project(): flows[piece] = lax.ppermute(flow + part(rows, away), 'head', ring)]
    pallas_call x2 -> x3, Pallas kernels: 16.9 us -> 19.5 us  [the longest x1 14.8 us: solve(): pl.pallas_call(solve_kernel, out_shape=(jax.ShapeDtypeStruct((tokens // 2...]
    ppermute x4 -> x3, waiting for transfers between devices: 2.34 us -> 0.01 us  [swapped(): return lax.ppermute(value, 'head', [(i, i ^ 1) for i in range(heads)])]
    add x5 -> x4, other arithmetic: 2.19 us -> 0.27 us  [the longest x2 0.14 us: project(): last = flows[piece] + part(rows, 1)]
    select_n x4, other arithmetic: 1.9 us -> 0.15 us  [the longest x2 0.08 us: own_columns(): return jnp.where(left_going, value[:, width:], value[:, :width])]
    dot_general x9 -> x8, matrix products: 2.87 us -> 1.81 us  [part(): return jnp.dot(rows, columns, preferred_element_type=F32)]
  transfers between devices with their start and end apart: 13 -> 15, of which waited for: 9 -> 8; matrix products, arithmetic and copies ran while one was open for 4% -> 2% of each run, Pallas kernels for 2% -> 6%
where the time goes in v3:
time: 124 us
  starting transfers between devices  65.3 us (53%)
  Pallas kernels  25.7 us (21%)
  waiting for transfers between devices  24 us (19%)
  local copies, waits for them, and re-layouts  3.71 us (3%)
  other arithmetic  1.94 us (2%)
  matrix products  1.81 us (1%)
    ppermute x3, starting transfers between devices, swapped(): return lax.ppermute(value, 'head', [(i, i ^ 1) for i in range(heads)])  15.2 us
    pallas_call x1, Pallas kernels, solve(): pl.pallas_call(solve_kernel, out_shape=(jax.ShapeDtypeStruct((tokens // 2...  14.8 us
    ppermute x4, starting transfers between devices, project(): flows[piece] = lax.ppermute(flow + part(rows, away), 'head', ring)  14.8 us
    ppermute x2, starting transfers between devices, project(): crossed = lax.ppermute(other_columns(last), 'head', cross)  9.3 us
    all_to_all x1, waiting for transfers between devices, body(): before = lax.all_to_all(exclusive(parts), 'seq', 0, 0)  8.54 us
    ppermute x2, starting transfers between devices, project(): flows.append(lax.ppermute(far, 'head', ring))  8.2 us
    all_to_all x1, starting transfers between devices, body(): parts = lax.all_to_all(state.reshape(devices, rows, width), 'seq', 0, 0)  7.52 us
    ppermute x2, starting transfers between devices, project(): same = lax.ppermute(own_columns(last), 'head', ring)  5.81 us
  transfers between devices with their start and end apart: 15, of which 8 were waited for; matrix products, arithmetic and copies ran while one was open for 2% of the time, Pallas kernels for 6%

profile of v3, /device:TPU:1, one launch (start us, length us, event | category | flops | bytes accessed | tf_op | source)
XLA Modules:
  0.0 123.6 jit_solution(12796210858628693550)
XLA Ops:
  0.0 2.1 %local_state.1 = f32[256,128]{1,0:T(8,128)} custom-call(bf16[1024,128]{1,0:T(8,128)(2,1)} %bitcast.39, bf16[1024,128]{1,0:T(8,128)(2,1)} %bitcast.41, f32[1,128]{1,0:T(1,128)} %gain_ref.3), custom_call_target="tpu_custom_call" | custom-call | tf_op jit(solution)/shard_map/local_state/pallas_call | solution.py:39
  2.2 8.8 %collective-permute-start = (f32[128,2048]{1,0:T(8,128)S(1)}, f32[128,2048]{1,0:T(8,128)S(1)}, u32[]{:S(2)}, u32[]{:S(2)}) collective-permute-start(f32[128,2048]{1,0:T(8,128)S(1)} %convert_element_type.17), channel_id=1, source_target_pairs={{0,1},{1,0},{2,3},{3,2},{4,5},{5,4},{6,7},{7,6},{8,9},{9,8},{10,11... | collective-permute-start | bytes 3145736 | tf_op jit(solution)/shard_map/ppermute | solution.py:194
  11.0 7.5 %all-to-all-start = ((f32[32,8,128]{2,1,0:T(8,128)}), f32[32,8,128]{2,1,0:T(8,128)S(1)}, u32[]{:S(2)}, u32[]{:S(2)}) async-start(f32[32,8,128]{2,1,0:T(8,128)} %bitcast.5), calls=%async_computation | async-start | bytes 262144 | tf_op jit(solution)/shard_map/all_to_all | solution.py:300
  19.5 2.5 %join_weight.1.weights_ref = bf16[8,256,256]{2,1,0:T(8,128)(2,1)} custom-call(bf16[128,2048]{1,0:T(8,128)(2,1)} %own_ref, f32[128,2048]{1,0:T(8,128)} %copy-done.11), custom_call_target="tpu_custom_call" | custom-call | tf_op jit(solution)/shard_map/join_weight/pallas_call | solution.py:208
  22.0 5.7 %all-to-all-done.x_ref = f32[32,8,128]{2,1,0:T(8,128)S(1)} async-done(((f32[32,8,128]{2,1,0:T(8,128)}), f32[32,8,128]{2,1,0:T(8,128)S(1)}, u32[]{:S(2)}, u32[]{:S(2)}) %all-to-all-start) | async-done | bytes 131104 | tf_op jit(solution)/shard_map/all_to_all | solution.py:300
  28.3 1.6 %prefix.1 = f32[32,8,128]{2,1,0:T(8,128)} custom-call(f32[32,8,128]{2,1,0:T(8,128)} %copy-done.12), custom_call_target="tpu_custom_call" | custom-call | tf_op jit(solution)/shard_map/prefix/pallas_call | solution.py:55
  29.9 4.5 %all-to-all-start.1 = ((f32[32,8,128]{2,1,0:T(8,128)}), f32[32,8,128]{2,1,0:T(8,128)S(1)}, u32[]{:S(2)}, u32[]{:S(2)}) async-start(f32[32,8,128]{2,1,0:T(8,128)} %prefix.1), calls=%async_computation.1 | async-start | bytes 262144 | tf_op jit(solution)/shard_map/all_to_all | solution.py:303
  35.1 8.5 %all-to-all-done.1 = f32[32,8,128]{2,1,0:T(8,128)S(1)} async-done(((f32[32,8,128]{2,1,0:T(8,128)}), f32[32,8,128]{2,1,0:T(8,128)S(1)}, u32[]{:S(2)}, u32[]{:S(2)}) %all-to-all-start.1) | async-done | bytes 131104 | tf_op jit(solution)/shard_map/all_to_all | solution.py:303
  44.3 14.8 %solve.1 = (f32[512,128]{1,0:T(8,128)S(1)}, f32[512,128]{1,0:T(8,128)S(1)}) custom-call(f32[1]{0:T(128)S(6)} %copy.8.reg_ref, bf16[1024,128]{1,0:T(8,128)(2,1)S(1)} %bitcast.44, bf16[1024,128]{1,0:T(8,128)(2,1)S(1)} %bitcast.40, bf16[1024,128]{1,0:T(8,128)(2,1)S(1)} %bitcast.42, f32[256,128]{1,0:T(8,128)S(1)} %bitcast.43, f32[1,128]{1,0:T(1,128)S(1)} %copy-done.4, ...), custom_call_target="tpu_custom_call" | custom-call | flops 60000002048 | bytes 2097152 | tf_op jit(solution)/shard_map/solve/pallas_call | solution.py:165
  59.2 4.5 %collective-permute-start.1 = (f32[512,128]{1,0:T(8,128)S(1)}, f32[512,128]{1,0:T(8,128)S(1)}, u32[]{:S(2)}, u32[]{:S(2)}) collective-permute-start(f32[512,128]{1,0:T(8,128)S(1)} %get-tuple-element.18.own_ref), channel_id=1, source_target_pairs={{0,1},{1,0},{2,3},{3,2},{4,5},{5,4},{6,7},{7,6},{8,9},{9,8},{10,11... | collective-permute-start | bytes 786440 | tf_op jit(solution)/shard_map/ppermute | solution.py:194
  64.3 1.9 %collective-permute-start.7 = (f32[512,128]{1,0:T(8,128)S(1)}, f32[512,128]{1,0:T(8,128)S(1)}, u32[]{:S(2)}, u32[]{:S(2)}) collective-permute-start(f32[512,128]{1,0:T(8,128)S(1)} %get-tuple-element.22.own_ref), channel_id=1, source_target_pairs={{0,1},{1,0},{2,3},{3,2},{4,5},{5,4},{6,7},{7,6},{8,9},{9,8},{10,11... | collective-permute-start | bytes 786440 | tf_op jit(solution)/shard_map/ppermute | solution.py:194
  67.0 2.3 %opening.2 = (bf16[512,256]{1,0:T(8,128)(2,1)}, f32[512,128]{1,0:T(8,128)}) custom-call(s32[2]{0:T(128)} %add_convert_fusion.where_ref, f32[512,128]{1,0:T(8,128)} %copy-done.3, f32[512,128]{1,0:T(8,128)} %copy-done.14, bf16[8,256,256]{2,1,0:T(8,128)(2,1)} %join_weight.1.weights_ref), custom_call_target="tpu_custom_call" | custom-call | tf_op jit(solution)/shard_map/opening/pallas_call | solution.py:227
  69.3 5.1 %collective-permute-start.2 = (f32[512,128]{1,0:T(8,128)}, f32[512,128]{1,0:T(8,128)S(1)}, u32[]{:S(2)}, u32[]{:S(2)}) collective-permute-start(f32[512,128]{1,0:T(8,128)} %get-tuple-element.21), channel_id=1, source_target_pairs={{0,2},{1,15},{2,4},{3,1},{4,6},{5,3},{6,8},{7,5},{8,10},{9,7},{10,... | collective-permute-start | bytes 786440 | tf_op jit(solution)/shard_map/ppermute | solution.py:270
  75.1 2.4 %opening.3 = (bf16[512,256]{1,0:T(8,128)(2,1)}, f32[512,128]{1,0:T(8,128)}) custom-call(s32[2]{0:T(128)} %add_convert_fusion.where_ref, f32[512,128]{1,0:T(8,128)} %copy-done.2, f32[512,128]{1,0:T(8,128)} %copy-done.13, bf16[8,256,256]{2,1,0:T(8,128)(2,1)} %join_weight.1.weights_ref), custom_call_target="tpu_custom_call" | custom-call | tf_op jit(solution)/shard_map/opening/pallas_call | solution.py:227
  77.5 3.1 %collective-permute-start.8 = (f32[512,128]{1,0:T(8,128)}, f32[512,128]{1,0:T(8,128)S(1)}, u32[]{:S(2)}, u32[]{:S(2)}) collective-permute-start(f32[512,128]{1,0:T(8,128)} %get-tuple-element.24), channel_id=1, source_target_pairs={{0,2},{1,15},{2,4},{3,1},{4,6},{5,3},{6,8},{7,5},{8,10},{9,7},{10,... | collective-permute-start | bytes 786440 | tf_op jit(solution)/shard_map/ppermute | solution.py:270
  81.0 3.1 %collective-permute-start.3 = (f32[512,256]{1,0:T(8,128)S(1)}, f32[512,256]{1,0:T(8,128)S(1)}, u32[]{:S(2)}, u32[]{:S(2)}) collective-permute-start(f32[512,256]{1,0:T(8,128)S(1)} %maximum_add_fusion), channel_id=1, source_target_pairs={{0,2},{1,15},{2,4},{3,1},{4,6},{5,3},{6,8},{7,5},{8,10},{9,7},{10,... | collective-permute-start | bytes 1572872 | tf_op jit(solution)/shard_map/ppermute | solution.py:283
  85.5 3.9 %collective-permute-start.9 = (f32[512,256]{1,0:T(8,128)S(1)}, f32[512,256]{1,0:T(8,128)S(1)}, u32[]{:S(2)}, u32[]{:S(2)}) collective-permute-start(f32[512,256]{1,0:T(8,128)S(1)} %maximum_add_fusion.1), channel_id=1, source_target_pairs={{0,2},{1,15},{2,4},{3,1},{4,6},{5,3},{6,8},{7,5},{8,10},{9,7},{10,... | collective-permute-start | bytes 1572872 | tf_op jit(solution)/shard_map/ppermute | solution.py:283
  91.4 3.9 %collective-permute-start.4 = (f32[512,256]{1,0:T(8,128)S(1)}, f32[512,256]{1,0:T(8,128)S(1)}, u32[]{:S(2)}, u32[]{:S(2)}) collective-permute-start(f32[512,256]{1,0:T(8,128)S(1)} %add.54), channel_id=1, source_target_pairs={{0,2},{1,15},{2,4},{3,1},{4,6},{5,3},{6,8},{7,5},{8,10},{9,7},{10,... | collective-permute-start | bytes 1572872 | tf_op jit(solution)/shard_map/ppermute | solution.py:283
  97.0 3.9 %collective-permute-start.10 = (f32[512,256]{1,0:T(8,128)S(1)}, f32[512,256]{1,0:T(8,128)S(1)}, u32[]{:S(2)}, u32[]{:S(2)}) collective-permute-start(f32[512,256]{1,0:T(8,128)S(1)} %add.60), channel_id=1, source_target_pairs={{0,2},{1,15},{2,4},{3,1},{4,6},{5,3},{6,8},{7,5},{8,10},{9,7},{10,... | collective-permute-start | bytes 1572872 | tf_op jit(solution)/shard_map/ppermute | solution.py:283
  102.7 3.9 %collective-permute-start.5 = (f32[512,128]{1,0:T(8,128)S(1)}, f32[512,128]{1,0:T(8,128)S(1)}, u32[]{:S(2)}, u32[]{:S(2)}) collective-permute-start(f32[512,128]{1,0:T(8,128)S(1)} %get-tuple-element.25), channel_id=1, source_target_pairs={{0,2},{1,15},{2,4},{3,1},{4,6},{5,3},{6,8},{7,5},{8,10},{9,7},{10,... | collective-permute-start | bytes 786440 | tf_op jit(solution)/shard_map/ppermute | solution.py:287
  106.5 5.3 %collective-permute-start.6 = (f32[512,128]{1,0:T(8,128)S(1)}, f32[512,128]{1,0:T(8,128)S(1)}, u32[]{:S(2)}, u32[]{:S(2)}) collective-permute-start(f32[512,128]{1,0:T(8,128)S(1)} %get-tuple-element.26), channel_id=1, source_target_pairs={{0,3},{1,14},{2,5},{3,0},{4,7},{5,2},{6,9},{7,4},{8,11},{9,6},{10,... | collective-permute-start | bytes 786440 | tf_op jit(solution)/shard_map/ppermute | solution.py:288
  112.0 1.9 %collective-permute-start.11 = (f32[512,128]{1,0:T(8,128)S(1)}, f32[512,128]{1,0:T(8,128)S(1)}, u32[]{:S(2)}, u32[]{:S(2)}) collective-permute-start(f32[512,128]{1,0:T(8,128)S(1)} %get-tuple-element.27), channel_id=1, source_target_pairs={{0,2},{1,15},{2,4},{3,1},{4,6},{5,3},{6,8},{7,5},{8,10},{9,7},{10,... | collective-permute-start | bytes 786440 | tf_op jit(solution)/shard_map/ppermute | solution.py:287
  114.0 4.0 %collective-permute-start.12 = (f32[512,128]{1,0:T(8,128)S(1)}, f32[512,128]{1,0:T(8,128)S(1)}, u32[]{:S(2)}, u32[]{:S(2)}) collective-permute-start(f32[512,128]{1,0:T(8,128)S(1)} %get-tuple-element.28), channel_id=1, source_target_pairs={{0,3},{1,14},{2,5},{3,0},{4,7},{5,2},{6,9},{7,4},{8,11},{9,6},{10,... | collective-permute-start | bytes 786440 | tf_op jit(solution)/shard_map/ppermute | solution.py:288
  119.4 3.4 %collective-permute-done.12 = f32[512,128]{1,0:T(8,128)S(1)} collective-permute-done((f32[512,128]{1,0:T(8,128)S(1)}, f32[512,128]{1,0:T(8,128)S(1)}, u32[]{:S(2)}, u32[]{:S(2)}) %collective-permute-start.12) | collective-permute-done | bytes 262176 | tf_op jit(solution)/shard_map/ppermute | solution.py:288
  (63 shorter events, 13.9 us)
Async XLA Ops:
  0.0 2.1 %copy-start.10 = (bf16[128,2048]{1,0:T(8,128)(2,1)S(1)}, bf16[128,2048]{1,0:T(8,128)(2,1)}, u32[]{:S(2)}) copy-start(bf16[128,2048]{1,0:T(8,128)(2,1)} %own_ref) | copy-start | bytes 1572868
  2.2 16.3 %collective-permute-start = (f32[128,2048]{1,0:T(8,128)S(1)}, f32[128,2048]{1,0:T(8,128)S(1)}, u32[]{:S(2)}, u32[]{:S(2)}) collective-permute-start(f32[128,2048]{1,0:T(8,128)S(1)} %convert_element_type.17), channel_id=1, source_target_pairs={{0,1},{1,0},{2,3},{3,2},{4,5},{5,4},{6,7},{7,6},{8,9},{9,8},{10,11... | collective-permute-start | bytes 3145736 | tf_op jit(solution)/shard_map/ppermute | solution.py:194
  11.0 16.7 %all-to-all-start = ((f32[32,8,128]{2,1,0:T(8,128)}), f32[32,8,128]{2,1,0:T(8,128)S(1)}, u32[]{:S(2)}, u32[]{:S(2)}) async-start(f32[32,8,128]{2,1,0:T(8,128)} %bitcast.5), calls=%async_computation | async-start | bytes 262144 | tf_op jit(solution)/shard_map/all_to_all | solution.py:300
  19.5 24.1 %copy-start.5 = (bf16[1024,1,128]{2,0,1:T(8,128)(2,1)S(1)}, bf16[1024,1,128]{2,0,1:T(8,128)(2,1)}, u32[]{:S(2)}) copy-start(bf16[1024,1,128]{2,0,1:T(8,128)(2,1)} %param.7) | copy-start | bytes 786436
  22.0 21.7 %copy-start = (bf16[1024,1,128]{2,0,1:T(8,128)(2,1)S(1)}, bf16[1024,1,128]{2,0,1:T(8,128)(2,1)}, u32[]{:S(2)}) copy-start(bf16[1024,1,128]{2,0,1:T(8,128)(2,1)} %param.8) | copy-start | bytes 786436
  22.0 21.7 %copy-start.1 = (bf16[1024,1,128]{2,0,1:T(8,128)(2,1)S(1)}, bf16[1024,1,128]{2,0,1:T(8,128)(2,1)}, u32[]{:S(2)}) copy-start(bf16[1024,1,128]{2,0,1:T(8,128)(2,1)} %param.9) | copy-start | bytes 786436
  29.9 13.7 %all-to-all-start.1 = ((f32[32,8,128]{2,1,0:T(8,128)}), f32[32,8,128]{2,1,0:T(8,128)S(1)}, u32[]{:S(2)}, u32[]{:S(2)}) async-start(f32[32,8,128]{2,1,0:T(8,128)} %prefix.1), calls=%async_computation.1 | async-start | bytes 262144 | tf_op jit(solution)/shard_map/all_to_all | solution.py:303
  59.2 7.1 %copy-start.3 = (f32[512,128]{1,0:T(8,128)}, f32[512,128]{1,0:T(8,128)S(1)}, u32[]{:S(2)}) copy-start(f32[512,128]{1,0:T(8,128)S(1)} %get-tuple-element.18.own_ref) | copy-start | bytes 786436
  59.2 10.1 %copy-start.2 = (f32[512,128]{1,0:T(8,128)}, f32[512,128]{1,0:T(8,128)S(1)}, u32[]{:S(2)}) copy-start(f32[512,128]{1,0:T(8,128)S(1)} %get-tuple-element.22.own_ref) | copy-start | bytes 786436
  59.2 7.0 %collective-permute-start.1 = (f32[512,128]{1,0:T(8,128)S(1)}, f32[512,128]{1,0:T(8,128)S(1)}, u32[]{:S(2)}, u32[]{:S(2)}) collective-permute-start(f32[512,128]{1,0:T(8,128)S(1)} %get-tuple-element.18.own_ref), channel_id=1, source_target_pairs={{0,1},{1,0},{2,3},{3,2},{4,5},{5,4},{6,7},{7,6},{8,9},{9,8},{10,11... | collective-permute-start | bytes 786440 | tf_op jit(solution)/shard_map/ppermute | solution.py:194
  64.3 10.1 %collective-permute-start.7 = (f32[512,128]{1,0:T(8,128)S(1)}, f32[512,128]{1,0:T(8,128)S(1)}, u32[]{:S(2)}, u32[]{:S(2)}) collective-permute-start(f32[512,128]{1,0:T(8,128)S(1)} %get-tuple-element.22.own_ref), channel_id=1, source_target_pairs={{0,1},{1,0},{2,3},{3,2},{4,5},{5,4},{6,7},{7,6},{8,9},{9,8},{10,11... | collective-permute-start | bytes 786440 | tf_op jit(solution)/shard_map/ppermute | solution.py:194
  69.3 11.3 %collective-permute-start.2 = (f32[512,128]{1,0:T(8,128)}, f32[512,128]{1,0:T(8,128)S(1)}, u32[]{:S(2)}, u32[]{:S(2)}) collective-permute-start(f32[512,128]{1,0:T(8,128)} %get-tuple-element.21), channel_id=1, source_target_pairs={{0,2},{1,15},{2,4},{3,1},{4,6},{5,3},{6,8},{7,5},{8,10},{9,7},{10,... | collective-permute-start | bytes 786440 | tf_op jit(solution)/shard_map/ppermute | solution.py:270
  74.4 6.3 %copy-start.7 = (bf16[8,256,256]{2,1,0:T(8,128)(2,1)S(1)}, bf16[8,256,256]{2,1,0:T(8,128)(2,1)}, u32[]{:S(2)}) copy-start(bf16[8,256,256]{2,1,0:T(8,128)(2,1)} %join_weight.1.weights_ref) | copy-start | bytes 3145732
  77.5 3.2 %copy-start.9 = (bf16[512,256]{1,0:T(8,128)(2,1)S(1)}, bf16[512,256]{1,0:T(8,128)(2,1)}, u32[]{:S(2)}) copy-start(bf16[512,256]{1,0:T(8,128)(2,1)} %get-tuple-element.20) | copy-start | bytes 786436
  77.5 7.7 %collective-permute-start.8 = (f32[512,128]{1,0:T(8,128)}, f32[512,128]{1,0:T(8,128)S(1)}, u32[]{:S(2)}, u32[]{:S(2)}) collective-permute-start(f32[512,128]{1,0:T(8,128)} %get-tuple-element.24), channel_id=1, source_target_pairs={{0,2},{1,15},{2,4},{3,1},{4,6},{5,3},{6,8},{7,5},{8,10},{9,7},{10,... | collective-permute-start | bytes 786440 | tf_op jit(solution)/shard_map/ppermute | solution.py:270
  80.9 4.3 %copy-start.8 = (bf16[512,256]{1,0:T(8,128)(2,1)S(1)}, bf16[512,256]{1,0:T(8,128)(2,1)}, u32[]{:S(2)}) copy-start(bf16[512,256]{1,0:T(8,128)(2,1)} %get-tuple-element.23) | copy-start | bytes 786436
  81.0 10.4 %collective-permute-start.3 = (f32[512,256]{1,0:T(8,128)S(1)}, f32[512,256]{1,0:T(8,128)S(1)}, u32[]{:S(2)}, u32[]{:S(2)}) collective-permute-start(f32[512,256]{1,0:T(8,128)S(1)} %maximum_add_fusion), channel_id=1, source_target_pairs={{0,2},{1,15},{2,4},{3,1},{4,6},{5,3},{6,8},{7,5},{8,10},{9,7},{10,... | collective-permute-start | bytes 1572872 | tf_op jit(solution)/shard_map/ppermute | solution.py:283
  85.5 11.4 %collective-permute-start.9 = (f32[512,256]{1,0:T(8,128)S(1)}, f32[512,256]{1,0:T(8,128)S(1)}, u32[]{:S(2)}, u32[]{:S(2)}) collective-permute-start(f32[512,256]{1,0:T(8,128)S(1)} %maximum_add_fusion.1), channel_id=1, source_target_pairs={{0,2},{1,15},{2,4},{3,1},{4,6},{5,3},{6,8},{7,5},{8,10},{9,7},{10,... | collective-permute-start | bytes 1572872 | tf_op jit(solution)/shard_map/ppermute | solution.py:283
  91.4 11.2 %collective-permute-start.4 = (f32[512,256]{1,0:T(8,128)S(1)}, f32[512,256]{1,0:T(8,128)S(1)}, u32[]{:S(2)}, u32[]{:S(2)}) collective-permute-start(f32[512,256]{1,0:T(8,128)S(1)} %add.54), channel_id=1, source_target_pairs={{0,2},{1,15},{2,4},{3,1},{4,6},{5,3},{6,8},{7,5},{8,10},{9,7},{10,... | collective-permute-start | bytes 1572872 | tf_op jit(solution)/shard_map/ppermute | solution.py:283
  97.0 14.9 %collective-permute-start.10 = (f32[512,256]{1,0:T(8,128)S(1)}, f32[512,256]{1,0:T(8,128)S(1)}, u32[]{:S(2)}, u32[]{:S(2)}) collective-permute-start(f32[512,256]{1,0:T(8,128)S(1)} %add.60), channel_id=1, source_target_pairs={{0,2},{1,15},{2,4},{3,1},{4,6},{5,3},{6,8},{7,5},{8,10},{9,7},{10,... | collective-permute-start | bytes 1572872 | tf_op jit(solution)/shard_map/ppermute | solution.py:283
  102.7 15.5 %collective-permute-start.5 = (f32[512,128]{1,0:T(8,128)S(1)}, f32[512,128]{1,0:T(8,128)S(1)}, u32[]{:S(2)}, u32[]{:S(2)}) collective-permute-start(f32[512,128]{1,0:T(8,128)S(1)} %get-tuple-element.25), channel_id=1, source_target_pairs={{0,2},{1,15},{2,4},{3,1},{4,6},{5,3},{6,8},{7,5},{8,10},{9,7},{10,... | collective-permute-start | bytes 786440 | tf_op jit(solution)/shard_map/ppermute | solution.py:287
  106.5 11.6 %collective-permute-start.6 = (f32[512,128]{1,0:T(8,128)S(1)}, f32[512,128]{1,0:T(8,128)S(1)}, u32[]{:S(2)}, u32[]{:S(2)}) collective-permute-start(f32[512,128]{1,0:T(8,128)S(1)} %get-tuple-element.26), channel_id=1, source_target_pairs={{0,3},{1,14},{2,5},{3,0},{4,7},{5,2},{6,9},{7,4},{8,11},{9,6},{10,... | collective-permute-start | bytes 786440 | tf_op jit(solution)/shard_map/ppermute | solution.py:288
  112.0 7.4 %collective-permute-start.11 = (f32[512,128]{1,0:T(8,128)S(1)}, f32[512,128]{1,0:T(8,128)S(1)}, u32[]{:S(2)}, u32[]{:S(2)}) collective-permute-start(f32[512,128]{1,0:T(8,128)S(1)} %get-tuple-element.27), channel_id=1, source_target_pairs={{0,2},{1,15},{2,4},{3,1},{4,6},{5,3},{6,8},{7,5},{8,10},{9,7},{10,... | collective-permute-start | bytes 786440 | tf_op jit(solution)/shard_map/ppermute | solution.py:287
  114.0 8.9 %collective-permute-start.12 = (f32[512,128]{1,0:T(8,128)S(1)}, f32[512,128]{1,0:T(8,128)S(1)}, u32[]{:S(2)}, u32[]{:S(2)}) collective-permute-start(f32[512,128]{1,0:T(8,128)S(1)} %get-tuple-element.28), channel_id=1, source_target_pairs={{0,3},{1,14},{2,5},{3,0},{4,7},{5,2},{6,9},{7,4},{8,11},{9,6},{10,... | collective-permute-start | bytes 786440 | tf_op jit(solution)/shard_map/ppermute | solution.py:288
  (6 other events, 4.4 us)

commit v4 on v3

--- a/solution.py
+++ b/solution.py
@@ -22,25 +22,36 @@
     return high, (value - high.astype(F32)).astype(BF16)
 
 
-def state_kernel(k_ref, v_ref, gain_ref, out_ref):
+def small(mebibytes):
+    return pltpu.CompilerParams(vmem_limit_bytes=mebibytes * 2**20)
+
+
+def state_kernel(k_ref, v_ref, gain_ref, norm_ref, state_ref, gained_ref, column_ref):
     gained = (k_ref[...].astype(F32) * gain_ref[...]).astype(BF16)
     width = gained.shape[1]
+    gained_ref[...] = gained
     over_tokens = (((0,), (0,)), ((), ()))
-    out_ref[0:width, :] = lax.dot_general(
+    state_ref[0:width, :] = lax.dot_general(
         gained, gained, over_tokens, preferred_element_type=F32
     )
-    out_ref[width:, :] = lax.dot_general(
+    state_ref[width:, :] = lax.dot_general(
         v_ref[...], gained, over_tokens, preferred_element_type=F32
     )
-
-
-def local_state(keys, values, gain):
+    column_ref[...] = jnp.broadcast_to(norm_ref[...], column_ref.shape).T
+
+
+def local_state(keys, values, gain, norm_gain):
     width = keys.shape[1]
     return pl.pallas_call(
         state_kernel,
-        out_shape=jax.ShapeDtypeStruct((2 * width, width), F32),
+        out_shape=(
+            jax.ShapeDtypeStruct((2 * width, width), F32),
+            jax.ShapeDtypeStruct(keys.shape, BF16),
+            jax.ShapeDtypeStruct((width, width), F32),
+        ),
+        compiler_params=small(6),
         name="local_state",
-    )(keys, values, gain)
+    )(keys, values, gain, norm_gain)
 
 
 def prefix_kernel(x_ref, o_ref):
@@ -55,24 +66,15 @@
     return pl.pallas_call(
         prefix_kernel,
         out_shape=jax.ShapeDtypeStruct(pieces.shape, F32),
+        compiler_params=small(2),
         name="prefix",
     )(pieces)
 
 
 def solve_kernel(
-    reg_ref, q_ref, k_ref, v_ref, before_ref, gain_ref, norm_ref, early_ref, late_ref,
-    q_buf, k_buf, v_buf, first, second, last, x_ref, r_ref, p_ref, sems,
+    reg_ref, q_ref, k_ref, v_ref, before_ref, column_ref, early_ref, late_ref,
+    first, second, last, x_ref, r_ref, p_ref,
 ):
-    copies = [
-        pltpu.make_async_copy(source, target, sems.at[i])
-        for i, (source, target) in enumerate(
-            ((k_ref, k_buf), (v_ref, v_buf), (q_ref, q_buf))
-        )
-    ]
-    for copy in copies:
-        copy.start()
-    for copy in copies:
-        copy.wait()
     width = q_ref.shape[1]
     blocks = q_ref.shape[0] // BLOCK
     lam = reg_ref[0]
@@ -81,13 +83,12 @@
     causal = row <= col
     h_state = before_ref[0:width, :]
     g_state = before_ref[width:, :]
-    gain = gain_ref[...]
     starts = []
     for b in range(blocks):
         rows = pl.ds(b * BLOCK, BLOCK)
-        key = (k_buf[rows, :].astype(F32) * gain).astype(BF16)
+        key = k_ref[rows, :]
         key_t = key.astype(F32).T.astype(BF16)
-        val_t = v_buf[rows, :].astype(F32).T.astype(BF16)
+        val_t = v_ref[rows, :].astype(F32).T.astype(BF16)
         high, low = halves(h_state)
         first[b, 0:width, 0:width] = high
         first[b, 0:width, width:] = high
@@ -104,7 +105,7 @@
         if b + 1 < blocks:
             h_state = h_state + mm(key_t, key)
             g_state = g_state + mm(val_t, key)
-        query = q_buf[rows, :].astype(F32).T
+        query = q_ref[rows, :].astype(F32).T
         x_ref[b] = jnp.zeros_like(query)
         r_ref[b] = query
         p_ref[b] = query
@@ -141,7 +142,7 @@
 
     lax.fori_loop(0, ITERS, step, tuple(starts))
 
-    norm_col = jnp.broadcast_to(norm_ref[...], (BLOCK, width)).T
+    column = column_ref[...]
     for b in range(blocks):
         x_high, x_low = halves(x_ref[b])
         key = first[b, width:, :]
@@ -152,41 +153,35 @@
             jnp.concatenate([s_high, s_low, x_high, x_high], axis=0),
         ) + mm(last[b, :, 3 * BLOCK :], x_low)
         square = jnp.mean(read * read, axis=0, keepdims=True)
-        normed = read * norm_col * lax.rsqrt(square + 1e-06)
+        normed = read * column * lax.rsqrt(square + 1e-06)
         out_ref = early_ref if 2 * b < blocks else late_ref
         place = (b % (blocks // 2)) * BLOCK
         out_ref[place : place + BLOCK, :] = normed.T.astype(BF16).astype(F32)
 
 
-def solve(reg, queries, keys, values, before, gain, norm_gain):
+def solve(reg, queries, keys, values, before, column):
     tokens, width = queries.shape
     blocks = tokens // BLOCK
     vmem = pl.BlockSpec(memory_space=pltpu.VMEM)
     return pl.pallas_call(
         solve_kernel,
         out_shape=(jax.ShapeDtypeStruct((tokens // 2, width), F32),) * 2,
-        in_specs=[pl.BlockSpec(memory_space=pltpu.SMEM)]
-        + [pl.BlockSpec(memory_space=pl.ANY)] * 3
-        + [vmem] * 3,
+        in_specs=[pl.BlockSpec(memory_space=pltpu.SMEM)] + [vmem] * 5,
         out_specs=(vmem, vmem),
         scratch_shapes=[
-            pltpu.VMEM((tokens, width), BF16),
-            pltpu.VMEM((tokens, width), BF16),
-            pltpu.VMEM((tokens, width), BF16),
             pltpu.VMEM((blocks, 2 * BLOCK, 2 * width), BF16),
             pltpu.VMEM((blocks, width, 3 * BLOCK), BF16),
             pltpu.VMEM((blocks, width, 4 * BLOCK), BF16),
             pltpu.VMEM((blocks, width, BLOCK), F32),
             pltpu.VMEM((blocks, width, BLOCK), F32),
             pltpu.VMEM((blocks, width, BLOCK), F32),
-            pltpu.SemaphoreType.DMA((3,)),
         ],
         cost_estimate=pl.CostEstimate(
             flops=60 * 10**9, bytes_accessed=2**21, transcendentals=0
         ),
-        compiler_params=pltpu.CompilerParams(vmem_limit_bytes=40 * 2**20),
+        compiler_params=pltpu.CompilerParams(vmem_limit_bytes=20 * 2**20),
         name="solve",
-    )(reg, queries, keys, values, before, gain, norm_gain)
+    )(reg, queries, keys, values, before, column)
 
 
 def swapped(value):
@@ -208,6 +203,7 @@
     return pl.pallas_call(
         join_weight_kernel,
         out_shape=jax.ShapeDtypeStruct((columns // (2 * width), 2 * width, 2 * width), BF16),
+        compiler_params=small(8),
         name="join_weight",
     )(own, other)
 
@@ -221,6 +217,13 @@
     far_ref[...] = mm(rows, columns)
 
 
+def opposite():
+    place, heads = lax.axis_index("head").astype(jnp.uint32), lax.axis_size("head")
+    chip, core = lax.div(place, jnp.uint32(2)), lax.rem(place, jnp.uint32(2))
+    far = lax.rem(chip + jnp.uint32(heads // 4), jnp.uint32(heads // 2))
+    return jnp.stack([far, core]).astype(jnp.int32)
+
+
 def opening(where, own, other, weights):
     tokens, width = own.shape
     vmem = pl.BlockSpec(memory_space=pltpu.VMEM)
@@ -232,11 +235,12 @@
         ),
         in_specs=[pl.BlockSpec(memory_space=pltpu.SMEM), vmem, vmem, vmem],
         out_specs=(vmem, vmem),
+        compiler_params=small(8),
         name="opening",
     )(where, own, other, weights)
 
 
-def project(normed, weights):
+def project(normed, weights, where):
     width = normed[0].shape[1]
     heads = lax.axis_size("head")
     place = lax.axis_index("head").astype(jnp.uint32)
@@ -261,7 +265,6 @@
     def other_columns(value):
         return jnp.where(left_going, value[:, :width], value[:, width:])
 
-    where = jnp.stack([index_of(chips // 2), core]).astype(jnp.int32)
     others = [swapped(half) for half in normed]
     halves_of, flows = [], []
     for own, other in zip(normed, others):
@@ -294,16 +297,16 @@
     width = keys.shape[2]
     devices = lax.axis_size("seq")
     key_rows, value_rows, query_rows = keys[:, 0, :], values[:, 0, :], queries[:, 0, :]
-    state = local_state(key_rows, value_rows, key_gain)
+    state, gained, column = local_state(key_rows, value_rows, key_gain, norm_gain)
     rows = 2 * width // devices
     state, out_weight = lax.optimization_barrier((state, out_weight))
     parts = lax.all_to_all(state.reshape(devices, rows, width), "seq", 0, 0)
     weights = join_weight(out_weight, swapped(out_weight.astype(F32)))
-    parts, weights = lax.optimization_barrier((parts, weights))
+    parts, weights, where = lax.optimization_barrier((parts, weights, opposite()))
     before = lax.all_to_all(exclusive(parts), "seq", 0, 0)
     before = before.reshape(2 * width, width)
-    normed = solve(reg, query_rows, key_rows, value_rows, before, key_gain, norm_gain)
-    return project(normed, weights)
+    normed = solve(reg, query_rows, gained, value_rows, before, column)
+    return project(normed, weights, where)
 
 
 def solution(mesh):

time: 124 us -> 120 us (0.968)
  Pallas kernels: 25.7 us -> 18.1 us
  starting transfers between devices: 65.3 us -> 68.3 us
    all_to_all x1, waiting for transfers between devices: 5.66 us -> 8.94 us  [body(): parts = lax.all_to_all(state.reshape(devices, rows, width), 'seq', 0, 0)]
    ppermute x4, starting transfers between devices: 14.8 us -> 18 us  [project(): flows[piece] = lax.ppermute(flow + part(rows, away), 'head', ring)]
    pallas_call x2, Pallas kernels: 4.7 us -> 1.56 us  [opening(): pl.pallas_call(open_kernel, out_shape=(jax.ShapeDtypeStruct((tokens, 2 *...]
    pallas_call x1, Pallas kernels: 2.49 us -> 0.1 us  [join_weight(): pl.pallas_call(join_weight_kernel, out_shape=jax.ShapeDtypeStruct((column...]
    ppermute x4, waiting for transfers between devices: 4 us -> 2.2 us  [project(): flows[piece] = lax.ppermute(flow + part(rows, away), 'head', ring)]
    ppermute x2, waiting for transfers between devices: 1.2 us -> 2.62 us  [project(): same = lax.ppermute(own_columns(last), 'head', ring)]
    unnamed x30 -> x14, local copies, waits for them, and re-layouts: 3.71 us -> 3.28 us
  transfers between devices with their start and end apart: 15 -> 15, of which waited for: 8 -> 7; matrix products, arithmetic and copies ran while one was open for 2% -> 2% of each run, Pallas kernels for 6% -> 1%
where the time goes in v4:
time: 120 us; the launch traced here: 118 us
  starting transfers between devices  68.3 us (57%)
  waiting for transfers between devices  24.6 us (20%)
  Pallas kernels  18.1 us (15%)
  local copies, waits for them, and re-layouts  3.28 us (3%)
  matrix products  1.81 us (2%)
  other arithmetic  1.43 us (1%)
    ppermute x4, starting transfers between devices, project(): flows[piece] = lax.ppermute(flow + part(rows, away), 'head', ring)  18 us
    ppermute x3, starting transfers between devices, swapped(): return lax.ppermute(value, 'head', [(i, i ^ 1) for i in range(heads)])  15.2 us
    pallas_call x1, Pallas kernels, solve(): pl.pallas_call(solve_kernel, out_shape=(jax.ShapeDtypeStruct((tokens // 2...  14.7 us
    ppermute x2, starting transfers between devices, project(): crossed = lax.ppermute(other_columns(last), 'head', cross)  9.71 us
    all_to_all x1, waiting for transfers between devices, body(): parts = lax.all_to_all(state.reshape(devices, rows, width), 'seq', 0, 0)  8.94 us
    all_to_all x1, waiting for transfers between devices, body(): before = lax.all_to_all(exclusive(parts), 'seq', 0, 0)  8.53 us
    ppermute x2, starting transfers between devices, project(): flows.append(lax.ppermute(far, 'head', ring))  8.07 us
    all_to_all x1, starting transfers between devices, body(): parts = lax.all_to_all(state.reshape(devices, rows, width), 'seq', 0, 0)  7.52 us
  transfers between devices with their start and end apart: 15, of which 7 were waited for; matrix products, arithmetic and copies ran while one was open for 2% of the time, Pallas kernels for 1%

profile of v4, /device:TPU:1, one launch (start us, length us, event | category | flops | bytes accessed | tf_op | source)
XLA Modules:
  0.0 118.5 jit_solution(16747929350210620558)
XLA Ops:
  0.0 1.0 copy-done.1
  1.0 0.9 copy-done.2
  3.3 1.0 local_state.1
  4.4 8.8 %collective-permute-start = (f32[128,2048]{1,0:T(8,128)S(1)}, f32[128,2048]{1,0:T(8,128)S(1)}, u32[]{:S(2)}, u32[]{:S(2)}) collective-permute-start(f32[128,2048]{1,0:T(8,128)S(1)} %convert_element_type.17), channel_id=1, source_target_pairs={{0,1},{1,0},{2,3},{3,2},{4,5},{5,4},{6,7},{7,6},{8,9},{9,8},{10,11... | collective-permute-start | bytes 3145736 | tf_op jit(solution)/shard_map/ppermute | solution.py:189
  13.2 7.5 %all-to-all-start = ((f32[32,8,128]{2,1,0:T(8,128)}), f32[32,8,128]{2,1,0:T(8,128)S(1)}, u32[]{:S(2)}, u32[]{:S(2)}) async-start(f32[32,8,128]{2,1,0:T(8,128)} %bitcast.2), calls=%async_computation | async-start | bytes 262144 | tf_op jit(solution)/shard_map/all_to_all | solution.py:303
  20.9 8.9 %all-to-all-done.x_ref = f32[32,8,128]{2,1,0:T(8,128)S(1)} async-done(((f32[32,8,128]{2,1,0:T(8,128)}), f32[32,8,128]{2,1,0:T(8,128)S(1)}, u32[]{:S(2)}, u32[]{:S(2)}) %all-to-all-start) | async-done | bytes 131104 | tf_op jit(solution)/shard_map/all_to_all | solution.py:303
  30.6 4.5 %all-to-all-start.1 = ((f32[32,8,128]{2,1,0:T(8,128)}), f32[32,8,128]{2,1,0:T(8,128)S(1)}, u32[]{:S(2)}, u32[]{:S(2)}) async-start(f32[32,8,128]{2,1,0:T(8,128)} %prefix.1), calls=%async_computation.1 | async-start | bytes 262144 | tf_op jit(solution)/shard_map/all_to_all | solution.py:306
  35.8 8.5 %all-to-all-done.1 = f32[32,8,128]{2,1,0:T(8,128)S(1)} async-done(((f32[32,8,128]{2,1,0:T(8,128)}), f32[32,8,128]{2,1,0:T(8,128)S(1)}, u32[]{:S(2)}, u32[]{:S(2)}) %all-to-all-start.1) | async-done | bytes 131104 | tf_op jit(solution)/shard_map/all_to_all | solution.py:306
  44.3 14.7 %solve.1 = (f32[512,128]{1,0:T(8,128)S(1)}, f32[512,128]{1,0:T(8,128)S(1)}) custom-call(f32[1]{0:T(128)S(6)} %copy.8.reg_ref, bf16[1024,128]{1,0:T(8,128)(2,1)S(1)} %bitcast.43, bf16[1024,128]{1,0:T(8,128)(2,1)S(1)} %get-tuple-element.23.k_ref, bf16[1024,128]{1,0:T(8,128)(2,1)S(1)} %bitcast.41, f32[256,128]{1,0:T(8,128)S(1)} %bitcast.42, ...), custom_call_target="tpu_custom_call" | custom-call | flops 60000002048 | bytes 2097152 | tf_op jit(solution)/shard_map/solve/pallas_call | solution.py:166
  59.0 4.5 %collective-permute-start.7 = (f32[512,128]{1,0:T(8,128)S(1)}, f32[512,128]{1,0:T(8,128)S(1)}, u32[]{:S(2)}, u32[]{:S(2)}) collective-permute-start(f32[512,128]{1,0:T(8,128)S(1)} %get-tuple-element.30.own_ref), channel_id=1, source_target_pairs={{0,1},{1,0},{2,3},{3,2},{4,5},{5,4},{6,7},{7,6},{8,9},{9,8},{10,11... | collective-permute-start | bytes 786440 | tf_op jit(solution)/shard_map/ppermute | solution.py:189
  63.6 1.9 %collective-permute-start.1 = (f32[512,128]{1,0:T(8,128)S(1)}, f32[512,128]{1,0:T(8,128)S(1)}, u32[]{:S(2)}, u32[]{:S(2)}) collective-permute-start(f32[512,128]{1,0:T(8,128)S(1)} %get-tuple-element.26.own_ref), channel_id=1, source_target_pairs={{0,1},{1,0},{2,3},{3,2},{4,5},{5,4},{6,7},{7,6},{8,9},{9,8},{10,11... | collective-permute-start | bytes 786440 | tf_op jit(solution)/shard_map/ppermute | solution.py:189
  66.3 5.1 %collective-permute-start.8 = (f32[512,128]{1,0:T(8,128)S(1)}, f32[512,128]{1,0:T(8,128)S(1)}, u32[]{:S(2)}, u32[]{:S(2)}) collective-permute-start(f32[512,128]{1,0:T(8,128)S(1)} %get-tuple-element.32), channel_id=1, source_target_pairs={{0,2},{1,15},{2,4},{3,1},{4,6},{5,3},{6,8},{7,5},{8,10},{9,7},{10,... | collective-permute-start | bytes 786440 | tf_op jit(solution)/shard_map/ppermute | solution.py:273
  72.2 3.0 %collective-permute-start.2 = (f32[512,128]{1,0:T(8,128)S(1)}, f32[512,128]{1,0:T(8,128)S(1)}, u32[]{:S(2)}, u32[]{:S(2)}) collective-permute-start(f32[512,128]{1,0:T(8,128)S(1)} %get-tuple-element.29), channel_id=1, source_target_pairs={{0,2},{1,15},{2,4},{3,1},{4,6},{5,3},{6,8},{7,5},{8,10},{9,7},{10,... | collective-permute-start | bytes 786440 | tf_op jit(solution)/shard_map/ppermute | solution.py:273
  75.5 4.5 %collective-permute-start.9 = (f32[512,256]{1,0:T(8,128)S(1)}, f32[512,256]{1,0:T(8,128)S(1)}, u32[]{:S(2)}, u32[]{:S(2)}) collective-permute-start(f32[512,256]{1,0:T(8,128)S(1)} %maximum_add_fusion.1), channel_id=1, source_target_pairs={{0,2},{1,15},{2,4},{3,1},{4,6},{5,3},{6,8},{7,5},{8,10},{9,7},{10,... | collective-permute-start | bytes 1572872 | tf_op jit(solution)/shard_map/ppermute | solution.py:286
  80.3 3.5 %collective-permute-start.3 = (f32[512,256]{1,0:T(8,128)S(1)}, f32[512,256]{1,0:T(8,128)S(1)}, u32[]{:S(2)}, u32[]{:S(2)}) collective-permute-start(f32[512,256]{1,0:T(8,128)S(1)} %maximum_add_fusion), channel_id=1, source_target_pairs={{0,2},{1,15},{2,4},{3,1},{4,6},{5,3},{6,8},{7,5},{8,10},{9,7},{10,... | collective-permute-start | bytes 1572872 | tf_op jit(solution)/shard_map/ppermute | solution.py:286
  84.2 1.9 %collective-permute-done.9 = f32[512,256]{1,0:T(8,128)S(1)} collective-permute-done((f32[512,256]{1,0:T(8,128)S(1)}, f32[512,256]{1,0:T(8,128)S(1)}, u32[]{:S(2)}, u32[]{:S(2)}) %collective-permute-start.9) | collective-permute-done | bytes 524320 | tf_op jit(solution)/shard_map/ppermute | solution.py:286
  86.2 5.0 %collective-permute-start.10 = (f32[512,256]{1,0:T(8,128)S(1)}, f32[512,256]{1,0:T(8,128)S(1)}, u32[]{:S(2)}, u32[]{:S(2)}) collective-permute-start(f32[512,256]{1,0:T(8,128)S(1)} %add.60), channel_id=1, source_target_pairs={{0,2},{1,15},{2,4},{3,1},{4,6},{5,3},{6,8},{7,5},{8,10},{9,7},{10,... | collective-permute-start | bytes 1572872 | tf_op jit(solution)/shard_map/ppermute | solution.py:286
  91.8 5.0 %collective-permute-start.4 = (f32[512,256]{1,0:T(8,128)S(1)}, f32[512,256]{1,0:T(8,128)S(1)}, u32[]{:S(2)}, u32[]{:S(2)}) collective-permute-start(f32[512,256]{1,0:T(8,128)S(1)} %add.54), channel_id=1, source_target_pairs={{0,2},{1,15},{2,4},{3,1},{4,6},{5,3},{6,8},{7,5},{8,10},{9,7},{10,... | collective-permute-start | bytes 1572872 | tf_op jit(solution)/shard_map/ppermute | solution.py:286
  97.5 5.3 %collective-permute-start.12 = (f32[512,128]{1,0:T(8,128)S(1)}, f32[512,128]{1,0:T(8,128)S(1)}, u32[]{:S(2)}, u32[]{:S(2)}) collective-permute-start(f32[512,128]{1,0:T(8,128)S(1)} %get-tuple-element.36), channel_id=1, source_target_pairs={{0,3},{1,14},{2,5},{3,0},{4,7},{5,2},{6,9},{7,4},{8,11},{9,6},{10,... | collective-permute-start | bytes 786440 | tf_op jit(solution)/shard_map/ppermute | solution.py:291
  102.8 3.0 %collective-permute-start.11 = (f32[512,128]{1,0:T(8,128)S(1)}, f32[512,128]{1,0:T(8,128)S(1)}, u32[]{:S(2)}, u32[]{:S(2)}) collective-permute-start(f32[512,128]{1,0:T(8,128)S(1)} %get-tuple-element.35), channel_id=1, source_target_pairs={{0,2},{1,15},{2,4},{3,1},{4,6},{5,3},{6,8},{7,5},{8,10},{9,7},{10,... | collective-permute-start | bytes 786440 | tf_op jit(solution)/shard_map/ppermute | solution.py:290
  105.8 4.4 %collective-permute-start.6 = (f32[512,128]{1,0:T(8,128)S(1)}, f32[512,128]{1,0:T(8,128)S(1)}, u32[]{:S(2)}, u32[]{:S(2)}) collective-permute-start(f32[512,128]{1,0:T(8,128)S(1)} %get-tuple-element.34), channel_id=1, source_target_pairs={{0,3},{1,14},{2,5},{3,0},{4,7},{5,2},{6,9},{7,4},{8,11},{9,6},{10,... | collective-permute-start | bytes 786440 | tf_op jit(solution)/shard_map/ppermute | solution.py:291
  110.3 2.2 %collective-permute-start.5 = (f32[512,128]{1,0:T(8,128)S(1)}, f32[512,128]{1,0:T(8,128)S(1)}, u32[]{:S(2)}, u32[]{:S(2)}) collective-permute-start(f32[512,128]{1,0:T(8,128)S(1)} %get-tuple-element.33), channel_id=1, source_target_pairs={{0,2},{1,15},{2,4},{3,1},{4,6},{5,3},{6,8},{7,5},{8,10},{9,7},{10,... | collective-permute-start | bytes 786440 | tf_op jit(solution)/shard_map/ppermute | solution.py:290
  112.8 2.3 %collective-permute-done.6 = f32[512,128]{1,0:T(8,128)S(1)} collective-permute-done((f32[512,128]{1,0:T(8,128)S(1)}, f32[512,128]{1,0:T(8,128)S(1)}, u32[]{:S(2)}, u32[]{:S(2)}) %collective-permute-start.6) | collective-permute-done | bytes 262176 | tf_op jit(solution)/shard_map/ppermute | solution.py:291
  115.1 2.6 %collective-permute-done.5 = f32[512,128]{1,0:T(8,128)S(1)} collective-permute-done((f32[512,128]{1,0:T(8,128)S(1)}, f32[512,128]{1,0:T(8,128)S(1)}, u32[]{:S(2)}, u32[]{:S(2)}) %collective-permute-start.5) | collective-permute-done | bytes 262176 | tf_op jit(solution)/shard_map/ppermute | solution.py:290
  (47 shorter events, 7.3 us)
Async XLA Ops:
  0.0 4.3 %copy-start = (bf16[128,2048]{1,0:T(8,128)(2,1)S(1)}, bf16[128,2048]{1,0:T(8,128)(2,1)}, u32[]{:S(2)}) copy-start(bf16[128,2048]{1,0:T(8,128)(2,1)} %own_ref) | copy-start | bytes 1572868
  0.0 1.0 copy-start.1
  1.0 0.9 copy-start.2
  2.0 0.7 copy-start.4
  2.6 0.7 copy-start.5
  4.4 16.4 %collective-permute-start = (f32[128,2048]{1,0:T(8,128)S(1)}, f32[128,2048]{1,0:T(8,128)S(1)}, u32[]{:S(2)}, u32[]{:S(2)}) collective-permute-start(f32[128,2048]{1,0:T(8,128)S(1)} %convert_element_type.17), channel_id=1, source_target_pairs={{0,1},{1,0},{2,3},{3,2},{4,5},{5,4},{6,7},{7,6},{8,9},{9,8},{10,11... | collective-permute-start | bytes 3145736 | tf_op jit(solution)/shard_map/ppermute | solution.py:189
  13.2 16.7 %all-to-all-start = ((f32[32,8,128]{2,1,0:T(8,128)}), f32[32,8,128]{2,1,0:T(8,128)S(1)}, u32[]{:S(2)}, u32[]{:S(2)}) async-start(f32[32,8,128]{2,1,0:T(8,128)} %bitcast.2), calls=%async_computation | async-start | bytes 262144 | tf_op jit(solution)/shard_map/all_to_all | solution.py:303
  20.9 23.4 %copy-start.3 = (bf16[1024,1,128]{2,0,1:T(8,128)(2,1)S(1)}, bf16[1024,1,128]{2,0,1:T(8,128)(2,1)}, u32[]{:S(2)}) copy-start(bf16[1024,1,128]{2,0,1:T(8,128)(2,1)} %param.9) | copy-start | bytes 786436
  20.9 23.4 %copy-start.6 = (bf16[1024,1,128]{2,0,1:T(8,128)(2,1)S(1)}, bf16[1024,1,128]{2,0,1:T(8,128)(2,1)}, u32[]{:S(2)}) copy-start(bf16[1024,1,128]{2,0,1:T(8,128)(2,1)} %param.7) | copy-start | bytes 786436
  30.6 13.7 %all-to-all-start.1 = ((f32[32,8,128]{2,1,0:T(8,128)}), f32[32,8,128]{2,1,0:T(8,128)S(1)}, u32[]{:S(2)}, u32[]{:S(2)}) async-start(f32[32,8,128]{2,1,0:T(8,128)} %prefix.1), calls=%async_computation.1 | async-start | bytes 262144 | tf_op jit(solution)/shard_map/all_to_all | solution.py:306
  59.0 6.5 %collective-permute-start.7 = (f32[512,128]{1,0:T(8,128)S(1)}, f32[512,128]{1,0:T(8,128)S(1)}, u32[]{:S(2)}, u32[]{:S(2)}) collective-permute-start(f32[512,128]{1,0:T(8,128)S(1)} %get-tuple-element.30.own_ref), channel_id=1, source_target_pairs={{0,1},{1,0},{2,3},{3,2},{4,5},{5,4},{6,7},{7,6},{8,9},{9,8},{10,11... | collective-permute-start | bytes 786440 | tf_op jit(solution)/shard_map/ppermute | solution.py:189
  63.6 7.9 %collective-permute-start.1 = (f32[512,128]{1,0:T(8,128)S(1)}, f32[512,128]{1,0:T(8,128)S(1)}, u32[]{:S(2)}, u32[]{:S(2)}) collective-permute-start(f32[512,128]{1,0:T(8,128)S(1)} %get-tuple-element.26.own_ref), channel_id=1, source_target_pairs={{0,1},{1,0},{2,3},{3,2},{4,5},{5,4},{6,7},{7,6},{8,9},{9,8},{10,11... | collective-permute-start | bytes 786440 | tf_op jit(solution)/shard_map/ppermute | solution.py:189
  66.3 8.9 %collective-permute-start.8 = (f32[512,128]{1,0:T(8,128)S(1)}, f32[512,128]{1,0:T(8,128)S(1)}, u32[]{:S(2)}, u32[]{:S(2)}) collective-permute-start(f32[512,128]{1,0:T(8,128)S(1)} %get-tuple-element.32), channel_id=1, source_target_pairs={{0,2},{1,15},{2,4},{3,1},{4,6},{5,3},{6,8},{7,5},{8,10},{9,7},{10,... | collective-permute-start | bytes 786440 | tf_op jit(solution)/shard_map/ppermute | solution.py:273
  72.2 7.8 %collective-permute-start.2 = (f32[512,128]{1,0:T(8,128)S(1)}, f32[512,128]{1,0:T(8,128)S(1)}, u32[]{:S(2)}, u32[]{:S(2)}) collective-permute-start(f32[512,128]{1,0:T(8,128)S(1)} %get-tuple-element.29), channel_id=1, source_target_pairs={{0,2},{1,15},{2,4},{3,1},{4,6},{5,3},{6,8},{7,5},{8,10},{9,7},{10,... | collective-permute-start | bytes 786440 | tf_op jit(solution)/shard_map/ppermute | solution.py:273
  75.5 10.6 %collective-permute-start.9 = (f32[512,256]{1,0:T(8,128)S(1)}, f32[512,256]{1,0:T(8,128)S(1)}, u32[]{:S(2)}, u32[]{:S(2)}) collective-permute-start(f32[512,256]{1,0:T(8,128)S(1)} %maximum_add_fusion.1), channel_id=1, source_target_pairs={{0,2},{1,15},{2,4},{3,1},{4,6},{5,3},{6,8},{7,5},{8,10},{9,7},{10,... | collective-permute-start | bytes 1572872 | tf_op jit(solution)/shard_map/ppermute | solution.py:286
  80.3 11.4 %collective-permute-start.3 = (f32[512,256]{1,0:T(8,128)S(1)}, f32[512,256]{1,0:T(8,128)S(1)}, u32[]{:S(2)}, u32[]{:S(2)}) collective-permute-start(f32[512,256]{1,0:T(8,128)S(1)} %maximum_add_fusion), channel_id=1, source_target_pairs={{0,2},{1,15},{2,4},{3,1},{4,6},{5,3},{6,8},{7,5},{8,10},{9,7},{10,... | collective-permute-start | bytes 1572872 | tf_op jit(solution)/shard_map/ppermute | solution.py:286
  86.2 11.2 %collective-permute-start.10 = (f32[512,256]{1,0:T(8,128)S(1)}, f32[512,256]{1,0:T(8,128)S(1)}, u32[]{:S(2)}, u32[]{:S(2)}) collective-permute-start(f32[512,256]{1,0:T(8,128)S(1)} %add.60), channel_id=1, source_target_pairs={{0,2},{1,15},{2,4},{3,1},{4,6},{5,3},{6,8},{7,5},{8,10},{9,7},{10,... | collective-permute-start | bytes 1572872 | tf_op jit(solution)/shard_map/ppermute | solution.py:286
  91.8 13.9 %collective-permute-start.4 = (f32[512,256]{1,0:T(8,128)S(1)}, f32[512,256]{1,0:T(8,128)S(1)}, u32[]{:S(2)}, u32[]{:S(2)}) collective-permute-start(f32[512,256]{1,0:T(8,128)S(1)} %add.54), channel_id=1, source_target_pairs={{0,2},{1,15},{2,4},{3,1},{4,6},{5,3},{6,8},{7,5},{8,10},{9,7},{10,... | collective-permute-start | bytes 1572872 | tf_op jit(solution)/shard_map/ppermute | solution.py:286
  97.5 15.3 %collective-permute-start.12 = (f32[512,128]{1,0:T(8,128)S(1)}, f32[512,128]{1,0:T(8,128)S(1)}, u32[]{:S(2)}, u32[]{:S(2)}) collective-permute-start(f32[512,128]{1,0:T(8,128)S(1)} %get-tuple-element.36), channel_id=1, source_target_pairs={{0,3},{1,14},{2,5},{3,0},{4,7},{5,2},{6,9},{7,4},{8,11},{9,6},{10,... | collective-permute-start | bytes 786440 | tf_op jit(solution)/shard_map/ppermute | solution.py:291
  102.8 10.0 %collective-permute-start.11 = (f32[512,128]{1,0:T(8,128)S(1)}, f32[512,128]{1,0:T(8,128)S(1)}, u32[]{:S(2)}, u32[]{:S(2)}) collective-permute-start(f32[512,128]{1,0:T(8,128)S(1)} %get-tuple-element.35), channel_id=1, source_target_pairs={{0,2},{1,15},{2,4},{3,1},{4,6},{5,3},{6,8},{7,5},{8,10},{9,7},{10,... | collective-permute-start | bytes 786440 | tf_op jit(solution)/shard_map/ppermute | solution.py:290
  105.8 9.2 %collective-permute-start.6 = (f32[512,128]{1,0:T(8,128)S(1)}, f32[512,128]{1,0:T(8,128)S(1)}, u32[]{:S(2)}, u32[]{:S(2)}) collective-permute-start(f32[512,128]{1,0:T(8,128)S(1)} %get-tuple-element.34), channel_id=1, source_target_pairs={{0,3},{1,14},{2,5},{3,0},{4,7},{5,2},{6,9},{7,4},{8,11},{9,6},{10,... | collective-permute-start | bytes 786440 | tf_op jit(solution)/shard_map/ppermute | solution.py:291
  110.3 7.4 %collective-permute-start.5 = (f32[512,128]{1,0:T(8,128)S(1)}, f32[512,128]{1,0:T(8,128)S(1)}, u32[]{:S(2)}, u32[]{:S(2)}) collective-permute-start(f32[512,128]{1,0:T(8,128)S(1)} %get-tuple-element.33), channel_id=1, source_target_pairs={{0,2},{1,15},{2,4},{3,1},{4,6},{5,3},{6,8},{7,5},{8,10},{9,7},{10,... | collective-permute-start | bytes 786440 | tf_op jit(solution)/shard_map/ppermute | solution.py:290

commit v5 on v4

--- a/solution.py
+++ b/solution.py
@@ -49,7 +49,6 @@
             jax.ShapeDtypeStruct(keys.shape, BF16),
             jax.ShapeDtypeStruct((width, width), F32),
         ),
-        compiler_params=small(6),
         name="local_state",
     )(keys, values, gain, norm_gain)
 
@@ -246,50 +245,51 @@
     place = lax.axis_index("head").astype(jnp.uint32)
     chips = heads // 2
     chip, core = lax.div(place, jnp.uint32(2)), lax.rem(place, jnp.uint32(2))
-    left_going = core == 1
-    step = lambda i: 2 if i % 2 == 0 else heads - 2
-    ring = [(i, (i + step(i)) % heads) for i in range(heads)]
-    cross = [(i, ((i + step(i)) % heads) ^ 1) for i in range(heads)]
-
-    def index_of(away):
-        ahead = jnp.where(left_going, jnp.uint32(chips - away), jnp.uint32(away % chips))
-        return lax.rem(chip + ahead, jnp.uint32(chips))
-
-    def part(rows, away):
-        columns = lax.dynamic_index_in_dim(weights, index_of(away), axis=0, keepdims=False)
-        return jnp.dot(rows, columns, preferred_element_type=F32)
-
-    def own_columns(value):
-        return jnp.where(left_going, value[:, width:], value[:, :width])
-
-    def other_columns(value):
-        return jnp.where(left_going, value[:, :width], value[:, width:])
-
     others = [swapped(half) for half in normed]
-    halves_of, flows = [], []
-    for own, other in zip(normed, others):
+    rings, crosses, leftward, halves_of, flows = [], [], [], [], []
+    for piece, (own, other) in enumerate(zip(normed, others)):
+        step = [2 if (i + piece) % 2 == 0 else heads - 2 for i in range(heads)]
+        rings.append([(i, (i + step[i]) % heads) for i in range(heads)])
+        crosses.append([(i, ((i + step[i]) % heads) ^ 1) for i in range(heads)])
+        leftward.append(core != piece)
         rows, far = opening(where, own, other, weights)
         halves_of.append(rows)
-        flows.append(lax.ppermute(far, "head", ring))
+        flows.append(lax.ppermute(far, "head", rings[piece]))
+
+    def part(piece, away):
+        ahead = jnp.where(
+            leftward[piece], jnp.uint32(chips - away), jnp.uint32(away % chips)
+        )
+        index = lax.rem(chip + ahead, jnp.uint32(chips))
+        columns = lax.dynamic_index_in_dim(weights, index, axis=0, keepdims=False)
+        return jnp.dot(halves_of[piece], columns, preferred_element_type=F32)
+
+    def own_columns(value):
+        return jnp.where(core == 1, value[:, width:], value[:, :width])
+
+    def other_columns(value):
+        return jnp.where(core == 1, value[:, :width], value[:, width:])
+
     for away in range(chips // 2 - 1, 1, -1):
-        for piece, rows in enumerate(halves_of):
-            flow = flows[piece]
+        for piece, flow in enumerate(flows):
             if flow.shape[1] == width:
                 blank = jnp.zeros_like(flow)
                 flow = jnp.concatenate(
                     [
-                        jnp.where(left_going, blank, flow),
-                        jnp.where(left_going, flow, blank),
+                        jnp.where(core == 1, blank, flow),
+                        jnp.where(core == 1, flow, blank),
                     ],
                     axis=1,
                 )
-            flows[piece] = lax.ppermute(flow + part(rows, away), "head", ring)
+            flows[piece] = lax.ppermute(
+                flow + part(piece, away), "head", rings[piece]
+            )
     done = []
-    for piece, rows in enumerate(halves_of):
-        last = flows[piece] + part(rows, 1)
-        same = lax.ppermute(own_columns(last), "head", ring)
-        crossed = lax.ppermute(other_columns(last), "head", cross)
-        done.append((own_columns(part(rows, 0)) + same + crossed).astype(BF16))
+    for piece, flow in enumerate(flows):
+        last = flow + part(piece, 1)
+        same = lax.ppermute(own_columns(last), "head", rings[piece])
+        crossed = lax.ppermute(other_columns(last), "head", crosses[piece])
+        done.append((own_columns(part(piece, 0)) + same + crossed).astype(BF16))
     return jnp.concatenate(done, axis=0)
 
 

time: 120 us -> 129 us (1.075)
  waiting for transfers between devices: 24.6 us -> 34.6 us
  local copies, waits for them, and re-layouts: 3.28 us -> 0.02 us
  starting transfers between devices: 68.3 us -> 70.4 us
    ppermute x10, waiting for transfers between devices: 7.09 us -> 17.2 us  [the longest x4 8.72 us: project(): flows[piece] = lax.ppermute(flow + part(piece, away), 'head', rings[piece])]
    unnamed x14 -> x10, local copies, waits for them, and re-layouts: 3.28 us -> 0.02 us
    ppermute x10, starting transfers between devices: 41 us -> 43.1 us  [the longest x2 18.4 us: project(): crossed = lax.ppermute(other_columns(last), 'head', crosses[piece])]
  transfers between devices with their start and end apart: 15 -> 15, of which waited for: 7 -> 10; matrix products, arithmetic and copies ran while one was open for 2% -> 2% of each run, Pallas kernels for 1% -> 1%
where the time goes in v5:
time: 129 us
  starting transfers between devices  70.4 us (55%)
  waiting for transfers between devices  34.6 us (27%)
  Pallas kernels  19.2 us (15%)
  matrix products  1.82 us (1%)
  other arithmetic  1.42 us (1%)
    ppermute x2, starting transfers between devices, project(): crossed = lax.ppermute(other_columns(last), 'head', crosses[piece])  18.4 us
    ppermute x3, starting transfers between devices, swapped(): return lax.ppermute(value, 'head', [(i, i ^ 1) for i in range(heads)])  15.2 us
    pallas_call x1, Pallas kernels, solve(): pl.pallas_call(solve_kernel, out_shape=(jax.ShapeDtypeStruct((tokens // 2...  14.8 us
    ppermute x4, starting transfers between devices, project(): flows[piece] = lax.ppermute(flow + part(piece, away), 'head', rings[piece])  13.9 us
    all_to_all x1, waiting for transfers between devices, body(): parts = lax.all_to_all(state.reshape(devices, rows, width), 'seq', 0, 0)  8.93 us
    ppermute x4, waiting for transfers between devices, project(): flows[piece] = lax.ppermute(flow + part(piece, away), 'head', rings[piece])  8.72 us
    all_to_all x1, waiting for transfers between devices, body(): before = lax.all_to_all(exclusive(parts), 'seq', 0, 0)  8.53 us
    all_to_all x1, starting transfers between devices, body(): parts = lax.all_to_all(state.reshape(devices, rows, width), 'seq', 0, 0)  7.52 us
  transfers between devices with their start and end apart: 15, of which 10 were waited for; matrix products, arithmetic and copies ran while one was open for 2% of the time, Pallas kernels for 1%

profile of v5, /device:TPU:1, one launch (start us, length us, event | category | flops | bytes accessed | tf_op | source)
XLA Modules:
  0.0 128.5 jit_solution(2740773495989210952)
XLA Ops:
  0.0 2.1 %local_state.1 = (f32[256,128]{1,0:T(8,128)}, bf16[1024,128]{1,0:T(8,128)(2,1)}, f32[128,128]{1,0:T(8,128)}) custom-call(bf16[1024,128]{1,0:T(8,128)(2,1)} %bitcast.47, bf16[1024,128]{1,0:T(8,128)(2,1)} %bitcast.43, f32[1,128]{1,0:T(1,128)} %gain_ref.1, f32[1,128]{1,0:T(1,128)} %norm_ref.1), custom_call_target="tpu_custom_call" | custom-call | tf_op jit(solution)/shard_map/local_state/pallas_call | solution.py:45
  2.2 8.8 %collective-permute-start = (f32[128,2048]{1,0:T(8,128)S(1)}, f32[128,2048]{1,0:T(8,128)S(1)}, u32[]{:S(2)}, u32[]{:S(2)}) collective-permute-start(f32[128,2048]{1,0:T(8,128)S(1)} %convert_element_type.17), channel_id=1, source_target_pairs={{0,1},{1,0},{2,3},{3,2},{4,5},{5,4},{6,7},{7,6},{8,9},{9,8},{10,11... | collective-permute-start | bytes 3145736 | tf_op jit(solution)/shard_map/ppermute | solution.py:188
  11.0 7.5 %all-to-all-start = ((f32[32,8,128]{2,1,0:T(8,128)}), f32[32,8,128]{2,1,0:T(8,128)S(1)}, u32[]{:S(2)}, u32[]{:S(2)}) async-start(f32[32,8,128]{2,1,0:T(8,128)} %bitcast.2), calls=%async_computation | async-start | bytes 262144 | tf_op jit(solution)/shard_map/all_to_all | solution.py:303
  18.8 8.9 %all-to-all-done.x_ref = f32[32,8,128]{2,1,0:T(8,128)S(1)} async-done(((f32[32,8,128]{2,1,0:T(8,128)}), f32[32,8,128]{2,1,0:T(8,128)S(1)}, u32[]{:S(2)}, u32[]{:S(2)}) %all-to-all-start) | async-done | bytes 131104 | tf_op jit(solution)/shard_map/all_to_all | solution.py:303
  28.4 4.5 %all-to-all-start.1 = ((f32[32,8,128]{2,1,0:T(8,128)}), f32[32,8,128]{2,1,0:T(8,128)S(1)}, u32[]{:S(2)}, u32[]{:S(2)}) async-start(f32[32,8,128]{2,1,0:T(8,128)} %prefix.1), calls=%async_computation.1 | async-start | bytes 262144 | tf_op jit(solution)/shard_map/all_to_all | solution.py:306
  33.6 8.5 %all-to-all-done.1 = f32[32,8,128]{2,1,0:T(8,128)S(1)} async-done(((f32[32,8,128]{2,1,0:T(8,128)}), f32[32,8,128]{2,1,0:T(8,128)S(1)}, u32[]{:S(2)}, u32[]{:S(2)}) %all-to-all-start.1) | async-done | bytes 131104 | tf_op jit(solution)/shard_map/all_to_all | solution.py:306
  42.1 14.8 %solve.1 = (f32[512,128]{1,0:T(8,128)S(1)}, f32[512,128]{1,0:T(8,128)S(1)}) custom-call(f32[1]{0:T(128)S(6)} %copy.8.reg_ref, bf16[1024,128]{1,0:T(8,128)(2,1)S(1)} %bitcast.46, bf16[1024,128]{1,0:T(8,128)(2,1)S(1)} %copy-done.3, bf16[1024,128]{1,0:T(8,128)(2,1)S(1)} %bitcast.44, f32[256,128]{1,0:T(8,128)S(1)} %bitcast.45, f32[128,128]{1,0:T(8,128)S(1)} %copy-done.4), custom_call_target="tpu_custom_call" | custom-call | flops 60000002048 | bytes 2097152 | tf_op jit(solution)/shard_map/solve/pallas_call | solution.py:165
  56.9 4.5 %collective-permute-start.7 = (f32[512,128]{1,0:T(8,128)S(1)}, f32[512,128]{1,0:T(8,128)S(1)}, u32[]{:S(2)}, u32[]{:S(2)}) collective-permute-start(f32[512,128]{1,0:T(8,128)S(1)} %get-tuple-element.30.own_ref), channel_id=1, source_target_pairs={{0,1},{1,0},{2,3},{3,2},{4,5},{5,4},{6,7},{7,6},{8,9},{9,8},{10,11... | collective-permute-start | bytes 786440 | tf_op jit(solution)/shard_map/ppermute | solution.py:188
  61.4 1.9 %collective-permute-start.1 = (f32[512,128]{1,0:T(8,128)S(1)}, f32[512,128]{1,0:T(8,128)S(1)}, u32[]{:S(2)}, u32[]{:S(2)}) collective-permute-start(f32[512,128]{1,0:T(8,128)S(1)} %get-tuple-element.26.own_ref), channel_id=1, source_target_pairs={{0,1},{1,0},{2,3},{3,2},{4,5},{5,4},{6,7},{7,6},{8,9},{9,8},{10,11... | collective-permute-start | bytes 786440 | tf_op jit(solution)/shard_map/ppermute | solution.py:188
  64.1 3.2 %collective-permute-start.8 = (f32[512,128]{1,0:T(8,128)S(1)}, f32[512,128]{1,0:T(8,128)S(1)}, u32[]{:S(2)}, u32[]{:S(2)}) collective-permute-start(f32[512,128]{1,0:T(8,128)S(1)} %get-tuple-element.32), channel_id=1, source_target_pairs={{0,14},{1,3},{2,0},{3,5},{4,2},{5,7},{6,4},{7,9},{8,6},{9,11},{10,... | collective-permute-start | bytes 786440 | tf_op jit(solution)/shard_map/ppermute | solution.py:257
  68.1 3.9 %collective-permute-start.2 = (f32[512,128]{1,0:T(8,128)S(1)}, f32[512,128]{1,0:T(8,128)S(1)}, u32[]{:S(2)}, u32[]{:S(2)}) collective-permute-start(f32[512,128]{1,0:T(8,128)S(1)} %get-tuple-element.29), channel_id=1, source_target_pairs={{0,2},{1,15},{2,4},{3,1},{4,6},{5,3},{6,8},{7,5},{8,10},{9,7},{10,... | collective-permute-start | bytes 786440 | tf_op jit(solution)/shard_map/ppermute | solution.py:257
  73.3 1.9 %collective-permute-start.9 = (f32[512,256]{1,0:T(8,128)S(1)}, f32[512,256]{1,0:T(8,128)S(1)}, u32[]{:S(2)}, u32[]{:S(2)}) collective-permute-start(f32[512,256]{1,0:T(8,128)S(1)} %maximum_add_fusion.1), channel_id=1, source_target_pairs={{0,14},{1,3},{2,0},{3,5},{4,2},{5,7},{6,4},{7,9},{8,6},{9,11},{10,... | collective-permute-start | bytes 1572872 | tf_op jit(solution)/shard_map/ppermute | solution.py:284
  75.2 1.1 collective-permute-done.2
  76.6 5.0 %collective-permute-start.3 = (f32[512,256]{1,0:T(8,128)S(1)}, f32[512,256]{1,0:T(8,128)S(1)}, u32[]{:S(2)}, u32[]{:S(2)}) collective-permute-start(f32[512,256]{1,0:T(8,128)S(1)} %maximum_add_fusion), channel_id=1, source_target_pairs={{0,2},{1,15},{2,4},{3,1},{4,6},{5,3},{6,8},{7,5},{8,10},{9,7},{10,... | collective-permute-start | bytes 1572872 | tf_op jit(solution)/shard_map/ppermute | solution.py:284
  82.1 3.2 %collective-permute-done.9 = f32[512,256]{1,0:T(8,128)S(1)} collective-permute-done((f32[512,256]{1,0:T(8,128)S(1)}, f32[512,256]{1,0:T(8,128)S(1)}, u32[]{:S(2)}, u32[]{:S(2)}) %collective-permute-start.9) | collective-permute-done | bytes 524320 | tf_op jit(solution)/shard_map/ppermute | solution.py:284
  85.3 1.9 %collective-permute-start.10 = (f32[512,256]{1,0:T(8,128)S(1)}, f32[512,256]{1,0:T(8,128)S(1)}, u32[]{:S(2)}, u32[]{:S(2)}) collective-permute-start(f32[512,256]{1,0:T(8,128)S(1)} %add.71), channel_id=1, source_target_pairs={{0,14},{1,3},{2,0},{3,5},{4,2},{5,7},{6,4},{7,9},{8,6},{9,11},{10,... | collective-permute-start | bytes 1572872 | tf_op jit(solution)/shard_map/ppermute | solution.py:284
  87.5 5.1 %collective-permute-done.3 = f32[512,256]{1,0:T(8,128)S(1)} collective-permute-done((f32[512,256]{1,0:T(8,128)S(1)}, f32[512,256]{1,0:T(8,128)S(1)}, u32[]{:S(2)}, u32[]{:S(2)}) %collective-permute-start.3) | collective-permute-done | bytes 524320 | tf_op jit(solution)/shard_map/ppermute | solution.py:284
  92.7 5.0 %collective-permute-start.4 = (f32[512,256]{1,0:T(8,128)S(1)}, f32[512,256]{1,0:T(8,128)S(1)}, u32[]{:S(2)}, u32[]{:S(2)}) collective-permute-start(f32[512,256]{1,0:T(8,128)S(1)} %add.62), channel_id=1, source_target_pairs={{0,2},{1,15},{2,4},{3,1},{4,6},{5,3},{6,8},{7,5},{8,10},{9,7},{10,... | collective-permute-start | bytes 1572872 | tf_op jit(solution)/shard_map/ppermute | solution.py:284
  98.7 11.4 %collective-permute-start.12 = (f32[512,128]{1,0:T(8,128)S(1)}, f32[512,128]{1,0:T(8,128)S(1)}, u32[]{:S(2)}, u32[]{:S(2)}) collective-permute-start(f32[512,128]{1,0:T(8,128)S(1)} %get-tuple-element.36), channel_id=1, source_target_pairs={{0,15},{1,2},{2,1},{3,4},{4,3},{5,6},{6,5},{7,8},{8,7},{9,10},{10,... | collective-permute-start | bytes 786440 | tf_op jit(solution)/shard_map/ppermute | solution.py:291
  110.1 1.9 %collective-permute-start.11 = (f32[512,128]{1,0:T(8,128)S(1)}, f32[512,128]{1,0:T(8,128)S(1)}, u32[]{:S(2)}, u32[]{:S(2)}) collective-permute-start(f32[512,128]{1,0:T(8,128)S(1)} %get-tuple-element.35), channel_id=1, source_target_pairs={{0,14},{1,3},{2,0},{3,5},{4,2},{5,7},{6,4},{7,9},{8,6},{9,11},{10,... | collective-permute-start | bytes 786440 | tf_op jit(solution)/shard_map/ppermute | solution.py:290
  112.2 7.0 %collective-permute-start.6 = (f32[512,128]{1,0:T(8,128)S(1)}, f32[512,128]{1,0:T(8,128)S(1)}, u32[]{:S(2)}, u32[]{:S(2)}) collective-permute-start(f32[512,128]{1,0:T(8,128)S(1)} %get-tuple-element.34), channel_id=1, source_target_pairs={{0,3},{1,14},{2,5},{3,0},{4,7},{5,2},{6,9},{7,4},{8,11},{9,6},{10,... | collective-permute-start | bytes 786440 | tf_op jit(solution)/shard_map/ppermute | solution.py:291
  119.2 1.9 %collective-permute-start.5 = (f32[512,128]{1,0:T(8,128)S(1)}, f32[512,128]{1,0:T(8,128)S(1)}, u32[]{:S(2)}, u32[]{:S(2)}) collective-permute-start(f32[512,128]{1,0:T(8,128)S(1)} %get-tuple-element.33), channel_id=1, source_target_pairs={{0,2},{1,15},{2,4},{3,1},{4,6},{5,3},{6,8},{7,5},{8,10},{9,7},{10,... | collective-permute-start | bytes 786440 | tf_op jit(solution)/shard_map/ppermute | solution.py:290
  121.6 2.2 %collective-permute-done.6 = f32[512,128]{1,0:T(8,128)S(1)} collective-permute-done((f32[512,128]{1,0:T(8,128)S(1)}, f32[512,128]{1,0:T(8,128)S(1)}, u32[]{:S(2)}, u32[]{:S(2)}) %collective-permute-start.6) | collective-permute-done | bytes 262176 | tf_op jit(solution)/shard_map/ppermute | solution.py:291
  123.8 3.9 %collective-permute-done.5 = f32[512,128]{1,0:T(8,128)S(1)} collective-permute-done((f32[512,128]{1,0:T(8,128)S(1)}, f32[512,128]{1,0:T(8,128)S(1)}, u32[]{:S(2)}, u32[]{:S(2)}) %collective-permute-start.5) | collective-permute-done | bytes 262176 | tf_op jit(solution)/shard_map/ppermute | solution.py:290
  (43 shorter events, 7.2 us)
Async XLA Ops:
  0.0 2.1 %copy-start = (bf16[128,2048]{1,0:T(8,128)(2,1)S(1)}, bf16[128,2048]{1,0:T(8,128)(2,1)}, u32[]{:S(2)}) copy-start(bf16[128,2048]{1,0:T(8,128)(2,1)} %own_ref) | copy-start | bytes 1572868
  2.2 16.4 %collective-permute-start = (f32[128,2048]{1,0:T(8,128)S(1)}, f32[128,2048]{1,0:T(8,128)S(1)}, u32[]{:S(2)}, u32[]{:S(2)}) collective-permute-start(f32[128,2048]{1,0:T(8,128)S(1)} %convert_element_type.17), channel_id=1, source_target_pairs={{0,1},{1,0},{2,3},{3,2},{4,5},{5,4},{6,7},{7,6},{8,9},{9,8},{10,11... | collective-permute-start | bytes 3145736 | tf_op jit(solution)/shard_map/ppermute | solution.py:188
  11.0 16.7 %all-to-all-start = ((f32[32,8,128]{2,1,0:T(8,128)}), f32[32,8,128]{2,1,0:T(8,128)S(1)}, u32[]{:S(2)}, u32[]{:S(2)}) async-start(f32[32,8,128]{2,1,0:T(8,128)} %bitcast.2), calls=%async_computation | async-start | bytes 262144 | tf_op jit(solution)/shard_map/all_to_all | solution.py:303
  18.6 23.5 %copy-start.3 = (bf16[1024,128]{1,0:T(8,128)(2,1)S(1)}, bf16[1024,128]{1,0:T(8,128)(2,1)}, u32[]{:S(2)}) copy-start(bf16[1024,128]{1,0:T(8,128)(2,1)} %get-tuple-element.23.k_ref) | copy-start | bytes 786436
  18.6 23.5 %copy-start.4 = (f32[128,128]{1,0:T(8,128)S(1)}, f32[128,128]{1,0:T(8,128)}, u32[]{:S(2)}) copy-start(f32[128,128]{1,0:T(8,128)} %get-tuple-element.25.column_ref) | copy-start | bytes 196612
  18.7 23.4 %copy-start.1 = (bf16[1024,1,128]{2,0,1:T(8,128)(2,1)S(1)}, bf16[1024,1,128]{2,0,1:T(8,128)(2,1)}, u32[]{:S(2)}) copy-start(bf16[1024,1,128]{2,0,1:T(8,128)(2,1)} %param.9) | copy-start | bytes 786436
  18.7 23.4 %copy-start.2 = (bf16[1024,1,128]{2,0,1:T(8,128)(2,1)S(1)}, bf16[1024,1,128]{2,0,1:T(8,128)(2,1)}, u32[]{:S(2)}) copy-start(bf16[1024,1,128]{2,0,1:T(8,128)(2,1)} %param.7) | copy-start | bytes 786436
  28.4 13.7 %all-to-all-start.1 = ((f32[32,8,128]{2,1,0:T(8,128)}), f32[32,8,128]{2,1,0:T(8,128)S(1)}, u32[]{:S(2)}, u32[]{:S(2)}) async-start(f32[32,8,128]{2,1,0:T(8,128)} %prefix.1), calls=%async_computation.1 | async-start | bytes 262144 | tf_op jit(solution)/shard_map/all_to_all | solution.py:306
  56.9 6.5 %collective-permute-start.7 = (f32[512,128]{1,0:T(8,128)S(1)}, f32[512,128]{1,0:T(8,128)S(1)}, u32[]{:S(2)}, u32[]{:S(2)}) collective-permute-start(f32[512,128]{1,0:T(8,128)S(1)} %get-tuple-element.30.own_ref), channel_id=1, source_target_pairs={{0,1},{1,0},{2,3},{3,2},{4,5},{5,4},{6,7},{7,6},{8,9},{9,8},{10,11... | collective-permute-start | bytes 786440 | tf_op jit(solution)/shard_map/ppermute | solution.py:188
  61.4 5.9 %collective-permute-start.1 = (f32[512,128]{1,0:T(8,128)S(1)}, f32[512,128]{1,0:T(8,128)S(1)}, u32[]{:S(2)}, u32[]{:S(2)}) collective-permute-start(f32[512,128]{1,0:T(8,128)S(1)} %get-tuple-element.26.own_ref), channel_id=1, source_target_pairs={{0,1},{1,0},{2,3},{3,2},{4,5},{5,4},{6,7},{7,6},{8,9},{9,8},{10,11... | collective-permute-start | bytes 786440 | tf_op jit(solution)/shard_map/ppermute | solution.py:188
  64.1 8.9 %collective-permute-start.8 = (f32[512,128]{1,0:T(8,128)S(1)}, f32[512,128]{1,0:T(8,128)S(1)}, u32[]{:S(2)}, u32[]{:S(2)}) collective-permute-start(f32[512,128]{1,0:T(8,128)S(1)} %get-tuple-element.32), channel_id=1, source_target_pairs={{0,14},{1,3},{2,0},{3,5},{4,2},{5,7},{6,4},{7,9},{8,6},{9,11},{10,... | collective-permute-start | bytes 786440 | tf_op jit(solution)/shard_map/ppermute | solution.py:257
  68.1 8.2 %collective-permute-start.2 = (f32[512,128]{1,0:T(8,128)S(1)}, f32[512,128]{1,0:T(8,128)S(1)}, u32[]{:S(2)}, u32[]{:S(2)}) collective-permute-start(f32[512,128]{1,0:T(8,128)S(1)} %get-tuple-element.29), channel_id=1, source_target_pairs={{0,2},{1,15},{2,4},{3,1},{4,6},{5,3},{6,8},{7,5},{8,10},{9,7},{10,... | collective-permute-start | bytes 786440 | tf_op jit(solution)/shard_map/ppermute | solution.py:257
  73.3 12.0 %collective-permute-start.9 = (f32[512,256]{1,0:T(8,128)S(1)}, f32[512,256]{1,0:T(8,128)S(1)}, u32[]{:S(2)}, u32[]{:S(2)}) collective-permute-start(f32[512,256]{1,0:T(8,128)S(1)} %maximum_add_fusion.1), channel_id=1, source_target_pairs={{0,14},{1,3},{2,0},{3,5},{4,2},{5,7},{6,4},{7,9},{8,6},{9,11},{10,... | collective-permute-start | bytes 1572872 | tf_op jit(solution)/shard_map/ppermute | solution.py:284
  76.6 16.0 %collective-permute-start.3 = (f32[512,256]{1,0:T(8,128)S(1)}, f32[512,256]{1,0:T(8,128)S(1)}, u32[]{:S(2)}, u32[]{:S(2)}) collective-permute-start(f32[512,256]{1,0:T(8,128)S(1)} %maximum_add_fusion), channel_id=1, source_target_pairs={{0,2},{1,15},{2,4},{3,1},{4,6},{5,3},{6,8},{7,5},{8,10},{9,7},{10,... | collective-permute-start | bytes 1572872 | tf_op jit(solution)/shard_map/ppermute | solution.py:284
  85.3 13.3 %collective-permute-start.10 = (f32[512,256]{1,0:T(8,128)S(1)}, f32[512,256]{1,0:T(8,128)S(1)}, u32[]{:S(2)}, u32[]{:S(2)}) collective-permute-start(f32[512,256]{1,0:T(8,128)S(1)} %add.71), channel_id=1, source_target_pairs={{0,14},{1,3},{2,0},{3,5},{4,2},{5,7},{6,4},{7,9},{8,6},{9,11},{10,... | collective-permute-start | bytes 1572872 | tf_op jit(solution)/shard_map/ppermute | solution.py:284
  92.7 19.3 %collective-permute-start.4 = (f32[512,256]{1,0:T(8,128)S(1)}, f32[512,256]{1,0:T(8,128)S(1)}, u32[]{:S(2)}, u32[]{:S(2)}) collective-permute-start(f32[512,256]{1,0:T(8,128)S(1)} %add.62), channel_id=1, source_target_pairs={{0,2},{1,15},{2,4},{3,1},{4,6},{5,3},{6,8},{7,5},{8,10},{9,7},{10,... | collective-permute-start | bytes 1572872 | tf_op jit(solution)/shard_map/ppermute | solution.py:284
  98.7 22.6 %collective-permute-start.12 = (f32[512,128]{1,0:T(8,128)S(1)}, f32[512,128]{1,0:T(8,128)S(1)}, u32[]{:S(2)}, u32[]{:S(2)}) collective-permute-start(f32[512,128]{1,0:T(8,128)S(1)} %get-tuple-element.36), channel_id=1, source_target_pairs={{0,15},{1,2},{2,1},{3,4},{4,3},{5,6},{6,5},{7,8},{8,7},{9,10},{10,... | collective-permute-start | bytes 786440 | tf_op jit(solution)/shard_map/ppermute | solution.py:291
  110.1 11.4 %collective-permute-start.11 = (f32[512,128]{1,0:T(8,128)S(1)}, f32[512,128]{1,0:T(8,128)S(1)}, u32[]{:S(2)}, u32[]{:S(2)}) collective-permute-start(f32[512,128]{1,0:T(8,128)S(1)} %get-tuple-element.35), channel_id=1, source_target_pairs={{0,14},{1,3},{2,0},{3,5},{4,2},{5,7},{6,4},{7,9},{8,6},{9,11},{10,... | collective-permute-start | bytes 786440 | tf_op jit(solution)/shard_map/ppermute | solution.py:290
  112.2 11.6 %collective-permute-start.6 = (f32[512,128]{1,0:T(8,128)S(1)}, f32[512,128]{1,0:T(8,128)S(1)}, u32[]{:S(2)}, u32[]{:S(2)}) collective-permute-start(f32[512,128]{1,0:T(8,128)S(1)} %get-tuple-element.34), channel_id=1, source_target_pairs={{0,3},{1,14},{2,5},{3,0},{4,7},{5,2},{6,9},{7,4},{8,11},{9,6},{10,... | collective-permute-start | bytes 786440 | tf_op jit(solution)/shard_map/ppermute | solution.py:291
  119.2 8.6 %collective-permute-start.5 = (f32[512,128]{1,0:T(8,128)S(1)}, f32[512,128]{1,0:T(8,128)S(1)}, u32[]{:S(2)}, u32[]{:S(2)}) collective-permute-start(f32[512,128]{1,0:T(8,128)S(1)} %get-tuple-element.33), channel_id=1, source_target_pairs={{0,2},{1,15},{2,4},{3,1},{4,6},{5,3},{6,8},{7,5},{8,10},{9,7},{10,... | collective-permute-start | bytes 786440 | tf_op jit(solution)/shard_map/ppermute | solution.py:290

commit v6 on v5

--- a/solution.py
+++ b/solution.py
@@ -71,7 +71,7 @@
 
 
 def solve_kernel(
-    reg_ref, q_ref, k_ref, v_ref, before_ref, column_ref, early_ref, late_ref,
+    reg_ref, core_ref, q_ref, k_ref, v_ref, before_ref, column_ref, one_ref, two_ref,
     first, second, last, x_ref, r_ref, p_ref,
 ):
     width = q_ref.shape[1]
@@ -142,6 +142,7 @@
     lax.fori_loop(0, ITERS, step, tuple(starts))
 
     column = column_ref[...]
+    rows = []
     for b in range(blocks):
         x_high, x_low = halves(x_ref[b])
         key = first[b, width:, :]
@@ -153,19 +154,23 @@
         ) + mm(last[b, :, 3 * BLOCK :], x_low)
         square = jnp.mean(read * read, axis=0, keepdims=True)
         normed = read * column * lax.rsqrt(square + 1e-06)
-        out_ref = early_ref if 2 * b < blocks else late_ref
-        place = (b % (blocks // 2)) * BLOCK
-        out_ref[place : place + BLOCK, :] = normed.T.astype(BF16).astype(F32)
-
-
-def solve(reg, queries, keys, values, before, column):
+        rows.append(normed.T.astype(BF16).astype(F32))
+    half = blocks // 2
+    early_first = core_ref[0] == 0
+    for b in range(half):
+        place = pl.ds(b * BLOCK, BLOCK)
+        one_ref[place, :] = jnp.where(early_first, rows[b], rows[b + half])
+        two_ref[place, :] = jnp.where(early_first, rows[b + half], rows[b])
+
+
+def solve(reg, core, queries, keys, values, before, column):
     tokens, width = queries.shape
     blocks = tokens // BLOCK
     vmem = pl.BlockSpec(memory_space=pltpu.VMEM)
     return pl.pallas_call(
         solve_kernel,
         out_shape=(jax.ShapeDtypeStruct((tokens // 2, width), F32),) * 2,
-        in_specs=[pl.BlockSpec(memory_space=pltpu.SMEM)] + [vmem] * 5,
+        in_specs=[pl.BlockSpec(memory_space=pltpu.SMEM)] * 2 + [vmem] * 5,
         out_specs=(vmem, vmem),
         scratch_shapes=[
             pltpu.VMEM((blocks, 2 * BLOCK, 2 * width), BF16),
@@ -180,7 +185,7 @@
         ),
         compiler_params=pltpu.CompilerParams(vmem_limit_bytes=20 * 2**20),
         name="solve",
-    )(reg, queries, keys, values, before, column)
+    )(reg, core, queries, keys, values, before, column)
 
 
 def swapped(value):
@@ -207,20 +212,10 @@
     )(own, other)
 
 
-def open_kernel(where_ref, own_ref, other_ref, weights_ref, rows_ref, far_ref):
-    width = own_ref.shape[1]
+def open_kernel(where_ref, own_ref, other_ref, weights_ref, rows_ref, sums_ref):
     rows = jnp.concatenate([own_ref[...], other_ref[...]], axis=1).astype(BF16)
     rows_ref[...] = rows
-    columns = weights_ref[where_ref[0]]
-    columns = jnp.where(where_ref[1] == 0, columns[:, :width], columns[:, width:])
-    far_ref[...] = mm(rows, columns)
-
-
-def opposite():
-    place, heads = lax.axis_index("head").astype(jnp.uint32), lax.axis_size("head")
-    chip, core = lax.div(place, jnp.uint32(2)), lax.rem(place, jnp.uint32(2))
-    far = lax.rem(chip + jnp.uint32(heads // 4), jnp.uint32(heads // 2))
-    return jnp.stack([far, core]).astype(jnp.int32)
+    sums_ref[...] = mm(rows, weights_ref[where_ref[0]])
 
 
 def opening(where, own, other, weights):
@@ -230,7 +225,7 @@
         open_kernel,
         out_shape=(
             jax.ShapeDtypeStruct((tokens, 2 * width), BF16),
-            jax.ShapeDtypeStruct((tokens, width), F32),
+            jax.ShapeDtypeStruct((tokens, 2 * width), F32),
         ),
         in_specs=[pl.BlockSpec(memory_space=pltpu.SMEM), vmem, vmem, vmem],
         out_specs=(vmem, vmem),
@@ -239,30 +234,33 @@
     )(where, own, other, weights)
 
 
-def project(normed, weights, where):
+def chip_ahead(away):
+    chips = lax.axis_size("head") // 2
+    place = lax.axis_index("head").astype(jnp.uint32)
+    chip, core = lax.div(place, jnp.uint32(2)), lax.rem(place, jnp.uint32(2))
+    ahead = jnp.where(core == 1, jnp.uint32(chips - away), jnp.uint32(away % chips))
+    return lax.rem(chip + ahead, jnp.uint32(chips))
+
+
+def project(normed, weights, core, starts):
     width = normed[0].shape[1]
     heads = lax.axis_size("head")
-    place = lax.axis_index("head").astype(jnp.uint32)
-    chips = heads // 2
-    chip, core = lax.div(place, jnp.uint32(2)), lax.rem(place, jnp.uint32(2))
-    others = [swapped(half) for half in normed]
-    rings, crosses, leftward, halves_of, flows = [], [], [], [], []
-    for piece, (own, other) in enumerate(zip(normed, others)):
-        step = [2 if (i + piece) % 2 == 0 else heads - 2 for i in range(heads)]
-        rings.append([(i, (i + step[i]) % heads) for i in range(heads)])
-        crosses.append([(i, ((i + step[i]) % heads) ^ 1) for i in range(heads)])
-        leftward.append(core != piece)
-        rows, far = opening(where, own, other, weights)
-        halves_of.append(rows)
-        flows.append(lax.ppermute(far, "head", rings[piece]))
+    far = heads // 4
+    step = [2 if i % 2 == 0 else heads - 2 for i in range(heads)]
+    ring = [(i, (i + step[i]) % heads) for i in range(heads)]
+    cross = [(i, ((i + step[i]) % heads) ^ 1) for i in range(heads)]
+    others = [swapped(normed[1]), swapped(normed[0])]
+    rows, flows = [], []
+    for start, own, other in zip(starts, normed, others):
+        both, sums = opening(start, own, other, weights)
+        rows.append(both)
+        flows.append(sums)
 
     def part(piece, away):
-        ahead = jnp.where(
-            leftward[piece], jnp.uint32(chips - away), jnp.uint32(away % chips)
+        columns = lax.dynamic_index_in_dim(
+            weights, chip_ahead(away), axis=0, keepdims=False
         )
-        index = lax.rem(chip + ahead, jnp.uint32(chips))
-        columns = lax.dynamic_index_in_dim(weights, index, axis=0, keepdims=False)
-        return jnp.dot(halves_of[piece], columns, preferred_element_type=F32)
+        return jnp.dot(rows[piece], columns, preferred_element_type=F32)
 
     def own_columns(value):
         return jnp.where(core == 1, value[:, width:], value[:, :width])
@@ -270,27 +268,23 @@
     def other_columns(value):
         return jnp.where(core == 1, value[:, :width], value[:, width:])
 
-    for away in range(chips // 2 - 1, 1, -1):
-        for piece, flow in enumerate(flows):
-            if flow.shape[1] == width:
-                blank = jnp.zeros_like(flow)
-                flow = jnp.concatenate(
-                    [
-                        jnp.where(core == 1, blank, flow),
-                        jnp.where(core == 1, flow, blank),
-                    ],
-                    axis=1,
-                )
-            flows[piece] = lax.ppermute(
-                flow + part(piece, away), "head", rings[piece]
-            )
-    done = []
-    for piece, flow in enumerate(flows):
-        last = flow + part(piece, 1)
-        same = lax.ppermute(own_columns(last), "head", rings[piece])
-        crossed = lax.ppermute(other_columns(last), "head", crosses[piece])
-        done.append((own_columns(part(piece, 0)) + same + crossed).astype(BF16))
-    return jnp.concatenate(done, axis=0)
+    for away in range(far, 1, -1):
+        for piece in (0, 1):
+            if away - piece > 1:
+                sent = lax.ppermute(flows[piece], "head", ring)
+                flows[piece] = sent + part(piece, away - piece - 1)
+    same, crossed = [], []
+    for piece in (1, 0):
+        same.append(lax.ppermute(own_columns(flows[piece]), "head", ring))
+        crossed.append(lax.ppermute(other_columns(flows[piece]), "head", cross))
+    first = own_columns(part(0, 0)) + same[1] + crossed[0]
+    second = own_columns(part(1, 0)) + same[0] + crossed[1]
+    first, second = first.astype(BF16), second.astype(BF16)
+    return jnp.where(
+        core == 1,
+        jnp.concatenate([second, first], axis=0),
+        jnp.concatenate([first, second], axis=0),
+    )
 
 
 def body(queries, keys, values, key_gain, reg, norm_gain, out_weight):
@@ -302,11 +296,19 @@
     state, out_weight = lax.optimization_barrier((state, out_weight))
     parts = lax.all_to_all(state.reshape(devices, rows, width), "seq", 0, 0)
     weights = join_weight(out_weight, swapped(out_weight.astype(F32)))
-    parts, weights, where = lax.optimization_barrier((parts, weights, opposite()))
+    far = lax.axis_size("head") // 4
+    core = lax.rem(lax.axis_index("head").astype(jnp.uint32), jnp.uint32(2))
+    starts = [chip_ahead(away).astype(jnp.int32).reshape(1) for away in (far, far - 1)]
+    core = core.astype(jnp.int32)
+    parts, weights, core, starts = lax.optimization_barrier(
+        (parts, weights, core, starts)
+    )
     before = lax.all_to_all(exclusive(parts), "seq", 0, 0)
     before = before.reshape(2 * width, width)
-    normed = solve(reg, query_rows, gained, value_rows, before, column)
-    return project(normed, weights, where)
+    normed = solve(
+        reg, core.reshape(1), query_rows, gained, value_rows, before, column
+    )
+    return project(normed, weights, core, starts)
 
 
 def solution(mesh):

time: 129 us -> 119 us (0.922)
  starting transfers between devices: 70.4 us -> 65.2 us
  waiting for transfers between devices: 34.6 us -> 30.2 us
    ppermute x10 -> x9, waiting for transfers between devices: 17.2 us -> 9.98 us  [the longest x2 5.24 us: project(): crossed.append(lax.ppermute(other_columns(flows[piece]), 'head', cross))]
    ppermute x10 -> x9, starting transfers between devices: 43.1 us -> 37.9 us  [the longest x5 20.1 us: project(): sent = lax.ppermute(flows[piece], 'head', ring)]
    ppermute x3, waiting for transfers between devices: 0.01 us -> 2.64 us  [swapped(): return lax.ppermute(value, 'head', [(i, i ^ 1) for i in range(heads)])]
  transfers between devices with their start and end apart: 15 -> 14, of which waited for: 10 -> 8; matrix products, arithmetic and copies ran while one was open for 2% -> 3% of each run, Pallas kernels for 1% -> 0%
where the time goes in v6:
time: 119 us; the launch traced here: 118 us
  starting transfers between devices  65.2 us (55%)
  waiting for transfers between devices  30.2 us (25%)
  Pallas kernels  18.1 us (15%)
  other arithmetic  2.47 us (2%)
  matrix products  1.59 us (1%)
    ppermute x5, starting transfers between devices, project(): sent = lax.ppermute(flows[piece], 'head', ring)  20.1 us
    ppermute x3, starting transfers between devices, swapped(): return lax.ppermute(value, 'head', [(i, i ^ 1) for i in range(heads)])  15.2 us
    pallas_call x1, Pallas kernels, solve(): pl.pallas_call(solve_kernel, out_shape=(jax.ShapeDtypeStruct((tokens // 2...  14.7 us
    ppermute x2, starting transfers between devices, project(): crossed.append(lax.ppermute(other_columns(flows[piece]), 'head', cross))  11.1 us
    all_to_all x1, waiting for transfers between devices, body(): parts = lax.all_to_all(state.reshape(devices, rows, width), 'seq', 0, 0)  9.01 us
    all_to_all x1, waiting for transfers between devices, body(): before = lax.all_to_all(exclusive(parts), 'seq', 0, 0)  8.52 us
    all_to_all x1, starting transfers between devices, body(): parts = lax.all_to_all(state.reshape(devices, rows, width), 'seq', 0, 0)  7.52 us
    ppermute x2, starting transfers between devices, project(): same.append(lax.ppermute(own_columns(flows[piece]), 'head', ring))  6.72 us
  transfers between devices with their start and end apart: 14, of which 8 were waited for; matrix products, arithmetic and copies ran while one was open for 3% of the time, Pallas kernels for 0%

profile of v6, /device:TPU:1, one launch (start us, length us, event | category | flops | bytes accessed | tf_op | source)
XLA Modules:
  0.0 118.5 jit_solution(11091246015148556524)
XLA Ops:
  0.0 2.1 %local_state.1 = (f32[256,128]{1,0:T(8,128)}, bf16[1024,128]{1,0:T(8,128)(2,1)}, f32[128,128]{1,0:T(8,128)}) custom-call(bf16[1024,128]{1,0:T(8,128)(2,1)} %bitcast.37, bf16[1024,128]{1,0:T(8,128)(2,1)} %bitcast.33, f32[1,128]{1,0:T(1,128)} %gain_ref.1, f32[1,128]{1,0:T(1,128)} %norm_ref.1), custom_call_target="tpu_custom_call" | custom-call | tf_op jit(solution)/shard_map/local_state/pallas_call | solution.py:45
  2.2 8.8 %collective-permute-start = (f32[128,2048]{1,0:T(8,128)S(1)}, f32[128,2048]{1,0:T(8,128)S(1)}, u32[]{:S(2)}, u32[]{:S(2)}) collective-permute-start(f32[128,2048]{1,0:T(8,128)S(1)} %convert_element_type.14), channel_id=1, source_target_pairs={{0,1},{1,0},{2,3},{3,2},{4,5},{5,4},{6,7},{7,6},{8,9},{9,8},{10,11... | collective-permute-start | bytes 3145736 | tf_op jit(solution)/shard_map/ppermute | solution.py:193
  11.0 7.5 %all-to-all-start = ((f32[32,8,128]{2,1,0:T(8,128)}), f32[32,8,128]{2,1,0:T(8,128)S(1)}, u32[]{:S(2)}, u32[]{:S(2)}) async-start(f32[32,8,128]{2,1,0:T(8,128)} %bitcast.2), calls=%async_computation | async-start | bytes 262144 | tf_op jit(solution)/shard_map/all_to_all | solution.py:297
  18.7 9.0 %all-to-all-done.x_ref = f32[32,8,128]{2,1,0:T(8,128)S(1)} async-done(((f32[32,8,128]{2,1,0:T(8,128)}), f32[32,8,128]{2,1,0:T(8,128)S(1)}, u32[]{:S(2)}, u32[]{:S(2)}) %all-to-all-start) | async-done | bytes 131104 | tf_op jit(solution)/shard_map/all_to_all | solution.py:297
  28.4 4.5 %all-to-all-start.1 = ((f32[32,8,128]{2,1,0:T(8,128)}), f32[32,8,128]{2,1,0:T(8,128)S(1)}, u32[]{:S(2)}, u32[]{:S(2)}) async-start(f32[32,8,128]{2,1,0:T(8,128)} %prefix.1), calls=%async_computation.1 | async-start | bytes 262144 | tf_op jit(solution)/shard_map/all_to_all | solution.py:306
  33.6 8.5 %all-to-all-done.1 = f32[32,8,128]{2,1,0:T(8,128)S(1)} async-done(((f32[32,8,128]{2,1,0:T(8,128)}), f32[32,8,128]{2,1,0:T(8,128)S(1)}, u32[]{:S(2)}, u32[]{:S(2)}) %all-to-all-start.1) | async-done | bytes 131104 | tf_op jit(solution)/shard_map/all_to_all | solution.py:306
  42.1 14.7 %solve.1 = (f32[512,128]{1,0:T(8,128)S(1)}, f32[512,128]{1,0:T(8,128)S(1)}) custom-call(f32[1]{0:T(128)S(6)} %copy.8.reg_ref, s32[1]{0:T(128)} %bitcast.5.core_ref, bf16[1024,128]{1,0:T(8,128)(2,1)S(1)} %bitcast.36, bf16[1024,128]{1,0:T(8,128)(2,1)S(1)} %copy-done.3, bf16[1024,128]{1,0:T(8,128)(2,1)S(1)} %bitcast.34, f32[256,128]{1,0:T(8,128)S(1)} %bitcast.35, ...), custom_call_target="tpu_custom_call" | custom-call | flops 60000002048 | bytes 2097152 | tf_op jit(solution)/shard_map/solve/pallas_call | solution.py:170
  56.8 4.5 %collective-permute-start.5 = (f32[512,128]{1,0:T(8,128)S(1)}, f32[512,128]{1,0:T(8,128)S(1)}, u32[]{:S(2)}, u32[]{:S(2)}) collective-permute-start(f32[512,128]{1,0:T(8,128)S(1)} %get-tuple-element.29.own_ref), channel_id=1, source_target_pairs={{0,1},{1,0},{2,3},{3,2},{4,5},{5,4},{6,7},{7,6},{8,9},{9,8},{10,11... | collective-permute-start | bytes 786440 | tf_op jit(solution)/shard_map/ppermute | solution.py:193
  61.4 1.1 collective-permute-done.5.other_ref
  62.8 5.1 %collective-permute-start.6 = (f32[512,256]{1,0:T(8,128)S(1)}, f32[512,256]{1,0:T(8,128)S(1)}, u32[]{:S(2)}, u32[]{:S(2)}) collective-permute-start(f32[512,256]{1,0:T(8,128)S(1)} %get-tuple-element.35), channel_id=1, source_target_pairs={{0,2},{1,15},{2,4},{3,1},{4,6},{5,3},{6,8},{7,5},{8,10},{9,7},{10,... | collective-permute-start | bytes 1572872 | tf_op jit(solution)/shard_map/ppermute | solution.py:274
  67.9 1.9 %collective-permute-start.1 = (f32[512,128]{1,0:T(8,128)S(1)}, f32[512,128]{1,0:T(8,128)S(1)}, u32[]{:S(2)}, u32[]{:S(2)}) collective-permute-start(f32[512,128]{1,0:T(8,128)S(1)} %get-tuple-element.30.own_ref), channel_id=1, source_target_pairs={{0,1},{1,0},{2,3},{3,2},{4,5},{5,4},{6,7},{7,6},{8,9},{9,8},{10,11... | collective-permute-start | bytes 786440 | tf_op jit(solution)/shard_map/ppermute | solution.py:193
  69.8 1.5 %collective-permute-done.1.other_ref = f32[512,128]{1,0:T(8,128)S(1)} collective-permute-done((f32[512,128]{1,0:T(8,128)S(1)}, f32[512,128]{1,0:T(8,128)S(1)}, u32[]{:S(2)}, u32[]{:S(2)}) %collective-permute-start.1) | collective-permute-done | bytes 262176 | tf_op jit(solution)/shard_map/ppermute | solution.py:193
  71.5 3.0 %collective-permute-start.2 = (f32[512,256]{1,0:T(8,128)S(1)}, f32[512,256]{1,0:T(8,128)S(1)}, u32[]{:S(2)}, u32[]{:S(2)}) collective-permute-start(f32[512,256]{1,0:T(8,128)S(1)} %get-tuple-element.33), channel_id=1, source_target_pairs={{0,2},{1,15},{2,4},{3,1},{4,6},{5,3},{6,8},{7,5},{8,10},{9,7},{10,... | collective-permute-start | bytes 1572872 | tf_op jit(solution)/shard_map/ppermute | solution.py:274
  74.8 4.2 %collective-permute-start.7 = (f32[512,256]{1,0:T(8,128)S(1)}, f32[512,256]{1,0:T(8,128)}, u32[]{:S(2)}, u32[]{:S(2)}) collective-permute-start(f32[512,256]{1,0:T(8,128)S(1)} %add.54), channel_id=1, source_target_pairs={{0,2},{1,15},{2,4},{3,1},{4,6},{5,3},{6,8},{7,5},{8,10},{9,7},{10,... | collective-permute-start | bytes 1572872 | tf_op jit(solution)/shard_map/ppermute | solution.py:274
  79.3 2.4 %collective-permute-done.2 = f32[512,256]{1,0:T(8,128)S(1)} collective-permute-done((f32[512,256]{1,0:T(8,128)S(1)}, f32[512,256]{1,0:T(8,128)S(1)}, u32[]{:S(2)}, u32[]{:S(2)}) %collective-permute-start.2) | collective-permute-done | bytes 524320 | tf_op jit(solution)/shard_map/ppermute | solution.py:274
  81.8 3.9 %collective-permute-start.3 = (f32[512,256]{1,0:T(8,128)S(1)}, f32[512,256]{1,0:T(8,128)S(1)}, u32[]{:S(2)}, u32[]{:S(2)}) collective-permute-start(f32[512,256]{1,0:T(8,128)S(1)} %add.50), channel_id=1, source_target_pairs={{0,2},{1,15},{2,4},{3,1},{4,6},{5,3},{6,8},{7,5},{8,10},{9,7},{10,... | collective-permute-start | bytes 1572872 | tf_op jit(solution)/shard_map/ppermute | solution.py:274
  86.0 1.5 %collective-permute-done.7 = f32[512,256]{1,0:T(8,128)} collective-permute-done((f32[512,256]{1,0:T(8,128)S(1)}, f32[512,256]{1,0:T(8,128)}, u32[]{:S(2)}, u32[]{:S(2)}) %collective-permute-start.7) | collective-permute-done | bytes 524320 | tf_op jit(solution)/shard_map/ppermute | solution.py:274
  87.5 1.1 add.55
  88.6 3.9 %collective-permute-start.8 = (f32[512,256]{1,0:T(8,128)S(1)}, f32[512,256]{1,0:T(8,128)S(1)}, u32[]{:S(2)}, u32[]{:S(2)}) collective-permute-start(f32[512,256]{1,0:T(8,128)S(1)} %add.55), channel_id=1, source_target_pairs={{0,2},{1,15},{2,4},{3,1},{4,6},{5,3},{6,8},{7,5},{8,10},{9,7},{10,... | collective-permute-start | bytes 1572872 | tf_op jit(solution)/shard_map/ppermute | solution.py:274
  93.1 5.0 %collective-permute-start.11 = (f32[512,128]{1,0:T(8,128)S(1)}, f32[512,128]{1,0:T(8,128)S(1)}, u32[]{:S(2)}, u32[]{:S(2)}) collective-permute-start(f32[512,128]{1,0:T(8,128)S(1)} %get-tuple-element.38), channel_id=1, source_target_pairs={{0,3},{1,14},{2,5},{3,0},{4,7},{5,2},{6,9},{7,4},{8,11},{9,6},{10,... | collective-permute-start | bytes 786440 | tf_op jit(solution)/shard_map/ppermute | solution.py:279
  98.9 4.8 %collective-permute-start.10 = (f32[512,128]{1,0:T(8,128)S(1)}, f32[512,128]{1,0:T(8,128)S(1)}, u32[]{:S(2)}, u32[]{:S(2)}) collective-permute-start(f32[512,128]{1,0:T(8,128)S(1)} %get-tuple-element.40), channel_id=1, source_target_pairs={{0,2},{1,15},{2,4},{3,1},{4,6},{5,3},{6,8},{7,5},{8,10},{9,7},{10,... | collective-permute-start | bytes 786440 | tf_op jit(solution)/shard_map/ppermute | solution.py:278
  104.0 1.9 %collective-permute-start.4 = (f32[512,128]{1,0:T(8,128)S(1)}, f32[512,128]{1,0:T(8,128)S(1)}, u32[]{:S(2)}, u32[]{:S(2)}) collective-permute-start(f32[512,128]{1,0:T(8,128)S(1)} %get-tuple-element.37), channel_id=1, source_target_pairs={{0,2},{1,15},{2,4},{3,1},{4,6},{5,3},{6,8},{7,5},{8,10},{9,7},{10,... | collective-permute-start | bytes 786440 | tf_op jit(solution)/shard_map/ppermute | solution.py:278
  105.9 6.1 %collective-permute-start.9 = (f32[512,128]{1,0:T(8,128)S(1)}, f32[512,128]{1,0:T(8,128)S(1)}, u32[]{:S(2)}, u32[]{:S(2)}) collective-permute-start(f32[512,128]{1,0:T(8,128)S(1)} %get-tuple-element.39), channel_id=1, source_target_pairs={{0,3},{1,14},{2,5},{3,0},{4,7},{5,2},{6,9},{7,4},{8,11},{9,6},{10,... | collective-permute-start | bytes 786440 | tf_op jit(solution)/shard_map/ppermute | solution.py:279
  112.4 5.2 %collective-permute-done.9 = f32[512,128]{1,0:T(8,128)S(1)} collective-permute-done((f32[512,128]{1,0:T(8,128)S(1)}, f32[512,128]{1,0:T(8,128)S(1)}, u32[]{:S(2)}, u32[]{:S(2)}) %collective-permute-start.9) | collective-permute-done | bytes 262176 | tf_op jit(solution)/shard_map/ppermute | solution.py:279
  (38 shorter events, 5.0 us)
Async XLA Ops:
  0.0 2.1 %copy-start = (bf16[128,2048]{1,0:T(8,128)(2,1)S(1)}, bf16[128,2048]{1,0:T(8,128)(2,1)}, u32[]{:S(2)}) copy-start(bf16[128,2048]{1,0:T(8,128)(2,1)} %own_ref) | copy-start | bytes 1572868
  2.2 16.3 %collective-permute-start = (f32[128,2048]{1,0:T(8,128)S(1)}, f32[128,2048]{1,0:T(8,128)S(1)}, u32[]{:S(2)}, u32[]{:S(2)}) collective-permute-start(f32[128,2048]{1,0:T(8,128)S(1)} %convert_element_type.14), channel_id=1, source_target_pairs={{0,1},{1,0},{2,3},{3,2},{4,5},{5,4},{6,7},{7,6},{8,9},{9,8},{10,11... | collective-permute-start | bytes 3145736 | tf_op jit(solution)/shard_map/ppermute | solution.py:193
  11.0 16.7 %all-to-all-start = ((f32[32,8,128]{2,1,0:T(8,128)}), f32[32,8,128]{2,1,0:T(8,128)S(1)}, u32[]{:S(2)}, u32[]{:S(2)}) async-start(f32[32,8,128]{2,1,0:T(8,128)} %bitcast.2), calls=%async_computation | async-start | bytes 262144 | tf_op jit(solution)/shard_map/all_to_all | solution.py:297
  18.6 23.5 %copy-start.3 = (bf16[1024,128]{1,0:T(8,128)(2,1)S(1)}, bf16[1024,128]{1,0:T(8,128)(2,1)}, u32[]{:S(2)}) copy-start(bf16[1024,128]{1,0:T(8,128)(2,1)} %get-tuple-element.26.k_ref) | copy-start | bytes 786436
  18.6 23.5 %copy-start.4 = (f32[128,128]{1,0:T(8,128)S(1)}, f32[128,128]{1,0:T(8,128)}, u32[]{:S(2)}) copy-start(f32[128,128]{1,0:T(8,128)} %get-tuple-element.28.column_ref) | copy-start | bytes 196612
  27.7 14.4 %copy-start.1 = (bf16[1024,1,128]{2,0,1:T(8,128)(2,1)S(1)}, bf16[1024,1,128]{2,0,1:T(8,128)(2,1)}, u32[]{:S(2)}) copy-start(bf16[1024,1,128]{2,0,1:T(8,128)(2,1)} %param.9) | copy-start | bytes 786436
  27.7 14.4 %copy-start.2 = (bf16[1024,1,128]{2,0,1:T(8,128)(2,1)S(1)}, bf16[1024,1,128]{2,0,1:T(8,128)(2,1)}, u32[]{:S(2)}) copy-start(bf16[1024,1,128]{2,0,1:T(8,128)(2,1)} %param.7) | copy-start | bytes 786436
  28.4 13.7 %all-to-all-start.1 = ((f32[32,8,128]{2,1,0:T(8,128)}), f32[32,8,128]{2,1,0:T(8,128)S(1)}, u32[]{:S(2)}, u32[]{:S(2)}) async-start(f32[32,8,128]{2,1,0:T(8,128)} %prefix.1), calls=%async_computation.1 | async-start | bytes 262144 | tf_op jit(solution)/shard_map/all_to_all | solution.py:306
  56.8 5.7 %collective-permute-start.5 = (f32[512,128]{1,0:T(8,128)S(1)}, f32[512,128]{1,0:T(8,128)S(1)}, u32[]{:S(2)}, u32[]{:S(2)}) collective-permute-start(f32[512,128]{1,0:T(8,128)S(1)} %get-tuple-element.29.own_ref), channel_id=1, source_target_pairs={{0,1},{1,0},{2,3},{3,2},{4,5},{5,4},{6,7},{7,6},{8,9},{9,8},{10,11... | collective-permute-start | bytes 786440 | tf_op jit(solution)/shard_map/ppermute | solution.py:193
  62.8 12.0 %collective-permute-start.6 = (f32[512,256]{1,0:T(8,128)S(1)}, f32[512,256]{1,0:T(8,128)S(1)}, u32[]{:S(2)}, u32[]{:S(2)}) collective-permute-start(f32[512,256]{1,0:T(8,128)S(1)} %get-tuple-element.35), channel_id=1, source_target_pairs={{0,2},{1,15},{2,4},{3,1},{4,6},{5,3},{6,8},{7,5},{8,10},{9,7},{10,... | collective-permute-start | bytes 1572872 | tf_op jit(solution)/shard_map/ppermute | solution.py:274
  67.9 3.4 %collective-permute-start.1 = (f32[512,128]{1,0:T(8,128)S(1)}, f32[512,128]{1,0:T(8,128)S(1)}, u32[]{:S(2)}, u32[]{:S(2)}) collective-permute-start(f32[512,128]{1,0:T(8,128)S(1)} %get-tuple-element.30.own_ref), channel_id=1, source_target_pairs={{0,1},{1,0},{2,3},{3,2},{4,5},{5,4},{6,7},{7,6},{8,9},{9,8},{10,11... | collective-permute-start | bytes 786440 | tf_op jit(solution)/shard_map/ppermute | solution.py:193
  71.5 10.2 %collective-permute-start.2 = (f32[512,256]{1,0:T(8,128)S(1)}, f32[512,256]{1,0:T(8,128)S(1)}, u32[]{:S(2)}, u32[]{:S(2)}) collective-permute-start(f32[512,256]{1,0:T(8,128)S(1)} %get-tuple-element.33), channel_id=1, source_target_pairs={{0,2},{1,15},{2,4},{3,1},{4,6},{5,3},{6,8},{7,5},{8,10},{9,7},{10,... | collective-permute-start | bytes 1572872 | tf_op jit(solution)/shard_map/ppermute | solution.py:274
  74.8 12.6 %collective-permute-start.7 = (f32[512,256]{1,0:T(8,128)S(1)}, f32[512,256]{1,0:T(8,128)}, u32[]{:S(2)}, u32[]{:S(2)}) collective-permute-start(f32[512,256]{1,0:T(8,128)S(1)} %add.54), channel_id=1, source_target_pairs={{0,2},{1,15},{2,4},{3,1},{4,6},{5,3},{6,8},{7,5},{8,10},{9,7},{10,... | collective-permute-start | bytes 1572872 | tf_op jit(solution)/shard_map/ppermute | solution.py:274
  81.8 11.2 %collective-permute-start.3 = (f32[512,256]{1,0:T(8,128)S(1)}, f32[512,256]{1,0:T(8,128)S(1)}, u32[]{:S(2)}, u32[]{:S(2)}) collective-permute-start(f32[512,256]{1,0:T(8,128)S(1)} %add.50), channel_id=1, source_target_pairs={{0,2},{1,15},{2,4},{3,1},{4,6},{5,3},{6,8},{7,5},{8,10},{9,7},{10,... | collective-permute-start | bytes 1572872 | tf_op jit(solution)/shard_map/ppermute | solution.py:274
  88.6 10.2 %collective-permute-start.8 = (f32[512,256]{1,0:T(8,128)S(1)}, f32[512,256]{1,0:T(8,128)S(1)}, u32[]{:S(2)}, u32[]{:S(2)}) collective-permute-start(f32[512,256]{1,0:T(8,128)S(1)} %add.55), channel_id=1, source_target_pairs={{0,2},{1,15},{2,4},{3,1},{4,6},{5,3},{6,8},{7,5},{8,10},{9,7},{10,... | collective-permute-start | bytes 1572872 | tf_op jit(solution)/shard_map/ppermute | solution.py:274
  93.1 19.2 %collective-permute-start.11 = (f32[512,128]{1,0:T(8,128)S(1)}, f32[512,128]{1,0:T(8,128)S(1)}, u32[]{:S(2)}, u32[]{:S(2)}) collective-permute-start(f32[512,128]{1,0:T(8,128)S(1)} %get-tuple-element.38), channel_id=1, source_target_pairs={{0,3},{1,14},{2,5},{3,0},{4,7},{5,2},{6,9},{7,4},{8,11},{9,6},{10,... | collective-permute-start | bytes 786440 | tf_op jit(solution)/shard_map/ppermute | solution.py:279
  98.9 13.4 %collective-permute-start.10 = (f32[512,128]{1,0:T(8,128)S(1)}, f32[512,128]{1,0:T(8,128)S(1)}, u32[]{:S(2)}, u32[]{:S(2)}) collective-permute-start(f32[512,128]{1,0:T(8,128)S(1)} %get-tuple-element.40), channel_id=1, source_target_pairs={{0,2},{1,15},{2,4},{3,1},{4,6},{5,3},{6,8},{7,5},{8,10},{9,7},{10,... | collective-permute-start | bytes 786440 | tf_op jit(solution)/shard_map/ppermute | solution.py:278
  104.0 8.4 %collective-permute-start.4 = (f32[512,128]{1,0:T(8,128)S(1)}, f32[512,128]{1,0:T(8,128)S(1)}, u32[]{:S(2)}, u32[]{:S(2)}) collective-permute-start(f32[512,128]{1,0:T(8,128)S(1)} %get-tuple-element.37), channel_id=1, source_target_pairs={{0,2},{1,15},{2,4},{3,1},{4,6},{5,3},{6,8},{7,5},{8,10},{9,7},{10,... | collective-permute-start | bytes 786440 | tf_op jit(solution)/shard_map/ppermute | solution.py:278
  105.9 11.7 %collective-permute-start.9 = (f32[512,128]{1,0:T(8,128)S(1)}, f32[512,128]{1,0:T(8,128)S(1)}, u32[]{:S(2)}, u32[]{:S(2)}) collective-permute-start(f32[512,128]{1,0:T(8,128)S(1)} %get-tuple-element.39), channel_id=1, source_target_pairs={{0,3},{1,14},{2,5},{3,0},{4,7},{5,2},{6,9},{7,4},{8,11},{9,6},{10,... | collective-permute-start | bytes 786440 | tf_op jit(solution)/shard_map/ppermute | solution.py:279

commit v7 on v6

--- a/solution.py
+++ b/solution.py
@@ -71,7 +71,7 @@
 
 
 def solve_kernel(
-    reg_ref, core_ref, q_ref, k_ref, v_ref, before_ref, column_ref, one_ref, two_ref,
+    reg_ref, core_ref, q_ref, k_ref, v_ref, before_ref, column_ref, out_ref,
     first, second, last, x_ref, r_ref, p_ref,
 ):
     width = q_ref.shape[1]
@@ -105,41 +105,38 @@
             h_state = h_state + mm(key_t, key)
             g_state = g_state + mm(val_t, key)
         query = q_ref[rows, :].astype(F32).T
-        x_ref[b] = jnp.zeros_like(query)
-        r_ref[b] = query
         p_ref[b] = query
         starts.append(jnp.sum(query * query, axis=0, keepdims=True))
 
-    def step(_, rrs):
+    rrs = starts
+    for step in range(ITERS):
+        begun, last_step = step > 0, step == ITERS - 1
+        splits = [halves(p_ref[b]) for b in range(blocks)]
+        ones = [
+            mm(first[b], jnp.concatenate(splits[b], axis=0)) for b in range(blocks)
+        ]
+        scores = [halves(jnp.where(causal, one[width:], 0.0)) for one in ones]
+        twos = [
+            mm(second[b], jnp.concatenate([*scores[b], splits[b][0]], axis=0))
+            for b in range(blocks)
+        ]
         news = []
-        for group in (range(blocks),):
-            ps = {b: p_ref[b] for b in group}
-            hs = {b: halves(ps[b]) for b in group}
-            one = {
-                b: mm(first[b], jnp.concatenate(hs[b], axis=0)) for b in group
-            }
-            ss = {b: halves(jnp.where(causal, one[b][width:], 0.0)) for b in group}
-            two = {
-                b: mm(second[b], jnp.concatenate([*ss[b], hs[b][0]], axis=0))
-                for b in group
-            }
-            for b in group:
-                p = p_ref[b]
-                w = one[b][:width] + two[b] + lam * p
-                rr = rrs[b]
-                active = rr > 1e-30
-                curve = jnp.sum(p * w, axis=0, keepdims=True)
-                alpha = jnp.where(active, rr / jnp.where(active, curve, 1.0), 0.0)
-                x_ref[b] = x_ref[b] + alpha * p
-                r = r_ref[b] - alpha * w
-                r_ref[b] = r
-                new = jnp.sum(r * r, axis=0, keepdims=True)
-                ratio = jnp.where(active, new / jnp.where(active, rr, 1.0), 0.0)
-                p_ref[b] = r + ratio * p
-                news.append(new)
-        return tuple(news)
-
-    lax.fori_loop(0, ITERS, step, tuple(starts))
+        for b in range(blocks):
+            p, rr = p_ref[b], rrs[b]
+            w = ones[b][:width] + twos[b] + lam * p
+            active = rr > 1e-30
+            curve = jnp.sum(p * w, axis=0, keepdims=True)
+            alpha = jnp.where(active, rr / jnp.where(active, curve, 1.0), 0.0)
+            x_ref[b] = x_ref[b] + alpha * p if begun else alpha * p
+            if last_step:
+                continue
+            r = (r_ref[b] if begun else p) - alpha * w
+            r_ref[b] = r
+            new = jnp.sum(r * r, axis=0, keepdims=True)
+            ratio = jnp.where(active, new / jnp.where(active, rr, 1.0), 0.0)
+            p_ref[b] = r + ratio * p
+            news.append(new)
+        rrs = news
 
     column = column_ref[...]
     rows = []
@@ -158,9 +155,10 @@
     half = blocks // 2
     early_first = core_ref[0] == 0
     for b in range(half):
-        place = pl.ds(b * BLOCK, BLOCK)
-        one_ref[place, :] = jnp.where(early_first, rows[b], rows[b + half])
-        two_ref[place, :] = jnp.where(early_first, rows[b + half], rows[b])
+        one = jnp.where(early_first, rows[b], rows[b + half])
+        two = jnp.where(early_first, rows[b + half], rows[b])
+        out_ref[b * BLOCK : (b + 1) * BLOCK, :] = one
+        out_ref[(b + half) * BLOCK : (b + half + 1) * BLOCK, :] = two
 
 
 def solve(reg, core, queries, keys, values, before, column):
@@ -169,9 +167,9 @@
     vmem = pl.BlockSpec(memory_space=pltpu.VMEM)
     return pl.pallas_call(
         solve_kernel,
-        out_shape=(jax.ShapeDtypeStruct((tokens // 2, width), F32),) * 2,
+        out_shape=jax.ShapeDtypeStruct((tokens, width), F32),
         in_specs=[pl.BlockSpec(memory_space=pltpu.SMEM)] * 2 + [vmem] * 5,
-        out_specs=(vmem, vmem),
+        out_specs=vmem,
         scratch_shapes=[
             pltpu.VMEM((blocks, 2 * BLOCK, 2 * width), BF16),
             pltpu.VMEM((blocks, width, 3 * BLOCK), BF16),
@@ -212,26 +210,33 @@
     )(own, other)
 
 
-def open_kernel(where_ref, own_ref, other_ref, weights_ref, rows_ref, sums_ref):
-    rows = jnp.concatenate([own_ref[...], other_ref[...]], axis=1).astype(BF16)
-    rows_ref[...] = rows
-    sums_ref[...] = mm(rows, weights_ref[where_ref[0]])
-
-
-def opening(where, own, other, weights):
+def open_kernel(
+    starts_ref, own_ref, other_ref, weights_ref, rows_one, rows_two, sums_one, sums_two
+):
+    half = own_ref.shape[0] // 2
+    for piece, (rows_ref, sums_ref) in enumerate(
+        ((rows_one, sums_one), (rows_two, sums_two))
+    ):
+        own = own_ref[piece * half : (piece + 1) * half, :]
+        other = other_ref[(1 - piece) * half : (2 - piece) * half, :]
+        rows = jnp.concatenate([own, other], axis=1).astype(BF16)
+        rows_ref[...] = rows
+        sums_ref[...] = mm(rows, weights_ref[starts_ref[piece]])
+
+
+def opening(starts, own, other, weights):
     tokens, width = own.shape
     vmem = pl.BlockSpec(memory_space=pltpu.VMEM)
+    rows = jax.ShapeDtypeStruct((tokens // 2, 2 * width), BF16)
+    sums = jax.ShapeDtypeStruct((tokens // 2, 2 * width), F32)
     return pl.pallas_call(
         open_kernel,
-        out_shape=(
-            jax.ShapeDtypeStruct((tokens, 2 * width), BF16),
-            jax.ShapeDtypeStruct((tokens, 2 * width), F32),
-        ),
+        out_shape=(rows, rows, sums, sums),
         in_specs=[pl.BlockSpec(memory_space=pltpu.SMEM), vmem, vmem, vmem],
-        out_specs=(vmem, vmem),
-        compiler_params=small(8),
+        out_specs=(vmem,) * 4,
+        compiler_params=small(10),
         name="opening",
-    )(where, own, other, weights)
+    )(starts, own, other, weights)
 
 
 def chip_ahead(away):
@@ -243,18 +248,14 @@
 
 
 def project(normed, weights, core, starts):
-    width = normed[0].shape[1]
+    width = normed.shape[1]
     heads = lax.axis_size("head")
     far = heads // 4
     step = [2 if i % 2 == 0 else heads - 2 for i in range(heads)]
     ring = [(i, (i + step[i]) % heads) for i in range(heads)]
     cross = [(i, ((i + step[i]) % heads) ^ 1) for i in range(heads)]
-    others = [swapped(normed[1]), swapped(normed[0])]
-    rows, flows = [], []
-    for start, own, other in zip(starts, normed, others):
-        both, sums = opening(start, own, other, weights)
-        rows.append(both)
-        flows.append(sums)
+    *rows, one, two = opening(starts, normed, swapped(normed), weights)
+    flows = [one, two]
 
     def part(piece, away):
         columns = lax.dynamic_index_in_dim(
@@ -270,15 +271,14 @@
 
     for away in range(far, 1, -1):
         for piece in (0, 1):
+            flows[piece] = lax.ppermute(flows[piece], "head", ring)
             if away - piece > 1:
-                sent = lax.ppermute(flows[piece], "head", ring)
-                flows[piece] = sent + part(piece, away - piece - 1)
-    same, crossed = [], []
-    for piece in (1, 0):
-        same.append(lax.ppermute(own_columns(flows[piece]), "head", ring))
-        crossed.append(lax.ppermute(other_columns(flows[piece]), "head", cross))
-    first = own_columns(part(0, 0)) + same[1] + crossed[0]
-    second = own_columns(part(1, 0)) + same[0] + crossed[1]
+                flows[piece] = flows[piece] + part(piece, away - piece - 1)
+    crossed = lax.ppermute(other_columns(flows[0]), "head", cross)
+    same = lax.ppermute(own_columns(flows[0]), "head", ring)
+    given = swapped(other_columns(flows[1]))
+    first = own_columns(part(0, 0)) + same + given
+    second = own_columns(part(1, 0) + flows[1]) + crossed
     first, second = first.astype(BF16), second.astype(BF16)
     return jnp.where(
         core == 1,
@@ -298,7 +298,7 @@
     weights = join_weight(out_weight, swapped(out_weight.astype(F32)))
     far = lax.axis_size("head") // 4
     core = lax.rem(lax.axis_index("head").astype(jnp.uint32), jnp.uint32(2))
-    starts = [chip_ahead(away).astype(jnp.int32).reshape(1) for away in (far, far - 1)]
+    starts = jnp.stack([chip_ahead(far), chip_ahead(far - 1)]).astype(jnp.int32)
     core = core.astype(jnp.int32)
     parts, weights, core, starts = lax.optimization_barrier(
         (parts, weights, core, starts)

time: 119 us -> 117 us (0.983)
  Pallas kernels: 18.1 us -> 14.9 us
    ppermute x9 -> x8, starting transfers between devices: 37.9 us -> 33.9 us  [the longest x6 27.5 us: project(): flows[piece] = lax.ppermute(flows[piece], 'head', ring)]
    ppermute x3, starting transfers between devices: 15.2 us -> 19.2 us  [swapped(): return lax.ppermute(value, 'head', [(i, i ^ 1) for i in range(heads)])]
    pallas_call x3 -> x2, Pallas kernels: 15.2 us -> 12 us  [the longest x1 11.2 us: solve(): pl.pallas_call(solve_kernel, out_shape=jax.ShapeDtypeStruct((tokens, widt...]
    ppermute x9 -> x8, waiting for transfers between devices: 9.98 us -> 10.7 us  [the longest x6 5.58 us: project(): flows[piece] = lax.ppermute(flows[piece], 'head', ring)]
  transfers between devices with their start and end apart: 14 -> 13, of which waited for: 8 -> 8; matrix products, arithmetic and copies ran while one was open for 3% -> 4% of each run, Pallas kernels for 0% -> 0%
where the time goes in v7:
time: 117 us; the launch traced here: 116 us
  starting transfers between devices  65.2 us (56%)
  waiting for transfers between devices  29.7 us (25%)
  Pallas kernels  14.9 us (13%)
  other arithmetic  3.56 us (3%)
  matrix products  1.59 us (1%)
    ppermute x6, starting transfers between devices, project(): flows[piece] = lax.ppermute(flows[piece], 'head', ring)  27.5 us
    ppermute x3, starting transfers between devices, swapped(): return lax.ppermute(value, 'head', [(i, i ^ 1) for i in range(heads)])  19.2 us
    pallas_call x1, Pallas kernels, solve(): pl.pallas_call(solve_kernel, out_shape=jax.ShapeDtypeStruct((tokens, widt...  11.2 us
    all_to_all x1, waiting for transfers between devices, body(): parts = lax.all_to_all(state.reshape(devices, rows, width), 'seq', 0, 0)  8.93 us
    all_to_all x1, waiting for transfers between devices, body(): before = lax.all_to_all(exclusive(parts), 'seq', 0, 0)  8.54 us
    all_to_all x1, starting transfers between devices, body(): parts = lax.all_to_all(state.reshape(devices, rows, width), 'seq', 0, 0)  7.52 us
    ppermute x6, waiting for transfers between devices, project(): flows[piece] = lax.ppermute(flows[piece], 'head', ring)  5.58 us
    ppermute x1, waiting for transfers between devices, project(): same = lax.ppermute(own_columns(flows[0]), 'head', ring)  5.16 us
  transfers between devices with their start and end apart: 13, of which 8 were waited for; matrix products, arithmetic and copies ran while one was open for 4% of the time, Pallas kernels for 0%

profile of v7, /device:TPU:1, one launch (start us, length us, event | category | flops | bytes accessed | tf_op | source)
XLA Modules:
  0.0 115.9 jit_solution(7020528163287854366)
XLA Ops:
  0.0 2.1 %local_state.1 = (f32[256,128]{1,0:T(8,128)}, bf16[1024,128]{1,0:T(8,128)(2,1)}, f32[128,128]{1,0:T(8,128)}) custom-call(bf16[1024,128]{1,0:T(8,128)(2,1)} %bitcast.37, bf16[1024,128]{1,0:T(8,128)(2,1)} %bitcast.33, f32[1,128]{1,0:T(1,128)} %gain_ref.1, f32[1,128]{1,0:T(1,128)} %norm_ref.1), custom_call_target="tpu_custom_call" | custom-call | tf_op jit(solution)/shard_map/local_state/pallas_call | solution.py:45
  2.2 8.8 %collective-permute-start = (f32[128,2048]{1,0:T(8,128)S(1)}, f32[128,2048]{1,0:T(8,128)S(1)}, u32[]{:S(2)}, u32[]{:S(2)}) collective-permute-start(f32[128,2048]{1,0:T(8,128)S(1)} %convert_element_type.12), channel_id=1, source_target_pairs={{0,1},{1,0},{2,3},{3,2},{4,5},{5,4},{6,7},{7,6},{8,9},{9,8},{10,11... | collective-permute-start | bytes 3145736 | tf_op jit(solution)/shard_map/ppermute | solution.py:191
  11.0 7.5 %all-to-all-start = ((f32[32,8,128]{2,1,0:T(8,128)}), f32[32,8,128]{2,1,0:T(8,128)S(1)}, u32[]{:S(2)}, u32[]{:S(2)}) async-start(f32[32,8,128]{2,1,0:T(8,128)} %bitcast.2), calls=%async_computation | async-start | bytes 262144 | tf_op jit(solution)/shard_map/all_to_all | solution.py:297
  18.8 8.9 %all-to-all-done.x_ref = f32[32,8,128]{2,1,0:T(8,128)S(1)} async-done(((f32[32,8,128]{2,1,0:T(8,128)}), f32[32,8,128]{2,1,0:T(8,128)S(1)}, u32[]{:S(2)}, u32[]{:S(2)}) %all-to-all-start) | async-done | bytes 131104 | tf_op jit(solution)/shard_map/all_to_all | solution.py:297
  28.4 4.5 %all-to-all-start.1 = ((f32[32,8,128]{2,1,0:T(8,128)}), f32[32,8,128]{2,1,0:T(8,128)S(1)}, u32[]{:S(2)}, u32[]{:S(2)}) async-start(f32[32,8,128]{2,1,0:T(8,128)} %prefix.1), calls=%async_computation.1 | async-start | bytes 262144 | tf_op jit(solution)/shard_map/all_to_all | solution.py:306
  33.6 8.5 %all-to-all-done.1 = f32[32,8,128]{2,1,0:T(8,128)S(1)} async-done(((f32[32,8,128]{2,1,0:T(8,128)}), f32[32,8,128]{2,1,0:T(8,128)S(1)}, u32[]{:S(2)}, u32[]{:S(2)}) %all-to-all-start.1) | async-done | bytes 131104 | tf_op jit(solution)/shard_map/all_to_all | solution.py:306
  42.1 11.2 %solve.1.own_ref = f32[1024,128]{1,0:T(8,128)S(1)} custom-call(f32[1]{0:T(128)S(6)} %copy.8.reg_ref, s32[1]{0:T(128)} %bitcast.5.core_ref, bf16[1024,128]{1,0:T(8,128)(2,1)S(1)} %bitcast.36, bf16[1024,128]{1,0:T(8,128)(2,1)S(1)} %copy-done.3, bf16[1024,128]{1,0:T(8,128)(2,1)S(1)} %bitcast.34, f32[256,128]{1,0:T(8,128)S(1)} %bitcast.35, f32[128,128]{1,0:T(8,128)S(1)} %copy-done.4), custom_call_target="tpu_custom_call" | custom-call | flops 60000002048 | bytes 2097152 | tf_op jit(solution)/shard_map/solve/pallas_call | solution.py:168
  53.3 4.5 %collective-permute-start.1 = (f32[1024,128]{1,0:T(8,128)S(1)}, f32[1024,128]{1,0:T(8,128)S(1)}, u32[]{:S(2)}, u32[]{:S(2)}) collective-permute-start(f32[1024,128]{1,0:T(8,128)S(1)} %solve.1.own_ref), channel_id=1, source_target_pairs={{0,1},{1,0},{2,3},{3,2},{4,5},{5,4},{6,7},{7,6},{8,9},{9,8},{10,11... | collective-permute-start | bytes 1572872 | tf_op jit(solution)/shard_map/ppermute | solution.py:191
  57.8 1.5 %collective-permute-done.1.other_ref = f32[1024,128]{1,0:T(8,128)S(1)} collective-permute-done((f32[1024,128]{1,0:T(8,128)S(1)}, f32[1024,128]{1,0:T(8,128)S(1)}, u32[]{:S(2)}, u32[]{:S(2)}) %collective-permute-start.1) | collective-permute-done | bytes 524320 | tf_op jit(solution)/shard_map/ppermute | solution.py:191
  60.2 5.1 %collective-permute-start.5 = (f32[512,256]{1,0:T(8,128)S(1)}, f32[512,256]{1,0:T(8,128)S(1)}, u32[]{:S(2)}, u32[]{:S(2)}) collective-permute-start(f32[512,256]{1,0:T(8,128)S(1)} %get-tuple-element.29), channel_id=1, source_target_pairs={{0,2},{1,15},{2,4},{3,1},{4,6},{5,3},{6,8},{7,5},{8,10},{9,7},{10,... | collective-permute-start | bytes 1572872 | tf_op jit(solution)/shard_map/ppermute | solution.py:274
  65.3 3.0 %collective-permute-start.2 = (f32[512,256]{1,0:T(8,128)S(1)}, f32[512,256]{1,0:T(8,128)}, u32[]{:S(2)}, u32[]{:S(2)}) collective-permute-start(f32[512,256]{1,0:T(8,128)S(1)} %get-tuple-element.28), channel_id=1, source_target_pairs={{0,2},{1,15},{2,4},{3,1},{4,6},{5,3},{6,8},{7,5},{8,10},{9,7},{10,... | collective-permute-start | bytes 1572872 | tf_op jit(solution)/shard_map/ppermute | solution.py:274
  68.5 2.9 %collective-permute-done.5 = f32[512,256]{1,0:T(8,128)S(1)} collective-permute-done((f32[512,256]{1,0:T(8,128)S(1)}, f32[512,256]{1,0:T(8,128)S(1)}, u32[]{:S(2)}, u32[]{:S(2)}) %collective-permute-start.5) | collective-permute-done | bytes 524320 | tf_op jit(solution)/shard_map/ppermute | solution.py:274
  71.5 5.0 %collective-permute-start.6 = (f32[512,256]{1,0:T(8,128)S(1)}, f32[512,256]{1,0:T(8,128)S(1)}, u32[]{:S(2)}, u32[]{:S(2)}) collective-permute-start(f32[512,256]{1,0:T(8,128)S(1)} %add.54), channel_id=1, source_target_pairs={{0,2},{1,15},{2,4},{3,1},{4,6},{5,3},{6,8},{7,5},{8,10},{9,7},{10,... | collective-permute-start | bytes 1572872 | tf_op jit(solution)/shard_map/ppermute | solution.py:274
  77.0 1.1 add.50
  78.1 5.1 %collective-permute-start.3 = (f32[512,256]{1,0:T(8,128)S(1)}, f32[512,256]{1,0:T(8,128)}, u32[]{:S(2)}, u32[]{:S(2)}) collective-permute-start(f32[512,256]{1,0:T(8,128)S(1)} %add.50), channel_id=1, source_target_pairs={{0,2},{1,15},{2,4},{3,1},{4,6},{5,3},{6,8},{7,5},{8,10},{9,7},{10,... | collective-permute-start | bytes 1572872 | tf_op jit(solution)/shard_map/ppermute | solution.py:274
  83.6 4.1 %collective-permute-start.7 = (f32[512,256]{1,0:T(8,128)S(1)}, f32[512,256]{1,0:T(8,128)S(1)}, u32[]{:S(2)}, u32[]{:S(2)}) collective-permute-start(f32[512,256]{1,0:T(8,128)S(1)} %add.55), channel_id=1, source_target_pairs={{0,2},{1,15},{2,4},{3,1},{4,6},{5,3},{6,8},{7,5},{8,10},{9,7},{10,... | collective-permute-start | bytes 1572872 | tf_op jit(solution)/shard_map/ppermute | solution.py:274
  88.0 1.4 %collective-permute-done.3 = f32[512,256]{1,0:T(8,128)} collective-permute-done((f32[512,256]{1,0:T(8,128)S(1)}, f32[512,256]{1,0:T(8,128)}, u32[]{:S(2)}, u32[]{:S(2)}) %collective-permute-start.3) | collective-permute-done | bytes 524320 | tf_op jit(solution)/shard_map/ppermute | solution.py:274
  89.4 1.1 add.52
  90.5 5.1 %collective-permute-start.4 = (f32[512,256]{1,0:T(8,128)S(1)}, f32[512,256]{1,0:T(8,128)S(1)}, u32[]{:S(2)}, u32[]{:S(2)}) collective-permute-start(f32[512,256]{1,0:T(8,128)S(1)} %add.52), channel_id=1, source_target_pairs={{0,2},{1,15},{2,4},{3,1},{4,6},{5,3},{6,8},{7,5},{8,10},{9,7},{10,... | collective-permute-start | bytes 1572872 | tf_op jit(solution)/shard_map/ppermute | solution.py:274
  96.2 4.5 %collective-permute-start.8 = (f32[512,128]{1,0:T(8,128)S(1)}, f32[512,128]{1,0:T(8,128)S(1)}, u32[]{:S(2)}, u32[]{:S(2)}) collective-permute-start(f32[512,128]{1,0:T(8,128)S(1)} %get-tuple-element.31), channel_id=1, source_target_pairs={{0,3},{1,14},{2,5},{3,0},{4,7},{5,2},{6,9},{7,4},{8,11},{9,6},{10,... | collective-permute-start | bytes 786440 | tf_op jit(solution)/shard_map/ppermute | solution.py:277
  100.7 1.0 collective-permute-done.4
  101.8 5.9 %collective-permute-start.10 = (f32[512,128]{1,0:T(8,128)S(1)}, f32[512,128]{1,0:T(8,128)S(1)}, u32[]{:S(2)}, u32[]{:S(2)}) collective-permute-start(f32[512,128]{1,0:T(8,128)S(1)} %slice_select_fusion), channel_id=1, source_target_pairs={{0,1},{1,0},{2,3},{3,2},{4,5},{5,4},{6,7},{7,6},{8,9},{9,8},{10,11... | collective-permute-start | bytes 786440 | tf_op jit(solution)/shard_map/ppermute | solution.py:191
  107.7 1.9 %collective-permute-start.9 = (f32[512,128]{1,0:T(8,128)S(1)}, f32[512,128]{1,0:T(8,128)S(1)}, u32[]{:S(2)}, u32[]{:S(2)}) collective-permute-start(f32[512,128]{1,0:T(8,128)S(1)} %get-tuple-element.32), channel_id=1, source_target_pairs={{0,2},{1,15},{2,4},{3,1},{4,6},{5,3},{6,8},{7,5},{8,10},{9,7},{10,... | collective-permute-start | bytes 786440 | tf_op jit(solution)/shard_map/ppermute | solution.py:278
  109.9 5.2 %collective-permute-done.9 = f32[512,128]{1,0:T(8,128)S(1)} collective-permute-done((f32[512,128]{1,0:T(8,128)S(1)}, f32[512,128]{1,0:T(8,128)S(1)}, u32[]{:S(2)}, u32[]{:S(2)}) %collective-permute-start.9) | collective-permute-done | bytes 262176 | tf_op jit(solution)/shard_map/ppermute | solution.py:278
  (36 shorter events, 4.9 us)
Async XLA Ops:
  0.0 2.1 %copy-start = (bf16[128,2048]{1,0:T(8,128)(2,1)S(1)}, bf16[128,2048]{1,0:T(8,128)(2,1)}, u32[]{:S(2)}) copy-start(bf16[128,2048]{1,0:T(8,128)(2,1)} %own_ref) | copy-start | bytes 1572868
  2.2 16.4 %collective-permute-start = (f32[128,2048]{1,0:T(8,128)S(1)}, f32[128,2048]{1,0:T(8,128)S(1)}, u32[]{:S(2)}, u32[]{:S(2)}) collective-permute-start(f32[128,2048]{1,0:T(8,128)S(1)} %convert_element_type.12), channel_id=1, source_target_pairs={{0,1},{1,0},{2,3},{3,2},{4,5},{5,4},{6,7},{7,6},{8,9},{9,8},{10,11... | collective-permute-start | bytes 3145736 | tf_op jit(solution)/shard_map/ppermute | solution.py:191
  11.0 16.7 %all-to-all-start = ((f32[32,8,128]{2,1,0:T(8,128)}), f32[32,8,128]{2,1,0:T(8,128)S(1)}, u32[]{:S(2)}, u32[]{:S(2)}) async-start(f32[32,8,128]{2,1,0:T(8,128)} %bitcast.2), calls=%async_computation | async-start | bytes 262144 | tf_op jit(solution)/shard_map/all_to_all | solution.py:297
  18.6 23.5 %copy-start.3 = (bf16[1024,128]{1,0:T(8,128)(2,1)S(1)}, bf16[1024,128]{1,0:T(8,128)(2,1)}, u32[]{:S(2)}) copy-start(bf16[1024,128]{1,0:T(8,128)(2,1)} %get-tuple-element.23.k_ref) | copy-start | bytes 786436
  18.6 23.5 %copy-start.4 = (f32[128,128]{1,0:T(8,128)S(1)}, f32[128,128]{1,0:T(8,128)}, u32[]{:S(2)}) copy-start(f32[128,128]{1,0:T(8,128)} %get-tuple-element.25.column_ref) | copy-start | bytes 196612
  18.7 23.4 %copy-start.1 = (bf16[1024,1,128]{2,0,1:T(8,128)(2,1)S(1)}, bf16[1024,1,128]{2,0,1:T(8,128)(2,1)}, u32[]{:S(2)}) copy-start(bf16[1024,1,128]{2,0,1:T(8,128)(2,1)} %param.9) | copy-start | bytes 786436
  18.7 23.4 %copy-start.2 = (bf16[1024,1,128]{2,0,1:T(8,128)(2,1)S(1)}, bf16[1024,1,128]{2,0,1:T(8,128)(2,1)}, u32[]{:S(2)}) copy-start(bf16[1024,1,128]{2,0,1:T(8,128)(2,1)} %param.7) | copy-start | bytes 786436
  28.4 13.7 %all-to-all-start.1 = ((f32[32,8,128]{2,1,0:T(8,128)}), f32[32,8,128]{2,1,0:T(8,128)S(1)}, u32[]{:S(2)}, u32[]{:S(2)}) async-start(f32[32,8,128]{2,1,0:T(8,128)} %prefix.1), calls=%async_computation.1 | async-start | bytes 262144 | tf_op jit(solution)/shard_map/all_to_all | solution.py:306
  53.3 6.0 %collective-permute-start.1 = (f32[1024,128]{1,0:T(8,128)S(1)}, f32[1024,128]{1,0:T(8,128)S(1)}, u32[]{:S(2)}, u32[]{:S(2)}) collective-permute-start(f32[1024,128]{1,0:T(8,128)S(1)} %solve.1.own_ref), channel_id=1, source_target_pairs={{0,1},{1,0},{2,3},{3,2},{4,5},{5,4},{6,7},{7,6},{8,9},{9,8},{10,11... | collective-permute-start | bytes 1572872 | tf_op jit(solution)/shard_map/ppermute | solution.py:191
  60.2 11.2 %collective-permute-start.5 = (f32[512,256]{1,0:T(8,128)S(1)}, f32[512,256]{1,0:T(8,128)S(1)}, u32[]{:S(2)}, u32[]{:S(2)}) collective-permute-start(f32[512,256]{1,0:T(8,128)S(1)} %get-tuple-element.29), channel_id=1, source_target_pairs={{0,2},{1,15},{2,4},{3,1},{4,6},{5,3},{6,8},{7,5},{8,10},{9,7},{10,... | collective-permute-start | bytes 1572872 | tf_op jit(solution)/shard_map/ppermute | solution.py:274
  65.3 11.7 %collective-permute-start.2 = (f32[512,256]{1,0:T(8,128)S(1)}, f32[512,256]{1,0:T(8,128)}, u32[]{:S(2)}, u32[]{:S(2)}) collective-permute-start(f32[512,256]{1,0:T(8,128)S(1)} %get-tuple-element.28), channel_id=1, source_target_pairs={{0,2},{1,15},{2,4},{3,1},{4,6},{5,3},{6,8},{7,5},{8,10},{9,7},{10,... | collective-permute-start | bytes 1572872 | tf_op jit(solution)/shard_map/ppermute | solution.py:274
  71.5 12.0 %collective-permute-start.6 = (f32[512,256]{1,0:T(8,128)S(1)}, f32[512,256]{1,0:T(8,128)S(1)}, u32[]{:S(2)}, u32[]{:S(2)}) collective-permute-start(f32[512,256]{1,0:T(8,128)S(1)} %add.54), channel_id=1, source_target_pairs={{0,2},{1,15},{2,4},{3,1},{4,6},{5,3},{6,8},{7,5},{8,10},{9,7},{10,... | collective-permute-start | bytes 1572872 | tf_op jit(solution)/shard_map/ppermute | solution.py:274
  78.1 11.2 %collective-permute-start.3 = (f32[512,256]{1,0:T(8,128)S(1)}, f32[512,256]{1,0:T(8,128)}, u32[]{:S(2)}, u32[]{:S(2)}) collective-permute-start(f32[512,256]{1,0:T(8,128)S(1)} %add.50), channel_id=1, source_target_pairs={{0,2},{1,15},{2,4},{3,1},{4,6},{5,3},{6,8},{7,5},{8,10},{9,7},{10,... | collective-permute-start | bytes 1572872 | tf_op jit(solution)/shard_map/ppermute | solution.py:274
  83.6 12.5 %collective-permute-start.7 = (f32[512,256]{1,0:T(8,128)S(1)}, f32[512,256]{1,0:T(8,128)S(1)}, u32[]{:S(2)}, u32[]{:S(2)}) collective-permute-start(f32[512,256]{1,0:T(8,128)S(1)} %add.55), channel_id=1, source_target_pairs={{0,2},{1,15},{2,4},{3,1},{4,6},{5,3},{6,8},{7,5},{8,10},{9,7},{10,... | collective-permute-start | bytes 1572872 | tf_op jit(solution)/shard_map/ppermute | solution.py:274
  90.5 11.2 %collective-permute-start.4 = (f32[512,256]{1,0:T(8,128)S(1)}, f32[512,256]{1,0:T(8,128)S(1)}, u32[]{:S(2)}, u32[]{:S(2)}) collective-permute-start(f32[512,256]{1,0:T(8,128)S(1)} %add.52), channel_id=1, source_target_pairs={{0,2},{1,15},{2,4},{3,1},{4,6},{5,3},{6,8},{7,5},{8,10},{9,7},{10,... | collective-permute-start | bytes 1572872 | tf_op jit(solution)/shard_map/ppermute | solution.py:274
  96.2 13.6 %collective-permute-start.8 = (f32[512,128]{1,0:T(8,128)S(1)}, f32[512,128]{1,0:T(8,128)S(1)}, u32[]{:S(2)}, u32[]{:S(2)}) collective-permute-start(f32[512,128]{1,0:T(8,128)S(1)} %get-tuple-element.31), channel_id=1, source_target_pairs={{0,3},{1,14},{2,5},{3,0},{4,7},{5,2},{6,9},{7,4},{8,11},{9,6},{10,... | collective-permute-start | bytes 786440 | tf_op jit(solution)/shard_map/ppermute | solution.py:277
  101.8 8.2 %collective-permute-start.10 = (f32[512,128]{1,0:T(8,128)S(1)}, f32[512,128]{1,0:T(8,128)S(1)}, u32[]{:S(2)}, u32[]{:S(2)}) collective-permute-start(f32[512,128]{1,0:T(8,128)S(1)} %slice_select_fusion), channel_id=1, source_target_pairs={{0,1},{1,0},{2,3},{3,2},{4,5},{5,4},{6,7},{7,6},{8,9},{9,8},{10,11... | collective-permute-start | bytes 786440 | tf_op jit(solution)/shard_map/ppermute | solution.py:191
  107.7 7.4 %collective-permute-start.9 = (f32[512,128]{1,0:T(8,128)S(1)}, f32[512,128]{1,0:T(8,128)S(1)}, u32[]{:S(2)}, u32[]{:S(2)}) collective-permute-start(f32[512,128]{1,0:T(8,128)S(1)} %get-tuple-element.32), channel_id=1, source_target_pairs={{0,2},{1,15},{2,4},{3,1},{4,6},{5,3},{6,8},{7,5},{8,10},{9,7},{10,... | collective-permute-start | bytes 786440 | tf_op jit(solution)/shard_map/ppermute | solution.py:278

commit v8 on v7

--- a/solution.py
+++ b/solution.py
@@ -71,7 +71,7 @@
 
 
 def solve_kernel(
-    reg_ref, core_ref, q_ref, k_ref, v_ref, before_ref, column_ref, out_ref,
+    reg_ref, q_ref, k_ref, v_ref, before_ref, column_ref, out_ref,
     first, second, last, x_ref, r_ref, p_ref,
 ):
     width = q_ref.shape[1]
@@ -139,7 +139,6 @@
         rrs = news
 
     column = column_ref[...]
-    rows = []
     for b in range(blocks):
         x_high, x_low = halves(x_ref[b])
         key = first[b, width:, :]
@@ -151,24 +150,17 @@
         ) + mm(last[b, :, 3 * BLOCK :], x_low)
         square = jnp.mean(read * read, axis=0, keepdims=True)
         normed = read * column * lax.rsqrt(square + 1e-06)
-        rows.append(normed.T.astype(BF16).astype(F32))
-    half = blocks // 2
-    early_first = core_ref[0] == 0
-    for b in range(half):
-        one = jnp.where(early_first, rows[b], rows[b + half])
-        two = jnp.where(early_first, rows[b + half], rows[b])
-        out_ref[b * BLOCK : (b + 1) * BLOCK, :] = one
-        out_ref[(b + half) * BLOCK : (b + half + 1) * BLOCK, :] = two
-
-
-def solve(reg, core, queries, keys, values, before, column):
+        out_ref[b * BLOCK : (b + 1) * BLOCK, :] = normed.T.astype(BF16).astype(F32)
+
+
+def solve(reg, queries, keys, values, before, column):
     tokens, width = queries.shape
     blocks = tokens // BLOCK
     vmem = pl.BlockSpec(memory_space=pltpu.VMEM)
     return pl.pallas_call(
         solve_kernel,
         out_shape=jax.ShapeDtypeStruct((tokens, width), F32),
-        in_specs=[pl.BlockSpec(memory_space=pltpu.SMEM)] * 2 + [vmem] * 5,
+        in_specs=[pl.BlockSpec(memory_space=pltpu.SMEM)] + [vmem] * 5,
         out_specs=vmem,
         scratch_shapes=[
             pltpu.VMEM((blocks, 2 * BLOCK, 2 * width), BF16),
@@ -183,7 +175,7 @@
         ),
         compiler_params=pltpu.CompilerParams(vmem_limit_bytes=20 * 2**20),
         name="solve",
-    )(reg, core, queries, keys, values, before, column)
+    )(reg, queries, keys, values, before, column)
 
 
 def swapped(value):
@@ -191,100 +183,89 @@
     return lax.ppermute(value, "head", [(i, i ^ 1) for i in range(heads)])
 
 
-def join_weight_kernel(own_ref, other_ref, out_ref):
-    chips, double, columns = out_ref.shape
+def join_weight_kernel(core_ref, own_ref, other_ref, out_ref):
+    chips, double, width = out_ref.shape
     half = double // 2
+    first = core_ref[0] == 0
     for chip in range(chips):
-        here = slice(chip * columns, (chip + 1) * columns)
-        out_ref[chip, 0:half, :] = own_ref[:, here]
-        out_ref[chip, half:, :] = other_ref[:, here].astype(BF16)
-
-
-def join_weight(own, other):
+        zero = slice(2 * chip * width, (2 * chip + 1) * width)
+        one = slice((2 * chip + 1) * width, (2 * chip + 2) * width)
+        out_ref[chip, 0:half, :] = jnp.where(first, own_ref[:, zero], own_ref[:, one])
+        out_ref[chip, half:, :] = jnp.where(
+            first, other_ref[:, zero], other_ref[:, one]
+        ).astype(BF16)
+
+
+def join_weight(core, own, other):
     width, columns = own.shape
+    vmem = pl.BlockSpec(memory_space=pltpu.VMEM)
     return pl.pallas_call(
         join_weight_kernel,
-        out_shape=jax.ShapeDtypeStruct((columns // (2 * width), 2 * width, 2 * width), BF16),
+        out_shape=jax.ShapeDtypeStruct((columns // (2 * width), 2 * width, width), BF16),
+        in_specs=[pl.BlockSpec(memory_space=pltpu.SMEM), vmem, vmem],
+        out_specs=vmem,
         compiler_params=small(8),
         name="join_weight",
-    )(own, other)
-
-
-def open_kernel(
-    starts_ref, own_ref, other_ref, weights_ref, rows_one, rows_two, sums_one, sums_two
-):
+    )(core, own, other)
+
+
+def open_kernel(far_ref, own_ref, other_ref, weights_ref, rows_ref, right_ref, left_ref):
     half = own_ref.shape[0] // 2
-    for piece, (rows_ref, sums_ref) in enumerate(
-        ((rows_one, sums_one), (rows_two, sums_two))
-    ):
-        own = own_ref[piece * half : (piece + 1) * half, :]
-        other = other_ref[(1 - piece) * half : (2 - piece) * half, :]
-        rows = jnp.concatenate([own, other], axis=1).astype(BF16)
-        rows_ref[...] = rows
-        sums_ref[...] = mm(rows, weights_ref[starts_ref[piece]])
-
-
-def opening(starts, own, other, weights):
+    rows = jnp.concatenate([own_ref[...], other_ref[...]], axis=1).astype(BF16)
+    rows_ref[...] = rows
+    weight = weights_ref[far_ref[0]]
+    right_ref[...] = mm(rows[:half], weight)
+    left_ref[...] = mm(rows[half:], weight)
+
+
+def opening(far, own, other, weights):
     tokens, width = own.shape
     vmem = pl.BlockSpec(memory_space=pltpu.VMEM)
-    rows = jax.ShapeDtypeStruct((tokens // 2, 2 * width), BF16)
-    sums = jax.ShapeDtypeStruct((tokens // 2, 2 * width), F32)
+    sums = jax.ShapeDtypeStruct((tokens // 2, width), F32)
     return pl.pallas_call(
         open_kernel,
-        out_shape=(rows, rows, sums, sums),
+        out_shape=(jax.ShapeDtypeStruct((tokens, 2 * width), BF16), sums, sums),
         in_specs=[pl.BlockSpec(memory_space=pltpu.SMEM), vmem, vmem, vmem],
-        out_specs=(vmem,) * 4,
+        out_specs=(vmem,) * 3,
         compiler_params=small(10),
         name="opening",
-    )(starts, own, other, weights)
+    )(far, own, other, weights)
+
+
+def position():
+    place = lax.axis_index("head").astype(jnp.uint32)
+    return lax.div(place, jnp.uint32(2)), lax.rem(place, jnp.uint32(2))
 
 
 def chip_ahead(away):
     chips = lax.axis_size("head") // 2
-    place = lax.axis_index("head").astype(jnp.uint32)
-    chip, core = lax.div(place, jnp.uint32(2)), lax.rem(place, jnp.uint32(2))
-    ahead = jnp.where(core == 1, jnp.uint32(chips - away), jnp.uint32(away % chips))
-    return lax.rem(chip + ahead, jnp.uint32(chips))
-
-
-def project(normed, weights, core, starts):
-    width = normed.shape[1]
+    chip, _ = position()
+    return lax.rem(chip + jnp.uint32(away % chips), jnp.uint32(chips))
+
+
+def project(normed, weights, far):
     heads = lax.axis_size("head")
-    far = heads // 4
-    step = [2 if i % 2 == 0 else heads - 2 for i in range(heads)]
-    ring = [(i, (i + step[i]) % heads) for i in range(heads)]
-    cross = [(i, ((i + step[i]) % heads) ^ 1) for i in range(heads)]
-    *rows, one, two = opening(starts, normed, swapped(normed), weights)
-    flows = [one, two]
-
-    def part(piece, away):
+    half = normed.shape[0] // 2
+    right = [(i, (i + 2) % heads) for i in range(heads)]
+    left = [(i, (i - 2) % heads) for i in range(heads)]
+    rows, ahead, behind = opening(far, normed, swapped(normed), weights)
+    ahead = lax.ppermute(ahead, "head", right)
+    behind = lax.ppermute(behind, "head", left)
+
+    def part(away):
         columns = lax.dynamic_index_in_dim(
             weights, chip_ahead(away), axis=0, keepdims=False
         )
-        return jnp.dot(rows[piece], columns, preferred_element_type=F32)
-
-    def own_columns(value):
-        return jnp.where(core == 1, value[:, width:], value[:, :width])
-
-    def other_columns(value):
-        return jnp.where(core == 1, value[:, :width], value[:, width:])
-
-    for away in range(far, 1, -1):
-        for piece in (0, 1):
-            flows[piece] = lax.ppermute(flows[piece], "head", ring)
-            if away - piece > 1:
-                flows[piece] = flows[piece] + part(piece, away - piece - 1)
-    crossed = lax.ppermute(other_columns(flows[0]), "head", cross)
-    same = lax.ppermute(own_columns(flows[0]), "head", ring)
-    given = swapped(other_columns(flows[1]))
-    first = own_columns(part(0, 0)) + same + given
-    second = own_columns(part(1, 0) + flows[1]) + crossed
-    first, second = first.astype(BF16), second.astype(BF16)
-    return jnp.where(
-        core == 1,
-        jnp.concatenate([second, first], axis=0),
-        jnp.concatenate([first, second], axis=0),
-    )
+        return jnp.dot(rows, columns, preferred_element_type=F32)
+
+    for away in range(heads // 4 - 1, 0, -1):
+        to_right, to_left = part(away), part(-away)
+        if ahead.shape[0] == half:
+            ahead = jnp.pad(ahead, ((0, half), (0, 0)))
+            behind = jnp.pad(behind, ((half, 0), (0, 0)))
+        ahead = lax.ppermute(to_right + ahead, "head", right)
+        behind = lax.ppermute(to_left + behind, "head", left)
+    return (part(0) + ahead + behind).astype(BF16)
 
 
 def body(queries, keys, values, key_gain, reg, norm_gain, out_weight):
@@ -295,20 +276,15 @@
     rows = 2 * width // devices
     state, out_weight = lax.optimization_barrier((state, out_weight))
     parts = lax.all_to_all(state.reshape(devices, rows, width), "seq", 0, 0)
-    weights = join_weight(out_weight, swapped(out_weight.astype(F32)))
-    far = lax.axis_size("head") // 4
-    core = lax.rem(lax.axis_index("head").astype(jnp.uint32), jnp.uint32(2))
-    starts = jnp.stack([chip_ahead(far), chip_ahead(far - 1)]).astype(jnp.int32)
-    core = core.astype(jnp.int32)
-    parts, weights, core, starts = lax.optimization_barrier(
-        (parts, weights, core, starts)
-    )
+    _, core = position()
+    core = core.astype(jnp.int32).reshape(1)
+    weights = join_weight(core, out_weight, swapped(out_weight.astype(F32)))
+    far = chip_ahead(lax.axis_size("head") // 4).astype(jnp.int32).reshape(1)
+    parts, weights, far = lax.optimization_barrier((parts, weights, far))
     before = lax.all_to_all(exclusive(parts), "seq", 0, 0)
     before = before.reshape(2 * width, width)
-    normed = solve(
-        reg, core.reshape(1), query_rows, gained, value_rows, before, column
-    )
-    return project(normed, weights, core, starts)
+    normed = solve(reg, query_rows, gained, value_rows, before, column)
+    return project(normed, weights, far)
 
 
 def solution(mesh):

time: 117 us -> 123 us (1.051)
  the two profiles are of different devices: /device:TPU:1 before, /device:TPU:24 now
where the time goes in v8:
time: 123 us
  waiting for transfers between devices  54.4 us (44%)
  starting transfers between devices  50 us (41%)
  Pallas kernels  14.4 us (12%)
  matrix products  2.77 us (2%)
    ppermute x3, waiting for transfers between devices, project(): ahead = lax.ppermute(to_right + ahead, 'head', right)  22.5 us
    ppermute x3, starting transfers between devices, project(): ahead = lax.ppermute(to_right + ahead, 'head', right)  16.8 us
    all_to_all x1, starting transfers between devices, body(): parts = lax.all_to_all(state.reshape(devices, rows, width), 'seq', 0, 0)  13.2 us
    pallas_call x1, Pallas kernels, solve(): pl.pallas_call(solve_kernel, out_shape=jax.ShapeDtypeStruct((tokens, widt...  11.2 us
    all_to_all x1, waiting for transfers between devices, body(): parts = lax.all_to_all(state.reshape(devices, rows, width), 'seq', 0, 0)  10.8 us
    all_to_all x1, waiting for transfers between devices, body(): before = lax.all_to_all(exclusive(parts), 'seq', 0, 0)  9.76 us
    ppermute x3, starting transfers between devices, project(): behind = lax.ppermute(to_left + behind, 'head', left)  5.76 us
    ppermute x3, waiting for transfers between devices, project(): behind = lax.ppermute(to_left + behind, 'head', left)  5.65 us
  transfers between devices with their start and end apart: 12, of which 8 were waited for; matrix products, arithmetic and copies ran while one was open for 1% of the time, Pallas kernels for 0%

profile of v8, /device:TPU:24, one launch (start us, length us, event | category | flops | bytes accessed | tf_op | source)
XLA Modules:
  0.0 122.6 jit_solution(13270091644830710286)
XLA Ops:
  0.0 2.1 %local_state.1 = (f32[256,128]{1,0:T(8,128)}, bf16[1024,128]{1,0:T(8,128)(2,1)}, f32[128,128]{1,0:T(8,128)}) custom-call(bf16[1024,128]{1,0:T(8,128)(2,1)} %bitcast.39, bf16[1024,128]{1,0:T(8,128)(2,1)} %bitcast.35, f32[1,128]{1,0:T(1,128)} %gain_ref.1, f32[1,128]{1,0:T(1,128)} %norm_ref.1), custom_call_target="tpu_custom_call" | custom-call | tf_op jit(solution)/shard_map/local_state/pallas_call | solution.py:45
  2.2 1.9 %collective-permute-start = (f32[128,2048]{1,0:T(8,128)S(1)}, f32[128,2048]{1,0:T(8,128)S(1)}, u32[]{:S(2)}, u32[]{:S(2)}) collective-permute-start(f32[128,2048]{1,0:T(8,128)S(1)} %convert_element_type.16), channel_id=1, source_target_pairs={{0,1},{1,0},{2,3},{3,2},{4,5},{5,4},{6,7},{7,6},{8,9},{9,8},{10,11... | collective-permute-start | bytes 3145736 | tf_op jit(solution)/shard_map/ppermute | solution.py:183
  4.1 13.2 %all-to-all-start = ((f32[32,8,128]{2,1,0:T(8,128)}), f32[32,8,128]{2,1,0:T(8,128)S(1)}, u32[]{:S(2)}, u32[]{:S(2)}) async-start(f32[32,8,128]{2,1,0:T(8,128)} %bitcast.2), calls=%async_computation | async-start | bytes 262144 | tf_op jit(solution)/shard_map/all_to_all | solution.py:278
  17.5 10.8 %all-to-all-done.x_ref = f32[32,8,128]{2,1,0:T(8,128)S(1)} async-done(((f32[32,8,128]{2,1,0:T(8,128)}), f32[32,8,128]{2,1,0:T(8,128)S(1)}, u32[]{:S(2)}, u32[]{:S(2)}) %all-to-all-start) | async-done | bytes 131104 | tf_op jit(solution)/shard_map/all_to_all | solution.py:278
  28.3 0.7 prefix.1
  28.9 3.8 %all-to-all-start.1 = ((f32[32,8,128]{2,1,0:T(8,128)}), f32[32,8,128]{2,1,0:T(8,128)S(1)}, u32[]{:S(2)}, u32[]{:S(2)}) async-start(f32[32,8,128]{2,1,0:T(8,128)} %prefix.1), calls=%async_computation.1 | async-start | bytes 262144 | tf_op jit(solution)/shard_map/all_to_all | solution.py:284
  33.4 9.8 %all-to-all-done.1 = f32[32,8,128]{2,1,0:T(8,128)S(1)} async-done(((f32[32,8,128]{2,1,0:T(8,128)}), f32[32,8,128]{2,1,0:T(8,128)S(1)}, u32[]{:S(2)}, u32[]{:S(2)}) %all-to-all-start.1) | async-done | bytes 131104 | tf_op jit(solution)/shard_map/all_to_all | solution.py:284
  43.2 11.2 %solve.1.own_ref = f32[1024,128]{1,0:T(8,128)S(1)} custom-call(f32[1]{0:T(128)S(6)} %copy.8.reg_ref, bf16[1024,128]{1,0:T(8,128)(2,1)S(1)} %bitcast.38, bf16[1024,128]{1,0:T(8,128)(2,1)S(1)} %copy-done.3, bf16[1024,128]{1,0:T(8,128)(2,1)S(1)} %bitcast.36, f32[256,128]{1,0:T(8,128)S(1)} %bitcast.37, f32[128,128]{1,0:T(8,128)S(1)} %copy-done.4), custom_call_target="tpu_custom_call" | custom-call | flops 60000002048 | bytes 2097152 | tf_op jit(solution)/shard_map/solve/pallas_call | solution.py:160
  54.4 1.9 %collective-permute-start.1 = (f32[1024,128]{1,0:T(8,128)S(1)}, f32[1024,128]{1,0:T(8,128)S(1)}, u32[]{:S(2)}, u32[]{:S(2)}) collective-permute-start(f32[1024,128]{1,0:T(8,128)S(1)} %solve.1.own_ref), channel_id=1, source_target_pairs={{0,1},{1,0},{2,3},{3,2},{4,5},{5,4},{6,7},{7,6},{8,9},{9,8},{10,11... | collective-permute-start | bytes 1572872 | tf_op jit(solution)/shard_map/ppermute | solution.py:183
  56.3 1.9 %collective-permute-done.1.other_ref = f32[1024,128]{1,0:T(8,128)S(1)} collective-permute-done((f32[1024,128]{1,0:T(8,128)S(1)}, f32[1024,128]{1,0:T(8,128)S(1)}, u32[]{:S(2)}, u32[]{:S(2)}) %collective-permute-start.1) | collective-permute-done | bytes 524320 | tf_op jit(solution)/shard_map/ppermute | solution.py:183
  58.5 4.7 %collective-permute-start.2 = (f32[512,128]{1,0:T(8,128)S(1)}, f32[512,128]{1,0:T(8,128)S(1)}, u32[]{:S(2)}, u32[]{:S(2)}) collective-permute-start(f32[512,128]{1,0:T(8,128)S(1)} %get-tuple-element.25), channel_id=1, source_target_pairs={{0,2},{1,3},{2,4},{3,5},{4,6},{5,7},{6,8},{7,9},{8,10},{9,11},{10,... | collective-permute-start | bytes 786440 | tf_op jit(solution)/shard_map/ppermute | solution.py:252
  63.2 1.9 %collective-permute-start.6 = (f32[512,128]{1,0:T(8,128)S(1)}, f32[512,128]{1,0:T(8,128)S(1)}, u32[]{:S(2)}, u32[]{:S(2)}) collective-permute-start(f32[512,128]{1,0:T(8,128)S(1)} %get-tuple-element.26), channel_id=1, source_target_pairs={{0,14},{1,15},{2,0},{3,1},{4,2},{5,3},{6,4},{7,5},{8,6},{9,7},{10,... | collective-permute-start | bytes 786440 | tf_op jit(solution)/shard_map/ppermute | solution.py:253
  65.2 3.9 %collective-permute-done.2 = f32[512,128]{1,0:T(8,128)S(1)} collective-permute-done((f32[512,128]{1,0:T(8,128)S(1)}, f32[512,128]{1,0:T(8,128)S(1)}, u32[]{:S(2)}, u32[]{:S(2)}) %collective-permute-start.2) | collective-permute-done | bytes 262176 | tf_op jit(solution)/shard_map/ppermute | solution.py:252
  69.4 5.6 %collective-permute-start.3 = (f32[1024,128]{1,0:T(8,128)S(1)}, f32[1024,128]{1,0:T(8,128)S(1)}, u32[]{:S(2)}, u32[]{:S(2)}) collective-permute-start(f32[1024,128]{1,0:T(8,128)S(1)} %convolution_add_fusion.3), channel_id=1, source_target_pairs={{0,2},{1,3},{2,4},{3,5},{4,6},{5,7},{6,8},{7,9},{8,10},{9,11},{10,... | collective-permute-start | bytes 1572872 | tf_op jit(solution)/shard_map/ppermute | solution.py:266
  75.3 1.9 %collective-permute-start.7 = (f32[1024,128]{1,0:T(8,128)S(1)}, f32[1024,128]{1,0:T(8,128)S(1)}, u32[]{:S(2)}, u32[]{:S(2)}) collective-permute-start(f32[1024,128]{1,0:T(8,128)S(1)} %convolution_add_fusion), channel_id=1, source_target_pairs={{0,14},{1,15},{2,0},{3,1},{4,2},{5,3},{6,4},{7,5},{8,6},{9,7},{10,... | collective-permute-start | bytes 1572872 | tf_op jit(solution)/shard_map/ppermute | solution.py:267
  77.2 8.4 %collective-permute-done.3 = f32[1024,128]{1,0:T(8,128)S(1)} collective-permute-done((f32[1024,128]{1,0:T(8,128)S(1)}, f32[1024,128]{1,0:T(8,128)S(1)}, u32[]{:S(2)}, u32[]{:S(2)}) %collective-permute-start.3) | collective-permute-done | bytes 524320 | tf_op jit(solution)/shard_map/ppermute | solution.py:266
  85.9 5.6 %collective-permute-start.4 = (f32[1024,128]{1,0:T(8,128)S(1)}, f32[1024,128]{1,0:T(8,128)S(1)}, u32[]{:S(2)}, u32[]{:S(2)}) collective-permute-start(f32[1024,128]{1,0:T(8,128)S(1)} %convolution_add_fusion.4), channel_id=1, source_target_pairs={{0,2},{1,3},{2,4},{3,5},{4,6},{5,7},{6,8},{7,9},{8,10},{9,11},{10,... | collective-permute-start | bytes 1572872 | tf_op jit(solution)/shard_map/ppermute | solution.py:266
  91.8 1.9 %collective-permute-start.8 = (f32[1024,128]{1,0:T(8,128)S(1)}, f32[1024,128]{1,0:T(8,128)S(1)}, u32[]{:S(2)}, u32[]{:S(2)}) collective-permute-start(f32[1024,128]{1,0:T(8,128)S(1)} %convolution_add_fusion.1), channel_id=1, source_target_pairs={{0,14},{1,15},{2,0},{3,1},{4,2},{5,3},{6,4},{7,5},{8,6},{9,7},{10,... | collective-permute-start | bytes 1572872 | tf_op jit(solution)/shard_map/ppermute | solution.py:267
  93.8 7.5 %collective-permute-done.4 = f32[1024,128]{1,0:T(8,128)S(1)} collective-permute-done((f32[1024,128]{1,0:T(8,128)S(1)}, f32[1024,128]{1,0:T(8,128)S(1)}, u32[]{:S(2)}, u32[]{:S(2)}) %collective-permute-start.4) | collective-permute-done | bytes 524320 | tf_op jit(solution)/shard_map/ppermute | solution.py:266
  101.5 5.6 %collective-permute-start.5 = (f32[1024,128]{1,0:T(8,128)S(1)}, f32[1024,128]{1,0:T(8,128)S(1)}, u32[]{:S(2)}, u32[]{:S(2)}) collective-permute-start(f32[1024,128]{1,0:T(8,128)S(1)} %convolution_add_fusion.5), channel_id=1, source_target_pairs={{0,2},{1,3},{2,4},{3,5},{4,6},{5,7},{6,8},{7,9},{8,10},{9,11},{10,... | collective-permute-start | bytes 1572872 | tf_op jit(solution)/shard_map/ppermute | solution.py:266
  107.4 1.9 %collective-permute-start.9 = (f32[1024,128]{1,0:T(8,128)S(1)}, f32[1024,128]{1,0:T(8,128)S(1)}, u32[]{:S(2)}, u32[]{:S(2)}) collective-permute-start(f32[1024,128]{1,0:T(8,128)S(1)} %convolution_add_fusion.2), channel_id=1, source_target_pairs={{0,14},{1,15},{2,0},{3,1},{4,2},{5,3},{6,4},{7,5},{8,6},{9,7},{10,... | collective-permute-start | bytes 1572872 | tf_op jit(solution)/shard_map/ppermute | solution.py:267
  109.4 6.6 %collective-permute-done.5 = f32[1024,128]{1,0:T(8,128)S(1)} collective-permute-done((f32[1024,128]{1,0:T(8,128)S(1)}, f32[1024,128]{1,0:T(8,128)S(1)}, u32[]{:S(2)}, u32[]{:S(2)}) %collective-permute-start.5) | collective-permute-done | bytes 524320 | tf_op jit(solution)/shard_map/ppermute | solution.py:266
  116.0 5.6 %collective-permute-done.9 = f32[1024,128]{1,0:T(8,128)S(1)} collective-permute-done((f32[1024,128]{1,0:T(8,128)S(1)}, f32[1024,128]{1,0:T(8,128)S(1)}, u32[]{:S(2)}, u32[]{:S(2)}) %collective-permute-start.9) | collective-permute-done | bytes 524320 | tf_op jit(solution)/shard_map/ppermute | solution.py:267
  121.6 1.0 fusion.1
  (23 shorter events, 2.3 us)
Async XLA Ops:
  0.0 2.1 %copy-start = (bf16[128,2048]{1,0:T(8,128)(2,1)S(1)}, bf16[128,2048]{1,0:T(8,128)(2,1)}, u32[]{:S(2)}) copy-start(bf16[128,2048]{1,0:T(8,128)(2,1)} %own_ref) | copy-start | bytes 1572868
  2.2 15.1 %collective-permute-start = (f32[128,2048]{1,0:T(8,128)S(1)}, f32[128,2048]{1,0:T(8,128)S(1)}, u32[]{:S(2)}, u32[]{:S(2)}) collective-permute-start(f32[128,2048]{1,0:T(8,128)S(1)} %convert_element_type.16), channel_id=1, source_target_pairs={{0,1},{1,0},{2,3},{3,2},{4,5},{5,4},{6,7},{7,6},{8,9},{9,8},{10,11... | collective-permute-start | bytes 3145736 | tf_op jit(solution)/shard_map/ppermute | solution.py:183
  4.1 24.1 %all-to-all-start = ((f32[32,8,128]{2,1,0:T(8,128)}), f32[32,8,128]{2,1,0:T(8,128)S(1)}, u32[]{:S(2)}, u32[]{:S(2)}) async-start(f32[32,8,128]{2,1,0:T(8,128)} %bitcast.2), calls=%async_computation | async-start | bytes 262144 | tf_op jit(solution)/shard_map/all_to_all | solution.py:278
  17.3 25.9 %copy-start.3 = (bf16[1024,128]{1,0:T(8,128)(2,1)S(1)}, bf16[1024,128]{1,0:T(8,128)(2,1)}, u32[]{:S(2)}) copy-start(bf16[1024,128]{1,0:T(8,128)(2,1)} %get-tuple-element.20.k_ref) | copy-start | bytes 786436
  17.3 25.9 %copy-start.4 = (f32[128,128]{1,0:T(8,128)S(1)}, f32[128,128]{1,0:T(8,128)}, u32[]{:S(2)}) copy-start(f32[128,128]{1,0:T(8,128)} %get-tuple-element.22.column_ref) | copy-start | bytes 196612
  28.2 15.0 %copy-start.1 = (bf16[1024,1,128]{2,0,1:T(8,128)(2,1)S(1)}, bf16[1024,1,128]{2,0,1:T(8,128)(2,1)}, u32[]{:S(2)}) copy-start(bf16[1024,1,128]{2,0,1:T(8,128)(2,1)} %param.9) | copy-start | bytes 786436
  28.3 15.0 %copy-start.2 = (bf16[1024,1,128]{2,0,1:T(8,128)(2,1)S(1)}, bf16[1024,1,128]{2,0,1:T(8,128)(2,1)}, u32[]{:S(2)}) copy-start(bf16[1024,1,128]{2,0,1:T(8,128)(2,1)} %param.7) | copy-start | bytes 786436
  28.9 14.3 %all-to-all-start.1 = ((f32[32,8,128]{2,1,0:T(8,128)}), f32[32,8,128]{2,1,0:T(8,128)S(1)}, u32[]{:S(2)}, u32[]{:S(2)}) async-start(f32[32,8,128]{2,1,0:T(8,128)} %prefix.1), calls=%async_computation.1 | async-start | bytes 262144 | tf_op jit(solution)/shard_map/all_to_all | solution.py:284
  54.4 3.8 %collective-permute-start.1 = (f32[1024,128]{1,0:T(8,128)S(1)}, f32[1024,128]{1,0:T(8,128)S(1)}, u32[]{:S(2)}, u32[]{:S(2)}) collective-permute-start(f32[1024,128]{1,0:T(8,128)S(1)} %solve.1.own_ref), channel_id=1, source_target_pairs={{0,1},{1,0},{2,3},{3,2},{4,5},{5,4},{6,7},{7,6},{8,9},{9,8},{10,11... | collective-permute-start | bytes 1572872 | tf_op jit(solution)/shard_map/ppermute | solution.py:183
  58.5 10.6 %collective-permute-start.2 = (f32[512,128]{1,0:T(8,128)S(1)}, f32[512,128]{1,0:T(8,128)S(1)}, u32[]{:S(2)}, u32[]{:S(2)}) collective-permute-start(f32[512,128]{1,0:T(8,128)S(1)} %get-tuple-element.25), channel_id=1, source_target_pairs={{0,2},{1,3},{2,4},{3,5},{4,6},{5,7},{6,8},{7,9},{8,10},{9,11},{10,... | collective-permute-start | bytes 786440 | tf_op jit(solution)/shard_map/ppermute | solution.py:252
  63.2 11.8 %collective-permute-start.6 = (f32[512,128]{1,0:T(8,128)S(1)}, f32[512,128]{1,0:T(8,128)S(1)}, u32[]{:S(2)}, u32[]{:S(2)}) collective-permute-start(f32[512,128]{1,0:T(8,128)S(1)} %get-tuple-element.26), channel_id=1, source_target_pairs={{0,14},{1,15},{2,0},{3,1},{4,2},{5,3},{6,4},{7,5},{8,6},{9,7},{10,... | collective-permute-start | bytes 786440 | tf_op jit(solution)/shard_map/ppermute | solution.py:253
  69.4 16.3 %collective-permute-start.3 = (f32[1024,128]{1,0:T(8,128)S(1)}, f32[1024,128]{1,0:T(8,128)S(1)}, u32[]{:S(2)}, u32[]{:S(2)}) collective-permute-start(f32[1024,128]{1,0:T(8,128)S(1)} %convolution_add_fusion.3), channel_id=1, source_target_pairs={{0,2},{1,3},{2,4},{3,5},{4,6},{5,7},{6,8},{7,9},{8,10},{9,11},{10,... | collective-permute-start | bytes 1572872 | tf_op jit(solution)/shard_map/ppermute | solution.py:266
  75.3 16.2 %collective-permute-start.7 = (f32[1024,128]{1,0:T(8,128)S(1)}, f32[1024,128]{1,0:T(8,128)S(1)}, u32[]{:S(2)}, u32[]{:S(2)}) collective-permute-start(f32[1024,128]{1,0:T(8,128)S(1)} %convolution_add_fusion), channel_id=1, source_target_pairs={{0,14},{1,15},{2,0},{3,1},{4,2},{5,3},{6,4},{7,5},{8,6},{9,7},{10,... | collective-permute-start | bytes 1572872 | tf_op jit(solution)/shard_map/ppermute | solution.py:267
  85.9 15.3 %collective-permute-start.4 = (f32[1024,128]{1,0:T(8,128)S(1)}, f32[1024,128]{1,0:T(8,128)S(1)}, u32[]{:S(2)}, u32[]{:S(2)}) collective-permute-start(f32[1024,128]{1,0:T(8,128)S(1)} %convolution_add_fusion.4), channel_id=1, source_target_pairs={{0,2},{1,3},{2,4},{3,5},{4,6},{5,7},{6,8},{7,9},{8,10},{9,11},{10,... | collective-permute-start | bytes 1572872 | tf_op jit(solution)/shard_map/ppermute | solution.py:266
  91.8 15.3 %collective-permute-start.8 = (f32[1024,128]{1,0:T(8,128)S(1)}, f32[1024,128]{1,0:T(8,128)S(1)}, u32[]{:S(2)}, u32[]{:S(2)}) collective-permute-start(f32[1024,128]{1,0:T(8,128)S(1)} %convolution_add_fusion.1), channel_id=1, source_target_pairs={{0,14},{1,15},{2,0},{3,1},{4,2},{5,3},{6,4},{7,5},{8,6},{9,7},{10,... | collective-permute-start | bytes 1572872 | tf_op jit(solution)/shard_map/ppermute | solution.py:267
  101.5 14.4 %collective-permute-start.5 = (f32[1024,128]{1,0:T(8,128)S(1)}, f32[1024,128]{1,0:T(8,128)S(1)}, u32[]{:S(2)}, u32[]{:S(2)}) collective-permute-start(f32[1024,128]{1,0:T(8,128)S(1)} %convolution_add_fusion.5), channel_id=1, source_target_pairs={{0,2},{1,3},{2,4},{3,5},{4,6},{5,7},{6,8},{7,9},{8,10},{9,11},{10,... | collective-permute-start | bytes 1572872 | tf_op jit(solution)/shard_map/ppermute | solution.py:266
  107.4 14.1 %collective-permute-start.9 = (f32[1024,128]{1,0:T(8,128)S(1)}, f32[1024,128]{1,0:T(8,128)S(1)}, u32[]{:S(2)}, u32[]{:S(2)}) collective-permute-start(f32[1024,128]{1,0:T(8,128)S(1)} %convolution_add_fusion.2), channel_id=1, source_target_pairs={{0,14},{1,15},{2,0},{3,1},{4,2},{5,3},{6,4},{7,5},{8,6},{9,7},{10,... | collective-permute-start | bytes 1572872 | tf_op jit(solution)/shard_map/ppermute | solution.py:267

commit v9 on v7

--- a/solution.py
+++ b/solution.py
@@ -53,21 +53,45 @@
     )(keys, values, gain, norm_gain)
 
 
-def prefix_kernel(x_ref, o_ref):
-    pieces, rows = o_ref.shape[0], o_ref.shape[1]
+def near_kernel(x_ref, o_ref, totals_ref):
     total = jnp.zeros(o_ref.shape[1:], F32)
-    for piece in range(pieces):
+    for piece in range(o_ref.shape[0]):
         o_ref[piece] = total
         total = total + x_ref[piece]
-
-
-def exclusive(pieces):
-    return pl.pallas_call(
-        prefix_kernel,
+    for copy in range(totals_ref.shape[0]):
+        totals_ref[copy] = total
+
+
+def near_prefix(pieces, copies):
+    return pl.pallas_call(
+        near_kernel,
+        out_shape=(
+            jax.ShapeDtypeStruct(pieces.shape, F32),
+            jax.ShapeDtypeStruct((copies, *pieces.shape[1:]), F32),
+        ),
+        compiler_params=small(2),
+        name="near_prefix",
+    )(pieces)
+
+
+def far_kernel(place_ref, x_ref, totals_ref, o_ref):
+    earlier = jnp.zeros(o_ref.shape[1:], F32)
+    for group in range(totals_ref.shape[0]):
+        earlier = earlier + jnp.where(group < place_ref[0], totals_ref[group], 0.0)
+    for piece in range(o_ref.shape[0]):
+        o_ref[piece] = x_ref[piece] + earlier
+
+
+def far_prefix(place, pieces, totals):
+    vmem = pl.BlockSpec(memory_space=pltpu.VMEM)
+    return pl.pallas_call(
+        far_kernel,
         out_shape=jax.ShapeDtypeStruct(pieces.shape, F32),
+        in_specs=[pl.BlockSpec(memory_space=pltpu.SMEM), vmem, vmem],
+        out_specs=vmem,
         compiler_params=small(2),
-        name="prefix",
-    )(pieces)
+        name="far_prefix",
+    )(place, pieces, totals)
 
 
 def solve_kernel(
@@ -292,9 +316,15 @@
     devices = lax.axis_size("seq")
     key_rows, value_rows, query_rows = keys[:, 0, :], values[:, 0, :], queries[:, 0, :]
     state, gained, column = local_state(key_rows, value_rows, key_gain, norm_gain)
-    rows = 2 * width // devices
+    near = min(8, devices)
+    groups = devices // near
+    near_groups = [[g * near + i for i in range(near)] for g in range(groups)]
+    far_groups = [[g * near + i for g in range(groups)] for i in range(near)]
+    rows = 2 * width // near
     state, out_weight = lax.optimization_barrier((state, out_weight))
-    parts = lax.all_to_all(state.reshape(devices, rows, width), "seq", 0, 0)
+    parts = lax.all_to_all(
+        state.reshape(near, rows, width), "seq", 0, 0, axis_index_groups=near_groups
+    )
     weights = join_weight(out_weight, swapped(out_weight.astype(F32)))
     far = lax.axis_size("head") // 4
     core = lax.rem(lax.axis_index("head").astype(jnp.uint32), jnp.uint32(2))
@@ -303,7 +333,11 @@
     parts, weights, core, starts = lax.optimization_barrier(
         (parts, weights, core, starts)
     )
-    before = lax.all_to_all(exclusive(parts), "seq", 0, 0)
+    place = lax.div(lax.axis_index("seq").astype(jnp.uint32), jnp.uint32(near))
+    sums, totals = near_prefix(parts, groups)
+    totals = lax.all_to_all(totals, "seq", 0, 0, axis_index_groups=far_groups)
+    sums = far_prefix(place.astype(jnp.int32).reshape(1), sums, totals)
+    before = lax.all_to_all(sums, "seq", 0, 0, axis_index_groups=near_groups)
     before = before.reshape(2 * width, width)
     normed = solve(
         reg, core.reshape(1), query_rows, gained, value_rows, before, column

time: 117 us -> 122 us (1.043)
  waiting for transfers between devices: 29.7 us -> 32.3 us
  starting transfers between devices: 65.2 us -> 66.7 us
    all_to_all x2 -> x3, waiting for transfers between devices: 17.5 us -> 20 us  [the longest x1 8.33 us: body(): lax.all_to_all(state.reshape(near, rows, width), 'seq', 0, 0, axis_index_...]
    ppermute x3, starting transfers between devices: 19.2 us -> 20.7 us  [swapped(): return lax.ppermute(value, 'head', [(i, i ^ 1) for i in range(heads)])]
    all_to_all x2 -> x3, starting transfers between devices: 12.1 us -> 12.2 us  [the longest x1 4.67 us: body(): lax.all_to_all(state.reshape(near, rows, width), 'seq', 0, 0, axis_index_...]
  transfers between devices with their start and end apart: 13 -> 14, of which waited for: 8 -> 9; matrix products, arithmetic and copies ran while one was open for 4% -> 4% of each run, Pallas kernels for 0% -> 0%
where the time goes in v9:
time: 122 us; the launch traced here: 121 us
  starting transfers between devices  66.7 us (55%)
  waiting for transfers between devices  32.3 us (26%)
  Pallas kernels  15.5 us (13%)
  other arithmetic  3.56 us (3%)
  matrix products  1.6 us (1%)
    ppermute x6, starting transfers between devices, project(): flows[piece] = lax.ppermute(flows[piece], 'head', ring)  27.5 us
    ppermute x3, starting transfers between devices, swapped(): return lax.ppermute(value, 'head', [(i, i ^ 1) for i in range(heads)])  20.7 us
    pallas_call x1, Pallas kernels, solve(): pl.pallas_call(solve_kernel, out_shape=jax.ShapeDtypeStruct((tokens, widt...  11.2 us
    all_to_all x1, waiting for transfers between devices, body(): lax.all_to_all(state.reshape(near, rows, width), 'seq', 0, 0, axis_index_...  8.33 us
    all_to_all x1, waiting for transfers between devices, body(): before = lax.all_to_all(sums, 'seq', 0, 0, axis_index_groups=near_groups)  7.22 us
    ppermute x6, waiting for transfers between devices, project(): flows[piece] = lax.ppermute(flows[piece], 'head', ring)  5.59 us
    ppermute x1, waiting for transfers between devices, project(): same = lax.ppermute(own_columns(flows[0]), 'head', ring)  5.16 us
    all_to_all x1, starting transfers between devices, body(): lax.all_to_all(state.reshape(near, rows, width), 'seq', 0, 0, axis_index_...  4.67 us
  transfers between devices with their start and end apart: 14, of which 9 were waited for; matrix products, arithmetic and copies ran while one was open for 4% of the time, Pallas kernels for 0%

profile of v9, /device:TPU:1, one launch (start us, length us, event | category | flops | bytes accessed | tf_op | source)
XLA Modules:
  0.0 120.6 jit_solution(9614449596270616807)
XLA Ops:
  0.0 2.1 %local_state.1 = (f32[256,128]{1,0:T(8,128)}, bf16[1024,128]{1,0:T(8,128)(2,1)}, f32[128,128]{1,0:T(8,128)}) custom-call(bf16[1024,128]{1,0:T(8,128)(2,1)} %bitcast.38, bf16[1024,128]{1,0:T(8,128)(2,1)} %bitcast.34, f32[1,128]{1,0:T(1,128)} %gain_ref.1, f32[1,128]{1,0:T(1,128)} %norm_ref.1), custom_call_target="tpu_custom_call" | custom-call | tf_op jit(solution)/shard_map/local_state/pallas_call | solution.py:45
  2.2 8.8 %collective-permute-start = (f32[128,2048]{1,0:T(8,128)S(1)}, f32[128,2048]{1,0:T(8,128)S(1)}, u32[]{:S(2)}, u32[]{:S(2)}) collective-permute-start(f32[128,2048]{1,0:T(8,128)S(1)} %convert_element_type.16), channel_id=1, source_target_pairs={{0,1},{1,0},{2,3},{3,2},{4,5},{5,4},{6,7},{7,6},{8,9},{9,8},{10,11... | collective-permute-start | bytes 3145736 | tf_op jit(solution)/shard_map/ppermute | solution.py:215
  11.0 4.7 %all-to-all-start = ((f32[8,32,128]{2,1,0:T(8,128)}), f32[8,32,128]{2,1,0:T(8,128)S(1)}, u32[]{:S(2)}, u32[]{:S(2)}) async-start(f32[8,32,128]{2,1,0:T(8,128)} %bitcast.2), calls=%async_computation | async-start | bytes 262144 | tf_op jit(solution)/shard_map/all_to_all | solution.py:325
  15.8 8.3 %all-to-all-done.x_ref = f32[8,32,128]{2,1,0:T(8,128)S(1)} async-done(((f32[8,32,128]{2,1,0:T(8,128)}), f32[8,32,128]{2,1,0:T(8,128)S(1)}, u32[]{:S(2)}, u32[]{:S(2)}) %all-to-all-start) | async-done | bytes 131104 | tf_op jit(solution)/shard_map/all_to_all | solution.py:325
  24.8 4.0 %all-to-all-start.1 = ((f32[4,32,128]{2,1,0:T(8,128)}), f32[4,32,128]{2,1,0:T(8,128)S(1)}, u32[]{:S(2)}, u32[]{:S(2)}) async-start(f32[4,32,128]{2,1,0:T(8,128)} %get-tuple-element.28), calls=%async_computation.1 | async-start | bytes 131072 | tf_op jit(solution)/shard_map/all_to_all | solution.py:338
  28.8 4.5 %all-to-all-done.1.totals_ref = f32[4,32,128]{2,1,0:T(8,128)S(1)} async-done(((f32[4,32,128]{2,1,0:T(8,128)}), f32[4,32,128]{2,1,0:T(8,128)S(1)}, u32[]{:S(2)}, u32[]{:S(2)}) %all-to-all-start.1) | async-done | bytes 65568 | tf_op jit(solution)/shard_map/all_to_all | solution.py:338
  34.0 3.5 %all-to-all-start.2 = ((f32[8,32,128]{2,1,0:T(8,128)}), f32[8,32,128]{2,1,0:T(8,128)S(1)}, u32[]{:S(2)}, u32[]{:S(2)}) async-start(f32[8,32,128]{2,1,0:T(8,128)} %far_prefix.1), calls=%async_computation.2 | async-start | bytes 262144 | tf_op jit(solution)/shard_map/all_to_all | solution.py:340
  38.1 7.2 %all-to-all-done.2 = f32[8,32,128]{2,1,0:T(8,128)S(1)} async-done(((f32[8,32,128]{2,1,0:T(8,128)}), f32[8,32,128]{2,1,0:T(8,128)S(1)}, u32[]{:S(2)}, u32[]{:S(2)}) %all-to-all-start.2) | async-done | bytes 131104 | tf_op jit(solution)/shard_map/all_to_all | solution.py:340
  45.4 11.2 %solve.1.own_ref = f32[1024,128]{1,0:T(8,128)S(1)} custom-call(f32[1]{0:T(128)S(6)} %copy.8.reg_ref, s32[1]{0:T(128)} %bitcast.5.core_ref, bf16[1024,128]{1,0:T(8,128)(2,1)S(1)} %bitcast.37, bf16[1024,128]{1,0:T(8,128)(2,1)S(1)} %copy-done.3, bf16[1024,128]{1,0:T(8,128)(2,1)S(1)} %bitcast.35, f32[256,128]{1,0:T(8,128)S(1)} %bitcast.36, f32[128,128]{1,0:T(8,128)S(1)} %copy-done.4), custom_call_target="tpu_custom_call" | custom-call | flops 60000002048 | bytes 2097152 | tf_op jit(solution)/shard_map/solve/pallas_call | solution.py:192
  56.5 6.0 %collective-permute-start.1 = (f32[1024,128]{1,0:T(8,128)S(1)}, f32[1024,128]{1,0:T(8,128)S(1)}, u32[]{:S(2)}, u32[]{:S(2)}) collective-permute-start(f32[1024,128]{1,0:T(8,128)S(1)} %solve.1.own_ref), channel_id=1, source_target_pairs={{0,1},{1,0},{2,3},{3,2},{4,5},{5,4},{6,7},{7,6},{8,9},{9,8},{10,11... | collective-permute-start | bytes 1572872 | tf_op jit(solution)/shard_map/ppermute | solution.py:215
  62.5 1.5 %collective-permute-done.1.other_ref = f32[1024,128]{1,0:T(8,128)S(1)} collective-permute-done((f32[1024,128]{1,0:T(8,128)S(1)}, f32[1024,128]{1,0:T(8,128)S(1)}, u32[]{:S(2)}, u32[]{:S(2)}) %collective-permute-start.1) | collective-permute-done | bytes 524320 | tf_op jit(solution)/shard_map/ppermute | solution.py:215
  64.9 5.1 %collective-permute-start.5 = (f32[512,256]{1,0:T(8,128)S(1)}, f32[512,256]{1,0:T(8,128)S(1)}, u32[]{:S(2)}, u32[]{:S(2)}) collective-permute-start(f32[512,256]{1,0:T(8,128)S(1)} %get-tuple-element.33), channel_id=1, source_target_pairs={{0,2},{1,15},{2,4},{3,1},{4,6},{5,3},{6,8},{7,5},{8,10},{9,7},{10,... | collective-permute-start | bytes 1572872 | tf_op jit(solution)/shard_map/ppermute | solution.py:298
  70.0 3.0 %collective-permute-start.2 = (f32[512,256]{1,0:T(8,128)S(1)}, f32[512,256]{1,0:T(8,128)}, u32[]{:S(2)}, u32[]{:S(2)}) collective-permute-start(f32[512,256]{1,0:T(8,128)S(1)} %get-tuple-element.32), channel_id=1, source_target_pairs={{0,2},{1,15},{2,4},{3,1},{4,6},{5,3},{6,8},{7,5},{8,10},{9,7},{10,... | collective-permute-start | bytes 1572872 | tf_op jit(solution)/shard_map/ppermute | solution.py:298
  73.2 2.9 %collective-permute-done.5 = f32[512,256]{1,0:T(8,128)S(1)} collective-permute-done((f32[512,256]{1,0:T(8,128)S(1)}, f32[512,256]{1,0:T(8,128)S(1)}, u32[]{:S(2)}, u32[]{:S(2)}) %collective-permute-start.5) | collective-permute-done | bytes 524320 | tf_op jit(solution)/shard_map/ppermute | solution.py:298
  76.2 5.0 %collective-permute-start.6 = (f32[512,256]{1,0:T(8,128)S(1)}, f32[512,256]{1,0:T(8,128)S(1)}, u32[]{:S(2)}, u32[]{:S(2)}) collective-permute-start(f32[512,256]{1,0:T(8,128)S(1)} %add.54), channel_id=1, source_target_pairs={{0,2},{1,15},{2,4},{3,1},{4,6},{5,3},{6,8},{7,5},{8,10},{9,7},{10,... | collective-permute-start | bytes 1572872 | tf_op jit(solution)/shard_map/ppermute | solution.py:298
  81.7 1.1 add.50
  82.8 5.1 %collective-permute-start.3 = (f32[512,256]{1,0:T(8,128)S(1)}, f32[512,256]{1,0:T(8,128)}, u32[]{:S(2)}, u32[]{:S(2)}) collective-permute-start(f32[512,256]{1,0:T(8,128)S(1)} %add.50), channel_id=1, source_target_pairs={{0,2},{1,15},{2,4},{3,1},{4,6},{5,3},{6,8},{7,5},{8,10},{9,7},{10,... | collective-permute-start | bytes 1572872 | tf_op jit(solution)/shard_map/ppermute | solution.py:298
  88.3 4.1 %collective-permute-start.7 = (f32[512,256]{1,0:T(8,128)S(1)}, f32[512,256]{1,0:T(8,128)S(1)}, u32[]{:S(2)}, u32[]{:S(2)}) collective-permute-start(f32[512,256]{1,0:T(8,128)S(1)} %add.55), channel_id=1, source_target_pairs={{0,2},{1,15},{2,4},{3,1},{4,6},{5,3},{6,8},{7,5},{8,10},{9,7},{10,... | collective-permute-start | bytes 1572872 | tf_op jit(solution)/shard_map/ppermute | solution.py:298
  92.7 1.4 %collective-permute-done.3 = f32[512,256]{1,0:T(8,128)} collective-permute-done((f32[512,256]{1,0:T(8,128)S(1)}, f32[512,256]{1,0:T(8,128)}, u32[]{:S(2)}, u32[]{:S(2)}) %collective-permute-start.3) | collective-permute-done | bytes 524320 | tf_op jit(solution)/shard_map/ppermute | solution.py:298
  95.2 5.1 %collective-permute-start.4 = (f32[512,256]{1,0:T(8,128)S(1)}, f32[512,256]{1,0:T(8,128)S(1)}, u32[]{:S(2)}, u32[]{:S(2)}) collective-permute-start(f32[512,256]{1,0:T(8,128)S(1)} %add.52), channel_id=1, source_target_pairs={{0,2},{1,15},{2,4},{3,1},{4,6},{5,3},{6,8},{7,5},{8,10},{9,7},{10,... | collective-permute-start | bytes 1572872 | tf_op jit(solution)/shard_map/ppermute | solution.py:298
  100.9 4.5 %collective-permute-start.8 = (f32[512,128]{1,0:T(8,128)S(1)}, f32[512,128]{1,0:T(8,128)S(1)}, u32[]{:S(2)}, u32[]{:S(2)}) collective-permute-start(f32[512,128]{1,0:T(8,128)S(1)} %get-tuple-element.35), channel_id=1, source_target_pairs={{0,3},{1,14},{2,5},{3,0},{4,7},{5,2},{6,9},{7,4},{8,11},{9,6},{10,... | collective-permute-start | bytes 786440 | tf_op jit(solution)/shard_map/ppermute | solution.py:301
  106.5 5.9 %collective-permute-start.10 = (f32[512,128]{1,0:T(8,128)S(1)}, f32[512,128]{1,0:T(8,128)S(1)}, u32[]{:S(2)}, u32[]{:S(2)}) collective-permute-start(f32[512,128]{1,0:T(8,128)S(1)} %slice_select_fusion), channel_id=1, source_target_pairs={{0,1},{1,0},{2,3},{3,2},{4,5},{5,4},{6,7},{7,6},{8,9},{9,8},{10,11... | collective-permute-start | bytes 786440 | tf_op jit(solution)/shard_map/ppermute | solution.py:215
  112.4 1.9 %collective-permute-start.9 = (f32[512,128]{1,0:T(8,128)S(1)}, f32[512,128]{1,0:T(8,128)S(1)}, u32[]{:S(2)}, u32[]{:S(2)}) collective-permute-start(f32[512,128]{1,0:T(8,128)S(1)} %get-tuple-element.36), channel_id=1, source_target_pairs={{0,2},{1,15},{2,4},{3,1},{4,6},{5,3},{6,8},{7,5},{8,10},{9,7},{10,... | collective-permute-start | bytes 786440 | tf_op jit(solution)/shard_map/ppermute | solution.py:302
  114.6 5.2 %collective-permute-done.9 = f32[512,128]{1,0:T(8,128)S(1)} collective-permute-done((f32[512,128]{1,0:T(8,128)S(1)}, f32[512,128]{1,0:T(8,128)S(1)}, u32[]{:S(2)}, u32[]{:S(2)}) %collective-permute-start.9) | collective-permute-done | bytes 262176 | tf_op jit(solution)/shard_map/ppermute | solution.py:302
  (39 shorter events, 7.6 us)
Async XLA Ops:
  0.0 2.1 %copy-start = (bf16[128,2048]{1,0:T(8,128)(2,1)S(1)}, bf16[128,2048]{1,0:T(8,128)(2,1)}, u32[]{:S(2)}) copy-start(bf16[128,2048]{1,0:T(8,128)(2,1)} %own_ref) | copy-start | bytes 1572868
  2.2 13.5 %collective-permute-start = (f32[128,2048]{1,0:T(8,128)S(1)}, f32[128,2048]{1,0:T(8,128)S(1)}, u32[]{:S(2)}, u32[]{:S(2)}) collective-permute-start(f32[128,2048]{1,0:T(8,128)S(1)} %convert_element_type.16), channel_id=1, source_target_pairs={{0,1},{1,0},{2,3},{3,2},{4,5},{5,4},{6,7},{7,6},{8,9},{9,8},{10,11... | collective-permute-start | bytes 3145736 | tf_op jit(solution)/shard_map/ppermute | solution.py:215
  11.0 13.2 %all-to-all-start = ((f32[8,32,128]{2,1,0:T(8,128)}), f32[8,32,128]{2,1,0:T(8,128)S(1)}, u32[]{:S(2)}, u32[]{:S(2)}) async-start(f32[8,32,128]{2,1,0:T(8,128)} %bitcast.2), calls=%async_computation | async-start | bytes 262144 | tf_op jit(solution)/shard_map/all_to_all | solution.py:325
  24.2 21.2 %copy-start.3 = (bf16[1024,128]{1,0:T(8,128)(2,1)S(1)}, bf16[1024,128]{1,0:T(8,128)(2,1)}, u32[]{:S(2)}) copy-start(bf16[1024,128]{1,0:T(8,128)(2,1)} %get-tuple-element.25.k_ref) | copy-start | bytes 786436
  24.8 8.5 %all-to-all-start.1 = ((f32[4,32,128]{2,1,0:T(8,128)}), f32[4,32,128]{2,1,0:T(8,128)S(1)}, u32[]{:S(2)}, u32[]{:S(2)}) async-start(f32[4,32,128]{2,1,0:T(8,128)} %get-tuple-element.28), calls=%async_computation.1 | async-start | bytes 131072 | tf_op jit(solution)/shard_map/all_to_all | solution.py:338
  33.3 12.0 %copy-start.1 = (bf16[1024,1,128]{2,0,1:T(8,128)(2,1)S(1)}, bf16[1024,1,128]{2,0,1:T(8,128)(2,1)}, u32[]{:S(2)}) copy-start(bf16[1024,1,128]{2,0,1:T(8,128)(2,1)} %param.9) | copy-start | bytes 786436
  33.3 12.0 %copy-start.2 = (bf16[1024,1,128]{2,0,1:T(8,128)(2,1)S(1)}, bf16[1024,1,128]{2,0,1:T(8,128)(2,1)}, u32[]{:S(2)}) copy-start(bf16[1024,1,128]{2,0,1:T(8,128)(2,1)} %param.7) | copy-start | bytes 786436
  34.0 11.4 %copy-start.4 = (f32[128,128]{1,0:T(8,128)S(1)}, f32[128,128]{1,0:T(8,128)}, u32[]{:S(2)}) copy-start(f32[128,128]{1,0:T(8,128)} %get-tuple-element.29.column_ref) | copy-start | bytes 196612
  34.0 11.4 %all-to-all-start.2 = ((f32[8,32,128]{2,1,0:T(8,128)}), f32[8,32,128]{2,1,0:T(8,128)S(1)}, u32[]{:S(2)}, u32[]{:S(2)}) async-start(f32[8,32,128]{2,1,0:T(8,128)} %far_prefix.1), calls=%async_computation.2 | async-start | bytes 262144 | tf_op jit(solution)/shard_map/all_to_all | solution.py:340
  56.5 7.5 %collective-permute-start.1 = (f32[1024,128]{1,0:T(8,128)S(1)}, f32[1024,128]{1,0:T(8,128)S(1)}, u32[]{:S(2)}, u32[]{:S(2)}) collective-permute-start(f32[1024,128]{1,0:T(8,128)S(1)} %solve.1.own_ref), channel_id=1, source_target_pairs={{0,1},{1,0},{2,3},{3,2},{4,5},{5,4},{6,7},{7,6},{8,9},{9,8},{10,11... | collective-permute-start | bytes 1572872 | tf_op jit(solution)/shard_map/ppermute | solution.py:215
  64.9 11.2 %collective-permute-start.5 = (f32[512,256]{1,0:T(8,128)S(1)}, f32[512,256]{1,0:T(8,128)S(1)}, u32[]{:S(2)}, u32[]{:S(2)}) collective-permute-start(f32[512,256]{1,0:T(8,128)S(1)} %get-tuple-element.33), channel_id=1, source_target_pairs={{0,2},{1,15},{2,4},{3,1},{4,6},{5,3},{6,8},{7,5},{8,10},{9,7},{10,... | collective-permute-start | bytes 1572872 | tf_op jit(solution)/shard_map/ppermute | solution.py:298
  70.0 11.7 %collective-permute-start.2 = (f32[512,256]{1,0:T(8,128)S(1)}, f32[512,256]{1,0:T(8,128)}, u32[]{:S(2)}, u32[]{:S(2)}) collective-permute-start(f32[512,256]{1,0:T(8,128)S(1)} %get-tuple-element.32), channel_id=1, source_target_pairs={{0,2},{1,15},{2,4},{3,1},{4,6},{5,3},{6,8},{7,5},{8,10},{9,7},{10,... | collective-permute-start | bytes 1572872 | tf_op jit(solution)/shard_map/ppermute | solution.py:298
  76.2 12.0 %collective-permute-start.6 = (f32[512,256]{1,0:T(8,128)S(1)}, f32[512,256]{1,0:T(8,128)S(1)}, u32[]{:S(2)}, u32[]{:S(2)}) collective-permute-start(f32[512,256]{1,0:T(8,128)S(1)} %add.54), channel_id=1, source_target_pairs={{0,2},{1,15},{2,4},{3,1},{4,6},{5,3},{6,8},{7,5},{8,10},{9,7},{10,... | collective-permute-start | bytes 1572872 | tf_op jit(solution)/shard_map/ppermute | solution.py:298
  82.8 11.2 %collective-permute-start.3 = (f32[512,256]{1,0:T(8,128)S(1)}, f32[512,256]{1,0:T(8,128)}, u32[]{:S(2)}, u32[]{:S(2)}) collective-permute-start(f32[512,256]{1,0:T(8,128)S(1)} %add.50), channel_id=1, source_target_pairs={{0,2},{1,15},{2,4},{3,1},{4,6},{5,3},{6,8},{7,5},{8,10},{9,7},{10,... | collective-permute-start | bytes 1572872 | tf_op jit(solution)/shard_map/ppermute | solution.py:298
  88.3 12.5 %collective-permute-start.7 = (f32[512,256]{1,0:T(8,128)S(1)}, f32[512,256]{1,0:T(8,128)S(1)}, u32[]{:S(2)}, u32[]{:S(2)}) collective-permute-start(f32[512,256]{1,0:T(8,128)S(1)} %add.55), channel_id=1, source_target_pairs={{0,2},{1,15},{2,4},{3,1},{4,6},{5,3},{6,8},{7,5},{8,10},{9,7},{10,... | collective-permute-start | bytes 1572872 | tf_op jit(solution)/shard_map/ppermute | solution.py:298
  95.2 11.2 %collective-permute-start.4 = (f32[512,256]{1,0:T(8,128)S(1)}, f32[512,256]{1,0:T(8,128)S(1)}, u32[]{:S(2)}, u32[]{:S(2)}) collective-permute-start(f32[512,256]{1,0:T(8,128)S(1)} %add.52), channel_id=1, source_target_pairs={{0,2},{1,15},{2,4},{3,1},{4,6},{5,3},{6,8},{7,5},{8,10},{9,7},{10,... | collective-permute-start | bytes 1572872 | tf_op jit(solution)/shard_map/ppermute | solution.py:298
  100.9 13.6 %collective-permute-start.8 = (f32[512,128]{1,0:T(8,128)S(1)}, f32[512,128]{1,0:T(8,128)S(1)}, u32[]{:S(2)}, u32[]{:S(2)}) collective-permute-start(f32[512,128]{1,0:T(8,128)S(1)} %get-tuple-element.35), channel_id=1, source_target_pairs={{0,3},{1,14},{2,5},{3,0},{4,7},{5,2},{6,9},{7,4},{8,11},{9,6},{10,... | collective-permute-start | bytes 786440 | tf_op jit(solution)/shard_map/ppermute | solution.py:301
  106.5 8.2 %collective-permute-start.10 = (f32[512,128]{1,0:T(8,128)S(1)}, f32[512,128]{1,0:T(8,128)S(1)}, u32[]{:S(2)}, u32[]{:S(2)}) collective-permute-start(f32[512,128]{1,0:T(8,128)S(1)} %slice_select_fusion), channel_id=1, source_target_pairs={{0,1},{1,0},{2,3},{3,2},{4,5},{5,4},{6,7},{7,6},{8,9},{9,8},{10,11... | collective-permute-start | bytes 786440 | tf_op jit(solution)/shard_map/ppermute | solution.py:215
  112.4 7.4 %collective-permute-start.9 = (f32[512,128]{1,0:T(8,128)S(1)}, f32[512,128]{1,0:T(8,128)S(1)}, u32[]{:S(2)}, u32[]{:S(2)}) collective-permute-start(f32[512,128]{1,0:T(8,128)S(1)} %get-tuple-element.36), channel_id=1, source_target_pairs={{0,2},{1,15},{2,4},{3,1},{4,6},{5,3},{6,8},{7,5},{8,10},{9,7},{10,... | collective-permute-start | bytes 786440 | tf_op jit(solution)/shard_map/ppermute | solution.py:302

commit v10 on v7

--- a/solution.py
+++ b/solution.py
@@ -191,6 +191,22 @@
     return lax.ppermute(value, "head", [(i, i ^ 1) for i in range(heads)])
 
 
+def widen_kernel(weight_ref, out_ref):
+    out_ref[...] = weight_ref[...].astype(F32)
+
+
+def widened(weight):
+    return pl.pallas_call(
+        widen_kernel,
+        out_shape=jax.ShapeDtypeStruct(weight.shape, F32),
+        cost_estimate=pl.CostEstimate(
+            flops=20 * 10**9, bytes_accessed=2**21, transcendentals=0
+        ),
+        compiler_params=small(6),
+        name="widened",
+    )(weight)
+
+
 def join_weight_kernel(own_ref, other_ref, out_ref):
     chips, double, columns = out_ref.shape
     half = double // 2
@@ -295,7 +311,7 @@
     rows = 2 * width // devices
     state, out_weight = lax.optimization_barrier((state, out_weight))
     parts = lax.all_to_all(state.reshape(devices, rows, width), "seq", 0, 0)
-    weights = join_weight(out_weight, swapped(out_weight.astype(F32)))
+    weights = join_weight(out_weight, swapped(widened(out_weight)))
     far = lax.axis_size("head") // 4
     core = lax.rem(lax.axis_index("head").astype(jnp.uint32), jnp.uint32(2))
     starts = jnp.stack([chip_ahead(far), chip_ahead(far - 1)]).astype(jnp.int32)

time: 117 us -> 117 us (level)
  no operation moved by 1% of the time
where the time goes in v10:
time: 117 us; the launch traced here: 116 us
  starting transfers between devices  65.2 us (56%)
  waiting for transfers between devices  29.7 us (25%)
  Pallas kernels  15 us (13%)
  other arithmetic  3.47 us (3%)
  matrix products  1.59 us (1%)
    ppermute x6, starting transfers between devices, project(): flows[piece] = lax.ppermute(flows[piece], 'head', ring)  27.5 us
    ppermute x3, starting transfers between devices, swapped(): return lax.ppermute(value, 'head', [(i, i ^ 1) for i in range(heads)])  19.2 us
    pallas_call x1, Pallas kernels, solve(): pl.pallas_call(solve_kernel, out_shape=jax.ShapeDtypeStruct((tokens, widt...  11.2 us
    all_to_all x1, waiting for transfers between devices, body(): parts = lax.all_to_all(state.reshape(devices, rows, width), 'seq', 0, 0)  8.93 us
    all_to_all x1, waiting for transfers between devices, body(): before = lax.all_to_all(exclusive(parts), 'seq', 0, 0)  8.54 us
    all_to_all x1, starting transfers between devices, body(): parts = lax.all_to_all(state.reshape(devices, rows, width), 'seq', 0, 0)  7.52 us
    ppermute x6, waiting for transfers between devices, project(): flows[piece] = lax.ppermute(flows[piece], 'head', ring)  5.58 us
    ppermute x1, waiting for transfers between devices, project(): same = lax.ppermute(own_columns(flows[0]), 'head', ring)  5.16 us
  transfers between devices with their start and end apart: 13, of which 8 were waited for; matrix products, arithmetic and copies ran while one was open for 4% of the time, Pallas kernels for 0%

profile of v10, /device:TPU:1, one launch (start us, length us, event | category | flops | bytes accessed | tf_op | source)
XLA Modules:
  0.0 115.9 jit_solution(5453960365224061908)
XLA Ops:
  0.0 2.1 %local_state.1 = (f32[256,128]{1,0:T(8,128)}, bf16[1024,128]{1,0:T(8,128)(2,1)}, f32[128,128]{1,0:T(8,128)}) custom-call(bf16[1024,128]{1,0:T(8,128)(2,1)} %bitcast.37, bf16[1024,128]{1,0:T(8,128)(2,1)} %bitcast.33, f32[1,128]{1,0:T(1,128)} %gain_ref.1, f32[1,128]{1,0:T(1,128)} %norm_ref.1), custom_call_target="tpu_custom_call" | custom-call | tf_op jit(solution)/shard_map/local_state/pallas_call | solution.py:45
  2.2 8.8 %collective-permute-start = (f32[128,2048]{1,0:T(8,128)S(1)}, f32[128,2048]{1,0:T(8,128)S(1)}, u32[]{:S(2)}, u32[]{:S(2)}) collective-permute-start(f32[128,2048]{1,0:T(8,128)S(1)} %widened.1), channel_id=1, source_target_pairs={{0,1},{1,0},{2,3},{3,2},{4,5},{5,4},{6,7},{7,6},{8,9},{9,8},{10,11... | collective-permute-start | bytes 3145736 | tf_op jit(solution)/shard_map/ppermute | solution.py:191
  11.0 7.5 %all-to-all-start = ((f32[32,8,128]{2,1,0:T(8,128)}), f32[32,8,128]{2,1,0:T(8,128)S(1)}, u32[]{:S(2)}, u32[]{:S(2)}) async-start(f32[32,8,128]{2,1,0:T(8,128)} %bitcast.2), calls=%async_computation | async-start | bytes 262144 | tf_op jit(solution)/shard_map/all_to_all | solution.py:313
  18.7 8.9 %all-to-all-done.x_ref = f32[32,8,128]{2,1,0:T(8,128)S(1)} async-done(((f32[32,8,128]{2,1,0:T(8,128)}), f32[32,8,128]{2,1,0:T(8,128)S(1)}, u32[]{:S(2)}, u32[]{:S(2)}) %all-to-all-start) | async-done | bytes 131104 | tf_op jit(solution)/shard_map/all_to_all | solution.py:313
  28.3 4.5 %all-to-all-start.1 = ((f32[32,8,128]{2,1,0:T(8,128)}), f32[32,8,128]{2,1,0:T(8,128)S(1)}, u32[]{:S(2)}, u32[]{:S(2)}) async-start(f32[32,8,128]{2,1,0:T(8,128)} %prefix.1), calls=%async_computation.1 | async-start | bytes 262144 | tf_op jit(solution)/shard_map/all_to_all | solution.py:322
  33.5 8.5 %all-to-all-done.1 = f32[32,8,128]{2,1,0:T(8,128)S(1)} async-done(((f32[32,8,128]{2,1,0:T(8,128)}), f32[32,8,128]{2,1,0:T(8,128)S(1)}, u32[]{:S(2)}, u32[]{:S(2)}) %all-to-all-start.1) | async-done | bytes 131104 | tf_op jit(solution)/shard_map/all_to_all | solution.py:322
  42.1 11.2 %solve.1.own_ref = f32[1024,128]{1,0:T(8,128)S(1)} custom-call(f32[1]{0:T(128)S(6)} %copy.8.reg_ref, s32[1]{0:T(128)} %bitcast.5.core_ref, bf16[1024,128]{1,0:T(8,128)(2,1)S(1)} %bitcast.36, bf16[1024,128]{1,0:T(8,128)(2,1)S(1)} %copy-done.3, bf16[1024,128]{1,0:T(8,128)(2,1)S(1)} %bitcast.34, f32[256,128]{1,0:T(8,128)S(1)} %bitcast.35, f32[128,128]{1,0:T(8,128)S(1)} %copy-done.4), custom_call_target="tpu_custom_call" | custom-call | flops 60000002048 | bytes 2097152 | tf_op jit(solution)/shard_map/solve/pallas_call | solution.py:168
  53.3 4.5 %collective-permute-start.1 = (f32[1024,128]{1,0:T(8,128)S(1)}, f32[1024,128]{1,0:T(8,128)S(1)}, u32[]{:S(2)}, u32[]{:S(2)}) collective-permute-start(f32[1024,128]{1,0:T(8,128)S(1)} %solve.1.own_ref), channel_id=1, source_target_pairs={{0,1},{1,0},{2,3},{3,2},{4,5},{5,4},{6,7},{7,6},{8,9},{9,8},{10,11... | collective-permute-start | bytes 1572872 | tf_op jit(solution)/shard_map/ppermute | solution.py:191
  57.8 1.5 %collective-permute-done.1.other_ref = f32[1024,128]{1,0:T(8,128)S(1)} collective-permute-done((f32[1024,128]{1,0:T(8,128)S(1)}, f32[1024,128]{1,0:T(8,128)S(1)}, u32[]{:S(2)}, u32[]{:S(2)}) %collective-permute-start.1) | collective-permute-done | bytes 524320 | tf_op jit(solution)/shard_map/ppermute | solution.py:191
  60.2 5.1 %collective-permute-start.5 = (f32[512,256]{1,0:T(8,128)S(1)}, f32[512,256]{1,0:T(8,128)S(1)}, u32[]{:S(2)}, u32[]{:S(2)}) collective-permute-start(f32[512,256]{1,0:T(8,128)S(1)} %get-tuple-element.29), channel_id=1, source_target_pairs={{0,2},{1,15},{2,4},{3,1},{4,6},{5,3},{6,8},{7,5},{8,10},{9,7},{10,... | collective-permute-start | bytes 1572872 | tf_op jit(solution)/shard_map/ppermute | solution.py:290
  65.3 3.0 %collective-permute-start.2 = (f32[512,256]{1,0:T(8,128)S(1)}, f32[512,256]{1,0:T(8,128)}, u32[]{:S(2)}, u32[]{:S(2)}) collective-permute-start(f32[512,256]{1,0:T(8,128)S(1)} %get-tuple-element.28), channel_id=1, source_target_pairs={{0,2},{1,15},{2,4},{3,1},{4,6},{5,3},{6,8},{7,5},{8,10},{9,7},{10,... | collective-permute-start | bytes 1572872 | tf_op jit(solution)/shard_map/ppermute | solution.py:290
  68.5 2.9 %collective-permute-done.5 = f32[512,256]{1,0:T(8,128)S(1)} collective-permute-done((f32[512,256]{1,0:T(8,128)S(1)}, f32[512,256]{1,0:T(8,128)S(1)}, u32[]{:S(2)}, u32[]{:S(2)}) %collective-permute-start.5) | collective-permute-done | bytes 524320 | tf_op jit(solution)/shard_map/ppermute | solution.py:290
  71.4 5.0 %collective-permute-start.6 = (f32[512,256]{1,0:T(8,128)S(1)}, f32[512,256]{1,0:T(8,128)S(1)}, u32[]{:S(2)}, u32[]{:S(2)}) collective-permute-start(f32[512,256]{1,0:T(8,128)S(1)} %add.54), channel_id=1, source_target_pairs={{0,2},{1,15},{2,4},{3,1},{4,6},{5,3},{6,8},{7,5},{8,10},{9,7},{10,... | collective-permute-start | bytes 1572872 | tf_op jit(solution)/shard_map/ppermute | solution.py:290
  77.0 1.1 add.50
  78.1 5.1 %collective-permute-start.3 = (f32[512,256]{1,0:T(8,128)S(1)}, f32[512,256]{1,0:T(8,128)}, u32[]{:S(2)}, u32[]{:S(2)}) collective-permute-start(f32[512,256]{1,0:T(8,128)S(1)} %add.50), channel_id=1, source_target_pairs={{0,2},{1,15},{2,4},{3,1},{4,6},{5,3},{6,8},{7,5},{8,10},{9,7},{10,... | collective-permute-start | bytes 1572872 | tf_op jit(solution)/shard_map/ppermute | solution.py:290
  83.6 4.1 %collective-permute-start.7 = (f32[512,256]{1,0:T(8,128)S(1)}, f32[512,256]{1,0:T(8,128)S(1)}, u32[]{:S(2)}, u32[]{:S(2)}) collective-permute-start(f32[512,256]{1,0:T(8,128)S(1)} %add.55), channel_id=1, source_target_pairs={{0,2},{1,15},{2,4},{3,1},{4,6},{5,3},{6,8},{7,5},{8,10},{9,7},{10,... | collective-permute-start | bytes 1572872 | tf_op jit(solution)/shard_map/ppermute | solution.py:290
  87.9 1.4 %collective-permute-done.3 = f32[512,256]{1,0:T(8,128)} collective-permute-done((f32[512,256]{1,0:T(8,128)S(1)}, f32[512,256]{1,0:T(8,128)}, u32[]{:S(2)}, u32[]{:S(2)}) %collective-permute-start.3) | collective-permute-done | bytes 524320 | tf_op jit(solution)/shard_map/ppermute | solution.py:290
  89.3 1.1 add.52
  90.5 5.1 %collective-permute-start.4 = (f32[512,256]{1,0:T(8,128)S(1)}, f32[512,256]{1,0:T(8,128)S(1)}, u32[]{:S(2)}, u32[]{:S(2)}) collective-permute-start(f32[512,256]{1,0:T(8,128)S(1)} %add.52), channel_id=1, source_target_pairs={{0,2},{1,15},{2,4},{3,1},{4,6},{5,3},{6,8},{7,5},{8,10},{9,7},{10,... | collective-permute-start | bytes 1572872 | tf_op jit(solution)/shard_map/ppermute | solution.py:290
  96.2 4.5 %collective-permute-start.8 = (f32[512,128]{1,0:T(8,128)S(1)}, f32[512,128]{1,0:T(8,128)S(1)}, u32[]{:S(2)}, u32[]{:S(2)}) collective-permute-start(f32[512,128]{1,0:T(8,128)S(1)} %get-tuple-element.31), channel_id=1, source_target_pairs={{0,3},{1,14},{2,5},{3,0},{4,7},{5,2},{6,9},{7,4},{8,11},{9,6},{10,... | collective-permute-start | bytes 786440 | tf_op jit(solution)/shard_map/ppermute | solution.py:293
  100.7 1.0 collective-permute-done.4
  101.7 5.9 %collective-permute-start.10 = (f32[512,128]{1,0:T(8,128)S(1)}, f32[512,128]{1,0:T(8,128)S(1)}, u32[]{:S(2)}, u32[]{:S(2)}) collective-permute-start(f32[512,128]{1,0:T(8,128)S(1)} %slice_select_fusion), channel_id=1, source_target_pairs={{0,1},{1,0},{2,3},{3,2},{4,5},{5,4},{6,7},{7,6},{8,9},{9,8},{10,11... | collective-permute-start | bytes 786440 | tf_op jit(solution)/shard_map/ppermute | solution.py:191
  107.6 1.9 %collective-permute-start.9 = (f32[512,128]{1,0:T(8,128)S(1)}, f32[512,128]{1,0:T(8,128)S(1)}, u32[]{:S(2)}, u32[]{:S(2)}) collective-permute-start(f32[512,128]{1,0:T(8,128)S(1)} %get-tuple-element.32), channel_id=1, source_target_pairs={{0,2},{1,15},{2,4},{3,1},{4,6},{5,3},{6,8},{7,5},{8,10},{9,7},{10,... | collective-permute-start | bytes 786440 | tf_op jit(solution)/shard_map/ppermute | solution.py:294
  109.9 5.2 %collective-permute-done.9 = f32[512,128]{1,0:T(8,128)S(1)} collective-permute-done((f32[512,128]{1,0:T(8,128)S(1)}, f32[512,128]{1,0:T(8,128)S(1)}, u32[]{:S(2)}, u32[]{:S(2)}) %collective-permute-start.9) | collective-permute-done | bytes 262176 | tf_op jit(solution)/shard_map/ppermute | solution.py:294
  (36 shorter events, 4.9 us)
Async XLA Ops:
  0.0 2.1 %copy-start = (bf16[128,2048]{1,0:T(8,128)(2,1)S(1)}, bf16[128,2048]{1,0:T(8,128)(2,1)}, u32[]{:S(2)}) copy-start(bf16[128,2048]{1,0:T(8,128)(2,1)} %own_ref) | copy-start | bytes 1572868
  2.2 16.4 %collective-permute-start = (f32[128,2048]{1,0:T(8,128)S(1)}, f32[128,2048]{1,0:T(8,128)S(1)}, u32[]{:S(2)}, u32[]{:S(2)}) collective-permute-start(f32[128,2048]{1,0:T(8,128)S(1)} %widened.1), channel_id=1, source_target_pairs={{0,1},{1,0},{2,3},{3,2},{4,5},{5,4},{6,7},{7,6},{8,9},{9,8},{10,11... | collective-permute-start | bytes 3145736 | tf_op jit(solution)/shard_map/ppermute | solution.py:191
  11.0 16.7 %all-to-all-start = ((f32[32,8,128]{2,1,0:T(8,128)}), f32[32,8,128]{2,1,0:T(8,128)S(1)}, u32[]{:S(2)}, u32[]{:S(2)}) async-start(f32[32,8,128]{2,1,0:T(8,128)} %bitcast.2), calls=%async_computation | async-start | bytes 262144 | tf_op jit(solution)/shard_map/all_to_all | solution.py:313
  18.6 23.5 %copy-start.3 = (bf16[1024,128]{1,0:T(8,128)(2,1)S(1)}, bf16[1024,128]{1,0:T(8,128)(2,1)}, u32[]{:S(2)}) copy-start(bf16[1024,128]{1,0:T(8,128)(2,1)} %get-tuple-element.23.k_ref) | copy-start | bytes 786436
  18.6 23.5 %copy-start.4 = (f32[128,128]{1,0:T(8,128)S(1)}, f32[128,128]{1,0:T(8,128)}, u32[]{:S(2)}) copy-start(f32[128,128]{1,0:T(8,128)} %get-tuple-element.25.column_ref) | copy-start | bytes 196612
  18.7 23.4 %copy-start.1 = (bf16[1024,1,128]{2,0,1:T(8,128)(2,1)S(1)}, bf16[1024,1,128]{2,0,1:T(8,128)(2,1)}, u32[]{:S(2)}) copy-start(bf16[1024,1,128]{2,0,1:T(8,128)(2,1)} %param.9) | copy-start | bytes 786436
  18.7 23.4 %copy-start.2 = (bf16[1024,1,128]{2,0,1:T(8,128)(2,1)S(1)}, bf16[1024,1,128]{2,0,1:T(8,128)(2,1)}, u32[]{:S(2)}) copy-start(bf16[1024,1,128]{2,0,1:T(8,128)(2,1)} %param.7) | copy-start | bytes 786436
  28.3 13.7 %all-to-all-start.1 = ((f32[32,8,128]{2,1,0:T(8,128)}), f32[32,8,128]{2,1,0:T(8,128)S(1)}, u32[]{:S(2)}, u32[]{:S(2)}) async-start(f32[32,8,128]{2,1,0:T(8,128)} %prefix.1), calls=%async_computation.1 | async-start | bytes 262144 | tf_op jit(solution)/shard_map/all_to_all | solution.py:322
  53.3 6.0 %collective-permute-start.1 = (f32[1024,128]{1,0:T(8,128)S(1)}, f32[1024,128]{1,0:T(8,128)S(1)}, u32[]{:S(2)}, u32[]{:S(2)}) collective-permute-start(f32[1024,128]{1,0:T(8,128)S(1)} %solve.1.own_ref), channel_id=1, source_target_pairs={{0,1},{1,0},{2,3},{3,2},{4,5},{5,4},{6,7},{7,6},{8,9},{9,8},{10,11... | collective-permute-start | bytes 1572872 | tf_op jit(solution)/shard_map/ppermute | solution.py:191
  60.2 11.2 %collective-permute-start.5 = (f32[512,256]{1,0:T(8,128)S(1)}, f32[512,256]{1,0:T(8,128)S(1)}, u32[]{:S(2)}, u32[]{:S(2)}) collective-permute-start(f32[512,256]{1,0:T(8,128)S(1)} %get-tuple-element.29), channel_id=1, source_target_pairs={{0,2},{1,15},{2,4},{3,1},{4,6},{5,3},{6,8},{7,5},{8,10},{9,7},{10,... | collective-permute-start | bytes 1572872 | tf_op jit(solution)/shard_map/ppermute | solution.py:290
  65.3 11.7 %collective-permute-start.2 = (f32[512,256]{1,0:T(8,128)S(1)}, f32[512,256]{1,0:T(8,128)}, u32[]{:S(2)}, u32[]{:S(2)}) collective-permute-start(f32[512,256]{1,0:T(8,128)S(1)} %get-tuple-element.28), channel_id=1, source_target_pairs={{0,2},{1,15},{2,4},{3,1},{4,6},{5,3},{6,8},{7,5},{8,10},{9,7},{10,... | collective-permute-start | bytes 1572872 | tf_op jit(solution)/shard_map/ppermute | solution.py:290
  71.4 12.0 %collective-permute-start.6 = (f32[512,256]{1,0:T(8,128)S(1)}, f32[512,256]{1,0:T(8,128)S(1)}, u32[]{:S(2)}, u32[]{:S(2)}) collective-permute-start(f32[512,256]{1,0:T(8,128)S(1)} %add.54), channel_id=1, source_target_pairs={{0,2},{1,15},{2,4},{3,1},{4,6},{5,3},{6,8},{7,5},{8,10},{9,7},{10,... | collective-permute-start | bytes 1572872 | tf_op jit(solution)/shard_map/ppermute | solution.py:290
  78.1 11.2 %collective-permute-start.3 = (f32[512,256]{1,0:T(8,128)S(1)}, f32[512,256]{1,0:T(8,128)}, u32[]{:S(2)}, u32[]{:S(2)}) collective-permute-start(f32[512,256]{1,0:T(8,128)S(1)} %add.50), channel_id=1, source_target_pairs={{0,2},{1,15},{2,4},{3,1},{4,6},{5,3},{6,8},{7,5},{8,10},{9,7},{10,... | collective-permute-start | bytes 1572872 | tf_op jit(solution)/shard_map/ppermute | solution.py:290
  83.6 12.5 %collective-permute-start.7 = (f32[512,256]{1,0:T(8,128)S(1)}, f32[512,256]{1,0:T(8,128)S(1)}, u32[]{:S(2)}, u32[]{:S(2)}) collective-permute-start(f32[512,256]{1,0:T(8,128)S(1)} %add.55), channel_id=1, source_target_pairs={{0,2},{1,15},{2,4},{3,1},{4,6},{5,3},{6,8},{7,5},{8,10},{9,7},{10,... | collective-permute-start | bytes 1572872 | tf_op jit(solution)/shard_map/ppermute | solution.py:290
  90.5 11.2 %collective-permute-start.4 = (f32[512,256]{1,0:T(8,128)S(1)}, f32[512,256]{1,0:T(8,128)S(1)}, u32[]{:S(2)}, u32[]{:S(2)}) collective-permute-start(f32[512,256]{1,0:T(8,128)S(1)} %add.52), channel_id=1, source_target_pairs={{0,2},{1,15},{2,4},{3,1},{4,6},{5,3},{6,8},{7,5},{8,10},{9,7},{10,... | collective-permute-start | bytes 1572872 | tf_op jit(solution)/shard_map/ppermute | solution.py:290
  96.2 13.6 %collective-permute-start.8 = (f32[512,128]{1,0:T(8,128)S(1)}, f32[512,128]{1,0:T(8,128)S(1)}, u32[]{:S(2)}, u32[]{:S(2)}) collective-permute-start(f32[512,128]{1,0:T(8,128)S(1)} %get-tuple-element.31), channel_id=1, source_target_pairs={{0,3},{1,14},{2,5},{3,0},{4,7},{5,2},{6,9},{7,4},{8,11},{9,6},{10,... | collective-permute-start | bytes 786440 | tf_op jit(solution)/shard_map/ppermute | solution.py:293
  101.7 8.2 %collective-permute-start.10 = (f32[512,128]{1,0:T(8,128)S(1)}, f32[512,128]{1,0:T(8,128)S(1)}, u32[]{:S(2)}, u32[]{:S(2)}) collective-permute-start(f32[512,128]{1,0:T(8,128)S(1)} %slice_select_fusion), channel_id=1, source_target_pairs={{0,1},{1,0},{2,3},{3,2},{4,5},{5,4},{6,7},{7,6},{8,9},{9,8},{10,11... | collective-permute-start | bytes 786440 | tf_op jit(solution)/shard_map/ppermute | solution.py:191
  107.6 7.4 %collective-permute-start.9 = (f32[512,128]{1,0:T(8,128)S(1)}, f32[512,128]{1,0:T(8,128)S(1)}, u32[]{:S(2)}, u32[]{:S(2)}) collective-permute-start(f32[512,128]{1,0:T(8,128)S(1)} %get-tuple-element.32), channel_id=1, source_target_pairs={{0,2},{1,15},{2,4},{3,1},{4,6},{5,3},{6,8},{7,5},{8,10},{9,7},{10,... | collective-permute-start | bytes 786440 | tf_op jit(solution)/shard_map/ppermute | solution.py:294

commit v11 on v7

--- a/solution.py
+++ b/solution.py
@@ -239,6 +239,44 @@
     )(starts, own, other, weights)
 
 
+def hop_kernel(chip_ref, sums_ref, rows_ref, weights_ref, out_ref):
+    out_ref[...] = sums_ref[...] + mm(rows_ref[...], weights_ref[chip_ref[0]])
+
+
+def hop(chip, sums, rows, weights):
+    vmem = pl.BlockSpec(memory_space=pltpu.VMEM)
+    return pl.pallas_call(
+        hop_kernel,
+        out_shape=jax.ShapeDtypeStruct(sums.shape, F32),
+        in_specs=[pl.BlockSpec(memory_space=pltpu.SMEM), vmem, vmem, vmem],
+        out_specs=vmem,
+        compiler_params=small(8),
+        name="hop",
+    )(chip, sums, rows, weights)
+
+
+def finish_kernel(core_ref, one_a, one_b, two_a, two_b, out_ref):
+    half = one_a.shape[0]
+    one = one_a[...] + one_b[...]
+    two = two_a[...] + two_b[...]
+    early_first = core_ref[0] == 0
+    out_ref[0:half, :] = jnp.where(early_first, one, two).astype(BF16)
+    out_ref[half:, :] = jnp.where(early_first, two, one).astype(BF16)
+
+
+def finish(core, first, second):
+    half, width = first[0].shape
+    vmem = pl.BlockSpec(memory_space=pltpu.VMEM)
+    return pl.pallas_call(
+        finish_kernel,
+        out_shape=jax.ShapeDtypeStruct((2 * half, width), BF16),
+        in_specs=[pl.BlockSpec(memory_space=pltpu.SMEM)] + [vmem] * 4,
+        out_specs=vmem,
+        compiler_params=small(6),
+        name="finish",
+    )(core, *first, *second)
+
+
 def chip_ahead(away):
     chips = lax.axis_size("head") // 2
     place = lax.axis_index("head").astype(jnp.uint32)
@@ -247,7 +285,7 @@
     return lax.rem(chip + ahead, jnp.uint32(chips))
 
 
-def project(normed, weights, core, starts):
+def project(normed, weights, core, starts, hops):
     width = normed.shape[1]
     heads = lax.axis_size("head")
     far = heads // 4
@@ -273,18 +311,18 @@
         for piece in (0, 1):
             flows[piece] = lax.ppermute(flows[piece], "head", ring)
             if away - piece > 1:
-                flows[piece] = flows[piece] + part(piece, away - piece - 1)
+                next_away = away - piece - 1
+                if piece == 0:
+                    flows[piece] = flows[piece] + part(piece, next_away)
+                else:
+                    chip = hops[next_away - 1].reshape(1)
+                    flows[piece] = hop(chip, flows[piece], rows[piece], weights)
     crossed = lax.ppermute(other_columns(flows[0]), "head", cross)
     same = lax.ppermute(own_columns(flows[0]), "head", ring)
     given = swapped(other_columns(flows[1]))
-    first = own_columns(part(0, 0)) + same + given
-    second = own_columns(part(1, 0) + flows[1]) + crossed
-    first, second = first.astype(BF16), second.astype(BF16)
-    return jnp.where(
-        core == 1,
-        jnp.concatenate([second, first], axis=0),
-        jnp.concatenate([first, second], axis=0),
-    )
+    first = (own_columns(part(0, 0)) + given, same)
+    second = (own_columns(part(1, 0) + flows[1]), crossed)
+    return finish(core.reshape(1), first, second)
 
 
 def body(queries, keys, values, key_gain, reg, norm_gain, out_weight):
@@ -299,16 +337,17 @@
     far = lax.axis_size("head") // 4
     core = lax.rem(lax.axis_index("head").astype(jnp.uint32), jnp.uint32(2))
     starts = jnp.stack([chip_ahead(far), chip_ahead(far - 1)]).astype(jnp.int32)
+    hops = [chip_ahead(away).astype(jnp.int32) for away in (1, 2)]
     core = core.astype(jnp.int32)
-    parts, weights, core, starts = lax.optimization_barrier(
-        (parts, weights, core, starts)
+    parts, weights, core, starts, hops = lax.optimization_barrier(
+        (parts, weights, core, starts, hops)
     )
     before = lax.all_to_all(exclusive(parts), "seq", 0, 0)
     before = before.reshape(2 * width, width)
     normed = solve(
         reg, core.reshape(1), query_rows, gained, value_rows, before, column
     )
-    return project(normed, weights, core, starts)
+    return project(normed, weights, core, starts, hops)
 
 
 def solution(mesh):

time: 117 us -> 118 us (level)
  starting transfers between devices: 65.2 us -> 69.2 us
  other arithmetic: 3.56 us -> 1.55 us
  waiting for transfers between devices: 29.7 us -> 28.2 us
  Pallas kernels: 14.9 us -> 16.1 us
    ppermute x1, waiting for transfers between devices: 5.16 us -> 0.01 us  [project(): same = lax.ppermute(own_columns(flows[0]), 'head', ring)]
    ppermute x1, waiting for transfers between devices: 0.01 us -> 4.58 us  [project(): crossed = lax.ppermute(other_columns(flows[0]), 'head', cross)]
    ppermute x1, starting transfers between devices: 1.92 us -> 5.02 us  [project(): same = lax.ppermute(own_columns(flows[0]), 'head', ring)]
    pallas_call x0 -> x3, Pallas kernels: none -> 1.22 us  [the longest x1 0.77 us: finish(): pl.pallas_call(finish_kernel, out_shape=jax.ShapeDtypeStruct((2 * half, w...]
    add x5 -> x4, other arithmetic: 2.43 us -> 1.28 us  [the longest x3 1.25 us: project(): flows[piece] = flows[piece] + part(piece, next_away)]
  transfers between devices with their start and end apart: 13 -> 13, of which waited for: 8 -> 9; matrix products, arithmetic and copies ran while one was open for 4% -> 2% of each run, Pallas kernels for 0% -> 0%
where the time goes in v11:
time: 118 us; the launch traced here: 117 us
  starting transfers between devices  69.2 us (59%)
  waiting for transfers between devices  28.2 us (24%)
  Pallas kernels  16.1 us (14%)
  other arithmetic  1.55 us (1%)
    ppermute x6, starting transfers between devices, project(): flows[piece] = lax.ppermute(flows[piece], 'head', ring)  28.3 us
    ppermute x3, starting transfers between devices, swapped(): return lax.ppermute(value, 'head', [(i, i ^ 1) for i in range(heads)])  18.2 us
    pallas_call x1, Pallas kernels, solve(): pl.pallas_call(solve_kernel, out_shape=jax.ShapeDtypeStruct((tokens, widt...  11.2 us
    all_to_all x1, waiting for transfers between devices, body(): parts = lax.all_to_all(state.reshape(devices, rows, width), 'seq', 0, 0)  8.93 us
    all_to_all x1, waiting for transfers between devices, body(): before = lax.all_to_all(exclusive(parts), 'seq', 0, 0)  8.54 us
    all_to_all x1, starting transfers between devices, body(): parts = lax.all_to_all(state.reshape(devices, rows, width), 'seq', 0, 0)  7.52 us
    ppermute x1, starting transfers between devices, project(): crossed = lax.ppermute(other_columns(flows[0]), 'head', cross)  5.63 us
    ppermute x1, starting transfers between devices, project(): same = lax.ppermute(own_columns(flows[0]), 'head', ring)  5.02 us
  transfers between devices with their start and end apart: 13, of which 9 were waited for; matrix products, arithmetic and copies ran while one was open for 2% of the time, Pallas kernels for 0%

profile of v11, /device:TPU:1, one launch (start us, length us, event | category | flops | bytes accessed | tf_op | source)
XLA Modules:
  0.0 117.2 jit_solution(4414023842145944889)
XLA Ops:
  0.0 2.1 %local_state.1 = (f32[256,128]{1,0:T(8,128)}, bf16[1024,128]{1,0:T(8,128)(2,1)}, f32[128,128]{1,0:T(8,128)}) custom-call(bf16[1024,128]{1,0:T(8,128)(2,1)} %bitcast.33, bf16[1024,128]{1,0:T(8,128)(2,1)} %bitcast.29, f32[1,128]{1,0:T(1,128)} %gain_ref.1, f32[1,128]{1,0:T(1,128)} %norm_ref.1), custom_call_target="tpu_custom_call" | custom-call | tf_op jit(solution)/shard_map/local_state/pallas_call | solution.py:45
  2.2 8.8 %collective-permute-start = (f32[128,2048]{1,0:T(8,128)S(1)}, f32[128,2048]{1,0:T(8,128)S(1)}, u32[]{:S(2)}, u32[]{:S(2)}) collective-permute-start(f32[128,2048]{1,0:T(8,128)S(1)} %convert_element_type.12), channel_id=1, source_target_pairs={{0,1},{1,0},{2,3},{3,2},{4,5},{5,4},{6,7},{7,6},{8,9},{9,8},{10,11... | collective-permute-start | bytes 3145736 | tf_op jit(solution)/shard_map/ppermute | solution.py:191
  11.0 7.5 %all-to-all-start = ((f32[32,8,128]{2,1,0:T(8,128)}), f32[32,8,128]{2,1,0:T(8,128)S(1)}, u32[]{:S(2)}, u32[]{:S(2)}) async-start(f32[32,8,128]{2,1,0:T(8,128)} %bitcast.2), calls=%async_computation | async-start | bytes 262144 | tf_op jit(solution)/shard_map/all_to_all | solution.py:335
  18.8 8.9 %all-to-all-done.x_ref = f32[32,8,128]{2,1,0:T(8,128)S(1)} async-done(((f32[32,8,128]{2,1,0:T(8,128)}), f32[32,8,128]{2,1,0:T(8,128)S(1)}, u32[]{:S(2)}, u32[]{:S(2)}) %all-to-all-start) | async-done | bytes 131104 | tf_op jit(solution)/shard_map/all_to_all | solution.py:335
  27.7 0.7 prefix.1
  28.4 4.5 %all-to-all-start.1 = ((f32[32,8,128]{2,1,0:T(8,128)}), f32[32,8,128]{2,1,0:T(8,128)S(1)}, u32[]{:S(2)}, u32[]{:S(2)}) async-start(f32[32,8,128]{2,1,0:T(8,128)} %prefix.1), calls=%async_computation.1 | async-start | bytes 262144 | tf_op jit(solution)/shard_map/all_to_all | solution.py:345
  33.6 8.5 %all-to-all-done.1 = f32[32,8,128]{2,1,0:T(8,128)S(1)} async-done(((f32[32,8,128]{2,1,0:T(8,128)}), f32[32,8,128]{2,1,0:T(8,128)S(1)}, u32[]{:S(2)}, u32[]{:S(2)}) %all-to-all-start.1) | async-done | bytes 131104 | tf_op jit(solution)/shard_map/all_to_all | solution.py:345
  42.1 11.2 %solve.1.own_ref = f32[1024,128]{1,0:T(8,128)S(1)} custom-call(f32[1]{0:T(128)S(6)} %copy.8.reg_ref, s32[1]{0:T(128)} %bitcast.5.core_ref, bf16[1024,128]{1,0:T(8,128)(2,1)S(1)} %bitcast.32, bf16[1024,128]{1,0:T(8,128)(2,1)S(1)} %copy-done.3, bf16[1024,128]{1,0:T(8,128)(2,1)S(1)} %bitcast.30, f32[256,128]{1,0:T(8,128)S(1)} %bitcast.31, f32[128,128]{1,0:T(8,128)S(1)} %copy-done.4), custom_call_target="tpu_custom_call" | custom-call | flops 60000002048 | bytes 2097152 | tf_op jit(solution)/shard_map/solve/pallas_call | solution.py:168
  53.3 4.5 %collective-permute-start.1 = (f32[1024,128]{1,0:T(8,128)S(1)}, f32[1024,128]{1,0:T(8,128)S(1)}, u32[]{:S(2)}, u32[]{:S(2)}) collective-permute-start(f32[1024,128]{1,0:T(8,128)S(1)} %solve.1.own_ref), channel_id=1, source_target_pairs={{0,1},{1,0},{2,3},{3,2},{4,5},{5,4},{6,7},{7,6},{8,9},{9,8},{10,11... | collective-permute-start | bytes 1572872 | tf_op jit(solution)/shard_map/ppermute | solution.py:191
  57.8 1.5 %collective-permute-done.1.other_ref = f32[1024,128]{1,0:T(8,128)S(1)} collective-permute-done((f32[1024,128]{1,0:T(8,128)S(1)}, f32[1024,128]{1,0:T(8,128)S(1)}, u32[]{:S(2)}, u32[]{:S(2)}) %collective-permute-start.1) | collective-permute-done | bytes 524320 | tf_op jit(solution)/shard_map/ppermute | solution.py:191
  59.3 0.9 opening.1
  60.2 5.1 %collective-permute-start.2 = (f32[512,256]{1,0:T(8,128)S(1)}, f32[512,256]{1,0:T(8,128)S(1)}, u32[]{:S(2)}, u32[]{:S(2)}) collective-permute-start(f32[512,256]{1,0:T(8,128)S(1)} %get-tuple-element.32), channel_id=1, source_target_pairs={{0,2},{1,15},{2,4},{3,1},{4,6},{5,3},{6,8},{7,5},{8,10},{9,7},{10,... | collective-permute-start | bytes 1572872 | tf_op jit(solution)/shard_map/ppermute | solution.py:312
  65.3 3.0 %collective-permute-start.6 = (f32[512,256]{1,0:T(8,128)S(1)}, f32[512,256]{1,0:T(8,128)S(1)}, u32[]{:S(2)}, u32[]{:S(2)}) collective-permute-start(f32[512,256]{1,0:T(8,128)S(1)} %get-tuple-element.34), channel_id=1, source_target_pairs={{0,2},{1,15},{2,4},{3,1},{4,6},{5,3},{6,8},{7,5},{8,10},{9,7},{10,... | collective-permute-start | bytes 1572872 | tf_op jit(solution)/shard_map/ppermute | solution.py:312
  68.3 3.1 %collective-permute-done.2.sums_ref = f32[512,256]{1,0:T(8,128)S(1)} collective-permute-done((f32[512,256]{1,0:T(8,128)S(1)}, f32[512,256]{1,0:T(8,128)S(1)}, u32[]{:S(2)}, u32[]{:S(2)}) %collective-permute-start.2) | collective-permute-done | bytes 524320 | tf_op jit(solution)/shard_map/ppermute | solution.py:312
  71.6 5.0 %collective-permute-start.3 = (f32[512,256]{1,0:T(8,128)S(1)}, f32[512,256]{1,0:T(8,128)S(1)}, u32[]{:S(2)}, u32[]{:S(2)}) collective-permute-start(f32[512,256]{1,0:T(8,128)S(1)} %hop.2), channel_id=1, source_target_pairs={{0,2},{1,15},{2,4},{3,1},{4,6},{5,3},{6,8},{7,5},{8,10},{9,7},{10,... | collective-permute-start | bytes 1572872 | tf_op jit(solution)/shard_map/ppermute | solution.py:312
  77.1 5.0 %collective-permute-start.7 = (f32[512,256]{1,0:T(8,128)S(1)}, f32[512,256]{1,0:T(8,128)}, u32[]{:S(2)}, u32[]{:S(2)}) collective-permute-start(f32[512,256]{1,0:T(8,128)S(1)} %add.40), channel_id=1, source_target_pairs={{0,2},{1,15},{2,4},{3,1},{4,6},{5,3},{6,8},{7,5},{8,10},{9,7},{10,... | collective-permute-start | bytes 1572872 | tf_op jit(solution)/shard_map/ppermute | solution.py:312
  83.0 5.0 %collective-permute-start.4 = (f32[512,256]{1,0:T(8,128)S(1)}, f32[512,256]{1,0:T(8,128)S(1)}, u32[]{:S(2)}, u32[]{:S(2)}) collective-permute-start(f32[512,256]{1,0:T(8,128)S(1)} %hop.3), channel_id=1, source_target_pairs={{0,2},{1,15},{2,4},{3,1},{4,6},{5,3},{6,8},{7,5},{8,10},{9,7},{10,... | collective-permute-start | bytes 1572872 | tf_op jit(solution)/shard_map/ppermute | solution.py:312
  88.4 1.1 add.41
  89.5 5.1 %collective-permute-start.8 = (f32[512,256]{1,0:T(8,128)S(1)}, f32[512,256]{1,0:T(8,128)S(1)}, u32[]{:S(2)}, u32[]{:S(2)}) collective-permute-start(f32[512,256]{1,0:T(8,128)S(1)} %add.41), channel_id=1, source_target_pairs={{0,2},{1,15},{2,4},{3,1},{4,6},{5,3},{6,8},{7,5},{8,10},{9,7},{10,... | collective-permute-start | bytes 1572872 | tf_op jit(solution)/shard_map/ppermute | solution.py:312
  95.2 4.9 %collective-permute-start.5 = (f32[512,128]{1,0:T(8,128)S(1)}, f32[512,128]{1,0:T(8,128)S(1)}, u32[]{:S(2)}, u32[]{:S(2)}) collective-permute-start(f32[512,128]{1,0:T(8,128)S(1)} %slice_select_fusion.1), channel_id=1, source_target_pairs={{0,1},{1,0},{2,3},{3,2},{4,5},{5,4},{6,7},{7,6},{8,9},{9,8},{10,11... | collective-permute-start | bytes 786440 | tf_op jit(solution)/shard_map/ppermute | solution.py:191
  100.9 5.0 %collective-permute-start.9 = (f32[512,128]{1,0:T(8,128)S(1)}, f32[512,128]{1,0:T(8,128)S(1)}, u32[]{:S(2)}, u32[]{:S(2)}) collective-permute-start(f32[512,128]{1,0:T(8,128)S(1)} %get-tuple-element.36), channel_id=1, source_target_pairs={{0,2},{1,15},{2,4},{3,1},{4,6},{5,3},{6,8},{7,5},{8,10},{9,7},{10,... | collective-permute-start | bytes 786440 | tf_op jit(solution)/shard_map/ppermute | solution.py:321
  105.9 5.6 %collective-permute-start.10 = (f32[512,128]{1,0:T(8,128)S(1)}, f32[512,128]{1,0:T(8,128)S(1)}, u32[]{:S(2)}, u32[]{:S(2)}) collective-permute-start(f32[512,128]{1,0:T(8,128)S(1)} %get-tuple-element.35), channel_id=1, source_target_pairs={{0,3},{1,14},{2,5},{3,0},{4,7},{5,2},{6,9},{7,4},{8,11},{9,6},{10,... | collective-permute-start | bytes 786440 | tf_op jit(solution)/shard_map/ppermute | solution.py:320
  111.9 4.6 %collective-permute-done.10.two_b = f32[512,128]{1,0:T(8,128)S(1)} collective-permute-done((f32[512,128]{1,0:T(8,128)S(1)}, f32[512,128]{1,0:T(8,128)S(1)}, u32[]{:S(2)}, u32[]{:S(2)}) %collective-permute-start.10) | collective-permute-done | bytes 262176 | tf_op jit(solution)/shard_map/ppermute | solution.py:320
  116.4 0.8 finish.1
  (34 shorter events, 3.7 us)
Async XLA Ops:
  0.0 2.1 %copy-start = (bf16[128,2048]{1,0:T(8,128)(2,1)S(1)}, bf16[128,2048]{1,0:T(8,128)(2,1)}, u32[]{:S(2)}) copy-start(bf16[128,2048]{1,0:T(8,128)(2,1)} %own_ref) | copy-start | bytes 1572868
  2.2 16.4 %collective-permute-start = (f32[128,2048]{1,0:T(8,128)S(1)}, f32[128,2048]{1,0:T(8,128)S(1)}, u32[]{:S(2)}, u32[]{:S(2)}) collective-permute-start(f32[128,2048]{1,0:T(8,128)S(1)} %convert_element_type.12), channel_id=1, source_target_pairs={{0,1},{1,0},{2,3},{3,2},{4,5},{5,4},{6,7},{7,6},{8,9},{9,8},{10,11... | collective-permute-start | bytes 3145736 | tf_op jit(solution)/shard_map/ppermute | solution.py:191
  11.0 16.7 %all-to-all-start = ((f32[32,8,128]{2,1,0:T(8,128)}), f32[32,8,128]{2,1,0:T(8,128)S(1)}, u32[]{:S(2)}, u32[]{:S(2)}) async-start(f32[32,8,128]{2,1,0:T(8,128)} %bitcast.2), calls=%async_computation | async-start | bytes 262144 | tf_op jit(solution)/shard_map/all_to_all | solution.py:335
  18.6 23.5 %copy-start.3 = (bf16[1024,128]{1,0:T(8,128)(2,1)S(1)}, bf16[1024,128]{1,0:T(8,128)(2,1)}, u32[]{:S(2)}) copy-start(bf16[1024,128]{1,0:T(8,128)(2,1)} %get-tuple-element.25.k_ref) | copy-start | bytes 786436
  18.6 23.5 %copy-start.4 = (f32[128,128]{1,0:T(8,128)S(1)}, f32[128,128]{1,0:T(8,128)}, u32[]{:S(2)}) copy-start(f32[128,128]{1,0:T(8,128)} %get-tuple-element.27.column_ref) | copy-start | bytes 196612
  18.7 23.4 %copy-start.1 = (bf16[1024,1,128]{2,0,1:T(8,128)(2,1)S(1)}, bf16[1024,1,128]{2,0,1:T(8,128)(2,1)}, u32[]{:S(2)}) copy-start(bf16[1024,1,128]{2,0,1:T(8,128)(2,1)} %param.9) | copy-start | bytes 786436
  18.7 23.4 %copy-start.2 = (bf16[1024,1,128]{2,0,1:T(8,128)(2,1)S(1)}, bf16[1024,1,128]{2,0,1:T(8,128)(2,1)}, u32[]{:S(2)}) copy-start(bf16[1024,1,128]{2,0,1:T(8,128)(2,1)} %param.7) | copy-start | bytes 786436
  28.4 13.7 %all-to-all-start.1 = ((f32[32,8,128]{2,1,0:T(8,128)}), f32[32,8,128]{2,1,0:T(8,128)S(1)}, u32[]{:S(2)}, u32[]{:S(2)}) async-start(f32[32,8,128]{2,1,0:T(8,128)} %prefix.1), calls=%async_computation.1 | async-start | bytes 262144 | tf_op jit(solution)/shard_map/all_to_all | solution.py:345
  53.3 6.0 %collective-permute-start.1 = (f32[1024,128]{1,0:T(8,128)S(1)}, f32[1024,128]{1,0:T(8,128)S(1)}, u32[]{:S(2)}, u32[]{:S(2)}) collective-permute-start(f32[1024,128]{1,0:T(8,128)S(1)} %solve.1.own_ref), channel_id=1, source_target_pairs={{0,1},{1,0},{2,3},{3,2},{4,5},{5,4},{6,7},{7,6},{8,9},{9,8},{10,11... | collective-permute-start | bytes 1572872 | tf_op jit(solution)/shard_map/ppermute | solution.py:191
  60.2 11.2 %collective-permute-start.2 = (f32[512,256]{1,0:T(8,128)S(1)}, f32[512,256]{1,0:T(8,128)S(1)}, u32[]{:S(2)}, u32[]{:S(2)}) collective-permute-start(f32[512,256]{1,0:T(8,128)S(1)} %get-tuple-element.32), channel_id=1, source_target_pairs={{0,2},{1,15},{2,4},{3,1},{4,6},{5,3},{6,8},{7,5},{8,10},{9,7},{10,... | collective-permute-start | bytes 1572872 | tf_op jit(solution)/shard_map/ppermute | solution.py:312
  65.3 11.7 %collective-permute-start.6 = (f32[512,256]{1,0:T(8,128)S(1)}, f32[512,256]{1,0:T(8,128)S(1)}, u32[]{:S(2)}, u32[]{:S(2)}) collective-permute-start(f32[512,256]{1,0:T(8,128)S(1)} %get-tuple-element.34), channel_id=1, source_target_pairs={{0,2},{1,15},{2,4},{3,1},{4,6},{5,3},{6,8},{7,5},{8,10},{9,7},{10,... | collective-permute-start | bytes 1572872 | tf_op jit(solution)/shard_map/ppermute | solution.py:312
  71.6 11.1 %collective-permute-start.3 = (f32[512,256]{1,0:T(8,128)S(1)}, f32[512,256]{1,0:T(8,128)S(1)}, u32[]{:S(2)}, u32[]{:S(2)}) collective-permute-start(f32[512,256]{1,0:T(8,128)S(1)} %hop.2), channel_id=1, source_target_pairs={{0,2},{1,15},{2,4},{3,1},{4,6},{5,3},{6,8},{7,5},{8,10},{9,7},{10,... | collective-permute-start | bytes 1572872 | tf_op jit(solution)/shard_map/ppermute | solution.py:312
  77.1 11.3 %collective-permute-start.7 = (f32[512,256]{1,0:T(8,128)S(1)}, f32[512,256]{1,0:T(8,128)}, u32[]{:S(2)}, u32[]{:S(2)}) collective-permute-start(f32[512,256]{1,0:T(8,128)S(1)} %add.40), channel_id=1, source_target_pairs={{0,2},{1,15},{2,4},{3,1},{4,6},{5,3},{6,8},{7,5},{8,10},{9,7},{10,... | collective-permute-start | bytes 1572872 | tf_op jit(solution)/shard_map/ppermute | solution.py:312
  83.0 12.1 %collective-permute-start.4 = (f32[512,256]{1,0:T(8,128)S(1)}, f32[512,256]{1,0:T(8,128)S(1)}, u32[]{:S(2)}, u32[]{:S(2)}) collective-permute-start(f32[512,256]{1,0:T(8,128)S(1)} %hop.3), channel_id=1, source_target_pairs={{0,2},{1,15},{2,4},{3,1},{4,6},{5,3},{6,8},{7,5},{8,10},{9,7},{10,... | collective-permute-start | bytes 1572872 | tf_op jit(solution)/shard_map/ppermute | solution.py:312
  89.5 11.2 %collective-permute-start.8 = (f32[512,256]{1,0:T(8,128)S(1)}, f32[512,256]{1,0:T(8,128)S(1)}, u32[]{:S(2)}, u32[]{:S(2)}) collective-permute-start(f32[512,256]{1,0:T(8,128)S(1)} %add.41), channel_id=1, source_target_pairs={{0,2},{1,15},{2,4},{3,1},{4,6},{5,3},{6,8},{7,5},{8,10},{9,7},{10,... | collective-permute-start | bytes 1572872 | tf_op jit(solution)/shard_map/ppermute | solution.py:312
  95.2 16.6 %collective-permute-start.5 = (f32[512,128]{1,0:T(8,128)S(1)}, f32[512,128]{1,0:T(8,128)S(1)}, u32[]{:S(2)}, u32[]{:S(2)}) collective-permute-start(f32[512,128]{1,0:T(8,128)S(1)} %slice_select_fusion.1), channel_id=1, source_target_pairs={{0,1},{1,0},{2,3},{3,2},{4,5},{5,4},{6,7},{7,6},{8,9},{9,8},{10,11... | collective-permute-start | bytes 786440 | tf_op jit(solution)/shard_map/ppermute | solution.py:191
  100.9 11.0 %collective-permute-start.9 = (f32[512,128]{1,0:T(8,128)S(1)}, f32[512,128]{1,0:T(8,128)S(1)}, u32[]{:S(2)}, u32[]{:S(2)}) collective-permute-start(f32[512,128]{1,0:T(8,128)S(1)} %get-tuple-element.36), channel_id=1, source_target_pairs={{0,2},{1,15},{2,4},{3,1},{4,6},{5,3},{6,8},{7,5},{8,10},{9,7},{10,... | collective-permute-start | bytes 786440 | tf_op jit(solution)/shard_map/ppermute | solution.py:321
  105.9 10.6 %collective-permute-start.10 = (f32[512,128]{1,0:T(8,128)S(1)}, f32[512,128]{1,0:T(8,128)S(1)}, u32[]{:S(2)}, u32[]{:S(2)}) collective-permute-start(f32[512,128]{1,0:T(8,128)S(1)} %get-tuple-element.35), channel_id=1, source_target_pairs={{0,3},{1,14},{2,5},{3,0},{4,7},{5,2},{6,9},{7,4},{8,11},{9,6},{10,... | collective-permute-start | bytes 786440 | tf_op jit(solution)/shard_map/ppermute | solution.py:320

commit v12 on v11

--- a/solution.py
+++ b/solution.py
@@ -311,12 +311,8 @@
         for piece in (0, 1):
             flows[piece] = lax.ppermute(flows[piece], "head", ring)
             if away - piece > 1:
-                next_away = away - piece - 1
-                if piece == 0:
-                    flows[piece] = flows[piece] + part(piece, next_away)
-                else:
-                    chip = hops[next_away - 1].reshape(1)
-                    flows[piece] = hop(chip, flows[piece], rows[piece], weights)
+                chip = hops[away - piece - 2].reshape(1)
+                flows[piece] = hop(chip, flows[piece], rows[piece], weights)
     crossed = lax.ppermute(other_columns(flows[0]), "head", cross)
     same = lax.ppermute(own_columns(flows[0]), "head", ring)
     given = swapped(other_columns(flows[1]))
@@ -337,7 +333,7 @@
     far = lax.axis_size("head") // 4
     core = lax.rem(lax.axis_index("head").astype(jnp.uint32), jnp.uint32(2))
     starts = jnp.stack([chip_ahead(far), chip_ahead(far - 1)]).astype(jnp.int32)
-    hops = [chip_ahead(away).astype(jnp.int32) for away in (1, 2)]
+    hops = [chip_ahead(away).astype(jnp.int32) for away in range(1, far)]
     core = core.astype(jnp.int32)
     parts, weights, core, starts, hops = lax.optimization_barrier(
         (parts, weights, core, starts, hops)

time: 118 us -> 110 us (0.932)
  waiting for transfers between devices: 28.2 us -> 23.8 us
  starting transfers between devices: 69.2 us -> 64.9 us
    ppermute x1, waiting for transfers between devices: 4.58 us -> 0.01 us  [project(): crossed = lax.ppermute(other_columns(flows[0]), 'head', cross)]
    ppermute x1, starting transfers between devices: 5.02 us -> 2.98 us  [project(): same = lax.ppermute(own_columns(flows[0]), 'head', ring)]
    ppermute x3, starting transfers between devices: 18.2 us -> 16.5 us  [swapped(): return lax.ppermute(value, 'head', [(i, i ^ 1) for i in range(heads)])]
    add x3 -> x0, other arithmetic: 1.25 us -> none  [project(): flows[piece] = flows[piece] + part(piece, next_away)]
  transfers between devices with their start and end apart: 13 -> 13, of which waited for: 9 -> 9; matrix products, arithmetic and copies ran while one was open for 2% -> 3% of each run, Pallas kernels for 0% -> 1%
where the time goes in v12:
time: 110 us; the launch traced here: 109 us
  starting transfers between devices  64.9 us (59%)
  waiting for transfers between devices  23.8 us (22%)
  Pallas kernels  16.8 us (15%)
  matrix products  1.5 us (1%)
  other arithmetic  1.34 us (1%)
    ppermute x6, starting transfers between devices, project(): flows[piece] = lax.ppermute(flows[piece], 'head', ring)  28.2 us
    ppermute x3, starting transfers between devices, swapped(): return lax.ppermute(value, 'head', [(i, i ^ 1) for i in range(heads)])  16.5 us
    pallas_call x1, Pallas kernels, solve(): pl.pallas_call(solve_kernel, out_shape=jax.ShapeDtypeStruct((tokens, widt...  11.2 us
    all_to_all x1, waiting for transfers between devices, body(): parts = lax.all_to_all(state.reshape(devices, rows, width), 'seq', 0, 0)  8.93 us
    all_to_all x1, waiting for transfers between devices, body(): before = lax.all_to_all(exclusive(parts), 'seq', 0, 0)  8.54 us
    all_to_all x1, starting transfers between devices, body(): parts = lax.all_to_all(state.reshape(devices, rows, width), 'seq', 0, 0)  7.52 us
    ppermute x1, starting transfers between devices, project(): crossed = lax.ppermute(other_columns(flows[0]), 'head', cross)  5.09 us
    ppermute x6, waiting for transfers between devices, project(): flows[piece] = lax.ppermute(flows[piece], 'head', ring)  4.56 us
  transfers between devices with their start and end apart: 13, of which 9 were waited for; matrix products, arithmetic and copies ran while one was open for 3% of the time, Pallas kernels for 1%

profile of v12, /device:TPU:1, one launch (start us, length us, event | category | flops | bytes accessed | tf_op | source)
XLA Modules:
  0.0 109.3 jit_solution(13072817699575043516)
XLA Ops:
  0.0 2.1 %local_state.1 = (f32[256,128]{1,0:T(8,128)}, bf16[1024,128]{1,0:T(8,128)(2,1)}, f32[128,128]{1,0:T(8,128)}) custom-call(bf16[1024,128]{1,0:T(8,128)(2,1)} %bitcast.22, bf16[1024,128]{1,0:T(8,128)(2,1)} %bitcast.18, f32[1,128]{1,0:T(1,128)} %gain_ref.1, f32[1,128]{1,0:T(1,128)} %norm_ref.1), custom_call_target="tpu_custom_call" | custom-call | tf_op jit(solution)/shard_map/local_state/pallas_call | solution.py:45
  2.2 8.8 %collective-permute-start = (f32[128,2048]{1,0:T(8,128)S(1)}, f32[128,2048]{1,0:T(8,128)S(1)}, u32[]{:S(2)}, u32[]{:S(2)}) collective-permute-start(f32[128,2048]{1,0:T(8,128)S(1)} %convert_element_type.28), channel_id=1, source_target_pairs={{0,1},{1,0},{2,3},{3,2},{4,5},{5,4},{6,7},{7,6},{8,9},{9,8},{10,11... | collective-permute-start | bytes 3145736 | tf_op jit(solution)/shard_map/ppermute | solution.py:191
  11.0 7.5 %all-to-all-start = ((f32[32,8,128]{2,1,0:T(8,128)}), f32[32,8,128]{2,1,0:T(8,128)S(1)}, u32[]{:S(2)}, u32[]{:S(2)}) async-start(f32[32,8,128]{2,1,0:T(8,128)} %bitcast.2), calls=%async_computation | async-start | bytes 262144 | tf_op jit(solution)/shard_map/all_to_all | solution.py:331
  18.8 8.9 %all-to-all-done.x_ref = f32[32,8,128]{2,1,0:T(8,128)S(1)} async-done(((f32[32,8,128]{2,1,0:T(8,128)}), f32[32,8,128]{2,1,0:T(8,128)S(1)}, u32[]{:S(2)}, u32[]{:S(2)}) %all-to-all-start) | async-done | bytes 131104 | tf_op jit(solution)/shard_map/all_to_all | solution.py:331
  27.7 0.7 prefix.1
  28.4 4.5 %all-to-all-start.1 = ((f32[32,8,128]{2,1,0:T(8,128)}), f32[32,8,128]{2,1,0:T(8,128)S(1)}, u32[]{:S(2)}, u32[]{:S(2)}) async-start(f32[32,8,128]{2,1,0:T(8,128)} %prefix.1), calls=%async_computation.1 | async-start | bytes 262144 | tf_op jit(solution)/shard_map/all_to_all | solution.py:341
  33.6 8.5 %all-to-all-done.1 = f32[32,8,128]{2,1,0:T(8,128)S(1)} async-done(((f32[32,8,128]{2,1,0:T(8,128)}), f32[32,8,128]{2,1,0:T(8,128)S(1)}, u32[]{:S(2)}, u32[]{:S(2)}) %all-to-all-start.1) | async-done | bytes 131104 | tf_op jit(solution)/shard_map/all_to_all | solution.py:341
  42.1 11.2 %solve.1.own_ref = f32[1024,128]{1,0:T(8,128)S(1)} custom-call(f32[1]{0:T(128)S(6)} %copy.8.reg_ref, s32[1]{0:T(128)} %bitcast.5.core_ref, bf16[1024,128]{1,0:T(8,128)(2,1)S(1)} %bitcast.21, bf16[1024,128]{1,0:T(8,128)(2,1)S(1)} %copy-done.3, bf16[1024,128]{1,0:T(8,128)(2,1)S(1)} %bitcast.19, f32[256,128]{1,0:T(8,128)S(1)} %bitcast.20, f32[128,128]{1,0:T(8,128)S(1)} %copy-done.4), custom_call_target="tpu_custom_call" | custom-call | flops 60000002048 | bytes 2097152 | tf_op jit(solution)/shard_map/solve/pallas_call | solution.py:168
  53.3 4.5 %collective-permute-start.1 = (f32[1024,128]{1,0:T(8,128)S(1)}, f32[1024,128]{1,0:T(8,128)S(1)}, u32[]{:S(2)}, u32[]{:S(2)}) collective-permute-start(f32[1024,128]{1,0:T(8,128)S(1)} %solve.1.own_ref), channel_id=1, source_target_pairs={{0,1},{1,0},{2,3},{3,2},{4,5},{5,4},{6,7},{7,6},{8,9},{9,8},{10,11... | collective-permute-start | bytes 1572872 | tf_op jit(solution)/shard_map/ppermute | solution.py:191
  57.8 1.5 %collective-permute-done.1.other_ref = f32[1024,128]{1,0:T(8,128)S(1)} collective-permute-done((f32[1024,128]{1,0:T(8,128)S(1)}, f32[1024,128]{1,0:T(8,128)S(1)}, u32[]{:S(2)}, u32[]{:S(2)}) %collective-permute-start.1) | collective-permute-done | bytes 524320 | tf_op jit(solution)/shard_map/ppermute | solution.py:191
  59.3 0.9 opening.1
  60.2 5.1 %collective-permute-start.6 = (f32[512,256]{1,0:T(8,128)S(1)}, f32[512,256]{1,0:T(8,128)S(1)}, u32[]{:S(2)}, u32[]{:S(2)}) collective-permute-start(f32[512,256]{1,0:T(8,128)S(1)} %get-tuple-element.36), channel_id=1, source_target_pairs={{0,2},{1,15},{2,4},{3,1},{4,6},{5,3},{6,8},{7,5},{8,10},{9,7},{10,... | collective-permute-start | bytes 1572872 | tf_op jit(solution)/shard_map/ppermute | solution.py:312
  65.3 3.0 %collective-permute-start.2 = (f32[512,256]{1,0:T(8,128)S(1)}, f32[512,256]{1,0:T(8,128)S(1)}, u32[]{:S(2)}, u32[]{:S(2)}) collective-permute-start(f32[512,256]{1,0:T(8,128)S(1)} %get-tuple-element.33), channel_id=1, source_target_pairs={{0,2},{1,15},{2,4},{3,1},{4,6},{5,3},{6,8},{7,5},{8,10},{9,7},{10,... | collective-permute-start | bytes 1572872 | tf_op jit(solution)/shard_map/ppermute | solution.py:312
  68.3 3.1 %collective-permute-done.6.sums_ref = f32[512,256]{1,0:T(8,128)S(1)} collective-permute-done((f32[512,256]{1,0:T(8,128)S(1)}, f32[512,256]{1,0:T(8,128)S(1)}, u32[]{:S(2)}, u32[]{:S(2)}) %collective-permute-start.6) | collective-permute-done | bytes 524320 | tf_op jit(solution)/shard_map/ppermute | solution.py:312
  71.6 5.0 %collective-permute-start.7 = (f32[512,256]{1,0:T(8,128)S(1)}, f32[512,256]{1,0:T(8,128)S(1)}, u32[]{:S(2)}, u32[]{:S(2)}) collective-permute-start(f32[512,256]{1,0:T(8,128)S(1)} %hop.7), channel_id=1, source_target_pairs={{0,2},{1,15},{2,4},{3,1},{4,6},{5,3},{6,8},{7,5},{8,10},{9,7},{10,... | collective-permute-start | bytes 1572872 | tf_op jit(solution)/shard_map/ppermute | solution.py:312
  77.2 5.0 %collective-permute-start.3 = (f32[512,256]{1,0:T(8,128)S(1)}, f32[512,256]{1,0:T(8,128)S(1)}, u32[]{:S(2)}, u32[]{:S(2)}) collective-permute-start(f32[512,256]{1,0:T(8,128)S(1)} %hop.5), channel_id=1, source_target_pairs={{0,2},{1,15},{2,4},{3,1},{4,6},{5,3},{6,8},{7,5},{8,10},{9,7},{10,... | collective-permute-start | bytes 1572872 | tf_op jit(solution)/shard_map/ppermute | solution.py:312
  83.0 5.0 %collective-permute-start.8 = (f32[512,256]{1,0:T(8,128)S(1)}, f32[512,256]{1,0:T(8,128)S(1)}, u32[]{:S(2)}, u32[]{:S(2)}) collective-permute-start(f32[512,256]{1,0:T(8,128)S(1)} %hop.8), channel_id=1, source_target_pairs={{0,2},{1,15},{2,4},{3,1},{4,6},{5,3},{6,8},{7,5},{8,10},{9,7},{10,... | collective-permute-start | bytes 1572872 | tf_op jit(solution)/shard_map/ppermute | solution.py:312
  88.6 5.0 %collective-permute-start.4 = (f32[512,256]{1,0:T(8,128)S(1)}, f32[512,256]{1,0:T(8,128)}, u32[]{:S(2)}, u32[]{:S(2)}) collective-permute-start(f32[512,256]{1,0:T(8,128)S(1)} %hop.6), channel_id=1, source_target_pairs={{0,2},{1,15},{2,4},{3,1},{4,6},{5,3},{6,8},{7,5},{8,10},{9,7},{10,... | collective-permute-start | bytes 1572872 | tf_op jit(solution)/shard_map/ppermute | solution.py:312
  94.4 5.1 %collective-permute-start.10 = (f32[512,128]{1,0:T(8,128)S(1)}, f32[512,128]{1,0:T(8,128)S(1)}, u32[]{:S(2)}, u32[]{:S(2)}) collective-permute-start(f32[512,128]{1,0:T(8,128)S(1)} %get-tuple-element.37), channel_id=1, source_target_pairs={{0,3},{1,14},{2,5},{3,0},{4,7},{5,2},{6,9},{7,4},{8,11},{9,6},{10,... | collective-permute-start | bytes 786440 | tf_op jit(solution)/shard_map/ppermute | solution.py:316
  99.5 3.0 %collective-permute-start.9 = (f32[512,128]{1,0:T(8,128)S(1)}, f32[512,128]{1,0:T(8,128)S(1)}, u32[]{:S(2)}, u32[]{:S(2)}) collective-permute-start(f32[512,128]{1,0:T(8,128)S(1)} %get-tuple-element.38), channel_id=1, source_target_pairs={{0,2},{1,15},{2,4},{3,1},{4,6},{5,3},{6,8},{7,5},{8,10},{9,7},{10,... | collective-permute-start | bytes 786440 | tf_op jit(solution)/shard_map/ppermute | solution.py:317
  102.5 1.1 slice_select_fusion.1
  103.6 3.2 %collective-permute-start.5 = (f32[512,128]{1,0:T(8,128)S(1)}, f32[512,128]{1,0:T(8,128)S(1)}, u32[]{:S(2)}, u32[]{:S(2)}) collective-permute-start(f32[512,128]{1,0:T(8,128)S(1)} %slice_select_fusion.1), channel_id=1, source_target_pairs={{0,1},{1,0},{2,3},{3,2},{4,5},{5,4},{6,7},{7,6},{8,9},{9,8},{10,11... | collective-permute-start | bytes 786440 | tf_op jit(solution)/shard_map/ppermute | solution.py:191
  106.8 1.3 %convolution_add_fusion = f32[512,256]{1,0:T(8,128)S(1)} fusion(f32[512,256]{1,0:T(8,128)} %collective-permute-done.4, bf16[512,256]{1,0:T(8,128)(2,1)S(1)} %get-tuple-element.34.rows_ref, bf16[8,256,256]{2,1,0:T(8,128)(2,1)S(1)} %join_weight.1.weights_ref, u32[]{:T(128)S(6)} %rem.32), kind=kOutput, calls=%fused_computation | convolution fusion | flops 67239936 | bytes 1441796 | tf_op jit(solution)/shard_map/dot_general | solution.py:302
  108.5 0.8 finish.1
  (31 shorter events, 3.5 us)
Async XLA Ops:
  0.0 2.1 %copy-start = (bf16[128,2048]{1,0:T(8,128)(2,1)S(1)}, bf16[128,2048]{1,0:T(8,128)(2,1)}, u32[]{:S(2)}) copy-start(bf16[128,2048]{1,0:T(8,128)(2,1)} %own_ref) | copy-start | bytes 1572868
  2.2 16.4 %collective-permute-start = (f32[128,2048]{1,0:T(8,128)S(1)}, f32[128,2048]{1,0:T(8,128)S(1)}, u32[]{:S(2)}, u32[]{:S(2)}) collective-permute-start(f32[128,2048]{1,0:T(8,128)S(1)} %convert_element_type.28), channel_id=1, source_target_pairs={{0,1},{1,0},{2,3},{3,2},{4,5},{5,4},{6,7},{7,6},{8,9},{9,8},{10,11... | collective-permute-start | bytes 3145736 | tf_op jit(solution)/shard_map/ppermute | solution.py:191
  11.0 16.7 %all-to-all-start = ((f32[32,8,128]{2,1,0:T(8,128)}), f32[32,8,128]{2,1,0:T(8,128)S(1)}, u32[]{:S(2)}, u32[]{:S(2)}) async-start(f32[32,8,128]{2,1,0:T(8,128)} %bitcast.2), calls=%async_computation | async-start | bytes 262144 | tf_op jit(solution)/shard_map/all_to_all | solution.py:331
  18.6 23.5 %copy-start.3 = (bf16[1024,128]{1,0:T(8,128)(2,1)S(1)}, bf16[1024,128]{1,0:T(8,128)(2,1)}, u32[]{:S(2)}) copy-start(bf16[1024,128]{1,0:T(8,128)(2,1)} %get-tuple-element.26.k_ref) | copy-start | bytes 786436
  18.6 23.5 %copy-start.4 = (f32[128,128]{1,0:T(8,128)S(1)}, f32[128,128]{1,0:T(8,128)}, u32[]{:S(2)}) copy-start(f32[128,128]{1,0:T(8,128)} %get-tuple-element.28.column_ref) | copy-start | bytes 196612
  18.7 23.4 %copy-start.1 = (bf16[1024,1,128]{2,0,1:T(8,128)(2,1)S(1)}, bf16[1024,1,128]{2,0,1:T(8,128)(2,1)}, u32[]{:S(2)}) copy-start(bf16[1024,1,128]{2,0,1:T(8,128)(2,1)} %param.9) | copy-start | bytes 786436
  18.7 23.4 %copy-start.2 = (bf16[1024,1,128]{2,0,1:T(8,128)(2,1)S(1)}, bf16[1024,1,128]{2,0,1:T(8,128)(2,1)}, u32[]{:S(2)}) copy-start(bf16[1024,1,128]{2,0,1:T(8,128)(2,1)} %param.7) | copy-start | bytes 786436
  28.4 13.7 %all-to-all-start.1 = ((f32[32,8,128]{2,1,0:T(8,128)}), f32[32,8,128]{2,1,0:T(8,128)S(1)}, u32[]{:S(2)}, u32[]{:S(2)}) async-start(f32[32,8,128]{2,1,0:T(8,128)} %prefix.1), calls=%async_computation.1 | async-start | bytes 262144 | tf_op jit(solution)/shard_map/all_to_all | solution.py:341
  53.3 6.0 %collective-permute-start.1 = (f32[1024,128]{1,0:T(8,128)S(1)}, f32[1024,128]{1,0:T(8,128)S(1)}, u32[]{:S(2)}, u32[]{:S(2)}) collective-permute-start(f32[1024,128]{1,0:T(8,128)S(1)} %solve.1.own_ref), channel_id=1, source_target_pairs={{0,1},{1,0},{2,3},{3,2},{4,5},{5,4},{6,7},{7,6},{8,9},{9,8},{10,11... | collective-permute-start | bytes 1572872 | tf_op jit(solution)/shard_map/ppermute | solution.py:191
  60.2 11.2 %collective-permute-start.6 = (f32[512,256]{1,0:T(8,128)S(1)}, f32[512,256]{1,0:T(8,128)S(1)}, u32[]{:S(2)}, u32[]{:S(2)}) collective-permute-start(f32[512,256]{1,0:T(8,128)S(1)} %get-tuple-element.36), channel_id=1, source_target_pairs={{0,2},{1,15},{2,4},{3,1},{4,6},{5,3},{6,8},{7,5},{8,10},{9,7},{10,... | collective-permute-start | bytes 1572872 | tf_op jit(solution)/shard_map/ppermute | solution.py:312
  65.3 11.7 %collective-permute-start.2 = (f32[512,256]{1,0:T(8,128)S(1)}, f32[512,256]{1,0:T(8,128)S(1)}, u32[]{:S(2)}, u32[]{:S(2)}) collective-permute-start(f32[512,256]{1,0:T(8,128)S(1)} %get-tuple-element.33), channel_id=1, source_target_pairs={{0,2},{1,15},{2,4},{3,1},{4,6},{5,3},{6,8},{7,5},{8,10},{9,7},{10,... | collective-permute-start | bytes 1572872 | tf_op jit(solution)/shard_map/ppermute | solution.py:312
  71.6 11.1 %collective-permute-start.7 = (f32[512,256]{1,0:T(8,128)S(1)}, f32[512,256]{1,0:T(8,128)S(1)}, u32[]{:S(2)}, u32[]{:S(2)}) collective-permute-start(f32[512,256]{1,0:T(8,128)S(1)} %hop.7), channel_id=1, source_target_pairs={{0,2},{1,15},{2,4},{3,1},{4,6},{5,3},{6,8},{7,5},{8,10},{9,7},{10,... | collective-permute-start | bytes 1572872 | tf_op jit(solution)/shard_map/ppermute | solution.py:312
  77.2 11.1 %collective-permute-start.3 = (f32[512,256]{1,0:T(8,128)S(1)}, f32[512,256]{1,0:T(8,128)S(1)}, u32[]{:S(2)}, u32[]{:S(2)}) collective-permute-start(f32[512,256]{1,0:T(8,128)S(1)} %hop.5), channel_id=1, source_target_pairs={{0,2},{1,15},{2,4},{3,1},{4,6},{5,3},{6,8},{7,5},{8,10},{9,7},{10,... | collective-permute-start | bytes 1572872 | tf_op jit(solution)/shard_map/ppermute | solution.py:312
  83.0 11.1 %collective-permute-start.8 = (f32[512,256]{1,0:T(8,128)S(1)}, f32[512,256]{1,0:T(8,128)S(1)}, u32[]{:S(2)}, u32[]{:S(2)}) collective-permute-start(f32[512,256]{1,0:T(8,128)S(1)} %hop.8), channel_id=1, source_target_pairs={{0,2},{1,15},{2,4},{3,1},{4,6},{5,3},{6,8},{7,5},{8,10},{9,7},{10,... | collective-permute-start | bytes 1572872 | tf_op jit(solution)/shard_map/ppermute | solution.py:312
  88.6 13.9 %collective-permute-start.4 = (f32[512,256]{1,0:T(8,128)S(1)}, f32[512,256]{1,0:T(8,128)}, u32[]{:S(2)}, u32[]{:S(2)}) collective-permute-start(f32[512,256]{1,0:T(8,128)S(1)} %hop.6), channel_id=1, source_target_pairs={{0,2},{1,15},{2,4},{3,1},{4,6},{5,3},{6,8},{7,5},{8,10},{9,7},{10,... | collective-permute-start | bytes 1572872 | tf_op jit(solution)/shard_map/ppermute | solution.py:312
  94.4 13.8 %collective-permute-start.10 = (f32[512,128]{1,0:T(8,128)S(1)}, f32[512,128]{1,0:T(8,128)S(1)}, u32[]{:S(2)}, u32[]{:S(2)}) collective-permute-start(f32[512,128]{1,0:T(8,128)S(1)} %get-tuple-element.37), channel_id=1, source_target_pairs={{0,3},{1,14},{2,5},{3,0},{4,7},{5,2},{6,9},{7,4},{8,11},{9,6},{10,... | collective-permute-start | bytes 786440 | tf_op jit(solution)/shard_map/ppermute | solution.py:316
  99.5 9.0 %collective-permute-start.9 = (f32[512,128]{1,0:T(8,128)S(1)}, f32[512,128]{1,0:T(8,128)S(1)}, u32[]{:S(2)}, u32[]{:S(2)}) collective-permute-start(f32[512,128]{1,0:T(8,128)S(1)} %get-tuple-element.38), channel_id=1, source_target_pairs={{0,2},{1,15},{2,4},{3,1},{4,6},{5,3},{6,8},{7,5},{8,10},{9,7},{10,... | collective-permute-start | bytes 786440 | tf_op jit(solution)/shard_map/ppermute | solution.py:317
  103.6 4.6 %collective-permute-start.5 = (f32[512,128]{1,0:T(8,128)S(1)}, f32[512,128]{1,0:T(8,128)S(1)}, u32[]{:S(2)}, u32[]{:S(2)}) collective-permute-start(f32[512,128]{1,0:T(8,128)S(1)} %slice_select_fusion.1), channel_id=1, source_target_pairs={{0,1},{1,0},{2,3},{3,2},{4,5},{5,4},{6,7},{7,6},{8,9},{9,8},{10,11... | collective-permute-start | bytes 786440 | tf_op jit(solution)/shard_map/ppermute | solution.py:191

commit v13 on v12

--- a/solution.py
+++ b/solution.py
@@ -255,6 +255,28 @@
     )(chip, sums, rows, weights)
 
 
+def turn_kernel(starts_ref, sums_ref, rows_ref, weights_ref, own_ref, other_ref):
+    width = own_ref.shape[1]
+    sums = sums_ref[...]
+    total = sums + mm(rows_ref[...], weights_ref[starts_ref[2]])
+    first = starts_ref[3] == 0
+    own_ref[...] = jnp.where(first, total[:, :width], total[:, width:])
+    other_ref[...] = jnp.where(first, sums[:, width:], sums[:, :width])
+
+
+def turn(starts, sums, rows, weights):
+    tokens, double = sums.shape
+    vmem = pl.BlockSpec(memory_space=pltpu.VMEM)
+    return pl.pallas_call(
+        turn_kernel,
+        out_shape=(jax.ShapeDtypeStruct((tokens, double // 2), F32),) * 2,
+        in_specs=[pl.BlockSpec(memory_space=pltpu.SMEM), vmem, vmem, vmem],
+        out_specs=(vmem, vmem),
+        compiler_params=small(8),
+        name="turn",
+    )(starts, sums, rows, weights)
+
+
 def finish_kernel(core_ref, one_a, one_b, two_a, two_b, out_ref):
     half = one_a.shape[0]
     one = one_a[...] + one_b[...]
@@ -315,9 +337,10 @@
                 flows[piece] = hop(chip, flows[piece], rows[piece], weights)
     crossed = lax.ppermute(other_columns(flows[0]), "head", cross)
     same = lax.ppermute(own_columns(flows[0]), "head", ring)
-    given = swapped(other_columns(flows[1]))
+    kept, other = turn(starts, flows[1], rows[1], weights)
+    given = swapped(other)
     first = (own_columns(part(0, 0)) + given, same)
-    second = (own_columns(part(1, 0) + flows[1]), crossed)
+    second = (kept, crossed)
     return finish(core.reshape(1), first, second)
 
 
@@ -332,7 +355,8 @@
     weights = join_weight(out_weight, swapped(out_weight.astype(F32)))
     far = lax.axis_size("head") // 4
     core = lax.rem(lax.axis_index("head").astype(jnp.uint32), jnp.uint32(2))
-    starts = jnp.stack([chip_ahead(far), chip_ahead(far - 1)]).astype(jnp.int32)
+    starts = [chip_ahead(far), chip_ahead(far - 1), chip_ahead(0), core]
+    starts = jnp.stack(starts).astype(jnp.int32)
     hops = [chip_ahead(away).astype(jnp.int32) for away in range(1, far)]
     core = core.astype(jnp.int32)
     parts, weights, core, starts, hops = lax.optimization_barrier(

time: 110 us -> 115 us (1.045)
  waiting for transfers between devices: 23.8 us -> 29.5 us
  Pallas kernels: 16.8 us -> 18.1 us
  matrix products: 1.5 us -> 0.23 us
    ppermute x1, waiting for transfers between devices: 0.29 us -> 3.49 us  [project(): same = lax.ppermute(own_columns(flows[0]), 'head', ring)]
    ppermute x3, starting transfers between devices: 16.5 us -> 19.3 us  [swapped(): return lax.ppermute(value, 'head', [(i, i ^ 1) for i in range(heads)])]
    ppermute x1, waiting for transfers between devices: 0.01 us -> 2.22 us  [project(): crossed = lax.ppermute(other_columns(flows[0]), 'head', cross)]
    ppermute x1, starting transfers between devices: 5.09 us -> 3.4 us  [project(): crossed = lax.ppermute(other_columns(flows[0]), 'head', cross)]
    pallas_call x0 -> x1, Pallas kernels: none -> 1.28 us  [turn(): pl.pallas_call(turn_kernel, out_shape=(jax.ShapeDtypeStruct((tokens, doub...]
    dot_general x2 -> x1, matrix products: 1.5 us -> 0.23 us  [part(): return jnp.dot(rows[piece], columns, preferred_element_type=F32)]
  transfers between devices with their start and end apart: 13 -> 13, of which waited for: 9 -> 10; matrix products, arithmetic and copies ran while one was open for 3% -> 0% of each run, Pallas kernels for 1% -> 2%
where the time goes in v13:
time: 115 us
  starting transfers between devices  65.9 us (57%)
  waiting for transfers between devices  29.5 us (26%)
  Pallas kernels  18.1 us (16%)
    ppermute x6, starting transfers between devices, project(): flows[piece] = lax.ppermute(flows[piece], 'head', ring)  28.2 us
    ppermute x3, starting transfers between devices, swapped(): return lax.ppermute(value, 'head', [(i, i ^ 1) for i in range(heads)])  19.3 us
    pallas_call x1, Pallas kernels, solve(): pl.pallas_call(solve_kernel, out_shape=jax.ShapeDtypeStruct((tokens, widt...  11.2 us
    all_to_all x1, waiting for transfers between devices, body(): parts = lax.all_to_all(state.reshape(devices, rows, width), 'seq', 0, 0)  8.92 us
    all_to_all x1, waiting for transfers between devices, body(): before = lax.all_to_all(exclusive(parts), 'seq', 0, 0)  8.54 us
    all_to_all x1, starting transfers between devices, body(): parts = lax.all_to_all(state.reshape(devices, rows, width), 'seq', 0, 0)  7.52 us
    ppermute x6, waiting for transfers between devices, project(): flows[piece] = lax.ppermute(flows[piece], 'head', ring)  4.81 us
    all_to_all x1, starting transfers between devices, body(): before = lax.all_to_all(exclusive(parts), 'seq', 0, 0)  4.54 us
  transfers between devices with their start and end apart: 13, of which 10 were waited for; matrix products, arithmetic and copies ran while one was open for 0% of the time, Pallas kernels for 2%

profile of v13, /device:TPU:1, one launch (start us, length us, event | category | flops | bytes accessed | tf_op | source)
XLA Modules:
  0.0 114.8 jit_solution(7754920709761695416)
XLA Ops:
  0.0 2.1 %local_state.1 = (f32[256,128]{1,0:T(8,128)}, bf16[1024,128]{1,0:T(8,128)(2,1)}, f32[128,128]{1,0:T(8,128)}) custom-call(bf16[1024,128]{1,0:T(8,128)(2,1)} %bitcast.21, bf16[1024,128]{1,0:T(8,128)(2,1)} %bitcast.17, f32[1,128]{1,0:T(1,128)} %gain_ref.1, f32[1,128]{1,0:T(1,128)} %norm_ref.1), custom_call_target="tpu_custom_call" | custom-call | tf_op jit(solution)/shard_map/local_state/pallas_call | solution.py:45
  2.2 8.8 %collective-permute-start = (f32[128,2048]{1,0:T(8,128)S(1)}, f32[128,2048]{1,0:T(8,128)S(1)}, u32[]{:S(2)}, u32[]{:S(2)}) collective-permute-start(f32[128,2048]{1,0:T(8,128)S(1)} %convert_element_type.28), channel_id=1, source_target_pairs={{0,1},{1,0},{2,3},{3,2},{4,5},{5,4},{6,7},{7,6},{8,9},{9,8},{10,11... | collective-permute-start | bytes 3145736 | tf_op jit(solution)/shard_map/ppermute | solution.py:191
  11.0 7.5 %all-to-all-start = ((f32[32,8,128]{2,1,0:T(8,128)}), f32[32,8,128]{2,1,0:T(8,128)S(1)}, u32[]{:S(2)}, u32[]{:S(2)}) async-start(f32[32,8,128]{2,1,0:T(8,128)} %bitcast.2), calls=%async_computation | async-start | bytes 262144 | tf_op jit(solution)/shard_map/all_to_all | solution.py:354
  18.8 8.9 %all-to-all-done.x_ref = f32[32,8,128]{2,1,0:T(8,128)S(1)} async-done(((f32[32,8,128]{2,1,0:T(8,128)}), f32[32,8,128]{2,1,0:T(8,128)S(1)}, u32[]{:S(2)}, u32[]{:S(2)}) %all-to-all-start) | async-done | bytes 131104 | tf_op jit(solution)/shard_map/all_to_all | solution.py:354
  28.4 4.5 %all-to-all-start.1 = ((f32[32,8,128]{2,1,0:T(8,128)}), f32[32,8,128]{2,1,0:T(8,128)S(1)}, u32[]{:S(2)}, u32[]{:S(2)}) async-start(f32[32,8,128]{2,1,0:T(8,128)} %prefix.1), calls=%async_computation.1 | async-start | bytes 262144 | tf_op jit(solution)/shard_map/all_to_all | solution.py:365
  33.6 8.5 %all-to-all-done.1 = f32[32,8,128]{2,1,0:T(8,128)S(1)} async-done(((f32[32,8,128]{2,1,0:T(8,128)}), f32[32,8,128]{2,1,0:T(8,128)S(1)}, u32[]{:S(2)}, u32[]{:S(2)}) %all-to-all-start.1) | async-done | bytes 131104 | tf_op jit(solution)/shard_map/all_to_all | solution.py:365
  42.1 11.2 %solve.1.own_ref = f32[1024,128]{1,0:T(8,128)S(1)} custom-call(f32[1]{0:T(128)S(6)} %copy.8.reg_ref, s32[1]{0:T(128)} %bitcast.7.core_ref, bf16[1024,128]{1,0:T(8,128)(2,1)S(1)} %bitcast.20, bf16[1024,128]{1,0:T(8,128)(2,1)S(1)} %copy-done.3, bf16[1024,128]{1,0:T(8,128)(2,1)S(1)} %bitcast.18, f32[256,128]{1,0:T(8,128)S(1)} %bitcast.19, f32[128,128]{1,0:T(8,128)S(1)} %copy-done.4), custom_call_target="tpu_custom_call" | custom-call | flops 60000002048 | bytes 2097152 | tf_op jit(solution)/shard_map/solve/pallas_call | solution.py:168
  53.3 4.5 %collective-permute-start.1 = (f32[1024,128]{1,0:T(8,128)S(1)}, f32[1024,128]{1,0:T(8,128)S(1)}, u32[]{:S(2)}, u32[]{:S(2)}) collective-permute-start(f32[1024,128]{1,0:T(8,128)S(1)} %solve.1.own_ref), channel_id=1, source_target_pairs={{0,1},{1,0},{2,3},{3,2},{4,5},{5,4},{6,7},{7,6},{8,9},{9,8},{10,11... | collective-permute-start | bytes 1572872 | tf_op jit(solution)/shard_map/ppermute | solution.py:191
  57.8 1.5 %collective-permute-done.1.other_ref = f32[1024,128]{1,0:T(8,128)S(1)} collective-permute-done((f32[1024,128]{1,0:T(8,128)S(1)}, f32[1024,128]{1,0:T(8,128)S(1)}, u32[]{:S(2)}, u32[]{:S(2)}) %collective-permute-start.1) | collective-permute-done | bytes 524320 | tf_op jit(solution)/shard_map/ppermute | solution.py:191
  59.3 0.9 opening.1
  60.1 5.1 %collective-permute-start.2 = (f32[512,256]{1,0:T(8,128)S(1)}, f32[512,256]{1,0:T(8,128)S(1)}, u32[]{:S(2)}, u32[]{:S(2)}) collective-permute-start(f32[512,256]{1,0:T(8,128)S(1)} %get-tuple-element.35), channel_id=1, source_target_pairs={{0,2},{1,15},{2,4},{3,1},{4,6},{5,3},{6,8},{7,5},{8,10},{9,7},{10,... | collective-permute-start | bytes 1572872 | tf_op jit(solution)/shard_map/ppermute | solution.py:334
  65.3 3.0 %collective-permute-start.6 = (f32[512,256]{1,0:T(8,128)S(1)}, f32[512,256]{1,0:T(8,128)S(1)}, u32[]{:S(2)}, u32[]{:S(2)}) collective-permute-start(f32[512,256]{1,0:T(8,128)S(1)} %get-tuple-element.39), channel_id=1, source_target_pairs={{0,2},{1,15},{2,4},{3,1},{4,6},{5,3},{6,8},{7,5},{8,10},{9,7},{10,... | collective-permute-start | bytes 1572872 | tf_op jit(solution)/shard_map/ppermute | solution.py:334
  68.2 3.1 %collective-permute-done.2.sums_ref = f32[512,256]{1,0:T(8,128)S(1)} collective-permute-done((f32[512,256]{1,0:T(8,128)S(1)}, f32[512,256]{1,0:T(8,128)S(1)}, u32[]{:S(2)}, u32[]{:S(2)}) %collective-permute-start.2) | collective-permute-done | bytes 524320 | tf_op jit(solution)/shard_map/ppermute | solution.py:334
  71.6 5.0 %collective-permute-start.3 = (f32[512,256]{1,0:T(8,128)S(1)}, f32[512,256]{1,0:T(8,128)S(1)}, u32[]{:S(2)}, u32[]{:S(2)}) collective-permute-start(f32[512,256]{1,0:T(8,128)S(1)} %hop.5), channel_id=1, source_target_pairs={{0,2},{1,15},{2,4},{3,1},{4,6},{5,3},{6,8},{7,5},{8,10},{9,7},{10,... | collective-permute-start | bytes 1572872 | tf_op jit(solution)/shard_map/ppermute | solution.py:334
  77.2 5.0 %collective-permute-start.7 = (f32[512,256]{1,0:T(8,128)S(1)}, f32[512,256]{1,0:T(8,128)S(1)}, u32[]{:S(2)}, u32[]{:S(2)}) collective-permute-start(f32[512,256]{1,0:T(8,128)S(1)} %hop.7), channel_id=1, source_target_pairs={{0,2},{1,15},{2,4},{3,1},{4,6},{5,3},{6,8},{7,5},{8,10},{9,7},{10,... | collective-permute-start | bytes 1572872 | tf_op jit(solution)/shard_map/ppermute | solution.py:334
  83.0 5.0 %collective-permute-start.4 = (f32[512,256]{1,0:T(8,128)S(1)}, f32[512,256]{1,0:T(8,128)}, u32[]{:S(2)}, u32[]{:S(2)}) collective-permute-start(f32[512,256]{1,0:T(8,128)S(1)} %hop.6), channel_id=1, source_target_pairs={{0,2},{1,15},{2,4},{3,1},{4,6},{5,3},{6,8},{7,5},{8,10},{9,7},{10,... | collective-permute-start | bytes 1572872 | tf_op jit(solution)/shard_map/ppermute | solution.py:334
  88.6 5.0 %collective-permute-start.8 = (f32[512,256]{1,0:T(8,128)S(1)}, f32[512,256]{1,0:T(8,128)S(1)}, u32[]{:S(2)}, u32[]{:S(2)}) collective-permute-start(f32[512,256]{1,0:T(8,128)S(1)} %hop.8), channel_id=1, source_target_pairs={{0,2},{1,15},{2,4},{3,1},{4,6},{5,3},{6,8},{7,5},{8,10},{9,7},{10,... | collective-permute-start | bytes 1572872 | tf_op jit(solution)/shard_map/ppermute | solution.py:334
  94.1 1.3 %turn.1 = (f32[512,128]{1,0:T(8,128)S(1)}, f32[512,128]{1,0:T(8,128)S(1)}) custom-call(s32[4]{0:T(128)S(1)} %add_convert_fusion.starts_ref, f32[512,256]{1,0:T(8,128)} %collective-permute-done.4.sums_ref, bf16[512,256]{1,0:T(8,128)(2,1)S(1)} %get-tuple-element.36.rows_ref, bf16[8,256,256]{2,1,0:T(8,128)(2,1)S(1)} %join_weight.1.weights_ref), custom_call_target="tpu_custom_call" | custom-call | tf_op jit(solution)/shard_map/turn/pallas_call | solution.py:270
  95.4 6.0 %collective-permute-start.5 = (f32[512,128]{1,0:T(8,128)S(1)}, f32[512,128]{1,0:T(8,128)S(1)}, u32[]{:S(2)}, u32[]{:S(2)}) collective-permute-start(f32[512,128]{1,0:T(8,128)S(1)} %get-tuple-element.37), channel_id=1, source_target_pairs={{0,1},{1,0},{2,3},{3,2},{4,5},{5,4},{6,7},{7,6},{8,9},{9,8},{10,11... | collective-permute-start | bytes 786440 | tf_op jit(solution)/shard_map/ppermute | solution.py:191
  101.7 3.4 %collective-permute-start.10 = (f32[512,128]{1,0:T(8,128)S(1)}, f32[512,128]{1,0:T(8,128)S(1)}, u32[]{:S(2)}, u32[]{:S(2)}) collective-permute-start(f32[512,128]{1,0:T(8,128)S(1)} %get-tuple-element.41), channel_id=1, source_target_pairs={{0,3},{1,14},{2,5},{3,0},{4,7},{5,2},{6,9},{7,4},{8,11},{9,6},{10,... | collective-permute-start | bytes 786440 | tf_op jit(solution)/shard_map/ppermute | solution.py:338
  105.1 3.0 %collective-permute-start.9 = (f32[512,128]{1,0:T(8,128)S(1)}, f32[512,128]{1,0:T(8,128)S(1)}, u32[]{:S(2)}, u32[]{:S(2)}) collective-permute-start(f32[512,128]{1,0:T(8,128)S(1)} %get-tuple-element.42), channel_id=1, source_target_pairs={{0,2},{1,15},{2,4},{3,1},{4,6},{5,3},{6,8},{7,5},{8,10},{9,7},{10,... | collective-permute-start | bytes 786440 | tf_op jit(solution)/shard_map/ppermute | solution.py:339
  108.4 2.2 %collective-permute-done.10.two_b = f32[512,128]{1,0:T(8,128)S(1)} collective-permute-done((f32[512,128]{1,0:T(8,128)S(1)}, f32[512,128]{1,0:T(8,128)S(1)}, u32[]{:S(2)}, u32[]{:S(2)}) %collective-permute-start.10) | collective-permute-done | bytes 262176 | tf_op jit(solution)/shard_map/ppermute | solution.py:338
  110.6 3.5 %collective-permute-done.9.one_b = f32[512,128]{1,0:T(8,128)S(1)} collective-permute-done((f32[512,128]{1,0:T(8,128)S(1)}, f32[512,128]{1,0:T(8,128)S(1)}, u32[]{:S(2)}, u32[]{:S(2)}) %collective-permute-start.9) | collective-permute-done | bytes 262176 | tf_op jit(solution)/shard_map/ppermute | solution.py:339
  114.1 0.8 finish.1
  (29 shorter events, 4.1 us)
Async XLA Ops:
  0.0 2.1 %copy-start = (bf16[128,2048]{1,0:T(8,128)(2,1)S(1)}, bf16[128,2048]{1,0:T(8,128)(2,1)}, u32[]{:S(2)}) copy-start(bf16[128,2048]{1,0:T(8,128)(2,1)} %own_ref) | copy-start | bytes 1572868
  2.2 16.4 %collective-permute-start = (f32[128,2048]{1,0:T(8,128)S(1)}, f32[128,2048]{1,0:T(8,128)S(1)}, u32[]{:S(2)}, u32[]{:S(2)}) collective-permute-start(f32[128,2048]{1,0:T(8,128)S(1)} %convert_element_type.28), channel_id=1, source_target_pairs={{0,1},{1,0},{2,3},{3,2},{4,5},{5,4},{6,7},{7,6},{8,9},{9,8},{10,11... | collective-permute-start | bytes 3145736 | tf_op jit(solution)/shard_map/ppermute | solution.py:191
  11.0 16.7 %all-to-all-start = ((f32[32,8,128]{2,1,0:T(8,128)}), f32[32,8,128]{2,1,0:T(8,128)S(1)}, u32[]{:S(2)}, u32[]{:S(2)}) async-start(f32[32,8,128]{2,1,0:T(8,128)} %bitcast.2), calls=%async_computation | async-start | bytes 262144 | tf_op jit(solution)/shard_map/all_to_all | solution.py:354
  18.6 23.5 %copy-start.3 = (bf16[1024,128]{1,0:T(8,128)(2,1)S(1)}, bf16[1024,128]{1,0:T(8,128)(2,1)}, u32[]{:S(2)}) copy-start(bf16[1024,128]{1,0:T(8,128)(2,1)} %get-tuple-element.28.k_ref) | copy-start | bytes 786436
  18.6 23.5 %copy-start.4 = (f32[128,128]{1,0:T(8,128)S(1)}, f32[128,128]{1,0:T(8,128)}, u32[]{:S(2)}) copy-start(f32[128,128]{1,0:T(8,128)} %get-tuple-element.30.column_ref) | copy-start | bytes 196612
  18.7 23.4 %copy-start.1 = (bf16[1024,1,128]{2,0,1:T(8,128)(2,1)S(1)}, bf16[1024,1,128]{2,0,1:T(8,128)(2,1)}, u32[]{:S(2)}) copy-start(bf16[1024,1,128]{2,0,1:T(8,128)(2,1)} %param.9) | copy-start | bytes 786436
  18.8 23.4 %copy-start.2 = (bf16[1024,1,128]{2,0,1:T(8,128)(2,1)S(1)}, bf16[1024,1,128]{2,0,1:T(8,128)(2,1)}, u32[]{:S(2)}) copy-start(bf16[1024,1,128]{2,0,1:T(8,128)(2,1)} %param.7) | copy-start | bytes 786436
  28.4 13.7 %all-to-all-start.1 = ((f32[32,8,128]{2,1,0:T(8,128)}), f32[32,8,128]{2,1,0:T(8,128)S(1)}, u32[]{:S(2)}, u32[]{:S(2)}) async-start(f32[32,8,128]{2,1,0:T(8,128)} %prefix.1), calls=%async_computation.1 | async-start | bytes 262144 | tf_op jit(solution)/shard_map/all_to_all | solution.py:365
  53.3 6.0 %collective-permute-start.1 = (f32[1024,128]{1,0:T(8,128)S(1)}, f32[1024,128]{1,0:T(8,128)S(1)}, u32[]{:S(2)}, u32[]{:S(2)}) collective-permute-start(f32[1024,128]{1,0:T(8,128)S(1)} %solve.1.own_ref), channel_id=1, source_target_pairs={{0,1},{1,0},{2,3},{3,2},{4,5},{5,4},{6,7},{7,6},{8,9},{9,8},{10,11... | collective-permute-start | bytes 1572872 | tf_op jit(solution)/shard_map/ppermute | solution.py:191
  60.1 11.2 %collective-permute-start.2 = (f32[512,256]{1,0:T(8,128)S(1)}, f32[512,256]{1,0:T(8,128)S(1)}, u32[]{:S(2)}, u32[]{:S(2)}) collective-permute-start(f32[512,256]{1,0:T(8,128)S(1)} %get-tuple-element.35), channel_id=1, source_target_pairs={{0,2},{1,15},{2,4},{3,1},{4,6},{5,3},{6,8},{7,5},{8,10},{9,7},{10,... | collective-permute-start | bytes 1572872 | tf_op jit(solution)/shard_map/ppermute | solution.py:334
  65.3 11.7 %collective-permute-start.6 = (f32[512,256]{1,0:T(8,128)S(1)}, f32[512,256]{1,0:T(8,128)S(1)}, u32[]{:S(2)}, u32[]{:S(2)}) collective-permute-start(f32[512,256]{1,0:T(8,128)S(1)} %get-tuple-element.39), channel_id=1, source_target_pairs={{0,2},{1,15},{2,4},{3,1},{4,6},{5,3},{6,8},{7,5},{8,10},{9,7},{10,... | collective-permute-start | bytes 1572872 | tf_op jit(solution)/shard_map/ppermute | solution.py:334
  71.6 11.1 %collective-permute-start.3 = (f32[512,256]{1,0:T(8,128)S(1)}, f32[512,256]{1,0:T(8,128)S(1)}, u32[]{:S(2)}, u32[]{:S(2)}) collective-permute-start(f32[512,256]{1,0:T(8,128)S(1)} %hop.5), channel_id=1, source_target_pairs={{0,2},{1,15},{2,4},{3,1},{4,6},{5,3},{6,8},{7,5},{8,10},{9,7},{10,... | collective-permute-start | bytes 1572872 | tf_op jit(solution)/shard_map/ppermute | solution.py:334
  77.2 11.1 %collective-permute-start.7 = (f32[512,256]{1,0:T(8,128)S(1)}, f32[512,256]{1,0:T(8,128)S(1)}, u32[]{:S(2)}, u32[]{:S(2)}) collective-permute-start(f32[512,256]{1,0:T(8,128)S(1)} %hop.7), channel_id=1, source_target_pairs={{0,2},{1,15},{2,4},{3,1},{4,6},{5,3},{6,8},{7,5},{8,10},{9,7},{10,... | collective-permute-start | bytes 1572872 | tf_op jit(solution)/shard_map/ppermute | solution.py:334
  83.0 11.1 %collective-permute-start.4 = (f32[512,256]{1,0:T(8,128)S(1)}, f32[512,256]{1,0:T(8,128)}, u32[]{:S(2)}, u32[]{:S(2)}) collective-permute-start(f32[512,256]{1,0:T(8,128)S(1)} %hop.6), channel_id=1, source_target_pairs={{0,2},{1,15},{2,4},{3,1},{4,6},{5,3},{6,8},{7,5},{8,10},{9,7},{10,... | collective-permute-start | bytes 1572872 | tf_op jit(solution)/shard_map/ppermute | solution.py:334
  88.6 12.8 %collective-permute-start.8 = (f32[512,256]{1,0:T(8,128)S(1)}, f32[512,256]{1,0:T(8,128)S(1)}, u32[]{:S(2)}, u32[]{:S(2)}) collective-permute-start(f32[512,256]{1,0:T(8,128)S(1)} %hop.8), channel_id=1, source_target_pairs={{0,2},{1,15},{2,4},{3,1},{4,6},{5,3},{6,8},{7,5},{8,10},{9,7},{10,... | collective-permute-start | bytes 1572872 | tf_op jit(solution)/shard_map/ppermute | solution.py:334
  95.4 12.9 %collective-permute-start.5 = (f32[512,128]{1,0:T(8,128)S(1)}, f32[512,128]{1,0:T(8,128)S(1)}, u32[]{:S(2)}, u32[]{:S(2)}) collective-permute-start(f32[512,128]{1,0:T(8,128)S(1)} %get-tuple-element.37), channel_id=1, source_target_pairs={{0,1},{1,0},{2,3},{3,2},{4,5},{5,4},{6,7},{7,6},{8,9},{9,8},{10,11... | collective-permute-start | bytes 786440 | tf_op jit(solution)/shard_map/ppermute | solution.py:191
  101.7 8.9 %collective-permute-start.10 = (f32[512,128]{1,0:T(8,128)S(1)}, f32[512,128]{1,0:T(8,128)S(1)}, u32[]{:S(2)}, u32[]{:S(2)}) collective-permute-start(f32[512,128]{1,0:T(8,128)S(1)} %get-tuple-element.41), channel_id=1, source_target_pairs={{0,3},{1,14},{2,5},{3,0},{4,7},{5,2},{6,9},{7,4},{8,11},{9,6},{10,... | collective-permute-start | bytes 786440 | tf_op jit(solution)/shard_map/ppermute | solution.py:338
  105.1 9.0 %collective-permute-start.9 = (f32[512,128]{1,0:T(8,128)S(1)}, f32[512,128]{1,0:T(8,128)S(1)}, u32[]{:S(2)}, u32[]{:S(2)}) collective-permute-start(f32[512,128]{1,0:T(8,128)S(1)} %get-tuple-element.42), channel_id=1, source_target_pairs={{0,2},{1,15},{2,4},{3,1},{4,6},{5,3},{6,8},{7,5},{8,10},{9,7},{10,... | collective-permute-start | bytes 786440 | tf_op jit(solution)/shard_map/ppermute | solution.py:339
